TPU v7x, 32 devices: a whole 2x2x4 slice. The times are simulated.
32 devices in a mesh: dp: 2 (over core), fsdp: 16 (over z, y, x).
Axes of the slice: x: 2, y: 2, z: 4, core: 2. Of those that a mesh axis runs over, the one named last changes fastest.
Arguments:
- latents: float32 [32, 576, 1536], P(('dp', 'fsdp')), may hold values from -6 to 6
- text_embed: bfloat16 [32, 4, 77, 1280], P(('dp', 'fsdp')), may hold values from -6 to 6
- time_embed: float32 [32, 4, 64], P(('dp', 'fsdp')), may hold values from -6 to 6
- heights: int32 [32, 4], P(('dp', 'fsdp')), may hold values from 0 to 24, as said below
- widths: int32 [32, 4], P(('dp', 'fsdp')), may hold values from 0 to 24, as said below
- text_counts: int32 [32, 4], P(('dp', 'fsdp')), may hold values from 1 to 77
- res_vecs: float32 [11, 1536], P(None, ('dp', 'fsdp')), may hold values from -4 to 4
- fc1_w: float32 [1536, 6144], P(None, ('dp', 'fsdp')), may hold values from -0.15625 to 0.15625
- ff_vecs: float32 [3, 6144], P(None, ('dp', 'fsdp')), may hold values from -4 to 4
- fc2_w: float32 [6144, 1536], P(('dp', 'fsdp')), may hold values from -0.078125 to 0.078125
- time_w: float32 [64, 3072], P(None, ('dp', 'fsdp')), may hold values from -0.375 to 0.375
- time_b: float32 [3072], P(('dp', 'fsdp')), may hold values from -4 to 4
- kv_w: float32 [1280, 1536], P(('dp', 'fsdp')), may hold values from -0.15625 to 0.15625
- attn_w: float32 [1536, 6144], P(None, ('dp', 'fsdp'))
- attn_vecs: float32 [4, 1536], P(None, ('dp', 'fsdp')), may hold values from -4 to 4
- cotangent: float32 [32, 576, 1536], P(('dp', 'fsdp')), may hold values from -6 to 6
Outputs:
- output: float32 [32, 576, 1536], P(('dp', 'fsdp'))
- latents_grad: float32 [32, 576, 1536], P(('dp', 'fsdp'))
- text_grad: float32 [32, 4, 77, 1280], P(('dp', 'fsdp'))
- res_vecs_grad: float32 [11, 1536], P(None, ('dp', 'fsdp'))
- fc1_w_grad: float32 [1536, 6144], P(None, ('dp', 'fsdp'))
- ff_vecs_grad: float32 [3, 6144], P(None, ('dp', 'fsdp'))
- fc2_w_grad: float32 [6144, 1536], P(('dp', 'fsdp'))
- time_w_grad: float32 [64, 3072], P(None, ('dp', 'fsdp'))
- time_b_grad: float32 [3072], P(('dp', 'fsdp'))
- kv_w_grad: float32 [1280, 1536], P(('dp', 'fsdp'))
- attn_w_grad: float32 [1536, 6144], P(None, ('dp', 'fsdp'))
- attn_vecs_grad: float32 [4, 1536], P(None, ('dp', 'fsdp'))
Inputs may be any that keep to these rules, and one draw needn't show every extreme that they name: `heights`: each packed row holds its latents end to end from slot 0 in the order of the latent places; a present latent has height and width each one of 12, 16, 24; an absent one has height and width 0 and may stand before present ones; the pixels of a row never exceed 576. `widths`: A width is 0 exactly where the height is 0.
All inputs are finite; a program needn't handle non-finite values.
Results may differ from a plain program's by a relative error of at most 0.012.
The roundings to bfloat16 on the way count: a program that leaves them out, or rounds other values in their place, can miss the bound.
Values may be sent and summed in bfloat16 or wider, within the bound.
No kernel may reach another device: no remote copies, remote signals or barrier semaphores. Data moves between devices by JAX's collectives and lax.ppermute only.
A program may use at most 448 MiB of HBM per device.

v0:
```python
import jax
import jax.numpy as jnp
from jax import lax
from jax.sharding import PartitionSpec as P

HEADS = 24
TEXT = 77
SIDE_UNIT = 4
SLOTS = 576
LAT_ROW = 4


HIGHEST = lax.Precision.HIGHEST
NORM_EPS = 1e-06
MASKED = -1000000000.0


def layout(heights_row, widths_row):
    pixels = heights_row * widths_row
    ends_at = jnp.cumsum(pixels)
    starts_at = ends_at - pixels
    slot_ids = jnp.arange(SLOTS, dtype=jnp.int32)
    segment = jnp.sum((ends_at[None, :] <= slot_ids[:, None]).astype(jnp.int32), axis=1)
    member = segment[:, None] == jnp.arange(LAT_ROW, dtype=jnp.int32)[None, :]
    start_at = jnp.sum(jnp.where(member, starts_at[None, :], 0), axis=1)
    height_at = jnp.sum(jnp.where(member, heights_row[None, :], 0), axis=1)
    width_at = jnp.sum(jnp.where(member, widths_row[None, :], 0), axis=1)
    place_in = slot_ids - start_at
    safe_width = jnp.maximum(width_at, 1)
    column = place_in % safe_width
    row_index = place_in // safe_width
    return (segment, member, height_at, width_at, row_index, column)


def layer_norm(values):
    center = values - jnp.mean(values, axis=-1, keepdims=True)
    return center * lax.rsqrt(jnp.mean(center * center, axis=-1, keepdims=True) + NORM_EPS)


def depthwise(values, conv_taps, conv_bias, geometry):
    segment, member, height_at, width_at, row_index, column = geometry
    live_query = segment < LAT_ROW
    margin = 6 * SIDE_UNIT + 1
    padded = jnp.pad(values, ((0, 0), (margin, margin), (0, 0)))
    result = jnp.zeros_like(values) + conv_bias
    for step_y in (-1, 0, 1):
        for step_x in (-1, 0, 1):
            inside = live_query & (row_index + step_y >= 0) & (row_index + step_y < height_at)
            inside = inside & (column + step_x >= 0) & (column + step_x < width_at)
            weight_row = conv_taps[(step_y + 1) * 3 + step_x + 1]
            side_list = (1,) if step_y == 0 else (3 * SIDE_UNIT, 4 * SIDE_UNIT, 6 * SIDE_UNIT)
            for side_len in side_list:
                offset = step_y * side_len + step_x
                chosen = inside if step_y == 0 else inside & (width_at == side_len)
                shifted = lax.slice_in_dim(padded, margin + offset, margin + offset + SLOTS, axis=1)
                result = result + jnp.where(chosen[..., None], shifted, 0.0) * weight_row
    return result


def response_norm(hidden, grn_gain, grn_shift, onehot):
    active = jax.nn.gelu(hidden, approximate=False)
    power = jnp.einsum("rsl,rsf->rlf", onehot, active * active, precision=HIGHEST)
    global_norm = jnp.sqrt(power + NORM_EPS)
    scaled = global_norm / (jnp.mean(global_norm, axis=2, keepdims=True) + NORM_EPS)
    spread = jnp.einsum("rsl,rlf->rsf", onehot, scaled, precision=HIGHEST)
    return grn_gain * (active * spread) + grn_shift + active


def timestep(after_res, time_pair, onehot):
    per_slot = jnp.einsum("rsl,rlc->rsc", onehot, time_pair, precision=HIGHEST)
    half_width = time_pair.shape[-1] // 2
    return after_res + after_res * per_slot[..., :half_width] + per_slot[..., half_width:]


def attention_mask(segment, counts_row):
    live_query = segment < LAT_ROW
    image_ok = (segment[:, None] == segment[None, :]) & live_query[:, None]
    text_index = jnp.arange(LAT_ROW * TEXT, dtype=jnp.int32)
    text_latent = text_index // TEXT
    text_limit = jnp.sum(
        jnp.where(
            text_latent[:, None] == jnp.arange(LAT_ROW, dtype=jnp.int32)[None, :],
            counts_row[None, :],
            0,
        ),
        axis=1,
    )
    text_ok = (text_latent[None, :] == segment[:, None]) & (text_index % TEXT < text_limit)[None, :]
    return jnp.concatenate([image_ok, text_ok], axis=1)


def local(
    latents,
    text_embed,
    time_embed,
    heights,
    widths,
    text_counts,
    res_vecs,
    fc1_w,
    ff_vecs,
    fc2_w,
    time_w,
    time_b,
    kv_w,
    attn_w,
    attn_vecs,
    cotangent,
):
    half_type = jnp.bfloat16
    res_owned = (
        res_vecs.astype(half_type),
        fc1_w.astype(half_type),
        ff_vecs.astype(half_type),
        fc2_w.astype(half_type),
    )
    mid_owned = (
        time_w.astype(half_type),
        time_b.astype(half_type),
        kv_w.astype(half_type),
        attn_w.astype(half_type),
        attn_vecs.astype(half_type),
    )
    res_full = (
        lax.all_gather(res_owned[0], ("dp", "fsdp"), axis=1, tiled=True),
        lax.all_gather(res_owned[1], ("dp", "fsdp"), axis=1, tiled=True),
        lax.all_gather(res_owned[2], ("dp", "fsdp"), axis=1, tiled=True),
        lax.all_gather(res_owned[3], ("dp", "fsdp"), axis=0, tiled=True),
    )
    mid_full = (
        lax.all_gather(mid_owned[0], ("dp", "fsdp"), axis=1, tiled=True),
        lax.all_gather(mid_owned[1], ("dp", "fsdp"), axis=0, tiled=True),
        lax.all_gather(mid_owned[2], ("dp", "fsdp"), axis=0, tiled=True),
        lax.all_gather(mid_owned[3], ("dp", "fsdp"), axis=1, tiled=True),
        lax.all_gather(mid_owned[4], ("dp", "fsdp"), axis=1, tiled=True),
    )
    row_count, slot_count, model_width = latents.shape
    cond_width = text_embed.shape[3]
    head_dim = model_width // HEADS
    group_heads = 4
    group_count = HEADS // group_heads
    score_scale = head_dim ** (-0.5)
    geometry = jax.vmap(layout)(heights, widths)
    segment = geometry[0]
    onehot = geometry[1].astype(jnp.float32)
    live_mask = (segment < LAT_ROW).astype(jnp.float32)[..., None]
    key_masks = jax.vmap(attention_mask)(segment, text_counts)
    res_vals = res_full[0].astype(jnp.float32)
    ff_vals = res_full[2].astype(jnp.float32)

    def res_entry(values, conv_taps, conv_bias):
        return layer_norm(depthwise(values, conv_taps, conv_bias, geometry))

    normed, res_entry_back = jax.vjp(res_entry, latents, res_vals[:9], res_vals[9])
    normed_low = normed.astype(half_type)
    hidden = (
        jnp.einsum("rsc,cf->rsf", normed_low, res_full[1], preferred_element_type=jnp.float32)
        + ff_vals[0]
    )

    def grn_piece(hidden_in, grn_gain, grn_shift):
        return response_norm(hidden_in, grn_gain, grn_shift, onehot)

    response, grn_back = jax.vjp(grn_piece, hidden, ff_vals[1], ff_vals[2])
    response_low = response.astype(half_type)
    branch = (
        jnp.einsum("rsf,fc->rsc", response_low, res_full[3], preferred_element_type=jnp.float32)
        + res_vals[10]
    )
    after_res = latents + live_mask * branch
    mid_vals = mid_full[4].astype(jnp.float32)
    time_low = time_embed.astype(half_type)
    time_pair = jnp.einsum(
        "rlt,tc->rlc", time_low, mid_full[0], preferred_element_type=jnp.float32
    ) + mid_full[1].astype(jnp.float32)

    def time_piece(after_in, pair_in):
        return timestep(after_in, pair_in, onehot)

    after_time, time_back = jax.vjp(time_piece, after_res, time_pair)
    normed_two, norm_two_back = jax.vjp(layer_norm, after_time)
    normed_two_low = normed_two.astype(half_type)
    text_flat = text_embed.astype(jnp.float32).reshape(row_count, LAT_ROW * TEXT, cond_width)
    silu_text, silu_back = jax.vjp(jax.nn.silu, text_flat)
    silu_low = silu_text.astype(half_type)
    mapped_low = (
        jnp.einsum("rtk,kc->rtc", silu_low, mid_full[2], preferred_element_type=jnp.float32)
        + mid_vals[3]
    ).astype(half_type)
    source_low = jnp.concatenate([normed_two_low, mapped_low], axis=1)
    attn_full = mid_full[3]
    query_low = (
        jnp.einsum(
            "rsc,cd->rsd",
            normed_two_low,
            attn_full[:, :model_width],
            preferred_element_type=jnp.float32,
        )
        + mid_vals[0]
    ).astype(half_type)
    key_value = jnp.einsum(
        "rkc,cd->rkd",
        source_low,
        attn_full[:, model_width : 3 * model_width],
        preferred_element_type=jnp.float32,
    )
    key_low = key_value[..., :model_width].astype(half_type)
    value_low = (key_value[..., model_width:] + mid_vals[1]).astype(half_type)

    def by_groups(values):
        return values.reshape(
            values.shape[0], values.shape[1], group_count, group_heads * head_dim
        ).transpose(0, 2, 1, 3)

    def from_groups(values):
        return values.transpose(0, 2, 1, 3).reshape(values.shape[0], values.shape[2], model_width)

    query_groups = by_groups(query_low)
    key_groups = by_groups(key_low)
    value_groups = by_groups(value_low)

    def group_scores(query_part, key_part, mask_row):
        query_heads = query_part.reshape(-1, group_heads, head_dim)
        key_heads = key_part.reshape(-1, group_heads, head_dim)
        scores = (
            jnp.einsum("qhd,khd->hqk", query_heads, key_heads, preferred_element_type=jnp.float32)
            * score_scale
        )
        return jnp.where(mask_row[None], scores, MASKED)

    def attend_row(row_input):
        query_row, key_row, value_row, mask_row = row_input

        def attend_group(group_input):
            query_part, key_part, value_part = group_input
            scores = group_scores(query_part, key_part, mask_row)
            row_peak = jnp.max(scores, axis=2, keepdims=True)
            exponent = jnp.exp(scores - row_peak)
            row_total = jnp.sum(exponent, axis=2, keepdims=True)
            weights_low = (exponent / row_total).astype(half_type)
            value_heads = value_part.reshape(-1, group_heads, head_dim)
            attended_part = jnp.einsum(
                "hqk,khd->qhd", weights_low, value_heads, preferred_element_type=jnp.float32
            )
            return (
                attended_part.reshape(attended_part.shape[0], group_heads * head_dim),
                (row_peak + jnp.log(row_total))[..., 0],
            )

        return lax.map(attend_group, (query_row, key_row, value_row))

    attended_groups, log_totals = lax.map(
        attend_row, (query_groups, key_groups, value_groups, key_masks)
    )
    attended_low = from_groups(attended_groups).astype(half_type)
    output = after_time + live_mask * (
        jnp.einsum(
            "rsc,cd->rsd",
            attended_low,
            attn_full[:, 3 * model_width :],
            preferred_element_type=jnp.float32,
        )
        + mid_vals[2]
    )
    mid_back = (
        lax.all_gather(mid_owned[0], ("dp", "fsdp"), axis=1, tiled=True),
        lax.all_gather(mid_owned[1], ("dp", "fsdp"), axis=0, tiled=True),
        lax.all_gather(mid_owned[2], ("dp", "fsdp"), axis=0, tiled=True),
        lax.all_gather(mid_owned[3], ("dp", "fsdp"), axis=1, tiled=True),
        lax.all_gather(mid_owned[4], ("dp", "fsdp"), axis=1, tiled=True),
    )
    attn_back = mid_back[3]
    grad_proj = (live_mask * cotangent).astype(half_type)
    grad_w_out = jnp.einsum(
        "rsc,rsd->cd", attended_low, grad_proj, preferred_element_type=jnp.float32
    )
    grad_bias_out = jnp.sum(grad_proj.astype(jnp.float32), axis=(0, 1))
    grad_attended = jnp.einsum(
        "rsd,cd->rsc",
        grad_proj,
        attn_back[:, 3 * model_width :],
        preferred_element_type=jnp.float32,
    ).astype(half_type)
    grad_groups = by_groups(grad_attended)

    def back_row(row_input):
        query_row, key_row, value_row, mask_row, log_row, grad_row = row_input

        def back_group(group_input):
            query_part, key_part, value_part, log_part, grad_part = group_input
            scores = group_scores(query_part, key_part, mask_row)
            probs_full = jnp.exp(scores - log_part[..., None])
            query_heads = query_part.reshape(-1, group_heads, head_dim)
            key_heads = key_part.reshape(-1, group_heads, head_dim)
            value_heads = value_part.reshape(-1, group_heads, head_dim)
            grad_heads = grad_part.reshape(-1, group_heads, head_dim)
            grad_probs = jnp.einsum(
                "qhd,khd->hqk", grad_heads, value_heads, preferred_element_type=jnp.float32
            )
            grad_value = jnp.einsum(
                "hqk,qhd->khd",
                probs_full.astype(half_type),
                grad_heads,
                preferred_element_type=jnp.float32,
            )
            inner_sum = jnp.sum(probs_full * grad_probs, axis=2, keepdims=True)
            grad_scores = (probs_full * (grad_probs - inner_sum)).astype(half_type)
            grad_query = (
                jnp.einsum(
                    "hqk,khd->qhd", grad_scores, key_heads, preferred_element_type=jnp.float32
                )
                * score_scale
            )
            grad_key = (
                jnp.einsum(
                    "hqk,qhd->khd", grad_scores, query_heads, preferred_element_type=jnp.float32
                )
                * score_scale
            )
            flat_width = group_heads * head_dim
            return (
                grad_query.reshape(-1, flat_width).astype(half_type),
                grad_key.reshape(-1, flat_width).astype(half_type),
                grad_value.reshape(-1, flat_width).astype(half_type),
            )

        return lax.map(back_group, (query_row, key_row, value_row, log_row, grad_row))

    grad_query_g, grad_key_g, grad_value_g = lax.map(
        back_row, (query_groups, key_groups, value_groups, key_masks, log_totals, grad_groups)
    )
    grad_query = from_groups(grad_query_g)
    grad_kv = jnp.concatenate([from_groups(grad_key_g), from_groups(grad_value_g)], axis=2)
    grad_w_query = jnp.einsum(
        "rsc,rsd->cd", normed_two_low, grad_query, preferred_element_type=jnp.float32
    )
    grad_bias_query = jnp.sum(grad_query.astype(jnp.float32), axis=(0, 1))
    grad_w_kv = jnp.einsum("rkc,rkd->cd", source_low, grad_kv, preferred_element_type=jnp.float32)
    grad_bias_value = jnp.sum(grad_kv[..., model_width:].astype(jnp.float32), axis=(0, 1))
    grad_source = jnp.einsum(
        "rkd,cd->rkc",
        grad_kv,
        attn_back[:, model_width : 3 * model_width],
        preferred_element_type=jnp.float32,
    )
    grad_normed_two = (
        jnp.einsum(
            "rsd,cd->rsc",
            grad_query,
            attn_back[:, :model_width],
            preferred_element_type=jnp.float32,
        )
        + grad_source[:, :slot_count]
    )
    grad_mapped = grad_source[:, slot_count:].astype(half_type)
    grad_kv_w = jnp.einsum("rtk,rtc->kc", silu_low, grad_mapped, preferred_element_type=jnp.float32)
    grad_bias_kv = jnp.sum(grad_mapped.astype(jnp.float32), axis=(0, 1))
    grad_silu = jnp.einsum(
        "rtc,kc->rtk", grad_mapped, mid_back[2], preferred_element_type=jnp.float32
    )
    text_grad = silu_back(grad_silu)[0].reshape(row_count, LAT_ROW, TEXT, cond_width)
    grad_time = cotangent + norm_two_back(grad_normed_two)[0]
    grad_after_res, grad_pair = time_back(grad_time)
    grad_time_w = jnp.einsum(
        "rlt,rlc->tc", time_low.astype(jnp.float32), grad_pair, precision=HIGHEST
    )
    grad_time_b = jnp.sum(grad_pair, axis=(0, 1))
    grad_attn_w = jnp.concatenate([grad_w_query, grad_w_kv, grad_w_out], axis=1)
    grad_attn_vecs = jnp.stack([grad_bias_query, grad_bias_value, grad_bias_out, grad_bias_kv])
    mid_terms = (grad_time_w, grad_time_b, grad_kv_w, grad_attn_w, grad_attn_vecs)
    mid_grads = (
        lax.psum_scatter(mid_terms[0], ("dp", "fsdp"), scatter_dimension=1, tiled=True),
        lax.psum_scatter(mid_terms[1], ("dp", "fsdp"), scatter_dimension=0, tiled=True),
        lax.psum_scatter(mid_terms[2], ("dp", "fsdp"), scatter_dimension=0, tiled=True),
        lax.psum_scatter(mid_terms[3], ("dp", "fsdp"), scatter_dimension=1, tiled=True),
        lax.psum_scatter(mid_terms[4], ("dp", "fsdp"), scatter_dimension=1, tiled=True),
    )
    res_back = (
        lax.all_gather(res_owned[0], ("dp", "fsdp"), axis=1, tiled=True),
        lax.all_gather(res_owned[1], ("dp", "fsdp"), axis=1, tiled=True),
        lax.all_gather(res_owned[2], ("dp", "fsdp"), axis=1, tiled=True),
        lax.all_gather(res_owned[3], ("dp", "fsdp"), axis=0, tiled=True),
    )
    grad_branch = (live_mask * grad_after_res).astype(half_type)
    grad_fc2 = jnp.einsum(
        "rsf,rsc->fc", response_low, grad_branch, preferred_element_type=jnp.float32
    )
    grad_fc2_bias = jnp.sum(grad_branch.astype(jnp.float32), axis=(0, 1))
    grad_response = jnp.einsum(
        "rsc,fc->rsf", grad_branch, res_back[3], preferred_element_type=jnp.float32
    )
    grad_hidden, grad_gain, grad_shift = grn_back(grad_response)
    grad_hidden_low = grad_hidden.astype(half_type)
    grad_fc1 = jnp.einsum(
        "rsc,rsf->cf", normed_low, grad_hidden_low, preferred_element_type=jnp.float32
    )
    grad_fc1_bias = jnp.sum(grad_hidden_low.astype(jnp.float32), axis=(0, 1))
    grad_normed = jnp.einsum(
        "rsf,cf->rsc", grad_hidden_low, res_back[1], preferred_element_type=jnp.float32
    )
    grad_entry, grad_taps, grad_conv_bias = res_entry_back(grad_normed)
    latents_grad = grad_after_res + grad_entry
    grad_res_vecs = jnp.concatenate([grad_taps, grad_conv_bias[None], grad_fc2_bias[None]], axis=0)
    grad_ff_vecs = jnp.stack([grad_fc1_bias, grad_gain, grad_shift])
    res_terms = (grad_res_vecs, grad_fc1, grad_ff_vecs, grad_fc2)
    res_grads = (
        lax.psum_scatter(res_terms[0], ("dp", "fsdp"), scatter_dimension=1, tiled=True),
        lax.psum_scatter(res_terms[1], ("dp", "fsdp"), scatter_dimension=1, tiled=True),
        lax.psum_scatter(res_terms[2], ("dp", "fsdp"), scatter_dimension=1, tiled=True),
        lax.psum_scatter(res_terms[3], ("dp", "fsdp"), scatter_dimension=0, tiled=True),
    )
    return (
        output,
        latents_grad,
        text_grad,
        res_grads[0],
        res_grads[1],
        res_grads[2],
        res_grads[3],
        mid_grads[0],
        mid_grads[1],
        mid_grads[2],
        mid_grads[3],
        mid_grads[4],
    )


def solution(mesh):
    return jax.shard_map(
        local,
        mesh=mesh,
        in_specs=(
            P(("dp", "fsdp"), None, None),
            P(("dp", "fsdp"), None, None, None),
            P(("dp", "fsdp"), None, None),
            P(("dp", "fsdp"), None),
            P(("dp", "fsdp"), None),
            P(("dp", "fsdp"), None),
            P(None, ("dp", "fsdp")),
            P(None, ("dp", "fsdp")),
            P(None, ("dp", "fsdp")),
            P(("dp", "fsdp"), None),
            P(None, ("dp", "fsdp")),
            P(("dp", "fsdp")),
            P(("dp", "fsdp"), None),
            P(None, ("dp", "fsdp")),
            P(None, ("dp", "fsdp")),
            P(("dp", "fsdp"), None, None),
        ),
        out_specs=(
            P(("dp", "fsdp"), None, None),
            P(("dp", "fsdp"), None, None),
            P(("dp", "fsdp"), None, None, None),
            P(None, ("dp", "fsdp")),
            P(None, ("dp", "fsdp")),
            P(None, ("dp", "fsdp")),
            P(("dp", "fsdp"), None),
            P(None, ("dp", "fsdp")),
            P(("dp", "fsdp")),
            P(("dp", "fsdp"), None),
            P(None, ("dp", "fsdp")),
            P(None, ("dp", "fsdp")),
        ),
        check_vma=False,
    )
```

profile of v0, /device:TPU:0, one launch (start us, length us, event | category | flops | bytes accessed | tf_op | source)
XLA Modules:
  0.0 2449.8 jit_solution(15124512196969596615)
XLA Ops:
  13.8 42.1 %all-reduce.33 = bf16[3072]{0:T(1024)(128)(2,1)S(1)} all-reduce(bf16[3072]{0:T(1024)(128)(2,1)S(1)} %dynamic-update-slice), channel_id=1, replica_groups=mesh['dp'=2,'fsdp'=16] {'dp','fsdp'}, use_global_device_ids=true, to_apply=%add.33 | all-reduce | flops 3072 | bytes 12288
  56.6 66.4 %all-gather.3 = bf16[32,48,4]{1,2,0:T(4,128)(2,1)S(1)} all-gather(bf16[1,48,4]{1,2,0:T(4,128)(2,1)S(1)} %convert_bitcast_fusion.3), channel_id=1, replica_groups=mesh['dp'=2,'fsdp'=16] {'dp','fsdp'}, dimensions={0}, use_global_device_ids=true | all-gather | bytes 12672 | tf_op jit(solution)/shard_map/all_gather | solution.py:135
  123.8 65.5 %all-gather = bf16[32,192,3]{1,2,0:T(4,128)(2,1)S(1)} all-gather(bf16[1,192,3]{1,2,0:T(4,128)(2,1)S(1)} %convert_bitcast_fusion.2), channel_id=1, replica_groups=mesh['dp'=2,'fsdp'=16] {'dp','fsdp'}, dimensions={0}, use_global_device_ids=true | all-gather | bytes 38016 | tf_op jit(solution)/shard_map/all_gather | solution.py:127
  190.0 67.5 %all-gather.1 = bf16[32,48,11]{1,2,0:T(8,128)(2,1)S(1)} all-gather(bf16[1,48,11]{1,2,0:T(8,128)(2,1)S(1)} %convert_bitcast_fusion.1), channel_id=1, replica_groups=mesh['dp'=2,'fsdp'=16] {'dp','fsdp'}, dimensions={0}, use_global_device_ids=true | all-gather | bytes 34848 | tf_op jit(solution)/shard_map/all_gather | solution.py:125
  258.3 71.9 %all-gather.2 = bf16[32,96,64]{1,2,0:T(8,128)(2,1)S(1)} all-gather(bf16[1,96,64]{1,2,0:T(8,128)(2,1)S(1)} %convert_bitcast_fusion), channel_id=1, replica_groups=mesh['dp'=2,'fsdp'=16] {'dp','fsdp'}, dimensions={0}, use_global_device_ids=true | all-gather | bytes 405504 | tf_op jit(solution)/shard_map/all_gather | solution.py:131
  345.2 5.2 convolution_bitcast_fusion
  353.0 22.1 fusion.163
  379.6 5.0 fusion.86
  384.6 7.0 fusion.82
  395.5 48.1 %multiply_multiply_fusion.5 = (f32[576,6144]{1,0:T(8,128)}, f32[576,6144]{1,0:T(8,128)}, f32[576,6144]{1,0:T(8,128)}) fusion(f32[6144]{0:T(1024)} %bitcast.399, bf16[1536,6144]{0,1:T(8,128)(2,1)} %all-gather.9.cloned.1.call-done, f32[1,576,1536]{2,1,0:T(8,128)} %get-tuple-element.315, f32[576]{0:T(1024)S(1)} %copy-done.82, f32[576]{0:T(1024)S(1)} %broadcast_multiply_fusion.1), kind=kOutput, calls=%fused_computation.69 | convolution fusion | flops 11104321536 | bytes 64909824 | tf_op jit(solution)/shard_map/rsc,cf->rsf/dot_general | solution.py:157
  443.6 9.4 fusion.175
  454.1 18.7 add_convert_fusion
  472.8 20.3 fusion.159
  495.2 5.6 add_convert_fusion.1
  503.2 11.7 fusion.56
  526.9 63.0 %while.46 = (s32[]{:T(128)}, bf16[6,576,256]{1,2,0:T(8,128)(2,1)}, f32[6,4,576]{2,1,0:T(4,128)}, bf16[6,884,256]{1,2,0:T(8,128)(2,1)}, pred[576,884]{1,0:T(8,128...) while((s32[]{:T(128)}, bf16[6,576,256]{1,2,0:T(8,128)(2,1)}, ...), condition=%wide.region_14.15_spmd, body=%wide.region_11.14_spmd.sunk | while | flops 545842944 | bytes 30561132 | solution.py:250
  589.9 104.8 %while.47 = (s32[]{:T(128)}, bf16[6,576,256]{1,2,0:T(8,128)(2,1)}, bf16[6,884,256]{1,2,0:T(8,128)(2,1)}, bf16[6,884,256]{1,2,0:T(8,128)(2,1)}, bf16[6,884,256]{1...) while((s32[]{:T(128)}, bf16[6,576,256]{1,2,0:T(8,128)(2,1)}, ...), condition=%wide.region_17.18_spmd, body=%wide.region_15.17_spmd.sunk | while | flops 1335033600 | bytes 71867280 | solution.py:327
  698.1 13.1 fusion.68
  712.0 6.6 multiply_reduce_fusion.23
  720.7 4.7 fusion.156
  727.2 24.2 multiply_reduce_fusion.1
  751.4 12.7 fusion.116
  764.6 33.2 %convert_reduce_fusion = (f32[6144]{0:T(1024)}, bf16[1,576,6144]{2,1,0:T(8,128)(2,1)}) fusion(f32[576,6144]{1,0:T(8,128)} %get-tuple-element.313, s32[576]{0:T(1024)S(1)} %copy-done.32, f32[4,6144]{1,0:T(4,128)} %copy-done.29, f32[1,6144,4]{1,2,0:T(4,128)} %get-tuple-element.439, f32[4]{0:T(128)} %negate_multiply_fusion.3, f32[4]{0:T(128)} %copy-done.100, ...), kind=kOutput, calls=%fused_computation.49 | convolution fusion | flops 251359488 | bytes 78129440 | tf_op jit(solution)/shard_map/transpose(jvp(rsl,rsf->rlf))/dot_general | solution.py:62
  797.8 18.3 fusion.75
  818.5 8.7 multiply_reduce_fusion.21
  827.3 11.0 multiply_select_fusion.15
  838.4 11.4 multiply_select_fusion.6
  862.9 5.6 fusion.176
  875.2 6.9 fusion.101
  883.6 8.3 fusion.95
  892.0 6.2 fusion.92
  898.2 14.7 fusion.72
  912.9 24.6 %pad_maximum_fusion = f32[1536,6144]{1,0:T(8,128)} fusion(f32[1536,1536]{1,0:T(8,128)} %fusion.92, f32[1536,3072]{1,0:T(8,128)} %fusion.72, f32[1536,1536]{1,0:T(8,128)} %fusion.95), kind=kLoop, calls=%fused_computation.34 | loop fusion | flops 18874368 | bytes 75497472 | tf_op jit(solution)/shard_map/concatenate | solution.py:368
  937.5 37.0 %copy.101 = f32[1536,6144]{0,1:T(8,128)} copy(f32[1536,6144]{1,0:T(8,128)} %pad_maximum_fusion) | data formatting | bytes 75497472
  976.5 27.5 %fusion.39 = f32[1536,6144]{0,1:T(8,128)} fusion(bf16[1,576,6144]{2,1,0:T(8,128)(2,1)} %get-tuple-element.444, f32[1,576,1536]{2,1,0:T(8,128)S(1)} %copy-done.11, f32[576]{0:T(1024)S(1)} %copy-done.84, f32[576]{0:T(1024)S(1)} %copy-done.55), kind=kOutput, calls=%fused_computation.76 | convolution fusion | flops 10874290176 | bytes 48370176 | tf_op jit(solution)/shard_map/rsc,rsf->cf/dot_general | solution.py:394
  1005.5 22.3 fusion.88
  1029.2 5.4 fusion.99
  1041.2 37.8 %all-reduce.34 = f32[3072]{0:T(1024)} all-reduce(f32[3072]{0:T(1024)} %get-tuple-element.445), channel_id=7, replica_groups=mesh['dp'=2,'fsdp'=16] {'dp','fsdp'}, use_global_device_ids=true, to_apply=%region_55.56.clone | all-reduce | flops 3072 | bytes 24576
  1080.3 14.6 multiply_select_fusion.18
  1094.9 19.7 pad_add_fusion
  1114.6 8.4 bitcast_add_fusion
  1123.0 10.3 fusion.74
  1136.1 15.2 reduce-scatter.27.cloned.1.call-done
  1152.9 99.7 %reduce-scatter.29.cloned.1.call-done = f32[96,64]{1,0:T(8,128)} async-done(((f32[3072,64]{1,0:T(8,128)}), f32[96,64]{1,0:T(8,128)}) %reduce-scatter.29.cloned.1.call-update) | async-done | bytes 24592
  1254.1 126.2 %reduce-scatter.23.cloned.1.call-done = f32[40,1536]{1,0:T(8,128)} async-done(((f32[1280,1536]{1,0:T(8,128)}), f32[40,1536]{1,0:T(8,128)}) %reduce-scatter.23.cloned.1.call-update) | async-done | bytes 245776 | tf_op jit(solution)/shard_map/reduce_scatter | solution.py:374
  1380.3 354.6 %reduce-scatter.31.cloned.1.call-done = f32[192,1536]{1,0:T(8,128)} async-done(((f32[6144,1536]{1,0:T(8,128)}), f32[192,1536]{1,0:T(8,128)}) %reduce-scatter.31.cloned.1.call-update) | async-done | bytes 1179664
  1734.9 353.3 %reduce-scatter.19.cloned.1.call-done = f32[1536,192]{0,1:T(8,128)} async-done(((f32[1536,6144]{0,1:T(8,128)}), f32[1536,192]{0,1:T(8,128)}) %reduce-scatter.19.cloned.1.call-update) | async-done | bytes 1179664 | tf_op jit(solution)/shard_map/reduce_scatter | solution.py:408
  2088.2 354.3 %reduce-scatter.21.cloned.1.call-done = f32[192,1536]{1,0:T(8,128)} async-done(((f32[6144,1536]{1,0:T(8,128)}), f32[192,1536]{1,0:T(8,128)}) %reduce-scatter.21.cloned.1.call-update) | async-done | bytes 1179664 | tf_op jit(solution)/shard_map/reduce_scatter | solution.py:410
  (500 shorter events, 269.8 us)
Async XLA Ops:
  7.2 372.4 %all-gather.13.cloned.1.call-start = ((), (), s32[]{:S(2)}) async-start(), calls=%async_computation.10 | async-start | bytes 4055040 | tf_op jit(solution)/shard_map/all_gather | solution.py:133
  9.1 47.5 %copy-start.99 = (f32[4,48]{1,0:T(4,128)S(1)}, f32[4,48]{1,0:T(4,128)}, u32[]{:S(2)}) copy-start(f32[4,48]{1,0:T(4,128)} %param.34) | copy-start | bytes 2308
  9.1 114.7 %copy-start.98 = (f32[3,192]{1,0:T(4,128)S(1)}, f32[3,192]{1,0:T(4,128)}, u32[]{:S(2)}) copy-start(f32[3,192]{1,0:T(4,128)} %param.28) | copy-start | bytes 6916
  9.1 180.9 %copy-start.97 = (f32[11,48]{1,0:T(8,128)S(1)}, f32[11,48]{1,0:T(8,128)}, u32[]{:S(2)}) copy-start(f32[11,48]{1,0:T(8,128)} %param.26) | copy-start | bytes 6340
  9.1 375.5 %all-gather.15.cloned.1.call-start = ((), (), s32[]{:S(2)}) async-start(), calls=%async_computation.11 | async-start | bytes 19464192 | tf_op jit(solution)/shard_map/all_gather | solution.py:134
  11.3 247.0 %copy-start.64 = (f32[64,96]{1,0:T(8,128)S(1)}, f32[64,96]{1,0:T(8,128)}, u32[]{:S(2)}) copy-start(f32[64,96]{1,0:T(8,128)} %param.30) | copy-start | bytes 73732
  11.3 384.2 %all-gather.9.cloned.1.call-start = ((), (), s32[]{:S(2)}) async-start(), calls=%async_computation.8 | async-start | bytes 19464192 | tf_op jit(solution)/shard_map/all_gather | solution.py:126
  12.3 460.5 %all-gather.11.cloned.1.call-start = ((), (), s32[]{:S(2)}) async-start(), calls=%async_computation.9 | async-start | bytes 19464192 | tf_op jit(solution)/shard_map/all_gather | solution.py:128
  13.2 1120.0 %reduce-scatter.33.cloned.1.call-start = ((), (), s32[]{:S(2)}) async-start(), calls=%async_computation.19 | async-start | bytes 811008
  13.4 316.9 %copy-start.112 = (s32[1,4]{1,0:T(1,128)}, s32[1,4]{1,0:T(1,128)S(1)}, u32[]{:S(2)}) copy-start(s32[1,4]{1,0:T(1,128)S(1)} %mul.609) | copy-start | bytes 52
  13.6 325.8 %copy-start.107 = (s32[1,4]{1,0:T(1,128)}, s32[1,4]{1,0:T(1,128)S(1)}, u32[]{:S(2)}) copy-start(s32[1,4]{1,0:T(1,128)S(1)} %reduce_window_sum.11) | copy-start | bytes 52
  339.4 114.2 %copy-start.31 = (s32[576]{0:T(1024)}, s32[576]{0:T(1024)S(1)}, u32[]{:S(2)}) copy-start(s32[576]{0:T(1024)S(1)} %convert_reduce_fusion.6) | copy-start | bytes 6916
  339.5 133.4 %copy-start.51 = (f32[576]{0:T(1024)}, f32[576]{0:T(1024)S(1)}, u32[]{:S(2)}) copy-start(f32[576]{0:T(1024)S(1)} %get-tuple-element.308) | copy-start | bytes 6916
  375.8 19.7 copy-start.54
  454.1 18.7 copy-start.96
  698.0 14.0 copy-start.4
  698.0 14.0 copy-start.34
  725.4 137.5 %copy-start.6 = (f32[1,576,1536]{2,1,0:T(8,128)}, f32[1,576,1536]{2,1,0:T(8,128)S(1)}, u32[]{:S(2)}) copy-start(f32[1,576,1536]{2,1,0:T(8,128)S(1)} %get-tuple-element.299) | copy-start | bytes 10616836
  727.1 24.2 copy-start.21
  727.1 24.2 copy-start.30
  727.1 24.2 copy-start.32
  727.1 24.2 copy-start.38
  727.2 24.2 copy-start.101
  764.6 33.2 %copy-start.55 = (f32[576]{0:T(1024)S(1)}, f32[576]{0:T(1024)}, u32[]{:S(2)}) copy-start(f32[576]{0:T(1024)} %copy-done.54) | copy-start | bytes 6916
  797.8 18.3 copy-start.57
  797.8 18.3 copy-start.10
  797.8 18.4 copy-start.83
  817.1 21.2 copy-start.1
  817.1 21.2 copy-start.40
  838.4 11.5 copy-start.62
  838.4 11.5 copy-start.63
  838.4 11.5 copy-start.66
  852.5 282.2 %reduce-scatter.25.cloned.1.call-start = ((), (), s32[]{:S(2)}) async-start(), calls=%async_computation.15 | async-start | bytes 811008
  861.4 290.0 %reduce-scatter.27.cloned.1.call-start = ((), (), s32[]{:S(2)}) async-start(), calls=%async_computation.16 | async-start | bytes 3244032
  871.5 381.0 %reduce-scatter.29.cloned.1.call-start = ((), (), s32[]{:S(2)}) async-start(), calls=%async_computation.17 | async-start | bytes 1622016
  873.8 506.5 %reduce-scatter.23.cloned.1.call-start = ((), (), s32[]{:S(2)}) async-start(), calls=%async_computation.14 | async-start | bytes 8110080 | tf_op jit(solution)/shard_map/reduce_scatter | solution.py:374
  882.1 852.8 %reduce-scatter.31.cloned.1.call-start = ((), (), s32[]{:S(2)}) async-start(), calls=%async_computation.18 | async-start | bytes 38928384
  974.5 1113.7 %reduce-scatter.19.cloned.1.call-start = ((), (), s32[]{:S(2)}) async-start(), calls=%async_computation.12 | async-start | bytes 38928384 | tf_op jit(solution)/shard_map/reduce_scatter | solution.py:408
  1004.0 1438.5 %reduce-scatter.21.cloned.1.call-start = ((), (), s32[]{:S(2)}) async-start(), calls=%async_computation.13 | async-start | bytes 38928384 | tf_op jit(solution)/shard_map/reduce_scatter | solution.py:410
  1034.6 45.6 %copy-start.2 = (f32[1,576,1536]{2,1,0:T(8,128)S(1)}, f32[1,576,1536]{2,1,0:T(8,128)}, u32[]{:S(2)}) copy-start(f32[1,576,1536]{2,1,0:T(8,128)} %copy-done.1) | copy-start | bytes 10616836
  1034.7 45.6 %copy-start.41 = (f32[576]{0:T(1024)S(1)}, f32[576]{0:T(1024)}, u32[]{:S(2)}) copy-start(f32[576]{0:T(1024)} %copy-done.40) | copy-start | bytes 6916
  1034.7 45.6 %copy-start.49 = (f32[1536]{0:T(1024)S(1)}, f32[1536]{0:T(1024)}, u32[]{:S(2)}) copy-start(f32[1536]{0:T(1024)} %get-tuple-element.246) | copy-start | bytes 18436
  1034.7 45.6 %copy-start.68 = (pred[576]{0:T(1024)(128)(4,1)S(1)}, pred[576]{0:T(1024)(128)(4,1)}, u32[]{:S(2)}) copy-start(pred[576]{0:T(1024)(128)(4,1)} %get-tuple-element.421) | copy-start | bytes 1732
  1080.2 42.7 %slice-start.2 = ((s8[7077888]{0:T(1024)(128)(4,1)}), s8[4194304]{0:T(1024)(128)(4,1)S(1)}, s32[]{:S(2)}) async-start(s8[7077888]{0:T(1024)(128)(4,1)} %bitcast.371), calls=%async_computation.22 | async-start | bytes 8388608
  1094.8 19.8 copy-start.5
  1094.8 19.8 copy-start.53
  1094.8 19.8 copy-start.94
  1094.9 28.1 %slice-start.3 = ((s8[7077888]{0:T(1024)(128)(4,1)}), s8[2883584]{0:T(1024)(128)(4,1)S(1)}, s32[]{:S(2)}) async-start(s8[7077888]{0:T(1024)(128)(4,1)} %bitcast.371), calls=%async_computation.23 | async-start | bytes 5767168
  (83 other events, 440.9 us)
Sparse Core Ops, SparseCore 0:
  11.5 64.0 all-gather.12
  79.1 124.6 all-gather.14
  207.3 130.1 all-gather.8
  340.8 124.8 all-gather.10
  852.6 93.1 reduce-scatter.32
  950.8 94.4 reduce-scatter.24
  1050.7 100.5 reduce-scatter.26
  1156.6 95.9 reduce-scatter.28
  1258.8 121.4 reduce-scatter.22
  1388.3 346.5 reduce-scatter.30
  1741.9 346.2 reduce-scatter.18
  2096.2 346.2 reduce-scatter.20
where the time goes:
time: 2460 us; the launch traced here: 2450 us
  waiting for transfers between devices  1300 us (53%)
  matrix products  429 us (17%)
  blocking collectives  351 us (14%)
  other arithmetic  194 us (8%)
  local copies, waits for them, and re-layouts  154 us (6%)
    unnamed x17, waiting for transfers between devices  470 us
    reduce_scatter x1, waiting for transfers between devices, local(): lax.psum_scatter(res_terms[3], ('dp', 'fsdp'), scatter_dimension=0, tiled...  354 us
    reduce_scatter x1, waiting for transfers between devices, local(): lax.psum_scatter(res_terms[1], ('dp', 'fsdp'), scatter_dimension=1, tiled...  353 us
    reduce_scatter x1, waiting for transfers between devices, local(): lax.psum_scatter(mid_terms[2], ('dp', 'fsdp'), scatter_dimension=0, tiled...  126 us
    unnamed x2, blocking collectives  79.9 us
    all_gather x1, blocking collectives, local(): lax.all_gather(mid_owned[0], ('dp', 'fsdp'), axis=1, tiled=True)  71.9 us
    unnamed x254, local copies, waits for them, and re-layouts  69.6 us
    all_gather x1, blocking collectives, local(): lax.all_gather(res_owned[0], ('dp', 'fsdp'), axis=1, tiled=True)  67.5 us
  transfers between devices with their start and end apart: 12, of which 6 were waited for; matrix products, arithmetic and copies ran while one was open for 16% of the time, Pallas kernels for 0%

commit v1 on v0

v1 whole, which is shorter than its diff:
```python
import functools

import jax
import jax.numpy as jnp
from jax import lax
from jax.experimental import pallas as pl
from jax.experimental.pallas import tpu as pltpu
from jax.sharding import PartitionSpec as P

HEADS = 24
TEXT = 77
SIDE_UNIT = 4
SLOTS = 576
LAT_ROW = 4


HIGHEST = lax.Precision.HIGHEST
NORM_EPS = 1e-06
MASKED = -1000000000.0


def bit_count(size):
    return size.bit_length() - 1


def swap(values, axis_name, size, bit):
    return lax.ppermute(values, axis_name, [(i, i ^ (1 << bit)) for i in range(size)])


def scatter_orders(size):
    bits = list(range(bit_count(size)))
    orders = []
    for first in ([0, 1], [1, 0], [2, 0, 1]):
        first = [b for b in first if b in bits]
        orders.append(first + [b for b in bits if b not in first])
    return orders


def keep_kernel(*refs):
    pass


def tie(values, *others):
    some = pl.BlockSpec(memory_space=pl.ANY)
    return pl.pallas_call(
        keep_kernel,
        out_shape=jax.ShapeDtypeStruct(values.shape, values.dtype),
        in_specs=[some] * (1 + len(others)),
        out_specs=some,
        input_output_aliases={0: 0},
    )(values, *others)


class Gather:
    def __init__(self, shard, orders, inner, outer):
        self.rows, width = shard.shape
        self.piece = width // len(orders)
        self.inner, self.outer = inner, outer
        self.orders = [order[::-1] for order in orders]
        self.held = [
            shard[None, :, number * self.piece : (number + 1) * self.piece]
            for number in range(len(orders))
        ]
        self.offsets = [[0] for _ in orders]

    def step(self, number, after=()):
        came = []
        for index, order in enumerate(self.orders):
            bit = order[number]
            held = tie(self.held[index], *after) if after else self.held[index]
            came.append(swap(held, "fsdp", self.outer, bit))
            if number < len(order) - 1:
                self.held[index] = jnp.concatenate([held, came[-1]], axis=0)
                self.offsets[index] = self.offsets[index] + [o ^ (1 << bit) for o in self.offsets[index]]
        self.came = came
        return came

    def parts(self):
        last = [1 << order[-1] for order in self.orders]
        parts = [self.held, self.came]
        places = [self.offsets, [[o ^ b for o in offs] for offs, b in zip(self.offsets, last)]]
        for bit in range(bit_count(self.inner)):
            parts = parts + [[swap(p, "dp", self.inner, bit) for p in part] for part in parts]
            places = places + [
                [[o ^ (self.outer << bit) for o in offs] for offs in place] for place in places
            ]
        return parts, places

    def whole(self):
        parts, places = self.parts()
        return place_blocks(parts, places, self.rows, self.piece, self.inner * self.outer)


def place_blocks(parts, places, rows, piece, blocks):
    count, pieces = len(parts), len(parts[0])
    where = {}
    for number, place in enumerate(places):
        for index, offs in enumerate(place):
            for k, o in enumerate(offs):
                where[(index, o)] = (number, k)
    me = lax.axis_index("dp") * (blocks // lax.axis_size("dp")) + lax.axis_index("fsdp")
    offsets = [o for place in places for o in place[0]]
    part_of = [[where[(i, o)][0] for o in offsets] for i in range(pieces)]
    slot_of = [[where[(i, o)][1] for o in offsets] for i in range(pieces)]
    goal = jnp.asarray(offsets, jnp.int32) ^ me.astype(jnp.int32)

    shown = []
    for i in range(pieces):
        for p in range(count):
            now, row = 0, []
            for step in range(blocks):
                if part_of[i][step] == p:
                    now = slot_of[i][step]
                row.append(now)
            shown.append(row)
    shown = jnp.asarray(shown, jnp.int32)
    part_table = jnp.asarray(part_of, jnp.int32)
    return pl.pallas_call(
        functools.partial(place_kernel, count, pieces, piece),
        out_shape=jax.ShapeDtypeStruct((blocks, rows, piece * pieces), parts[0][0].dtype),
        grid_spec=pltpu.PrefetchScalarGridSpec(
            num_scalar_prefetch=3,
            grid=(blocks,),
            in_specs=[
                pl.BlockSpec(
                    (1, rows, piece),
                    lambda b, goal, shown, part, n=i * count + p: (shown[n, b], 0, 0),
                )
                for i in range(pieces)
                for p in range(count)
            ],
            out_specs=pl.BlockSpec((1, rows, piece * pieces), lambda b, goal, shown, part: (goal[b], 0, 0)),
        ),
        compiler_params=pltpu.CompilerParams(vmem_limit_bytes=40 << 20),
        cost_estimate=pl.CostEstimate(
            flops=0,
            transcendentals=0,
            bytes_accessed=2 * blocks * rows * piece * pieces * parts[0][0].dtype.itemsize,
        ),
    )(goal, shown, part_table, *[parts[p][i] for i in range(pieces) for p in range(count)])


def place_kernel(count, pieces, piece, goal_ref, shown_ref, part_ref, *refs):
    target = refs[-1]
    step = pl.program_id(0)
    for i in range(pieces):
        for p in range(count):

            @pl.when(part_ref[i, step] == p)
            def _(i=i, source=refs[i * count + p]):
                target[:, :, i * piece : (i + 1) * piece] = source[...]


def halve(values, axis, axis_name, size, bit):
    mine = (lax.axis_index(axis_name) >> bit) & 1
    away = lax.dynamic_index_in_dim(values, 1 - mine, axis, keepdims=False)
    kept = lax.dynamic_index_in_dim(values, mine, axis, keepdims=False)
    come = swap(away, axis_name, size, bit)
    return (kept.astype(jnp.float32) + come.astype(jnp.float32)).astype(values.dtype)


def scatter_sum(values, inner_left, orders, inner, outer):
    blocks, rows, width = values.shape
    outer_bits = bit_count(outer)
    values = values.reshape((2,) * (inner_left + outer_bits) + (rows, width))
    for bit in reversed(range(inner_left)):
        values = halve(values, 0, "dp", inner, bit)
    piece = width // len(orders)
    done = []
    for number, order in enumerate(orders):
        part = values[..., number * piece : (number + 1) * piece]
        left = list(reversed(range(outer_bits)))
        for bit in order:
            part = halve(part, left.index(bit), "fsdp", outer, bit)
            left.remove(bit)
        done.append(part)
    return jnp.concatenate(done, axis=1) if len(done) > 1 else done[0]


def scatter_made(make, orders, inner, outer):
    top = bit_count(inner) - 1
    mine = (lax.axis_index("dp") >> top) & 1
    away = make(1 - mine)
    come = swap(away, "dp", inner, top)
    kept = make(mine)
    both = (kept.astype(jnp.float32) + come.astype(jnp.float32)).astype(kept.dtype)
    blocks = both.reshape(inner * outer // 2, -1, both.shape[1])
    return scatter_sum(blocks, top, orders, inner, outer).astype(jnp.float32)


def attention_kernel(q_ref, k_ref, v_ref, g_ref, bias_ref, att_ref, dq_ref, dk_ref, dv_ref):
    width = q_ref.shape[1]
    half = width // 2
    low, full = jnp.bfloat16, jnp.float32
    lanes = lax.broadcasted_iota(jnp.int32, (1, width), 1)
    sublanes = lax.broadcasted_iota(jnp.int32, (width, 1), 0)
    keys, values = k_ref[...], v_ref[...]
    att_t = dq_t = d_key = d_value = None

    def product(a, b, da, db):
        return lax.dot_general(a, b, (((da,), (db,)), ((), ())), preferred_element_type=full)

    for head in range(2):
        own = (lanes >= head * half) & (lanes < (head + 1) * half)
        query = jnp.where(own, q_ref[...], jnp.zeros((), low))
        grad = jnp.where(own, g_ref[...], jnp.zeros((), low))
        scores = product(keys, query, 1, 1) + bias_ref[...]
        exponent = jnp.exp(scores - jnp.max(scores, axis=0, keepdims=True))
        probs = exponent * (1.0 / jnp.sum(exponent, axis=0, keepdims=True))
        probs_low = probs.astype(low)
        att_head = product(values, probs_low, 0, 0)
        grad_probs = product(values, grad, 1, 1)
        inner_sum = jnp.sum(probs * grad_probs, axis=0, keepdims=True)
        grad_scores = (probs * (grad_probs - inner_sum)).astype(low)
        value_part = product(probs_low, grad, 1, 0)
        key_part = product(grad_scores, query, 1, 0)
        dq_head = product(keys, grad_scores, 0, 0)
        if head == 0:
            att_t, dq_t, d_key, d_value = att_head, dq_head, key_part, value_part
        else:
            upper = sublanes < half
            att_t = jnp.where(upper, att_t, att_head)
            dq_t = jnp.where(upper, dq_t, dq_head)
            d_key, d_value = d_key + key_part, d_value + value_part
    att_ref[...] = att_t.T.astype(low)
    dq_ref[...] = (dq_t.T * ((width // 2) ** -0.5)).astype(low)
    dk_ref[...] = d_key.astype(low)
    dv_ref[...] = d_value.astype(low)


def attention(query, keys, values, grad, bias):
    slots, width = query.shape
    count = keys.shape[0]
    pair = 2 * (width // HEADS)

    def columns(rows):
        return pl.BlockSpec((rows, pair), lambda h: (0, h))

    low = jnp.bfloat16
    return pl.pallas_call(
        attention_kernel,
        grid=(width // pair,),
        in_specs=[columns(slots), columns(count), columns(count), columns(slots)]
        + [pl.BlockSpec((count, slots), lambda h: (0, 0))],
        out_specs=[columns(slots), columns(slots), columns(count), columns(count)],
        out_shape=[
            jax.ShapeDtypeStruct((slots, width), low),
            jax.ShapeDtypeStruct((slots, width), low),
            jax.ShapeDtypeStruct((count, width), low),
            jax.ShapeDtypeStruct((count, width), low),
        ],
        compiler_params=pltpu.CompilerParams(vmem_limit_bytes=56 << 20),
        cost_estimate=pl.CostEstimate(
            flops=6 * 2 * 2 * slots * count * width,
            transcendentals=slots * count * HEADS,
            bytes_accessed=2 * width * (4 * slots + 4 * count) + 4 * slots * count,
        ),
    )(query, keys, values, grad, bias)


def layout(heights_row, widths_row):
    pixels = heights_row * widths_row
    ends_at = jnp.cumsum(pixels)
    starts_at = ends_at - pixels
    slot_ids = jnp.arange(SLOTS, dtype=jnp.int32)
    segment = jnp.sum((ends_at[None, :] <= slot_ids[:, None]).astype(jnp.int32), axis=1)
    member = segment[:, None] == jnp.arange(LAT_ROW, dtype=jnp.int32)[None, :]
    start_at = jnp.sum(jnp.where(member, starts_at[None, :], 0), axis=1)
    height_at = jnp.sum(jnp.where(member, heights_row[None, :], 0), axis=1)
    width_at = jnp.sum(jnp.where(member, widths_row[None, :], 0), axis=1)
    place_in = slot_ids - start_at
    safe_width = jnp.maximum(width_at, 1)
    column = place_in % safe_width
    row_index = place_in // safe_width
    return (segment, member, height_at, width_at, row_index, column)


def layer_norm(values):
    center = values - jnp.mean(values, axis=-1, keepdims=True)
    return center * lax.rsqrt(jnp.mean(center * center, axis=-1, keepdims=True) + NORM_EPS)


def depthwise(values, conv_taps, conv_bias, geometry):
    segment, member, height_at, width_at, row_index, column = geometry
    live_query = segment < LAT_ROW
    margin = 6 * SIDE_UNIT + 1
    padded = jnp.pad(values, ((0, 0), (margin, margin), (0, 0)))
    result = jnp.zeros_like(values) + conv_bias
    for step_y in (-1, 0, 1):
        for step_x in (-1, 0, 1):
            inside = live_query & (row_index + step_y >= 0) & (row_index + step_y < height_at)
            inside = inside & (column + step_x >= 0) & (column + step_x < width_at)
            weight_row = conv_taps[(step_y + 1) * 3 + step_x + 1]
            side_list = (1,) if step_y == 0 else (3 * SIDE_UNIT, 4 * SIDE_UNIT, 6 * SIDE_UNIT)
            for side_len in side_list:
                offset = step_y * side_len + step_x
                chosen = inside if step_y == 0 else inside & (width_at == side_len)
                shifted = lax.slice_in_dim(padded, margin + offset, margin + offset + SLOTS, axis=1)
                result = result + jnp.where(chosen[..., None], shifted, 0.0) * weight_row
    return result


def response_norm(hidden, grn_gain, grn_shift, onehot):
    active = jax.nn.gelu(hidden, approximate=False)
    power = jnp.einsum("rsl,rsf->rlf", onehot, active * active, precision=HIGHEST)
    global_norm = jnp.sqrt(power + NORM_EPS)
    scaled = global_norm / (jnp.mean(global_norm, axis=2, keepdims=True) + NORM_EPS)
    spread = jnp.einsum("rsl,rlf->rsf", onehot, scaled, precision=HIGHEST)
    return grn_gain * (active * spread) + grn_shift + active


def timestep(after_res, time_pair, onehot):
    per_slot = jnp.einsum("rsl,rlc->rsc", onehot, time_pair, precision=HIGHEST)
    half_width = time_pair.shape[-1] // 2
    return after_res + after_res * per_slot[..., :half_width] + per_slot[..., half_width:]


def score_bias(segment, counts_row, key_pad):
    live_query = segment < LAT_ROW
    image_ok = (segment[:, None] == segment[None, :]) & live_query[None, :]
    text_index = jnp.arange(LAT_ROW * TEXT, dtype=jnp.int32)
    text_latent = text_index // TEXT
    text_limit = jnp.sum(
        jnp.where(
            text_latent[:, None] == jnp.arange(LAT_ROW, dtype=jnp.int32)[None, :],
            counts_row[None, :],
            0,
        ),
        axis=1,
    )
    text_ok = (text_latent[:, None] == segment[None, :]) & (text_index % TEXT < text_limit)[:, None]
    no_pad = jnp.zeros((key_pad, segment.shape[0]), bool)
    return jnp.where(jnp.concatenate([image_ok, text_ok, no_pad], axis=0), 0.0, MASKED)


def local(
    inner,
    outer,
    latents,
    text_embed,
    time_embed,
    heights,
    widths,
    text_counts,
    res_vecs,
    fc1_w,
    ff_vecs,
    fc2_w,
    time_w,
    time_b,
    kv_w,
    attn_w,
    attn_vecs,
    cotangent,
):
    half_type = jnp.bfloat16
    orders = scatter_orders(outer)
    small_owned = (res_vecs, ff_vecs, time_w, time_b[None], attn_vecs)
    small_sizes = [v.size for v in small_owned]
    small_pad = -sum(small_sizes) % 1024
    small_shard = jnp.concatenate(
        [v.astype(half_type).reshape(-1) for v in small_owned] + [jnp.zeros((small_pad,), half_type)]
    )
    low_fc1, low_fc2, low_attn, low_kv = (
        v.astype(half_type) for v in (fc1_w.T, fc2_w, attn_w.T, kv_w)
    )
    steps = bit_count(outer)
    small_gather = Gather(small_shard.reshape(-1, 128), orders[:1], inner, outer)
    fc1_gather = Gather(low_fc1, orders, inner, outer)
    fc2_gather = Gather(low_fc2, orders, inner, outer)
    attn_gather = Gather(low_attn, orders, inner, outer)
    kv_gather = Gather(low_kv, orders[1:2], inner, outer)
    for number in range(steps):
        small_gather.step(number)
    ahead = ()
    for number in range(steps):
        came = fc1_gather.step(number)
        ahead = came if number == 1 else ahead
    for number in range(steps):
        came = fc2_gather.step(number, ahead if number == 0 else ())
        ahead = came if number == 1 else ahead
    for number in range(steps):
        attn_gather.step(number, ahead if number == 0 else ())
        kv_gather.step(number, ahead if number == 0 else ())
    small_all = small_gather.whole().reshape(inner * outer, -1)
    small_full = []
    taken = 0
    for owned, size in zip(small_owned, small_sizes):
        some = small_all[:, taken : taken + size].reshape(inner * outer, owned.shape[0], owned.shape[1])
        small_full.append(some.transpose(1, 0, 2).reshape(owned.shape[0], -1))
        taken += size
    res_all, ff_all, time_w_all, time_b_all, vecs_all = small_full

    def rows_of(gathered):
        whole = gathered.whole()
        return whole.reshape(-1, whole.shape[2])

    fc1_t = rows_of(fc1_gather)
    fc2_full = rows_of(fc2_gather)
    attn_t = rows_of(attn_gather)
    kv_full = rows_of(kv_gather)
    row_count, slot_count, model_width = latents.shape
    cond_width = text_embed.shape[3]
    head_dim = model_width // HEADS
    score_scale = head_dim ** (-0.5)
    geometry = jax.vmap(layout)(heights, widths)
    segment = geometry[0]
    onehot = geometry[1].astype(jnp.float32)
    live_mask = (segment < LAT_ROW).astype(jnp.float32)[..., None]
    text_count = LAT_ROW * TEXT
    key_pad = -(slot_count + text_count) % 128
    bias = score_bias(segment[0], text_counts[0], key_pad)
    res_vals = res_all.astype(jnp.float32)
    ff_vals = ff_all.astype(jnp.float32)

    def res_entry(values, conv_taps, conv_bias):
        return layer_norm(depthwise(values, conv_taps, conv_bias, geometry))

    normed, res_entry_back = jax.vjp(res_entry, latents, res_vals[:9], res_vals[9])
    normed_low = normed.astype(half_type)
    hidden = (
        jnp.einsum("rsc,fc->rsf", normed_low, fc1_t, preferred_element_type=jnp.float32)
        + ff_vals[0]
    )

    def grn_piece(hidden_in, grn_gain, grn_shift):
        return response_norm(hidden_in, grn_gain, grn_shift, onehot)

    response, grn_back = jax.vjp(grn_piece, hidden, ff_vals[1], ff_vals[2])
    response_low = response.astype(half_type)
    branch = (
        jnp.einsum("rsf,fc->rsc", response_low, fc2_full, preferred_element_type=jnp.float32)
        + res_vals[10]
    )
    after_res = latents + live_mask * branch
    mid_vals = vecs_all.astype(jnp.float32)
    time_low = time_embed.astype(half_type)
    time_pair = jnp.einsum(
        "rlt,tc->rlc", time_low, time_w_all, preferred_element_type=jnp.float32
    ) + time_b_all[0].astype(jnp.float32)

    def time_piece(after_in, pair_in):
        return timestep(after_in, pair_in, onehot)

    after_time, time_back = jax.vjp(time_piece, after_res, time_pair)
    normed_two, norm_two_back = jax.vjp(layer_norm, after_time)
    normed_two_low = normed_two.astype(half_type)
    text_flat = text_embed.astype(jnp.float32).reshape(row_count, LAT_ROW * TEXT, cond_width)
    silu_text, silu_back = jax.vjp(jax.nn.silu, text_flat)
    silu_low = silu_text.astype(half_type)
    mapped_low = (
        jnp.einsum("rtk,kc->rtc", silu_low, kv_full, preferred_element_type=jnp.float32)
        + mid_vals[3]
    ).astype(half_type)
    normed_row = normed_two_low[0]
    source_low = jnp.concatenate(
        [normed_row, mapped_low[0], jnp.zeros((key_pad, model_width), half_type)], axis=0
    )

    def along(spec, a, b):
        return jnp.einsum(spec, a, b, preferred_element_type=jnp.float32)

    w_query, w_key, w_value, w_out = (
        attn_t[i * model_width : (i + 1) * model_width] for i in range(4)
    )
    query_low = (along("sc,dc->sd", normed_row, w_query) + mid_vals[0]).astype(half_type)
    query_low = query_low * jnp.asarray(score_scale, half_type)
    key_low = along("kc,dc->kd", source_low, w_key).astype(half_type)
    value_low = (along("kc,dc->kd", source_low, w_value) + mid_vals[1]).astype(half_type)
    grad_proj = (live_mask * cotangent)[0].astype(half_type)
    grad_attended = along("sd,dc->sc", grad_proj, w_out).astype(half_type)
    attended_low, grad_query, grad_key, grad_value = attention(
        query_low, key_low, value_low, grad_attended, bias
    )
    output = after_time + live_mask * (along("sc,dc->sd", attended_low, w_out) + mid_vals[2])

    def long(values):
        return jnp.pad(values, ((0, source_low.shape[0] - slot_count), (0, 0)))

    query_long, proj_long, attended_long = long(grad_query), long(grad_proj), long(attended_low)

    def attn_half(half):
        first = half == 0
        one = along("kd,kc->dc", jnp.where(first, query_long, grad_value), source_low)
        two = along(
            "kd,kc->dc",
            jnp.where(first, grad_key, proj_long),
            jnp.where(first, source_low, attended_long),
        )
        return jnp.concatenate([one, two], axis=0).astype(half_type)

    attn_grad = scatter_made(attn_half, orders, inner, outer).T
    grad_bias_out = jnp.sum(grad_proj.astype(jnp.float32), axis=0)
    grad_bias_query = jnp.sum(grad_query.astype(jnp.float32), axis=0)
    grad_bias_value = jnp.sum(grad_value.astype(jnp.float32), axis=0)
    grad_source = along("kd,dc->kc", grad_key, w_key) + along("kd,dc->kc", grad_value, w_value)
    grad_normed_two = (along("sd,dc->sc", grad_query, w_query) + grad_source[:slot_count])[None]
    grad_mapped = grad_source[None, slot_count : slot_count + text_count].astype(half_type)
    grad_kv_w = jnp.einsum("rtk,rtc->kc", silu_low, grad_mapped, preferred_element_type=jnp.float32)
    grad_bias_kv = jnp.sum(grad_mapped.astype(jnp.float32), axis=(0, 1))
    grad_silu = jnp.einsum(
        "rtc,kc->rtk", grad_mapped, kv_full, preferred_element_type=jnp.float32
    )
    text_grad = silu_back(grad_silu)[0].reshape(row_count, LAT_ROW, TEXT, cond_width)
    grad_time = cotangent + norm_two_back(grad_normed_two)[0]
    grad_after_res, grad_pair = time_back(grad_time)
    grad_time_w = jnp.einsum(
        "rlt,rlc->tc", time_low.astype(jnp.float32), grad_pair, precision=HIGHEST
    )
    grad_time_b = jnp.sum(grad_pair, axis=(0, 1))
    grad_attn_vecs = jnp.stack([grad_bias_query, grad_bias_value, grad_bias_out, grad_bias_kv])

    kv_grad = scatter_sum(
        grad_kv_w.astype(half_type).reshape(inner * outer, -1, model_width),
        bit_count(inner),
        orders[1:2],
        inner,
        outer,
    ).astype(jnp.float32)
    grad_branch = (live_mask * grad_after_res).astype(half_type)
    hidden_half = response_low.shape[2] // 2

    def rows_half(left, right):
        def make(half):
            some = lax.dynamic_slice_in_dim(left, half * hidden_half, hidden_half, axis=1)
            return along("sf,sc->fc", some, right).astype(half_type)

        return make

    fc2_grad = scatter_made(rows_half(response_low[0], grad_branch[0]), orders, inner, outer)
    grad_fc2_bias = jnp.sum(grad_branch.astype(jnp.float32), axis=(0, 1))
    grad_response = jnp.einsum(
        "rsc,fc->rsf", grad_branch, fc2_full, preferred_element_type=jnp.float32
    )
    grad_hidden, grad_gain, grad_shift = grn_back(grad_response)
    grad_hidden_low = grad_hidden.astype(half_type)
    fc1_grad = scatter_made(rows_half(grad_hidden_low[0], normed_low[0]), orders, inner, outer).T
    grad_fc1_bias = jnp.sum(grad_hidden_low.astype(jnp.float32), axis=(0, 1))
    grad_normed = jnp.einsum(
        "rsf,fc->rsc", grad_hidden_low, fc1_t, preferred_element_type=jnp.float32
    )
    grad_entry, grad_taps, grad_conv_bias = res_entry_back(grad_normed)
    latents_grad = grad_after_res + grad_entry
    grad_res_vecs = jnp.concatenate([grad_taps, grad_conv_bias[None], grad_fc2_bias[None]], axis=0)
    grad_ff_vecs = jnp.stack([grad_fc1_bias, grad_gain, grad_shift])
    small_terms = (grad_res_vecs, grad_ff_vecs, grad_time_w, grad_time_b[None], grad_attn_vecs)
    small_blocks = jnp.concatenate(
        [
            g.reshape(g.shape[0], inner * outer, -1).transpose(1, 0, 2).reshape(inner * outer, -1)
            for g in small_terms
        ]
        + [jnp.zeros((inner * outer, small_pad), jnp.float32)],
        axis=1,
    ).reshape(inner * outer, -1, 128)
    small_sum = scatter_sum(small_blocks, bit_count(inner), orders[1:2], inner, outer).reshape(-1)
    small_grads = []
    taken = 0
    for owned, size in zip(small_owned, small_sizes):
        small_grads.append(small_sum[taken : taken + size].reshape(owned.shape))
        taken += size
    return (
        output,
        latents_grad,
        text_grad,
        small_grads[0],
        fc1_grad,
        small_grads[1],
        fc2_grad,
        small_grads[2],
        small_grads[3][0],
        kv_grad,
        attn_grad,
        small_grads[4],
    )


def solution(mesh):
    return jax.shard_map(
        functools.partial(local, mesh.shape["dp"], mesh.shape["fsdp"]),
        mesh=mesh,
        in_specs=(
            P(("dp", "fsdp"), None, None),
            P(("dp", "fsdp"), None, None, None),
            P(("dp", "fsdp"), None, None),
            P(("dp", "fsdp"), None),
            P(("dp", "fsdp"), None),
            P(("dp", "fsdp"), None),
            P(None, ("dp", "fsdp")),
            P(None, ("dp", "fsdp")),
            P(None, ("dp", "fsdp")),
            P(("dp", "fsdp"), None),
            P(None, ("dp", "fsdp")),
            P(("dp", "fsdp")),
            P(("dp", "fsdp"), None),
            P(None, ("dp", "fsdp")),
            P(None, ("dp", "fsdp")),
            P(("dp", "fsdp"), None, None),
        ),
        out_specs=(
            P(("dp", "fsdp"), None, None),
            P(("dp", "fsdp"), None, None),
            P(("dp", "fsdp"), None, None, None),
            P(None, ("dp", "fsdp")),
            P(None, ("dp", "fsdp")),
            P(None, ("dp", "fsdp")),
            P(("dp", "fsdp"), None),
            P(None, ("dp", "fsdp")),
            P(("dp", "fsdp")),
            P(("dp", "fsdp"), None),
            P(None, ("dp", "fsdp")),
            P(None, ("dp", "fsdp")),
        ),
        check_vma=False,
    )
```

time: 2460 us -> 1340 us (0.54)
  waiting for transfers between devices: 1300 us -> 367 us
  blocking collectives: 351 us -> 0 us
  Pallas kernels: 0 us -> 157 us
  starting transfers between devices: 0.88 us -> 104 us
  matrix products: 429 us -> 327 us
  other arithmetic: 194 us -> 247 us
  local copies, waits for them, and re-layouts: 154 us -> 126 us
    reduce_scatter x3 -> x0, waiting for transfers between devices: 834 us -> none  [the longest x1 354 us: local(): lax.psum_scatter(res_terms[3], ('dp', 'fsdp'), scatter_dimension=0, tiled...]
    unnamed x17 -> x0, waiting for transfers between devices: 470 us -> none
    ppermute x0 -> x115, waiting for transfers between devices: none -> 367 us  [swap(): lax.ppermute(values, axis_name, [(i, i ^ 1 << bit) for i in range(size)])]
    all_gather x4 -> x0, blocking collectives: 271 us -> none  [the longest x1 71.9 us: local(): lax.all_gather(mid_owned[0], ('dp', 'fsdp'), axis=1, tiled=True)]
    pallas_call x0 -> x13, Pallas kernels: none -> 157 us  [the longest x5 92.4 us: place_blocks(): pl.pallas_call(functools.partial(place_kernel, count, pieces, piece), out...]
    ppermute x0 -> x115, starting transfers between devices: none -> 104 us  [swap(): lax.ppermute(values, axis_name, [(i, i ^ 1 << bit) for i in range(size)])]
    dot_general x60 -> x23, matrix products: 337 us -> 234 us  [the longest x16 119 us: along(): return jnp.einsum(spec, a, b, preferred_element_type=jnp.float32)]
    unnamed x2 -> x0, blocking collectives: 79.9 us -> none
  transfers between devices with their start and end apart: 12 -> 115, of which waited for: 6 -> 45; matrix products, arithmetic and copies ran while one was open for 16% -> 31% of each run, Pallas kernels for 0% -> 5%
where the time goes in v1:
time: 1340 us; the launch traced here: 1330 us
  waiting for transfers between devices  367 us (27%)
  matrix products  327 us (24%)
  other arithmetic  247 us (18%)
  Pallas kernels  157 us (12%)
  local copies, waits for them, and re-layouts  126 us (9%)
  starting transfers between devices  104 us (8%)
    ppermute x115, waiting for transfers between devices, swap(): lax.ppermute(values, axis_name, [(i, i ^ 1 << bit) for i in range(size)])  367 us
    dot_general x16, matrix products, along(): return jnp.einsum(spec, a, b, preferred_element_type=jnp.float32)  119 us
    ppermute x115, starting transfers between devices, swap(): lax.ppermute(values, axis_name, [(i, i ^ 1 << bit) for i in range(size)])  104 us
    pallas_call x5, Pallas kernels, place_blocks(): pl.pallas_call(functools.partial(place_kernel, count, pieces, piece), out...  92.4 us
    pallas_call x1, Pallas kernels, attention(): pl.pallas_call(attention_kernel, grid=(width // pair,), in_specs=[columns...  64.8 us
    concatenate x33, other arithmetic, step(): self.held[index] = jnp.concatenate([held, came[-1]], axis=0)  49.4 us
    dot_general x1, matrix products, local(): jnp.einsum('rsc,fc->rsf', normed_low, fc1_t, preferred_element_type=jnp.f...  44.4 us
    dot_general x2, matrix products, response_norm(): jnp.einsum('rsl,rsf->rlf', onehot, active * active, precision=HIGHEST)  43.2 us
  transfers between devices with their start and end apart: 115, of which 45 were waited for; matrix products, arithmetic and copies ran while one was open for 31% of the time, Pallas kernels for 5%

profile of v1, /device:TPU:0, one launch (start us, length us, event | category | flops | bytes accessed | tf_op | source)
XLA Modules:
  0.0 1330.9 jit_solution(2253359012390866196)
XLA Ops:
  26.8 13.1 collective-permute-done.1
  74.1 14.2 %collective-permute-done.24 = bf16[1,192,512]{2,1,0:T(8,128)(2,1)S(1)} collective-permute-done((bf16[1,192,512]{2,1,0:T(8,128)(2,1)}, bf16[1,192,512]{2,1,0:T(8,128)(2,1)S(1)}, u32[]{:S(2)}, u32[]{:S(2)}) %collective-permute-start.24) | collective-permute-done | bytes 196640 | tf_op jit(solution)/shard_map/ppermute | solution.py:27
  122.0 11.6 collective-permute-done.42
  201.3 27.4 %collective-permute-done.62 = bf16[4,40,1536]{2,1,0:T(8,128)(2,1)} collective-permute-done((bf16[4,40,1536]{2,1,0:T(8,128)(2,1)}, bf16[4,40,1536]{2,1,0:T(8,128)(2,1)}, u32[]{:S(2)}, u32[]{:S(2)}) %collective-permute-start.62) | collective-permute-done | bytes 491552 | tf_op jit(solution)/shard_map/ppermute | solution.py:27
  229.7 33.9 %fusion.162 = (f32[576]{0:T(1024)}, f32[1,576,1536]{2,1,0:T(8,128)}) fusion(pred[576]{0:T(1024)(128)(4,1)} %get-tuple-element.275, pred[576]{0:T(1024)(128)(4,1)} %get-tuple-element.276, f32[1536]{0:T(1024)} %mul.653, pred[576]{0:T(1024)(128)(4,1)} %get-tuple-element.264, pred[576]{0:T(1024)(128)(4,1)} %get-tuple-element.269, ...), kind=kLoop, calls=%fused_computation.557 | loop fusion | flops 56622528 | bytes 7153728 | tf_op jit(solution)/shard_map/jvp()/reduce_sum | solution.py:279
  266.0 12.3 collective-permute-done.56
  335.2 15.8 %shard_map.393 = bf16[32,40,1536]{2,1,0:T(8,128)(2,1)S(1)} custom-call(s32[32]{0:T(128)S(1)} %broadcast_xor_fusion.goal_ref, s32[4,32]{1,0:T(4,128)S(1)} %copy-done.16, s32[1,32]{1,0:T(1,128)S(1)} %copy-done.17, bf16[8,40,1536]{2,1,0:T(8,128)(2,1)} %pad_maximum_fusion.10.refs_0_, bf16[8,40,1536]{2,1,0:T(8,128)(2,1)} %collective-permute-done.63.refs_1_, ...), custom_call_target="tpu_custom_call" | custom-call | bytes 7864320 | tf_op jit(solution)/shard_map/pallas_call | solution.py:118
  358.5 25.4 %shard_map.383 = bf16[32,192,1536]{2,1,0:T(8,128)(2,1)} custom-call(s32[32]{0:T(128)S(1)} %broadcast_xor_fusion.1.goal_ref, s32[12,32]{1,0:T(8,128)S(1)} %copy-done.14, s32[3,32]{1,0:T(4,128)S(1)} %copy-done.15, bf16[8,192,512]{2,1,0:T(8,128)(2,1)S(1)} %pad_maximum_fusion.1.refs_0_, bf16[8,192,512]{2,1,0:T(8,128)(2,1)} %collective-permute-done.9.refs_1_, ...), custom_call_target="tpu_custom_call" | custom-call | bytes 37748736 | tf_op jit(solution)/shard_map/pallas_call | solution.py:118
  384.8 44.4 %multiply_multiply_fusion.5 = (f32[576,6144]{1,0:T(8,128)}, f32[576,6144]{1,0:T(8,128)}, f32[576,6144]{1,0:T(8,128)}) fusion(f32[6144]{0:T(1024)S(1)} %copy-done.132, bf16[576,1536]{1,0:T(8,128)(2,1)S(1)} %fusion.62, bf16[6144,1536]{1,0:T(8,128)(2,1)} %bitcast.493), kind=kOutput, calls=%fused_computation.37 | convolution fusion | flops 11101667328 | bytes 63135744 | tf_op jit(solution)/shard_map/rsc,fc->rsf/dot_general | solution.py:422
  429.2 9.6 fusion.177
  446.8 18.4 %add_convert_fusion.3 = (bf16[576,6144]{1,0:T(8,128)(2,1)}, f32[576,6144]{1,0:T(8,128)}, f32[576,6144]{1,0:T(8,128)}) fusion(f32[576,6144]{1,0:T(8,128)} %get-tuple-element.129, f32[6144]{0:T(1024)S(1)} %copy-done.113, f32[6144]{0:T(1024)S(1)} %copy-done.110, f32[4,6144]{1,0:T(4,128)S(1)} %get-tuple-element.281, f32[4]{0:T(128)S(1)} %get-tuple-element.278, ...), kind=kOutput, calls=%fused_computation.20 | convolution fusion | flops 187590912 | bytes 49694992 | tf_op jit(solution)/shard_map/jvp(rsl,rlf->rsf)/dot_general | solution.py:308
  470.0 24.6 %shard_map.387 = bf16[32,192,1536]{2,1,0:T(8,128)(2,1)} custom-call(s32[32]{0:T(128)S(1)} %broadcast_xor_fusion.1.goal_ref, s32[12,32]{1,0:T(8,128)S(1)} %copy-done.14, s32[3,32]{1,0:T(4,128)S(1)} %copy-done.15, bf16[8,192,512]{2,1,0:T(8,128)(2,1)S(1)} %copy-done.1, bf16[8,192,512]{2,1,0:T(8,128)(2,1)} %collective-permute-done.27.refs_1_, ...), custom_call_target="tpu_custom_call" | custom-call | bytes 37748736 | tf_op jit(solution)/shard_map/pallas_call | solution.py:118
  495.7 21.4 %fusion.158 = (f32[576]{0:T(1024)S(1)}, f32[1,576,1536]{2,1,0:T(8,128)}, f32[1,576,1536]{2,1,0:T(8,128)}) fusion(f32[1,576,3072]{2,1,0:T(8,128)} %convolution_bitcast_fusion, f32[1,576,1536]{2,1,0:T(8,128)} %param.31, f32[1536]{0:T(1024)S(1)} %copy-done.158, bf16[576,6144]{1,0:T(8,128)(2,1)} %get-tuple-element.127, bf16[6144,1536]{1,0:T(8,128)(2,1)} %bitcast.495, ...), kind=kOutput, calls=%fused_computation.555 | convolution fusion | flops 10877828096 | bytes 43657728 | tf_op jit(solution)/shard_map/rsf,fc->rsc/dot_general | solution.py:432
  520.7 24.4 %shard_map.391 = bf16[32,192,1536]{2,1,0:T(8,128)(2,1)} custom-call(s32[32]{0:T(128)S(1)} %broadcast_xor_fusion.1.goal_ref, s32[12,32]{1,0:T(8,128)S(1)} %copy-done.14, s32[3,32]{1,0:T(4,128)S(1)} %copy-done.15, bf16[8,192,512]{2,1,0:T(8,128)(2,1)S(1)} %pad_maximum_fusion.7.refs_0_, bf16[8,192,512]{2,1,0:T(8,128)(2,1)} %collective-permute-done.45.refs_1_, ...), custom_call_target="tpu_custom_call" | custom-call | bytes 37748736 | tf_op jit(solution)/shard_map/pallas_call | solution.py:118
  545.1 7.3 fusion.172
  563.4 7.4 add_convert_fusion.4.v_ref
  574.9 64.8 %shard_map.394 = (bf16[576,1536]{1,0:T(8,128)(2,1)}, bf16[576,1536]{1,0:T(8,128)(2,1)}, bf16[896,1536]{1,0:T(8,128)(2,1)}, bf16[896,1536]{1,0:T(8,128)(2,1)}) custom-call(bf16[576,1536]{1,0:T(8,128)(2,1)} %fusion.55.q_ref, bf16[896,1536]{1,0:T(8,128)(2,1)} %convolution_convert_fusion.9.k_ref, bf16[896,1536]{1,0:T(8,128)(2,1)} %add_convert_fusion.4.v_ref, ...), custom_call_target="tpu_custom_call" | custom-call | flops 19025362944 | bytes 20152320 | tf_op jit(solution)/shard_map/pallas_call | solution.py:240
  664.7 24.2 %multiply_reduce_fusion = (f32[6144]{0:T(1024)}, f32[6144]{0:T(1024)}, f32[576,6144]{1,0:T(8,128)}) fusion(f32[576,6144]{1,0:T(8,128)} %get-tuple-element.128, bf16[6144,1536]{1,0:T(8,128)(2,1)} %bitcast.496, bf16[1,576,1536]{2,1,0:T(8,128)(2,1)S(1)} %get-tuple-element.118), kind=kOutput, calls=%fused_computation.16 | convolution fusion | flops 10882240512 | bytes 49004544 | tf_op jit(solution)/shard_map/rsc,fc->rsf/dot_general | solution.py:532
  688.9 12.5 fusion.111
  701.9 33.6 %convert_reduce_fusion = (f32[6144]{0:T(1024)}, bf16[1,576,6144]{2,1,0:T(8,128)(2,1)}) fusion(f32[576,6144]{1,0:T(8,128)} %get-tuple-element.130, s32[576]{0:T(1024)S(1)} %copy-done.101, f32[4,6144]{1,0:T(4,128)} %copy-done.97, f32[1,6144,4]{1,2,0:T(4,128)} %get-tuple-element.287, f32[4]{0:T(128)} %negate_multiply_fusion.3, f32[4]{0:T(128)} %copy-done.162, ...), kind=kOutput, calls=%fused_computation.17 | convolution fusion | flops 251359488 | bytes 78129440 | tf_op jit(solution)/shard_map/transpose(jvp(rsl,rsf->rlf))/dot_general | solution.py:305
  735.5 17.9 %fusion.40 = (f32[576]{0:T(1024)S(1)}, f32[576,1536]{1,0:T(8,128)S(1)}) fusion(f32[1,576,1536]{2,1,0:T(8,128)} %get-tuple-element.132, f32[576]{0:T(1024)S(1)} %copy-done.124, bf16[6144,1536]{1,0:T(8,128)(2,1)} %bitcast.494, bf16[1,576,6144]{2,1,0:T(8,128)(2,1)} %get-tuple-element.292), kind=kOutput, calls=%fused_computation.85 | convolution fusion | flops 10874289152 | bytes 33034752 | tf_op jit(solution)/shard_map/rsf,fc->rsc/dot_general | solution.py:539
  755.7 11.7 multiply_select_fusion.5
  767.6 13.6 %multiply_select_fusion.17 = (f32[1,576,1536]{2,1,0:T(8,128)}, f32[1,576,1536]{2,1,0:T(8,128)}, f32[1,576,1536]{2,1,0:T(8,128)}, f32[1,576,1536]{2,1,0:T(8,128)}...) fusion(f32[1536]{0:T(1024)S(1)} %copy-done.118, ...), kind=kLoop, calls=%fused_computation.183 | loop fusion | flops 15040512 | bytes 42506688 | tf_op jit(solution)/shard_map/transpose(jvp(jit(_where)))/select_n | solution.py:299
  781.3 11.0 multiply_select_fusion.14
  792.3 8.7 multiply_reduce_fusion.20
  803.6 11.9 convolution_convert_fusion.2
  815.6 9.9 convolution_convert_fusion
  884.6 7.6 convolution_convert_fusion.4
  892.2 8.0 convolution_convert_fusion.6
  900.2 19.0 %pad_add_fusion = f32[1,626,1536]{2,1,0:T(8,128)S(1)} fusion(f32[1,576,1536]{2,1,0:T(8,128)} %get-tuple-element.214, f32[1,576,1536]{2,1,0:T(8,128)} %get-tuple-element.213, f32[1,576,1536]{2,1,0:T(8,128)} %get-tuple-element.215, f32[1,576,1536]{2,1,0:T(8,128)} %get-tuple-element.216, f32[1,576,1536]{2,1,0:T(8,128)} %get-tuple-element.209, ...), kind=kLoop, calls=%fused_computation.69 | loop fusion | flops 13461504 | bytes 56930304 | tf_op jit(solution)/shard_map/transpose(jvp())/add_any | solution.py:298
  919.2 10.3 fusion.37
  929.5 8.4 convolution_convert_fusion.5
  937.9 11.2 pad_maximum_fusion
  967.1 15.6 %collective-permute-done.98 = bf16[2,2,2,40,1536]{4,3,0,1,2:T(8,128)(2,1)S(1)} collective-permute-done((bf16[2,2,2,40,1536]{4,3,0,1,2:T(8,128)(2,1)S(1)}, bf16[2,2,2,40,1536]{4,3,0,1,2:T(8,128)(2,1)S(1)}, u32[]{:S(2)}, u32[]{:S(2)}) %collective-permute-start.98) | collective-permute-done | bytes 983072 | tf_op jit(solution)/shard_map/ppermute | solution.py:27
  1010.9 11.4 add_convert_fusion.2
  1029.9 10.4 add_convert_fusion.1
  1045.8 13.0 add_convert_fusion
  1071.3 25.7 %collective-permute-done.93 = bf16[2,2,2,192,512]{4,3,0,1,2:T(8,128)(2,1)} collective-permute-done((bf16[2,2,2,192,512]{4,3,0,1,2:T(8,128)(2,1)S(1)}, bf16[2,2,2,192,512]{4,3,0,1,2:T(8,128)(2,1)}, u32[]{:S(2)}, u32[]{:S(2)}) %collective-permute-start.93) | collective-permute-done | bytes 1572896 | tf_op jit(solution)/shard_map/ppermute | solution.py:27
  1104.6 20.0 %collective-permute-done.111 = bf16[2,2,2,192,512]{4,3,0,1,2:T(8,128)(2,1)S(1)} collective-permute-done((bf16[2,2,2,192,512]{4,3,0,1,2:T(8,128)(2,1)S(1)}, bf16[2,2,2,192,512]{4,3,0,1,2:T(8,128)(2,1)S(1)}, u32[]{:S(2)}, u32[]{:S(2)}) %collective-permute-start.111) | collective-permute-done | bytes 1572896 | tf_op jit(solution)/shard_map/ppermute | solution.py:27
  1135.7 15.4 %collective-permute-done.81 = bf16[2,2,192,512]{3,2,0,1:T(8,128)(2,1)S(1)} collective-permute-done((bf16[2,2,192,512]{3,2,0,1:T(8,128)(2,1)S(1)}, bf16[2,2,192,512]{3,2,0,1:T(8,128)(2,1)S(1)}, u32[]{:S(2)}, u32[]{:S(2)}) %collective-permute-start.81) | collective-permute-done | bytes 786464 | tf_op jit(solution)/shard_map/ppermute | solution.py:27
  1152.0 16.0 %collective-permute-done.77 = bf16[2,2,192,512]{3,2,0,1:T(8,128)(2,1)S(1)} collective-permute-done((bf16[2,2,192,512]{3,2,0,1:T(8,128)(2,1)S(1)}, bf16[2,2,192,512]{3,2,0,1:T(8,128)(2,1)S(1)}, u32[]{:S(2)}, u32[]{:S(2)}) %collective-permute-start.77) | collective-permute-done | bytes 786464 | tf_op jit(solution)/shard_map/ppermute | solution.py:27
  1170.6 14.3 %collective-permute-done.94 = bf16[2,2,192,512]{3,2,0,1:T(8,128)(2,1)S(1)} collective-permute-done((bf16[2,2,192,512]{3,2,0,1:T(8,128)(2,1)S(1)}, bf16[2,2,192,512]{3,2,0,1:T(8,128)(2,1)S(1)}, u32[]{:S(2)}, u32[]{:S(2)}) %collective-permute-start.94) | collective-permute-done | bytes 786464 | tf_op jit(solution)/shard_map/ppermute | solution.py:27
  1185.7 16.0 %collective-permute-done.90 = bf16[2,2,192,512]{3,2,0,1:T(8,128)(2,1)S(1)} collective-permute-done((bf16[2,2,192,512]{3,2,0,1:T(8,128)(2,1)S(1)}, bf16[2,2,192,512]{3,2,0,1:T(8,128)(2,1)S(1)}, u32[]{:S(2)}, u32[]{:S(2)}) %collective-permute-start.90) | collective-permute-done | bytes 786464 | tf_op jit(solution)/shard_map/ppermute | solution.py:27
  1203.5 15.1 %collective-permute-done.112 = bf16[2,2,192,512]{3,2,0,1:T(8,128)(2,1)S(1)} collective-permute-done((bf16[2,2,192,512]{3,2,0,1:T(8,128)(2,1)S(1)}, bf16[2,2,192,512]{3,2,0,1:T(8,128)(2,1)S(1)}, u32[]{:S(2)}, u32[]{:S(2)}) %collective-permute-start.112) | collective-permute-done | bytes 786464 | tf_op jit(solution)/shard_map/ppermute | solution.py:27
  1218.8 11.1 collective-permute-done.108
  1246.7 14.2 %collective-permute-done.87 = bf16[2,192,512]{2,1,0:T(8,128)(2,1)S(1)} collective-permute-done((bf16[2,192,512]{2,1,0:T(8,128)(2,1)S(1)}, bf16[2,192,512]{2,1,0:T(8,128)(2,1)S(1)}, u32[]{:S(2)}, u32[]{:S(2)}) %collective-permute-start.87) | collective-permute-done | bytes 393248 | tf_op jit(solution)/shard_map/ppermute | solution.py:27
  1264.2 8.9 collective-permute-done.109
  1280.7 18.0 %collective-permute-done.75 = bf16[192,512]{1,0:T(8,128)(2,1)S(1)} collective-permute-done((bf16[192,512]{1,0:T(8,128)(2,1)S(1)}, bf16[192,512]{1,0:T(8,128)(2,1)S(1)}, u32[]{:S(2)}, u32[]{:S(2)}) %collective-permute-start.75) | collective-permute-done | bytes 196640 | tf_op jit(solution)/shard_map/ppermute | solution.py:27
  (926 shorter events, 506.1 us)
Async XLA Ops:
  13.9 39.8 %collective-permute-start.18 = (bf16[1,192,512]{2,1,0:T(8,128)(2,1)S(1)}, bf16[1,192,512]{2,1,0:T(8,128)(2,1)}, u32[]{:S(2)}, u32[]{:S(2)}) collective-permute-start(bf16[1,192,512]{2,1,0:T(8,128)(2,1)S(1)} %get-tuple-element.242), channel_id=1, source_target_pairs={{0,8},{1,9},{2,10},{3,11},{4,12},{5,13},{6,14},{7,15},{8,0},{9,1},... | collective-permute-start | bytes 589832 | tf_op jit(solution)/shard_map/ppermute | solution.py:27
  100.1 40.3 %collective-permute-start.8 = (bf16[4,192,512]{2,1,0:T(8,128)(2,1)}, bf16[4,192,512]{2,1,0:T(8,128)(2,1)}, u32[]{:S(2)}, u32[]{:S(2)}) collective-permute-start(bf16[4,192,512]{2,1,0:T(8,128)(2,1)} %pad_maximum_fusion.11), channel_id=1, source_target_pairs={{0,2},{1,3},{2,0},{3,1},{4,6},{5,7},{6,4},{7,5},{8,10},{9,11},{10,... | collective-permute-start | bytes 2359304 | tf_op jit(solution)/shard_map/ppermute | solution.py:27
  106.1 57.6 %collective-permute-start.14 = (bf16[4,192,512]{2,1,0:T(8,128)(2,1)}, bf16[4,192,512]{2,1,0:T(8,128)(2,1)}, u32[]{:S(2)}, u32[]{:S(2)}) collective-permute-start(bf16[4,192,512]{2,1,0:T(8,128)(2,1)} %pad_maximum_fusion.12), channel_id=1, source_target_pairs={{0,1},{1,0},{2,3},{3,2},{4,5},{5,4},{6,7},{7,6},{8,9},{9,8},{10,11... | collective-permute-start | bytes 2359304 | tf_op jit(solution)/shard_map/ppermute | solution.py:27
  168.4 60.7 %collective-permute-start.44 = (bf16[4,192,512]{2,1,0:T(8,128)(2,1)}, bf16[4,192,512]{2,1,0:T(8,128)(2,1)}, u32[]{:S(2)}, u32[]{:S(2)}) collective-permute-start(bf16[4,192,512]{2,1,0:T(8,128)(2,1)} %pad_maximum_fusion.17), channel_id=1, source_target_pairs={{0,2},{1,3},{2,0},{3,1},{4,6},{5,7},{6,4},{7,5},{8,10},{9,11},{10,... | collective-permute-start | bytes 2359304 | tf_op jit(solution)/shard_map/ppermute | solution.py:27
  176.1 53.1 %collective-permute-start.50 = (bf16[4,192,512]{2,1,0:T(8,128)(2,1)}, bf16[4,192,512]{2,1,0:T(8,128)(2,1)}, u32[]{:S(2)}, u32[]{:S(2)}) collective-permute-start(bf16[4,192,512]{2,1,0:T(8,128)(2,1)} %pad_maximum_fusion.18), channel_id=1, source_target_pairs={{0,1},{1,0},{2,3},{3,2},{4,5},{5,4},{6,7},{7,6},{8,9},{9,8},{10,11... | collective-permute-start | bytes 2359304 | tf_op jit(solution)/shard_map/ppermute | solution.py:27
  182.0 46.6 %collective-permute-start.62 = (bf16[4,40,1536]{2,1,0:T(8,128)(2,1)}, bf16[4,40,1536]{2,1,0:T(8,128)(2,1)}, u32[]{:S(2)}, u32[]{:S(2)}) collective-permute-start(bf16[4,40,1536]{2,1,0:T(8,128)(2,1)} %pad_maximum_fusion.20), channel_id=1, source_target_pairs={{0,1},{1,0},{2,3},{3,2},{4,5},{5,4},{6,7},{7,6},{8,9},{9,8},{10,11... | collective-permute-start | bytes 1474568 | tf_op jit(solution)/shard_map/ppermute | solution.py:27
  195.2 87.8 %collective-permute-start.9 = (bf16[8,192,512]{2,1,0:T(8,128)(2,1)S(1)}, bf16[8,192,512]{2,1,0:T(8,128)(2,1)}, u32[]{:S(2)}, u32[]{:S(2)}) collective-permute-start(bf16[8,192,512]{2,1,0:T(8,128)(2,1)S(1)} %pad_maximum_fusion.1.refs_0_), channel_id=1, source_target_pairs={{0,1},{1,0},{2,3},{3,2},{4,5},{5,4},{6,7},{7,6},{8,9},{9,8},{10,11... | collective-permute-start | bytes 4718600 | tf_op jit(solution)/shard_map/ppermute | solution.py:27
  201.3 83.3 %collective-permute-start.10 = (bf16[8,192,512]{2,1,0:T(8,128)(2,1)S(1)}, bf16[8,192,512]{2,1,0:T(8,128)(2,1)}, u32[]{:S(2)}, u32[]{:S(2)}) collective-permute-start(bf16[8,192,512]{2,1,0:T(8,128)(2,1)S(1)} %pad_maximum_fusion.1.refs_0_), channel_id=1, source_target_pairs={{0,16},{16,0},{1,17},{17,1},{2,18},{18,2},{3,19},{19,3},{4,20},{20... | collective-permute-start | bytes 4718600 | tf_op jit(solution)/shard_map/ppermute | solution.py:27
  228.7 55.9 %collective-permute-start.15 = (bf16[8,192,512]{2,1,0:T(8,128)(2,1)S(1)}, bf16[8,192,512]{2,1,0:T(8,128)(2,1)}, u32[]{:S(2)}, u32[]{:S(2)}) collective-permute-start(bf16[8,192,512]{2,1,0:T(8,128)(2,1)S(1)} %pad_maximum_fusion.2.refs_4_), channel_id=1, source_target_pairs={{0,2},{1,3},{2,0},{3,1},{4,6},{5,7},{6,4},{7,5},{8,10},{9,11},{10,... | collective-permute-start | bytes 4718600 | tf_op jit(solution)/shard_map/ppermute | solution.py:27
  229.2 70.6 %collective-permute-start.16 = (bf16[8,192,512]{2,1,0:T(8,128)(2,1)S(1)}, bf16[8,192,512]{2,1,0:T(8,128)(2,1)}, u32[]{:S(2)}, u32[]{:S(2)}) collective-permute-start(bf16[8,192,512]{2,1,0:T(8,128)(2,1)S(1)} %pad_maximum_fusion.2.refs_4_), channel_id=1, source_target_pairs={{0,16},{16,0},{1,17},{17,1},{2,18},{18,2},{3,19},{19,3},{4,20},{20... | collective-permute-start | bytes 4718600 | tf_op jit(solution)/shard_map/ppermute | solution.py:27
  229.2 49.1 %collective-permute-start.56 = (bf16[4,192,512]{2,1,0:T(8,128)(2,1)}, bf16[4,192,512]{2,1,0:T(8,128)(2,1)}, u32[]{:S(2)}, u32[]{:S(2)}) collective-permute-start(bf16[4,192,512]{2,1,0:T(8,128)(2,1)} %pad_maximum_fusion.19), channel_id=1, source_target_pairs={{0,1},{1,0},{2,3},{3,2},{4,5},{5,4},{6,7},{7,6},{8,9},{9,8},{10,11... | collective-permute-start | bytes 2359304 | tf_op jit(solution)/shard_map/ppermute | solution.py:27
  282.9 41.4 %collective-permute-start.21 = (bf16[8,192,512]{2,1,0:T(8,128)(2,1)}, bf16[8,192,512]{2,1,0:T(8,128)(2,1)}, u32[]{:S(2)}, u32[]{:S(2)}) collective-permute-start(bf16[8,192,512]{2,1,0:T(8,128)(2,1)} %pad_maximum_fusion.3.refs_8_), channel_id=1, source_target_pairs={{0,4},{1,5},{2,6},{3,7},{4,0},{5,1},{6,2},{7,3},{8,12},{9,13},{10,... | collective-permute-start | bytes 4718600 | tf_op jit(solution)/shard_map/ppermute | solution.py:27
  284.5 40.4 %collective-permute-start.22 = (bf16[8,192,512]{2,1,0:T(8,128)(2,1)}, bf16[8,192,512]{2,1,0:T(8,128)(2,1)}, u32[]{:S(2)}, u32[]{:S(2)}) collective-permute-start(bf16[8,192,512]{2,1,0:T(8,128)(2,1)} %pad_maximum_fusion.3.refs_8_), channel_id=1, source_target_pairs={{0,16},{16,0},{1,17},{17,1},{2,18},{18,2},{3,19},{19,3},{4,20},{20... | collective-permute-start | bytes 4718600 | tf_op jit(solution)/shard_map/ppermute | solution.py:27
  284.6 41.1 %collective-permute-start.11 = (bf16[8,192,512]{2,1,0:T(8,128)(2,1)}, bf16[8,192,512]{2,1,0:T(8,128)(2,1)}, u32[]{:S(2)}, u32[]{:S(2)}) collective-permute-start(bf16[8,192,512]{2,1,0:T(8,128)(2,1)} %collective-permute-done.9.refs_1_), channel_id=1, source_target_pairs={{0,16},{16,0},{1,17},{17,1},{2,18},{18,2},{3,19},{19,3},{4,20},{20... | collective-permute-start | bytes 4718600 | tf_op jit(solution)/shard_map/ppermute | solution.py:27
  324.4 59.6 %collective-permute-start.27 = (bf16[8,192,512]{2,1,0:T(8,128)(2,1)S(1)}, bf16[8,192,512]{2,1,0:T(8,128)(2,1)}, u32[]{:S(2)}, u32[]{:S(2)}) collective-permute-start(bf16[8,192,512]{2,1,0:T(8,128)(2,1)S(1)} %pad_maximum_fusion.4.refs_0_), channel_id=1, source_target_pairs={{0,1},{1,0},{2,3},{3,2},{4,5},{5,4},{6,7},{7,6},{8,9},{9,8},{10,11... | collective-permute-start | bytes 4718600 | tf_op jit(solution)/shard_map/ppermute | solution.py:27
  325.0 59.3 %collective-permute-start.28 = (bf16[8,192,512]{2,1,0:T(8,128)(2,1)S(1)}, bf16[8,192,512]{2,1,0:T(8,128)(2,1)}, u32[]{:S(2)}, u32[]{:S(2)}) collective-permute-start(bf16[8,192,512]{2,1,0:T(8,128)(2,1)S(1)} %pad_maximum_fusion.4.refs_0_), channel_id=1, source_target_pairs={{0,16},{16,0},{1,17},{17,1},{2,18},{18,2},{3,19},{19,3},{4,20},{20... | collective-permute-start | bytes 4718600 | tf_op jit(solution)/shard_map/ppermute | solution.py:27
  325.2 59.3 %collective-permute-start.33 = (bf16[8,192,512]{2,1,0:T(8,128)(2,1)S(1)}, bf16[8,192,512]{2,1,0:T(8,128)(2,1)}, u32[]{:S(2)}, u32[]{:S(2)}) collective-permute-start(bf16[8,192,512]{2,1,0:T(8,128)(2,1)S(1)} %pad_maximum_fusion.5.refs_4_), channel_id=1, source_target_pairs={{0,2},{1,3},{2,0},{3,1},{4,6},{5,7},{6,4},{7,5},{8,10},{9,11},{10,... | collective-permute-start | bytes 4718600 | tf_op jit(solution)/shard_map/ppermute | solution.py:27
  354.5 84.3 %collective-permute-start.34 = (bf16[8,192,512]{2,1,0:T(8,128)(2,1)S(1)}, bf16[8,192,512]{2,1,0:T(8,128)(2,1)S(1)}, u32[]{:S(2)}, u32[]{:S(2)}) collective-permute-start(bf16[8,192,512]{2,1,0:T(8,128)(2,1)S(1)} %pad_maximum_fusion.5.refs_4_), channel_id=1, source_target_pairs={{0,16},{16,0},{1,17},{17,1},{2,18},{18,2},{3,19},{19,3},{4,20},{20... | collective-permute-start | bytes 4718600 | tf_op jit(solution)/shard_map/ppermute | solution.py:27
  355.8 85.7 %collective-permute-start.39 = (bf16[8,192,512]{2,1,0:T(8,128)(2,1)}, bf16[8,192,512]{2,1,0:T(8,128)(2,1)}, u32[]{:S(2)}, u32[]{:S(2)}) collective-permute-start(bf16[8,192,512]{2,1,0:T(8,128)(2,1)} %pad_maximum_fusion.6.refs_8_), channel_id=1, source_target_pairs={{0,4},{1,5},{2,6},{3,7},{4,0},{5,1},{6,2},{7,3},{8,12},{9,13},{10,... | collective-permute-start | bytes 4718600 | tf_op jit(solution)/shard_map/ppermute | solution.py:27
  383.9 57.6 %collective-permute-start.40 = (bf16[8,192,512]{2,1,0:T(8,128)(2,1)}, bf16[8,192,512]{2,1,0:T(8,128)(2,1)S(1)}, u32[]{:S(2)}, u32[]{:S(2)}) collective-permute-start(bf16[8,192,512]{2,1,0:T(8,128)(2,1)} %pad_maximum_fusion.6.refs_8_), channel_id=1, source_target_pairs={{0,16},{16,0},{1,17},{17,1},{2,18},{18,2},{3,19},{19,3},{4,20},{20... | collective-permute-start | bytes 4718600 | tf_op jit(solution)/shard_map/ppermute | solution.py:27
  384.3 58.9 %collective-permute-start.29 = (bf16[8,192,512]{2,1,0:T(8,128)(2,1)}, bf16[8,192,512]{2,1,0:T(8,128)(2,1)S(1)}, u32[]{:S(2)}, u32[]{:S(2)}) collective-permute-start(bf16[8,192,512]{2,1,0:T(8,128)(2,1)} %collective-permute-done.27.refs_1_), channel_id=1, source_target_pairs={{0,16},{16,0},{1,17},{17,1},{2,18},{18,2},{3,19},{19,3},{4,20},{20... | collective-permute-start | bytes 4718600 | tf_op jit(solution)/shard_map/ppermute | solution.py:27
  384.5 60.5 %collective-permute-start.35 = (bf16[8,192,512]{2,1,0:T(8,128)(2,1)}, bf16[8,192,512]{2,1,0:T(8,128)(2,1)S(1)}, u32[]{:S(2)}, u32[]{:S(2)}) collective-permute-start(bf16[8,192,512]{2,1,0:T(8,128)(2,1)} %collective-permute-done.33.refs_5_), channel_id=1, source_target_pairs={{0,16},{16,0},{1,17},{17,1},{2,18},{18,2},{3,19},{19,3},{4,20},{20... | collective-permute-start | bytes 4718600 | tf_op jit(solution)/shard_map/ppermute | solution.py:27
  440.0 54.6 %collective-permute-start.45 = (bf16[8,192,512]{2,1,0:T(8,128)(2,1)S(1)}, bf16[8,192,512]{2,1,0:T(8,128)(2,1)}, u32[]{:S(2)}, u32[]{:S(2)}) collective-permute-start(bf16[8,192,512]{2,1,0:T(8,128)(2,1)S(1)} %pad_maximum_fusion.7.refs_0_), channel_id=1, source_target_pairs={{0,1},{1,0},{2,3},{3,2},{4,5},{5,4},{6,7},{7,6},{8,9},{9,8},{10,11... | collective-permute-start | bytes 4718600 | tf_op jit(solution)/shard_map/ppermute | solution.py:27
  441.5 53.2 %collective-permute-start.46 = (bf16[8,192,512]{2,1,0:T(8,128)(2,1)S(1)}, bf16[8,192,512]{2,1,0:T(8,128)(2,1)}, u32[]{:S(2)}, u32[]{:S(2)}) collective-permute-start(bf16[8,192,512]{2,1,0:T(8,128)(2,1)S(1)} %pad_maximum_fusion.7.refs_0_), channel_id=1, source_target_pairs={{0,16},{16,0},{1,17},{17,1},{2,18},{18,2},{3,19},{19,3},{4,20},{20... | collective-permute-start | bytes 4718600 | tf_op jit(solution)/shard_map/ppermute | solution.py:27
  441.5 53.7 %collective-permute-start.51 = (bf16[8,192,512]{2,1,0:T(8,128)(2,1)S(1)}, bf16[8,192,512]{2,1,0:T(8,128)(2,1)}, u32[]{:S(2)}, u32[]{:S(2)}) collective-permute-start(bf16[8,192,512]{2,1,0:T(8,128)(2,1)S(1)} %pad_maximum_fusion.8.refs_4_), channel_id=1, source_target_pairs={{0,2},{1,3},{2,0},{3,1},{4,6},{5,7},{6,4},{7,5},{8,10},{9,11},{10,... | collective-permute-start | bytes 4718600 | tf_op jit(solution)/shard_map/ppermute | solution.py:27
  444.3 51.0 %collective-permute-start.57 = (bf16[8,192,512]{2,1,0:T(8,128)(2,1)}, bf16[8,192,512]{2,1,0:T(8,128)(2,1)}, u32[]{:S(2)}, u32[]{:S(2)}) collective-permute-start(bf16[8,192,512]{2,1,0:T(8,128)(2,1)} %pad_maximum_fusion.9.refs_8_), channel_id=1, source_target_pairs={{0,4},{1,5},{2,6},{3,7},{4,0},{5,1},{6,2},{7,3},{8,12},{9,13},{10,... | collective-permute-start | bytes 4718600 | tf_op jit(solution)/shard_map/ppermute | solution.py:27
  465.2 55.5 %collective-permute-start.52 = (bf16[8,192,512]{2,1,0:T(8,128)(2,1)S(1)}, bf16[8,192,512]{2,1,0:T(8,128)(2,1)S(1)}, u32[]{:S(2)}, u32[]{:S(2)}) collective-permute-start(bf16[8,192,512]{2,1,0:T(8,128)(2,1)S(1)} %pad_maximum_fusion.8.refs_4_), channel_id=1, source_target_pairs={{0,16},{16,0},{1,17},{17,1},{2,18},{18,2},{3,19},{19,3},{4,20},{20... | collective-permute-start | bytes 4718600 | tf_op jit(solution)/shard_map/ppermute | solution.py:27
  877.1 76.9 %collective-permute-start.66 = (f32[2,2,2,2,64,128]{5,4,3,2,1,0:T(8,128)}, f32[2,2,2,2,64,128]{5,4,3,2,1,0:T(8,128)S(1)}, u32[]{:S(2)}, u32[]{:S(2)}) collective-permute-start(f32[2,2,2,2,64,128]{5,4,3,2,1,0:T(8,128)} %dynamic-slice_bitcast_fusion.10), channel_id=1, source_target_pairs={{0,16},{16,0},{1,17},{17,1},{2,18},{18,2},{3,19},{19,3},{4,20},{20... | collective-permute-start | bytes 1572872 | tf_op jit(solution)/shard_map/ppermute | solution.py:27
  877.5 133.4 %collective-permute-start.71 = (bf16[3072,1536]{1,0:T(8,128)(2,1)}, bf16[3072,1536]{1,0:T(8,128)(2,1)}, u32[]{:S(2)}, u32[]{:S(2)}) collective-permute-start(bf16[3072,1536]{1,0:T(8,128)(2,1)} %convolution_convert_fusion.2), channel_id=1, source_target_pairs={{0,16},{16,0},{1,17},{17,1},{2,18},{18,2},{3,19},{19,3},{4,20},{20... | collective-permute-start | bytes 28311560 | tf_op jit(solution)/shard_map/ppermute | solution.py:27
  877.6 152.2 %collective-permute-start.84 = (bf16[3072,1536]{1,0:T(8,128)(2,1)}, bf16[3072,1536]{1,0:T(8,128)(2,1)}, u32[]{:S(2)}, u32[]{:S(2)}) collective-permute-start(bf16[3072,1536]{1,0:T(8,128)(2,1)} %convolution_convert_fusion), channel_id=1, source_target_pairs={{0,16},{16,0},{1,17},{17,1},{2,18},{18,2},{3,19},{19,3},{4,20},{20... | collective-permute-start | bytes 28311560 | tf_op jit(solution)/shard_map/ppermute | solution.py:27
  883.3 71.3 %collective-permute-start.97 = (bf16[2,2,2,2,40,1536]{5,4,0,1,3,2:T(8,128)(2,1)}, bf16[2,2,2,2,40,1536]{5,4,0,1,3,2:T(8,128)(2,1)}, u32[]{:S(2)}, u32[]{:S(2)}) collective-permute-start(bf16[2,2,2,2,40,1536]{5,4,0,1,3,2:T(8,128)(2,1)} %bitcast.474), channel_id=1, source_target_pairs={{0,16},{16,0},{1,17},{17,1},{2,18},{18,2},{3,19},{19,3},{4,20},{20... | collective-permute-start | bytes 5898248 | tf_op jit(solution)/shard_map/ppermute | solution.py:27
  965.9 78.0 %collective-permute-start.102 = (bf16[3072,1536]{1,0:T(8,128)(2,1)}, bf16[3072,1536]{1,0:T(8,128)(2,1)}, u32[]{:S(2)}, u32[]{:S(2)}) collective-permute-start(bf16[3072,1536]{1,0:T(8,128)(2,1)} %pad_maximum_fusion), channel_id=1, source_target_pairs={{0,16},{16,0},{1,17},{17,1},{2,18},{18,2},{3,19},{19,3},{4,20},{20... | collective-permute-start | bytes 28311560 | tf_op jit(solution)/shard_map/ppermute | solution.py:27
  1041.5 55.5 %collective-permute-start.93 = (bf16[2,2,2,192,512]{4,3,0,1,2:T(8,128)(2,1)S(1)}, bf16[2,2,2,192,512]{4,3,0,1,2:T(8,128)(2,1)}, u32[]{:S(2)}, u32[]{:S(2)}) collective-permute-start(bf16[2,2,2,192,512]{4,3,0,1,2:T(8,128)(2,1)S(1)} %bitcast.531), channel_id=1, source_target_pairs={{0,4},{1,5},{2,6},{3,7},{4,0},{5,1},{6,2},{7,3},{8,12},{9,13},{10,... | collective-permute-start | bytes 4718600 | tf_op jit(solution)/shard_map/ppermute | solution.py:27
  1043.9 55.9 %collective-permute-start.89 = (bf16[2,2,2,192,512]{4,3,0,1,2:T(8,128)(2,1)S(1)}, bf16[2,2,2,192,512]{4,3,0,1,2:T(8,128)(2,1)}, u32[]{:S(2)}, u32[]{:S(2)}) collective-permute-start(bf16[2,2,2,192,512]{4,3,0,1,2:T(8,128)(2,1)S(1)} %bitcast.529), channel_id=1, source_target_pairs={{0,2},{1,3},{2,0},{3,1},{4,6},{5,7},{6,4},{7,5},{8,10},{9,11},{10,... | collective-permute-start | bytes 4718600 | tf_op jit(solution)/shard_map/ppermute | solution.py:27
  1063.3 39.9 %collective-permute-start.85 = (bf16[2,2,2,192,512]{4,3,0,1,2:T(8,128)(2,1)S(1)}, bf16[2,2,2,192,512]{4,3,0,1,2:T(8,128)(2,1)S(1)}, u32[]{:S(2)}, u32[]{:S(2)}) collective-permute-start(bf16[2,2,2,192,512]{4,3,0,1,2:T(8,128)(2,1)S(1)} %bitcast.532), channel_id=1, source_target_pairs={{0,1},{1,0},{2,3},{3,2},{4,5},{5,4},{6,7},{7,6},{8,9},{9,8},{10,11... | collective-permute-start | bytes 4718600 | tf_op jit(solution)/shard_map/ppermute | solution.py:27
  1066.0 58.6 %collective-permute-start.111 = (bf16[2,2,2,192,512]{4,3,0,1,2:T(8,128)(2,1)S(1)}, bf16[2,2,2,192,512]{4,3,0,1,2:T(8,128)(2,1)S(1)}, u32[]{:S(2)}, u32[]{:S(2)}) collective-permute-start(bf16[2,2,2,192,512]{4,3,0,1,2:T(8,128)(2,1)S(1)} %bitcast.530), channel_id=1, source_target_pairs={{0,4},{1,5},{2,6},{3,7},{4,0},{5,1},{6,2},{7,3},{8,12},{9,13},{10,... | collective-permute-start | bytes 4718600 | tf_op jit(solution)/shard_map/ppermute | solution.py:27
  1068.7 63.4 %collective-permute-start.107 = (bf16[2,2,2,192,512]{4,3,0,1,2:T(8,128)(2,1)S(1)}, bf16[2,2,2,192,512]{4,3,0,1,2:T(8,128)(2,1)S(1)}, u32[]{:S(2)}, u32[]{:S(2)}) collective-permute-start(bf16[2,2,2,192,512]{4,3,0,1,2:T(8,128)(2,1)S(1)} %bitcast.528), channel_id=1, source_target_pairs={{0,2},{1,3},{2,0},{3,1},{4,6},{5,7},{6,4},{7,5},{8,10},{9,11},{10,... | collective-permute-start | bytes 4718600 | tf_op jit(solution)/shard_map/ppermute | solution.py:27
  1099.8 51.3 %collective-permute-start.81 = (bf16[2,2,192,512]{3,2,0,1:T(8,128)(2,1)S(1)}, bf16[2,2,192,512]{3,2,0,1:T(8,128)(2,1)S(1)}, u32[]{:S(2)}, u32[]{:S(2)}) collective-permute-start(bf16[2,2,192,512]{3,2,0,1:T(8,128)(2,1)S(1)} %dynamic-slice_bitcast_fusion.7), channel_id=1, source_target_pairs={{0,1},{1,0},{2,3},{3,2},{4,5},{5,4},{6,7},{7,6},{8,9},{9,8},{10,11... | collective-permute-start | bytes 2359304 | tf_op jit(solution)/shard_map/ppermute | solution.py:27
  1103.2 64.8 %collective-permute-start.77 = (bf16[2,2,192,512]{3,2,0,1:T(8,128)(2,1)S(1)}, bf16[2,2,192,512]{3,2,0,1:T(8,128)(2,1)S(1)}, u32[]{:S(2)}, u32[]{:S(2)}) collective-permute-start(bf16[2,2,192,512]{3,2,0,1:T(8,128)(2,1)S(1)} %dynamic-slice_bitcast_fusion.8), channel_id=1, source_target_pairs={{0,1},{1,0},{2,3},{3,2},{4,5},{5,4},{6,7},{7,6},{8,9},{9,8},{10,11... | collective-permute-start | bytes 2359304 | tf_op jit(solution)/shard_map/ppermute | solution.py:27
  1124.6 44.5 %collective-permute-start.73 = (bf16[2,2,192,512]{3,2,0,1:T(8,128)(2,1)S(1)}, bf16[2,2,192,512]{3,2,0,1:T(8,128)(2,1)S(1)}, u32[]{:S(2)}, u32[]{:S(2)}) collective-permute-start(bf16[2,2,192,512]{3,2,0,1:T(8,128)(2,1)S(1)} %dynamic-slice_bitcast_fusion.9), channel_id=1, source_target_pairs={{0,2},{1,3},{2,0},{3,1},{4,6},{5,7},{6,4},{7,5},{8,10},{9,11},{10,... | collective-permute-start | bytes 2359304 | tf_op jit(solution)/shard_map/ppermute | solution.py:27
  1132.1 52.8 %collective-permute-start.94 = (bf16[2,2,192,512]{3,2,0,1:T(8,128)(2,1)S(1)}, bf16[2,2,192,512]{3,2,0,1:T(8,128)(2,1)S(1)}, u32[]{:S(2)}, u32[]{:S(2)}) collective-permute-start(bf16[2,2,192,512]{3,2,0,1:T(8,128)(2,1)S(1)} %dynamic-slice_bitcast_fusion.4), channel_id=1, source_target_pairs={{0,1},{1,0},{2,3},{3,2},{4,5},{5,4},{6,7},{7,6},{8,9},{9,8},{10,11... | collective-permute-start | bytes 2359304 | tf_op jit(solution)/shard_map/ppermute | solution.py:27
  1134.3 67.4 %collective-permute-start.90 = (bf16[2,2,192,512]{3,2,0,1:T(8,128)(2,1)S(1)}, bf16[2,2,192,512]{3,2,0,1:T(8,128)(2,1)S(1)}, u32[]{:S(2)}, u32[]{:S(2)}) collective-permute-start(bf16[2,2,192,512]{3,2,0,1:T(8,128)(2,1)S(1)} %dynamic-slice_bitcast_fusion.5), channel_id=1, source_target_pairs={{0,1},{1,0},{2,3},{3,2},{4,5},{5,4},{6,7},{7,6},{8,9},{9,8},{10,11... | collective-permute-start | bytes 2359304 | tf_op jit(solution)/shard_map/ppermute | solution.py:27
  1151.2 51.5 %collective-permute-start.86 = (bf16[2,2,192,512]{3,2,0,1:T(8,128)(2,1)S(1)}, bf16[2,2,192,512]{3,2,0,1:T(8,128)(2,1)S(1)}, u32[]{:S(2)}, u32[]{:S(2)}) collective-permute-start(bf16[2,2,192,512]{3,2,0,1:T(8,128)(2,1)S(1)} %dynamic-slice_bitcast_fusion.6), channel_id=1, source_target_pairs={{0,2},{1,3},{2,0},{3,1},{4,6},{5,7},{6,4},{7,5},{8,10},{9,11},{10,... | collective-permute-start | bytes 2359304 | tf_op jit(solution)/shard_map/ppermute | solution.py:27
  1168.0 50.6 %collective-permute-start.112 = (bf16[2,2,192,512]{3,2,0,1:T(8,128)(2,1)S(1)}, bf16[2,2,192,512]{3,2,0,1:T(8,128)(2,1)S(1)}, u32[]{:S(2)}, u32[]{:S(2)}) collective-permute-start(bf16[2,2,192,512]{3,2,0,1:T(8,128)(2,1)S(1)} %dynamic-slice_bitcast_fusion.1), channel_id=1, source_target_pairs={{0,1},{1,0},{2,3},{3,2},{4,5},{5,4},{6,7},{7,6},{8,9},{9,8},{10,11... | collective-permute-start | bytes 2359304 | tf_op jit(solution)/shard_map/ppermute | solution.py:27
  1169.1 60.9 %collective-permute-start.108 = (bf16[2,2,192,512]{3,2,0,1:T(8,128)(2,1)S(1)}, bf16[2,2,192,512]{3,2,0,1:T(8,128)(2,1)S(1)}, u32[]{:S(2)}, u32[]{:S(2)}) collective-permute-start(bf16[2,2,192,512]{3,2,0,1:T(8,128)(2,1)S(1)} %dynamic-slice_bitcast_fusion.2), channel_id=1, source_target_pairs={{0,1},{1,0},{2,3},{3,2},{4,5},{5,4},{6,7},{7,6},{8,9},{9,8},{10,11... | collective-permute-start | bytes 2359304 | tf_op jit(solution)/shard_map/ppermute | solution.py:27
  1184.9 47.0 %collective-permute-start.104 = (bf16[2,2,192,512]{3,2,0,1:T(8,128)(2,1)S(1)}, bf16[2,2,192,512]{3,2,0,1:T(8,128)(2,1)S(1)}, u32[]{:S(2)}, u32[]{:S(2)}) collective-permute-start(bf16[2,2,192,512]{3,2,0,1:T(8,128)(2,1)S(1)} %dynamic-slice_bitcast_fusion.3), channel_id=1, source_target_pairs={{0,2},{1,3},{2,0},{3,1},{4,6},{5,7},{6,4},{7,5},{8,10},{9,11},{10,... | collective-permute-start | bytes 2359304 | tf_op jit(solution)/shard_map/ppermute | solution.py:27
  1277.5 42.3 %collective-permute-start.88 = (bf16[192,512]{1,0:T(8,128)(2,1)S(1)}, bf16[192,512]{1,0:T(8,128)(2,1)S(1)}, u32[]{:S(2)}, u32[]{:S(2)}) collective-permute-start(bf16[192,512]{1,0:T(8,128)(2,1)S(1)} %dynamic-slice_bitcast_fusion.28), channel_id=1, source_target_pairs={{0,8},{1,9},{2,10},{3,11},{4,12},{5,13},{6,14},{7,15},{8,0},{9,1},... | collective-permute-start | bytes 589832 | tf_op jit(solution)/shard_map/ppermute | solution.py:27
  1280.6 43.5 %collective-permute-start.114 = (bf16[192,512]{1,0:T(8,128)(2,1)S(1)}, bf16[192,512]{1,0:T(8,128)(2,1)S(1)}, u32[]{:S(2)}, u32[]{:S(2)}) collective-permute-start(bf16[192,512]{1,0:T(8,128)(2,1)S(1)} %dynamic-slice_bitcast_fusion.23), channel_id=1, source_target_pairs={{0,8},{1,9},{2,10},{3,11},{4,12},{5,13},{6,14},{7,15},{8,0},{9,1},... | collective-permute-start | bytes 589832 | tf_op jit(solution)/shard_map/ppermute | solution.py:27
  (262 other events, 3984.9 us)

commit v2 on v1

v2 whole, which is shorter than its diff:
```python
import functools

import jax
import jax.numpy as jnp
from jax import lax
from jax.experimental import pallas as pl
from jax.experimental.pallas import tpu as pltpu
from jax.sharding import PartitionSpec as P

HEADS = 24
TEXT = 77
SIDE_UNIT = 4
SLOTS = 576
LAT_ROW = 4
GROUP = 16
SEATS = 8

HEAD_SCALE = 64**-0.5
LANES = 128
UNITS = 768
HIGHEST = lax.Precision.HIGHEST
NORM_EPS = 1e-06
MASKED = -1000000000.0


def bit_count(size):
    return size.bit_length() - 1


def swap(values, axis_name, size, bit):
    return lax.ppermute(values, axis_name, [(i, i ^ (1 << bit)) for i in range(size)])


def scatter_orders(size):
    bits = list(range(bit_count(size) - 1))
    return [bits[turn:] + bits[:turn] + [len(bits)] for turn in range(3)]


def column_pieces(width, count):
    if count == 1:
        return [(0, width)]
    unit = width // 12
    return [(0, 5 * unit), (5 * unit, 5 * unit), (10 * unit, 2 * unit)]


class Chain:
    def __init__(self):
        self.token = None

    def call(self, kernel, grid, ins, outs, scratch, *operands, scalars=()):
        earlier = () if self.token is None else (self.token,)
        held, count = len(scalars), len(operands)

        def body(*refs):
            before, rest = refs[: held + count], refs[held + count + len(earlier) :]
            rest[len(outs)][...] = jnp.zeros_like(rest[len(outs)])
            kernel(*before, *rest[: len(outs)], *rest[len(outs) + 1 :])

        token_spec = pl.BlockSpec((8, 128), lambda *_: (0, 0))
        done = pl.pallas_call(
            body,
            grid_spec=pltpu.PrefetchScalarGridSpec(
                num_scalar_prefetch=held,
                grid=grid,
                in_specs=list(ins) + [pl.BlockSpec(memory_space=pl.ANY)] * len(earlier),
                out_specs=[spec for _, _, spec in outs] + [token_spec],
                scratch_shapes=list(scratch),
            ),
            out_shape=[jax.ShapeDtypeStruct(shape, dtype) for shape, dtype, _ in outs]
            + [jax.ShapeDtypeStruct((8, 128), jnp.float32)],
            compiler_params=pltpu.CompilerParams(vmem_limit_bytes=56 << 20),
        )(*scalars, *operands, *earlier)
        self.token = done[-1]
        return done[:-1]


def whole_array(shape):
    return pl.BlockSpec(shape, lambda *_: (0,) * len(shape))


class Weight:
    def __init__(self, gathered, place, rows, block=lambda step: step):
        if rows % GROUP:
            some = gathered[:, place * rows : (place + 1) * rows]
            gathered, place, rows = some.reshape(-1, UNITS, some.shape[2]), 0, UNITS
        self.gathered, self.place, self.rows, self.block = gathered, place, rows, block
        self.total = gathered.shape[0] * rows
        self.width = gathered.shape[2]

    def by(self, block):
        return Weight(self.gathered, self.place, self.rows, block)

    def spec(self):
        return pl.BlockSpec(
            (UNITS // self.rows, self.rows, self.width), lambda i, *_: (self.block(i), self.place, 0)
        )


def rows_of(ref):
    return ref[...].reshape(UNITS, ref.shape[2])


class Piece:
    def __init__(self, base, order, bits, cut=0, width=None):
        self.base, self.order, self.bits, self.cut = base, list(order), list(bits), cut
        self.free, self.fixed, self.come = list(bits), [], None
        self.width = base.shape[-1] if width is None else width


def fold(chain, pieces, inner, outer):
    if len(pieces[0].free) == 1:
        return fold_last(chain, pieces, inner, outer)
    low_bits = bit_count(outer)
    me = lax.axis_index("dp") * outer + lax.axis_index("fsdp")
    left = len(pieces[0].free) - 1
    inside = min(max(left - 1, 0), 2)
    ins, outs, operands, plans, bits = [], [], [], [], []
    for piece in pieces:
        lazy = piece.come is None
        bit = piece.order.pop(0)
        bits.append(bit)
        rest = [b for b in piece.free if b != bit]
        near = rest[len(rest) - inside :]
        far = rest[: len(rest) - inside]

        def spec(axes, cut, width, rows, bit=bit, near=near, far=far, fixed=tuple(piece.fixed), lazy=lazy):
            def where(k, me_ref):
                place = []
                for b in axes:
                    if b in fixed:
                        place.append((me_ref[0] >> b) & 1)
                    elif b == bit:
                        place.append(1 - ((me_ref[0] >> b) & 1) if lazy else 0)
                    elif b in near:
                        place.append(0)
                    else:
                        place.append((k >> (len(far) - 1 - far.index(b))) & 1)
                return tuple(place) + (0, cut)

            shape = tuple(
                2 if (b in near and b not in fixed) or (b == bit and not lazy) else None for b in axes
            )
            return pl.BlockSpec(shape + (rows, width), where)

        rows = piece.base.shape[-2]
        ins.append(spec(piece.bits, piece.cut, piece.width, rows))
        operands.append(piece.base)
        if not lazy:
            ins.append(spec(piece.free, 0, piece.width, rows))
            operands.append(piece.come)
        shape = (2,) * len(rest) + (rows, piece.width)
        outs += [(shape, piece.base.dtype, spec(rest, 0, piece.width, rows))] * (1 if lazy else 2)
        plans.append((lazy, bit, sum(1 for b in near if b > bit)))
        piece.free = rest
    done = list(
        chain.call(
            functools.partial(fold_kernel, plans),
            (1 << (left - inside),),
            ins,
            outs,
            [],
            *operands,
            scalars=(me.astype(jnp.int32)[None],),
        )
    )
    for piece, (lazy, bit, _) in zip(pieces, plans):
        away = done.pop(0)
        if lazy:
            piece.fixed.append(bit)
        else:
            piece.base, piece.cut, piece.fixed, piece.bits = done.pop(0), 0, [], list(piece.free)
        if bit < low_bits:
            piece.come = swap(away, "fsdp", outer, bit)
        else:
            piece.come = swap(away, "dp", inner, bit - low_bits)


def fold_kernel(plans, me_ref, *refs):
    count = sum(1 if lazy else 2 for lazy, _, _ in plans)
    ins, outs = list(refs[:count]), list(refs[count:])
    for lazy, bit, before in plans:
        if lazy:
            outs.pop(0)[...] = ins.pop(0)[...]
            continue
        base, come = ins.pop(0), ins.pop(0)
        own = (me_ref[0] >> bit) & 1
        for out, side in ((outs.pop(0), 1 - own), (outs.pop(0), own)):
            at = (slice(None),) * before + (side,)
            out[...] = (base[at].astype(jnp.float32) + come[at].astype(jnp.float32)).astype(out.dtype)


def turn_kernel(values_ref, late_ref, out_ref):
    out_ref[...] = values_ref[...].T.astype(jnp.bfloat16)


def turn_late(chain, values, late):
    shape = values.shape[::-1]
    return chain.call(
        turn_kernel,
        (1,),
        [whole_array(values.shape), pl.BlockSpec(memory_space=pl.ANY)],
        [(shape, jnp.bfloat16, whole_array(shape))],
        [],
        values,
        late,
    )[0]


def last_kernel(cuts, bit, me_ref, *refs):
    own = (me_ref[0] >> bit) & 1
    ins, outs = refs[: 2 * len(cuts)], refs[2 * len(cuts) :]
    for n, (group, cut) in enumerate(cuts):
        both = ins[2 * n][...].astype(jnp.float32) + ins[2 * n + 1][...].astype(jnp.float32)
        both = both.astype(outs[2 * group].dtype)
        outs[2 * group][:, :, cut] = jnp.where(own == 0, both[1:2], both[0:1])
        outs[2 * group + 1][:, :, cut] = jnp.where(own == 0, both[0:1], both[1:2])


def fold_last(chain, pieces, inner, outer):
    bit = pieces[0].order.pop(0)
    me = lax.axis_index("dp") * outer + lax.axis_index("fsdp")
    operands, cuts, shapes = [], [], []
    for piece in pieces:
        operands += [piece.base, piece.come]
        rows = piece.base.shape[1]
        if not shapes or shapes[-1][1] != rows:
            shapes.append([1, rows, 0])
        start = shapes[-1][2]
        cuts.append((len(shapes) - 1, slice(start, start + piece.width)))
        shapes[-1][2] = start + piece.width
    dtypes = {piece.base.shape[1]: piece.base.dtype for piece in pieces}
    done = chain.call(
        functools.partial(last_kernel, cuts, bit),
        (1,),
        [whole_array(v.shape) for v in operands],
        [(tuple(shape), dtypes[shape[1]], whole_array(tuple(shape))) for shape in shapes for _ in range(2)],
        [],
        *operands,
        scalars=(me.astype(jnp.int32)[None],),
    )
    pieces[:] = [Piece(kept, [], []) for kept in done[1::2]]
    for piece, away in zip(pieces, done[::2]):
        piece.come = swap(away, "fsdp", outer, bit)


def total_kernel(turned, *refs):
    for n, turn in enumerate(turned):
        total = (refs[2 * n][...].astype(jnp.float32) + refs[2 * n + 1][...].astype(jnp.float32))[0]
        refs[2 * len(turned) + n][...] = total.T if turn else total


def totals_of(chain, pieces, turned):
    shapes = [
        piece.base.shape[:0:-1] if turn else piece.base.shape[1:] for piece, turn in zip(pieces, turned)
    ]
    operands = [v for piece in pieces for v in (piece.base, piece.come)]
    return chain.call(
        functools.partial(total_kernel, turned),
        (1,),
        [whole_array(v.shape) for v in operands],
        [(shape, jnp.float32, whole_array(shape)) for shape in shapes],
        [],
        *operands,
    )


def product(a, b, da, db):
    return lax.dot_general(a, b, (((da,), (db,)), ((), ())), preferred_element_type=jnp.float32)


def by_group(values):
    return values.reshape(values.shape[0] // GROUP, GROUP, values.shape[1])


def spread(seats, member):
    total = member[:, 0:1] * seats[0:1, :]
    for place in range(1, LAT_ROW):
        total = total + member[:, place : place + 1] * seats[place : place + 1, :]
    return total[:, None, :]


def gathered(values, member):
    by = jnp.sum(by_group(values), axis=1)
    rows = [jnp.sum(by * member[:, place : place + 1], axis=0, keepdims=True) for place in range(LAT_ROW)]
    return jnp.concatenate(rows + [jnp.zeros((SEATS - LAT_ROW, values.shape[1]), jnp.float32)], axis=0)


def neighbours(x, geometry):
    slots = x.shape[0]
    above = below = None
    for index, side in enumerate((3 * SIDE_UNIT, 4 * SIDE_UNIT, 6 * SIDE_UNIT)):
        up = geometry[3 + index] * pltpu.roll(x, side, 0)
        down = geometry[6 + index] * pltpu.roll(x, slots - side, 0)
        above = up if above is None else above + up
        below = down if below is None else below + down
    return above, geometry[0] * x, below


def geometry_columns(geometry_ref):
    return [geometry_ref[:, k : k + 1] for k in range(9)]


def entry_kernel(x_ref, taps_ref, geometry_ref, low_ref, normed_ref, scale_ref, conv_ref):
    slots, width = x_ref.shape
    geometry = geometry_columns(geometry_ref)
    total = jnp.zeros((slots, LANES), jnp.float32)
    for start in range(0, width, LANES):
        cut = slice(start, start + LANES)
        rows = neighbours(x_ref[:, cut], geometry)
        left, mid, right = (
            sum(taps_ref[3 * a + b : 3 * a + b + 1, cut] * rows[a] for a in range(3)) for b in range(3)
        )
        conv = (
            taps_ref[9:10, cut]
            + mid
            + geometry[1] * pltpu.roll(left, 1, 0)
            + geometry[2] * pltpu.roll(right, slots - 1, 0)
        )
        conv_ref[:, cut] = conv
        total = total + conv
    mean = jnp.sum(total, axis=1, keepdims=True) * (1.0 / width)
    square = jnp.zeros((slots, LANES), jnp.float32)
    for start in range(0, width, LANES):
        center = conv_ref[:, start : start + LANES] - mean
        square = square + center * center
    scale = lax.rsqrt(jnp.sum(square, axis=1, keepdims=True) * (1.0 / width) + NORM_EPS)
    scale_ref[...] = jnp.broadcast_to(scale, scale_ref.shape)
    for start in range(0, width, LANES):
        cut = slice(start, start + LANES)
        normed = (conv_ref[:, cut] - mean) * scale
        normed_ref[:, cut] = normed
        low_ref[:, cut] = normed.astype(jnp.bfloat16)


def entry(chain, x, taps, geometry):
    slots, width = x.shape
    return chain.call(
        entry_kernel,
        (1,),
        [whole_array(v.shape) for v in (x, taps, geometry)],
        [
            ((slots, width), jnp.bfloat16, whole_array((slots, width))),
            ((slots, width), jnp.float32, whole_array((slots, width))),
            ((slots, LANES), jnp.float32, whole_array((slots, LANES))),
        ],
        [pltpu.VMEM((slots, width), jnp.float32)],
        x,
        taps,
        geometry,
    )


def entry_back_kernel(q_ref, normed_ref, scale_ref, x_ref, res_ref, taps_ref, geometry_ref, bias_grad_ref, grad_ref, taps_grad_ref):
    slots, width = x_ref.shape
    geometry = geometry_columns(geometry_ref)
    scale = scale_ref[:, 0:1]
    plain = jnp.zeros((slots, LANES), jnp.float32)
    along = jnp.zeros((slots, LANES), jnp.float32)
    for start in range(0, width, LANES):
        cut = slice(start, start + LANES)
        q = q_ref[:, cut]
        plain = plain + q
        along = along + q * normed_ref[:, cut]
    plain = jnp.sum(plain, axis=1, keepdims=True) * (1.0 / width)
    along = jnp.sum(along, axis=1, keepdims=True) * (1.0 / width)
    for start in range(0, width, LANES):
        cut = slice(start, start + LANES)
        grad = (q_ref[:, cut] - plain - normed_ref[:, cut] * along) * scale
        sides = (
            pltpu.roll(grad * geometry[1], slots - 1, 0),
            grad,
            pltpu.roll(grad * geometry[2], 1, 0),
        )
        rows = neighbours(x_ref[:, cut], geometry)
        sums = [
            jnp.sum(rows[a] * sides[b], axis=0, keepdims=True) for a in range(3) for b in range(3)
        ]
        sums.append(jnp.sum(grad, axis=0, keepdims=True))
        sums.append(bias_grad_ref[0:1, cut])
        sums.append(jnp.zeros((5, LANES), jnp.float32))
        taps_grad_ref[:, cut] = jnp.concatenate(sums, axis=0)
        above, mid, below = (
            sum(taps_ref[3 * a + b : 3 * a + b + 1, cut] * sides[b] for b in range(3)) for a in range(3)
        )
        back = res_ref[:, cut] + geometry[0] * mid
        for index, side in enumerate((3 * SIDE_UNIT, 4 * SIDE_UNIT, 6 * SIDE_UNIT)):
            back = back + pltpu.roll(geometry[3 + index] * above, slots - side, 0)
            back = back + pltpu.roll(geometry[6 + index] * below, side, 0)
        grad_ref[:, cut] = back


def entry_back(chain, q, normed, scale, x, res, taps, geometry, bias_grad):
    slots, width = x.shape
    operands = (q, normed, scale, x, res, taps, geometry, bias_grad)
    return chain.call(
        entry_back_kernel,
        (1,),
        [whole_array(v.shape) for v in operands],
        [
            ((slots, width), jnp.float32, whole_array((slots, width))),
            ((16, width), jnp.float32, whole_array((16, width))),
        ],
        [],
        *operands,
    )


def hidden_kernel(normed_ref, vecs_ref, member_ref, *refs):
    weight_ref, act_ref, slope_ref, power_ref = refs
    hidden = product(normed_ref[...], rows_of(weight_ref), 1, 1) + vecs_ref[0:1, :]
    below = 0.5 + 0.5 * lax.erf(hidden * (0.5**0.5))
    act = hidden * below
    act_ref[...] = act
    slope_ref[...] = below + hidden * (jnp.exp(-0.5 * hidden * hidden) * (0.5 / jnp.pi) ** 0.5)
    power_ref[...] = gathered(act * act, member_ref[...])


def unit_columns(rows):
    return pl.BlockSpec((rows, UNITS), lambda i, *_: (0, i))


def hidden_step(chain, normed, weight, vecs, member):
    slots, width = normed.shape
    units = weight.total
    return chain.call(
        hidden_kernel,
        (units // UNITS,),
        [whole_array((slots, width)), unit_columns(vecs.shape[0]), whole_array(member.shape)] + [weight.spec()],
        [
            ((slots, units), jnp.float32, unit_columns(slots)),
            ((slots, units), jnp.float32, unit_columns(slots)),
            ((SEATS, units), jnp.float32, unit_columns(SEATS)),
        ],
        [],
        normed,
        vecs,
        member,
        weight.gathered,
    )


def norm_rows(values):
    center = values - jnp.mean(values, axis=-1, keepdims=True)
    scale = lax.rsqrt(jnp.mean(center * center, axis=-1, keepdims=True) + NORM_EPS)
    return center * scale, scale


def branch_kernel(act_ref, norms_ref, vecs_ref, member_ref, live_ref, x_ref, bias_ref, pair_ref, *refs):
    weight_ref, response_ref, res_ref, time_ref, low_ref, total_ref = refs
    step = pl.program_id(0)
    member = member_ref[...]
    act = by_group(act_ref[...])
    response = act * (1.0 + vecs_ref[1:2, :][None] * spread(norms_ref[...], member)) + vecs_ref[2:3, :][None]
    response = response.reshape(act_ref.shape).astype(jnp.bfloat16)
    response_ref[...] = response
    part = product(response, rows_of(weight_ref), 1, 0)

    @pl.when(step == 0)
    def _():
        total_ref[...] = part

    @pl.when(step > 0)
    def _():
        total_ref[...] += part

    @pl.when(step == pl.num_programs(0) - 1)
    def _():
        width = x_ref.shape[1]
        after_res = x_ref[...] + live_ref[:, 0:1] * (total_ref[...] + bias_ref[...])
        res_ref[...] = after_res
        per = spread(pair_ref[...], member)
        after_time = by_group(after_res) * (1.0 + per[:, :, :width]) + per[:, :, width:]
        after_time = after_time.reshape(after_res.shape)
        time_ref[...] = after_time
        low_ref[...] = norm_rows(after_time)[0].astype(jnp.bfloat16)


def branch_step(chain, act, norms, vecs, weight, member, live, x, bias, pair):
    slots, units = act.shape
    width = x.shape[1]
    return chain.call(
        branch_kernel,
        (units // UNITS,),
        [
            unit_columns(slots),
            unit_columns(SEATS),
            unit_columns(vecs.shape[0]),
            whole_array(member.shape),
            whole_array(live.shape),
            whole_array(x.shape),
            whole_array(bias.shape),
            whole_array(pair.shape),
        ]
        + [weight.spec()],
        [
            ((slots, units), jnp.bfloat16, unit_columns(slots)),
            ((slots, width), jnp.float32, whole_array((slots, width))),
            ((slots, width), jnp.float32, whole_array((slots, width))),
            ((slots, width), jnp.bfloat16, whole_array((slots, width))),
        ],
        [pltpu.VMEM((slots, width), jnp.float32)],
        act,
        norms,
        vecs,
        member,
        live,
        x,
        bias,
        pair,
        weight.gathered,
    )


def time_back_kernel(q_ref, time_ref, res_ref, cot_ref, pair_ref, member_ref, live_ref, grad_ref, low_ref, pair_grad_ref, bias_grad_ref):
    width = q_ref.shape[1]
    member = member_ref[...]
    normed, scale = norm_rows(time_ref[...])
    q = q_ref[...]
    plain = jnp.mean(q, axis=-1, keepdims=True)
    along = jnp.mean(q * normed, axis=-1, keepdims=True)
    grad_time = cot_ref[...] + (q - plain - normed * along) * scale
    pair_grad_ref[:, :width] = gathered(grad_time * res_ref[...], member)
    pair_grad_ref[:, width:] = gathered(grad_time, member)
    per = spread(pair_ref[:, :width], member)
    grad_res = (by_group(grad_time) * (1.0 + per)).reshape(q.shape)
    grad_ref[...] = grad_res
    low = (live_ref[:, 0:1] * grad_res).astype(jnp.bfloat16)
    low_ref[...] = low
    bias_grad_ref[...] = jnp.broadcast_to(jnp.sum(low.astype(jnp.float32), axis=0, keepdims=True), bias_grad_ref.shape)


def time_back(chain, q, after_time, after_res, cot, pair, member, live):
    slots, width = q.shape
    operands = (q, after_time, after_res, cot, pair, member, live)
    return chain.call(
        time_back_kernel,
        (1,),
        [whole_array(v.shape) for v in operands],
        [
            ((slots, width), jnp.float32, whole_array((slots, width))),
            ((slots, width), jnp.bfloat16, whole_array((slots, width))),
            ((SEATS, 2 * width), jnp.float32, whole_array((SEATS, 2 * width))),
            ((SEATS, width), jnp.float32, whole_array((SEATS, width))),
        ],
        [],
        *operands,
    )


def response_back_kernel(branch_ref, act_ref, member_ref, *refs):
    weight_ref, grad_ref, sums_ref, shift_ref = refs
    grad = product(branch_ref[...], rows_of(weight_ref), 1, 1)
    grad_ref[...] = grad
    sums_ref[...] = gathered(grad * act_ref[...], member_ref[...])
    shift_ref[...] = jnp.broadcast_to(jnp.sum(grad, axis=0, keepdims=True), shift_ref.shape)


def response_back(chain, branch, weight, act, member):
    slots, width = branch.shape
    units = weight.total
    return chain.call(
        response_back_kernel,
        (units // UNITS,),
        [whole_array(branch.shape), unit_columns(slots), whole_array(member.shape)] + [weight.spec()],
        [
            ((slots, units), jnp.float32, unit_columns(slots)),
            ((SEATS, units), jnp.float32, unit_columns(SEATS)),
            ((SEATS, units), jnp.float32, unit_columns(SEATS)),
        ],
        [],
        branch,
        act,
        member,
        weight.gathered,
    )


def hidden_back_kernel(grad_ref, act_ref, slope_ref, vecs_ref, norms_ref, ratio_ref, member_ref, *refs):
    weight_ref, low_ref, bias_ref, normed_grad_ref, total_ref = refs
    step = pl.program_id(0)
    member = member_ref[...]
    grad = by_group(grad_ref[...]) * (1.0 + vecs_ref[1:2, :][None] * spread(norms_ref[...], member))
    grad = grad + by_group(act_ref[...]) * spread(ratio_ref[...], member)
    low = (grad.reshape(act_ref.shape) * slope_ref[...]).astype(jnp.bfloat16)
    low_ref[...] = low
    bias_ref[...] = jnp.broadcast_to(jnp.sum(low.astype(jnp.float32), axis=0, keepdims=True), bias_ref.shape)
    part = product(low, rows_of(weight_ref), 1, 0)

    @pl.when(step == 0)
    def _():
        total_ref[...] = part

    @pl.when(step > 0)
    def _():
        total_ref[...] += part

    @pl.when(step == pl.num_programs(0) - 1)
    def _():
        normed_grad_ref[...] = total_ref[...]


def hidden_back(chain, grad, act, slope, vecs, norms, ratio, member, weight):
    slots, units = act.shape
    width = weight.width
    return chain.call(
        hidden_back_kernel,
        (units // UNITS,),
        [unit_columns(slots)] * 3
        + [unit_columns(vecs.shape[0]), unit_columns(SEATS), unit_columns(SEATS)]
        + [whole_array(member.shape)]
        + [weight.spec()],
        [
            ((slots, units), jnp.bfloat16, unit_columns(slots)),
            ((SEATS, units), jnp.float32, unit_columns(SEATS)),
            ((slots, width), jnp.float32, whole_array((slots, width))),
        ],
        [pltpu.VMEM((slots, width), jnp.float32)],
        grad,
        act,
        slope,
        vecs,
        norms,
        ratio,
        member,
        weight.gathered,
    )


def project_kernel(source_ref, grad_ref, bias_ref, *refs):
    weight_ref, out_ref, att_grad_ref, total_ref = refs
    step = pl.program_id(0)
    each = pl.num_programs(0) // 4
    weight = rows_of(weight_ref)

    @pl.when(step < 3 * each)
    def _():
        out = (product(source_ref[...], weight, 1, 1) + bias_ref[0:1, :]).astype(jnp.bfloat16)
        scale = jnp.where(step < each, HEAD_SCALE, 1.0).astype(jnp.bfloat16)
        out_ref[...] = out * scale

    @pl.when(step >= 3 * each)
    def _():
        part = product(grad_ref[...], weight, 1, 0)

        @pl.when(step == 3 * each)
        def _():
            total_ref[...] = part

        @pl.when(step > 3 * each)
        def _():
            total_ref[...] += part

        @pl.when(step == 4 * each - 1)
        def _():
            att_grad_ref[...] = total_ref[...].astype(jnp.bfloat16)


def project(chain, source, grad, bias, weight):
    count, width = source.shape
    slots = grad.shape[0]
    each = width // UNITS
    return chain.call(
        project_kernel,
        (4 * each,),
        [
            whole_array(source.shape),
            pl.BlockSpec((slots, UNITS), lambda i, *_: (0, jnp.maximum(i - 3 * each, 0))),
            pl.BlockSpec((SEATS, UNITS), lambda i, *_: (0, jnp.minimum(i, 3 * each - 1))),
        ]
        + [weight.spec()],
        [
            (
                (count, 3 * width),
                jnp.bfloat16,
                pl.BlockSpec((count, UNITS), lambda i, *_: (0, jnp.minimum(i, 3 * each - 1))),
            ),
            ((slots, width), jnp.bfloat16, whole_array((slots, width))),
        ],
        [pltpu.VMEM((slots, width), jnp.float32)],
        source,
        grad,
        bias,
        weight.gathered,
    )


def source_back_kernel(query_ref, key_ref, value_ref, *refs):
    weight_ref, slot_ref, text_ref, total_ref = refs
    step = pl.program_id(0)
    each = pl.num_programs(0) // 3
    slots = slot_ref.shape[0]
    weight = rows_of(weight_ref)

    @pl.when(step == 0)
    def _():
        total_ref[...] = product(key_ref[...], weight, 1, 0)

    @pl.when((step > 0) & (step < each))
    def _():
        total_ref[...] += product(key_ref[...], weight, 1, 0)

    @pl.when((step >= each) & (step < 2 * each))
    def _():
        total_ref[...] += product(value_ref[...], weight, 1, 0)

    @pl.when(step >= 2 * each)
    def _():
        total_ref[:slots, :] += product(query_ref[...], weight, 1, 0)

    @pl.when(step == 3 * each - 1)
    def _():
        slot_ref[...] = total_ref[:slots, :]
        text_ref[...] = total_ref[slots:, :].astype(jnp.bfloat16)


def source_back(chain, query, keys, values, weight):
    slots, width = query.shape
    count = keys.shape[0]
    each = width // UNITS

    def columns(rows, turn):
        return pl.BlockSpec((rows, UNITS), lambda i, *_: (0, jnp.clip(i - turn * each, 0, each - 1)))

    return chain.call(
        source_back_kernel,
        (3 * each,),
        [columns(slots, 2), columns(count, 0), columns(count, 1)]
        + [weight.spec()],
        [
            ((slots, width), jnp.float32, whole_array((slots, width))),
            ((count - slots, width), jnp.bfloat16, whole_array((count - slots, width))),
        ],
        [pltpu.VMEM((count, width), jnp.float32)],
        query,
        keys,
        values,
        weight.gathered,
    )


def output_kernel(attended_ref, time_ref, live_ref, bias_ref, weight_ref, out_ref):
    out = product(attended_ref[...], rows_of(weight_ref), 1, 1) + bias_ref[0:1, :]
    out_ref[...] = time_ref[...] + live_ref[:, 0:1] * out


def output_step(chain, attended, after_time, live, bias, weight):
    slots, width = attended.shape
    each = width // UNITS
    columns = pl.BlockSpec((slots, UNITS), lambda i, *_: (0, i))
    return chain.call(
        output_kernel,
        (each,),
        [
            whole_array(attended.shape),
            columns,
            whole_array(live.shape),
            pl.BlockSpec((SEATS, UNITS), lambda i, *_: (0, i)),
        ]
        + [weight.spec()],
        [((slots, width), jnp.float32, columns)],
        [],
        attended,
        after_time,
        live,
        bias,
        weight.gathered,
    )[0]


def half_kernel(added, half_ref, left_ref, right_ref, *refs):
    total = product(left_ref[...], right_ref[...], 0, 0)
    if added:
        total = total + refs[0][...].astype(jnp.float32)
    refs[-1][...] = total.astype(jnp.bfloat16)


def half_rows(chain, left, right, half, come=None):
    slots, units = left.shape
    width = right.shape[1]
    steps = units // 2 // UNITS
    rows = pl.BlockSpec((UNITS, width), lambda i, *_: (i, 0))
    return chain.call(
        functools.partial(half_kernel, come is not None),
        (steps,),
        [
            pl.BlockSpec((slots, UNITS), lambda i, half_ref: (0, half_ref[0] * steps + i)),
            whole_array(right.shape),
        ]
        + ([] if come is None else [rows]),
        [((units // 2, width), jnp.bfloat16, rows)],
        [],
        left,
        right,
        *(() if come is None else (come,)),
        scalars=(half.astype(jnp.int32)[None],),
    )[0]


def attn_half_kernel(added, half_ref, query_ref, key_ref, value_ref, proj_ref, source_ref, attended_ref, *refs):
    out_ref = refs[-1]
    role = 2 * half_ref[0] + pl.program_id(0) // (pl.num_programs(0) // 2)
    slots = query_ref.shape[0]

    def store(total):
        if added:
            total = total + refs[0][...].astype(jnp.float32)
        out_ref[...] = total.astype(jnp.bfloat16)

    @pl.when(role == 0)
    def _():
        store(product(query_ref[...], source_ref[:slots, :], 0, 0))

    @pl.when(role == 1)
    def _():
        store(product(key_ref[...], source_ref[...], 0, 0))

    @pl.when(role == 2)
    def _():
        store(product(value_ref[...], source_ref[...], 0, 0))

    @pl.when(role == 3)
    def _():
        store(product(proj_ref[...], attended_ref[...], 0, 0))


def attn_half(chain, query, keys, values, proj, source, attended, half, come=None):
    width = source.shape[1]
    each = width // UNITS
    rows = pl.BlockSpec((UNITS, width), lambda i, *_: (i, 0))

    def columns(values, role):
        def where(i, half_ref):
            return (0, jnp.where(2 * half_ref[0] + i // each == role, i % each, 0))

        return pl.BlockSpec((values.shape[0], UNITS), where)

    return chain.call(
        functools.partial(attn_half_kernel, come is not None),
        (2 * each,),
        [columns(v, n) for n, v in enumerate((query, keys, values, proj))]
        + [whole_array(source.shape), whole_array(attended.shape)]
        + ([] if come is None else [rows]),
        [((2 * width, width), jnp.bfloat16, rows)],
        [],
        query,
        keys,
        values,
        proj,
        source,
        attended,
        *(() if come is None else (come,)),
        scalars=(half.astype(jnp.int32)[None],),
    )[0]


def attention_kernel(q_ref, k_ref, v_ref, g_ref, bias_ref, att_ref, dq_ref, dk_ref, dv_ref):
    width = q_ref.shape[1]
    half = width // 2
    low = jnp.bfloat16
    lanes = lax.broadcasted_iota(jnp.int32, (1, width), 1)
    sublanes = lax.broadcasted_iota(jnp.int32, (width, 1), 0)
    keys, values = k_ref[...], v_ref[...]
    att_t = dq_t = d_key = d_value = None

    for head in range(2):
        own = (lanes >= head * half) & (lanes < (head + 1) * half)
        query = jnp.where(own, q_ref[...], jnp.zeros((), low))
        grad = jnp.where(own, g_ref[...], jnp.zeros((), low))
        scores = product(keys, query, 1, 1) + bias_ref[...]
        exponent = jnp.exp(scores - jnp.max(scores, axis=0, keepdims=True))
        probs = exponent * (1.0 / jnp.sum(exponent, axis=0, keepdims=True))
        probs_low = probs.astype(low)
        att_head = product(values, probs_low, 0, 0)
        grad_probs = product(values, grad, 1, 1)
        inner_sum = jnp.sum(probs * grad_probs, axis=0, keepdims=True)
        grad_scores = (probs * (grad_probs - inner_sum)).astype(low)
        value_part = product(probs_low, grad, 1, 0)
        key_part = product(grad_scores, query, 1, 0)
        dq_head = product(keys, grad_scores, 0, 0)
        if head == 0:
            att_t, dq_t, d_key, d_value = att_head, dq_head, key_part, value_part
        else:
            upper = sublanes < half
            att_t = jnp.where(upper, att_t, att_head)
            dq_t = jnp.where(upper, dq_t, dq_head)
            d_key, d_value = d_key + key_part, d_value + value_part
    att_ref[...] = att_t.T.astype(low)
    dq_ref[...] = (dq_t.T * ((width // 2) ** -0.5)).astype(low)
    dk_ref[...] = d_key.astype(low)
    dv_ref[...] = d_value.astype(low)


def attention(chain, mixed, grad, bias):
    slots, width = grad.shape
    count = mixed.shape[0]
    pair = 2 * (width // HEADS)
    each = width // pair

    def columns(rows, turn=0):
        return pl.BlockSpec((rows, pair), lambda h, *_: (0, turn * each + h))

    low = jnp.bfloat16
    return chain.call(
        attention_kernel,
        (each,),
        [columns(slots), columns(count, 1), columns(count, 2), columns(slots), whole_array(bias.shape)],
        [
            ((slots, width), low, columns(slots)),
            ((slots, width), low, columns(slots)),
            ((count, width), low, columns(count)),
            ((count, width), low, columns(count)),
        ],
        [],
        mixed,
        mixed,
        mixed,
        grad,
        bias,
    )


def layout(heights_row, widths_row):
    pixels = heights_row * widths_row
    ends_at = jnp.cumsum(pixels)
    starts_at = ends_at - pixels
    slot_ids = jnp.arange(SLOTS, dtype=jnp.int32)
    segment = jnp.sum((ends_at[None, :] <= slot_ids[:, None]).astype(jnp.int32), axis=1)
    member = segment[:, None] == jnp.arange(LAT_ROW, dtype=jnp.int32)[None, :]
    start_at = jnp.sum(jnp.where(member, starts_at[None, :], 0), axis=1)
    height_at = jnp.sum(jnp.where(member, heights_row[None, :], 0), axis=1)
    width_at = jnp.sum(jnp.where(member, widths_row[None, :], 0), axis=1)
    place_in = slot_ids - start_at
    safe_width = jnp.maximum(width_at, 1)
    column = place_in % safe_width
    row_index = place_in // safe_width
    return (segment, member, height_at, width_at, row_index, column)


def score_bias(segment, counts_row, key_pad):
    live_query = segment < LAT_ROW
    image_ok = (segment[:, None] == segment[None, :]) & live_query[None, :]
    text_index = jnp.arange(LAT_ROW * TEXT, dtype=jnp.int32)
    text_latent = text_index // TEXT
    text_limit = jnp.sum(
        jnp.where(
            text_latent[:, None] == jnp.arange(LAT_ROW, dtype=jnp.int32)[None, :],
            counts_row[None, :],
            0,
        ),
        axis=1,
    )
    text_ok = (text_latent[:, None] == segment[None, :]) & (text_index % TEXT < text_limit)[:, None]
    no_pad = jnp.zeros((key_pad, segment.shape[0]), bool)
    return jnp.where(jnp.concatenate([image_ok, text_ok, no_pad], axis=0), 0.0, MASKED)


def geometry_table(heights_row, widths_row):
    segment, member, height_at, width_at, row_index, column = layout(heights_row, widths_row)
    live = segment < LAT_ROW
    left = live & (column >= 1)
    right = live & (column + 1 < width_at)
    up = live & (row_index >= 1)
    down = live & (row_index + 1 < height_at)
    sides = [width_at == k * SIDE_UNIT for k in (3, 4, 6)]
    columns = [live, left, right] + [up & s for s in sides] + [down & s for s in sides]
    columns = columns + [jnp.zeros_like(live)] * 7
    return segment, member, jnp.stack(columns, axis=1).astype(jnp.float32)


def local(
    inner,
    outer,
    latents,
    text_embed,
    time_embed,
    heights,
    widths,
    text_counts,
    res_vecs,
    fc1_w,
    ff_vecs,
    fc2_w,
    time_w,
    time_b,
    kv_w,
    attn_w,
    attn_vecs,
    cotangent,
):
    low, full = jnp.bfloat16, jnp.float32
    orders = scatter_orders(outer)
    outer_bits, inner_bits = bit_count(outer), bit_count(inner)
    blocks = inner * outer
    x, cot = latents[0], cotangent[0]
    slots, width = x.shape
    text_width = text_embed.shape[3]
    text_total = LAT_ROW * TEXT
    key_pad = -(slots + text_total) % 128
    mine = lax.axis_index("dp") >> (inner_bits - 1)
    chain = Chain()

    def along(spec, a, b):
        return jnp.einsum(spec, a, b, preferred_element_type=full)

    small_owned = (res_vecs, ff_vecs, time_w, time_b[None], attn_vecs)
    small_sizes = [v.size for v in small_owned]
    small_pad = -sum(small_sizes) % (8 * width)
    small_shard = jnp.concatenate(
        [v.astype(low).reshape(-1) for v in small_owned] + [jnp.zeros((small_pad,), low)]
    )

    def to_all(*shards):
        shard = jnp.concatenate([v.astype(low) for v in shards], axis=0)
        shard = jnp.pad(shard, ((0, -shard.shape[0] % 8), (0, 0)))
        full_rows = lax.all_gather(shard, ("dp", "fsdp"), axis=0, tiled=True)
        return full_rows.reshape(blocks, -1, width)

    rows, kv_rows = fc2_w.shape[0], kv_w.shape[0]
    small_rows = small_shard.size // width
    res_weights = to_all(fc1_w.T, fc2_w, kv_w, small_shard.reshape(-1, width))
    attn_weights = to_all(turn_late(chain, attn_w, res_weights))
    fc1_t, fc2_full = Weight(res_weights, 0, rows), Weight(res_weights, 1, rows)
    attn_t = Weight(attn_weights, 0, rows)
    kv_full = res_weights[:, 2 * rows : 2 * rows + kv_rows].reshape(-1, width)
    small_all = res_weights[:, 2 * rows + kv_rows : 2 * rows + kv_rows + small_rows].reshape(blocks, -1)
    small_full = []
    taken = 0
    for owned, size in zip(small_owned, small_sizes):
        some = small_all[:, taken : taken + size].reshape(blocks, owned.shape[0], owned.shape[1])
        small_full.append(some.transpose(1, 0, 2).reshape(owned.shape[0], -1).astype(full))
        taken += size
    res_all, ff_all, time_w_all, time_b_all, vecs_all = small_full
    taps = jnp.pad(res_all[:10], ((0, 6), (0, 0)))
    vecs = jnp.pad(ff_all, ((0, 5), (0, 0)))

    segment, member_slots, geometry = geometry_table(heights[0], widths[0])
    member = jnp.pad(member_slots[::GROUP].astype(full), ((0, 0), (0, SEATS - LAT_ROW)))
    bias = score_bias(segment, text_counts[0], key_pad)
    live = geometry

    normed_low, normed, entry_scale = entry(chain, x, taps, geometry)
    act, slope, power = hidden_step(chain, normed_low, fc1_t, vecs, member)
    units = act.shape[1]
    norm = jnp.sqrt(power + NORM_EPS)
    norm_mean = jnp.mean(norm, axis=1, keepdims=True) + NORM_EPS
    norms = norm / norm_mean
    time_low = jnp.pad(time_embed[0].astype(low), ((0, SEATS - LAT_ROW), (0, 0)))
    pair = along("lt,tc->lc", time_low, time_w_all.astype(low)) + time_b_all
    response, after_res, after_time, normed_two = branch_step(
        chain, act, norms, vecs, fc2_full, member, live, x, res_all[10:11], pair
    )

    each = width // UNITS
    text = text_embed[0].astype(full).reshape(text_total, text_width)
    silu_text, silu_back = jax.vjp(jax.nn.silu, text)
    silu_low = silu_text.astype(low)
    mapped = (along("tk,kc->tc", silu_low, kv_full) + vecs_all[3]).astype(low)
    source = jnp.concatenate([normed_two, mapped, jnp.zeros((key_pad, width), low)], axis=0)
    grad_proj = (live[:, 0:1] * cot).astype(low)
    mixed_bias = jnp.concatenate([vecs_all[0], jnp.zeros((width,), full), vecs_all[1]])
    mixed, grad_attended = project(
        chain, source, grad_proj, jnp.broadcast_to(mixed_bias, (SEATS, 3 * width)), attn_t
    )
    attended, grad_query, grad_key, grad_value = attention(chain, mixed, grad_attended, bias)

    free = list(reversed(range(outer_bits + inner_bits - 1)))
    early = [b for b in free if b >= outer_bits]

    def pieces_of(both):
        both = both.reshape((2,) * len(free) + (-1, width))
        return [
            Piece(both, early + order, free, start // size, size)
            for order, (start, size) in zip(orders, column_pieces(width, len(orders)))
        ]

    def to_partner(away):
        return swap(away, "dp", inner, inner_bits - 1)

    def halved(terms):
        half = blocks // 2
        come = to_partner(lax.dynamic_slice_in_dim(terms, (1 - mine) * half, half, axis=0))
        kept = lax.dynamic_slice_in_dim(terms, mine * half, half, axis=0)
        some = Piece(kept.reshape((2,) * len(free) + terms.shape[1:]), early + orders[1], free)
        some.come = come.reshape(some.base.shape)
        return some

    def step(*groups):
        for group in groups:
            fold(chain, group, inner, outer)

    def finished(group, *turned):
        while group[0].order:
            step(group)
        return totals_of(chain, group, turned)

    parts = (grad_query, grad_key, grad_value, grad_proj, source, attended)
    come = to_partner(attn_half(chain, *parts, 1 - mine))
    grad_normed_two, grad_text = source_back(
        chain,
        grad_query,
        grad_key,
        grad_value,
        attn_t.by(lambda i: jnp.where(i < 2 * each, i + each, i - 2 * each)),
    )
    grad_mapped = grad_text[:text_total]
    kv_terms = along("tk,tc->kc", silu_low, grad_mapped).astype(low)
    kv_piece = halved(kv_terms.reshape(blocks, -1, width))
    attn_sum = pieces_of(attn_half(chain, *parts, mine, come)) + [kv_piece]
    for _ in early:
        step(attn_sum)
    step(attn_sum)
    grad_res, grad_branch, pair_grad, res_bias_grad = time_back(
        chain, grad_normed_two, after_time, after_res, cot, pair, member, live
    )
    come = to_partner(half_rows(chain, response, grad_branch, 1 - mine))
    grad_response, act_sums, shift_grad = response_back(chain, grad_branch, fc2_full, act, member)
    step(attn_sum)
    fc2_sum = pieces_of(half_rows(chain, response, grad_branch, mine, come))
    step(attn_sum)
    for _ in early:
        step(fc2_sum)
    for _ in range(outer_bits - 3):
        step(attn_sum)
    step(fc2_sum)
    gain_grad = jnp.sum(act_sums * norms, axis=0, keepdims=True)
    norms_grad = vecs[1:2] * act_sums
    norm_grad = norms_grad / norm_mean - jnp.sum(norms_grad * norm, axis=1, keepdims=True) / (
        units * norm_mean * norm_mean
    )
    hidden_low, hidden_bias_grad, grad_normed = hidden_back(
        chain, grad_response, act, slope, vecs, norms, norm_grad / norm, member, fc1_t
    )
    attn_grad, kv_grad = finished(attn_sum, True, False)
    step(fc2_sum)
    come = to_partner(half_rows(chain, hidden_low, normed_low, 1 - mine))
    latents_grad, taps_grad = entry_back(
        chain, grad_normed, normed, entry_scale, x, grad_res, taps, geometry, res_bias_grad
    )
    step(fc2_sum)
    time_grad = jnp.einsum("lt,lc->tc", time_low.astype(full), pair_grad, precision=HIGHEST)
    small_terms = (
        taps_grad[: res_vecs.shape[0]],
        jnp.concatenate([hidden_bias_grad[:1], gain_grad, shift_grad[:1]], axis=0),
        time_grad,
        jnp.sum(pair_grad, axis=0, keepdims=True),
        jnp.stack(
            [
                jnp.sum(grad_query.astype(full), axis=0),
                jnp.sum(grad_value.astype(full), axis=0),
                jnp.sum(grad_proj.astype(full), axis=0),
                jnp.sum(grad_mapped.astype(full), axis=0),
            ]
        ),
    )
    small_blocks = jnp.concatenate(
        [g.reshape(g.shape[0], blocks, -1).transpose(1, 0, 2).reshape(blocks, -1) for g in small_terms]
        + [jnp.zeros((blocks, -sum(small_sizes) % 1024), full)],
        axis=1,
    ).reshape(blocks, -1, 128)
    small_piece = halved(small_blocks)
    fc1_sum = pieces_of(half_rows(chain, hidden_low, normed_low, mine, come)) + [small_piece]
    for _ in early:
        step(fc1_sum)
    for _ in range(outer_bits - 3):
        step(fc2_sum)
    step(fc1_sum)
    output = output_step(
        chain,
        attended,
        after_time,
        live,
        jnp.broadcast_to(vecs_all[2], (SEATS, width)),
        attn_t.by(lambda i: 3 * each + i),
    )
    (fc2_grad,) = finished(fc2_sum, False)
    step(fc1_sum)
    step(fc1_sum)
    fc1_grad, small_total = finished(fc1_sum, True, False)
    small_total = small_total.reshape(-1)
    text_grad = silu_back(along("tc,kc->tk", grad_mapped, kv_full))[0]

    small_grads = []
    taken = 0
    for owned, size in zip(small_owned, small_sizes):
        small_grads.append(small_total[taken : taken + size].reshape(owned.shape))
        taken += size
    return (
        output[None],
        latents_grad[None],
        text_grad.reshape(text_embed.shape),
        small_grads[0],
        fc1_grad,
        small_grads[1],
        fc2_grad,
        small_grads[2],
        small_grads[3][0],
        kv_grad,
        attn_grad,
        small_grads[4],
    )


def solution(mesh):
    return jax.shard_map(
        functools.partial(local, mesh.shape["dp"], mesh.shape["fsdp"]),
        mesh=mesh,
        in_specs=(
            P(("dp", "fsdp"), None, None),
            P(("dp", "fsdp"), None, None, None),
            P(("dp", "fsdp"), None, None),
            P(("dp", "fsdp"), None),
            P(("dp", "fsdp"), None),
            P(("dp", "fsdp"), None),
            P(None, ("dp", "fsdp")),
            P(None, ("dp", "fsdp")),
            P(None, ("dp", "fsdp")),
            P(("dp", "fsdp"), None),
            P(None, ("dp", "fsdp")),
            P(("dp", "fsdp")),
            P(("dp", "fsdp"), None),
            P(None, ("dp", "fsdp")),
            P(None, ("dp", "fsdp")),
            P(("dp", "fsdp"), None, None),
        ),
        out_specs=(
            P(("dp", "fsdp"), None, None),
            P(("dp", "fsdp"), None, None),
            P(("dp", "fsdp"), None, None, None),
            P(None, ("dp", "fsdp")),
            P(None, ("dp", "fsdp")),
            P(None, ("dp", "fsdp")),
            P(("dp", "fsdp"), None),
            P(None, ("dp", "fsdp")),
            P(("dp", "fsdp")),
            P(("dp", "fsdp"), None),
            P(None, ("dp", "fsdp")),
            P(None, ("dp", "fsdp")),
        ),
        check_vma=False,
    )
```

time: 1340 us -> 989 us (0.74)
  matrix products: 327 us -> 9.01 us
  Pallas kernels: 157 us -> 408 us
  other arithmetic: 247 us -> 24.4 us
  local copies, waits for them, and re-layouts: 126 us -> 55.3 us
  starting transfers between devices: 104 us -> 44 us
  waiting for transfers between devices: 367 us -> 423 us
    dot_general x31 -> x5, matrix products: 327 us -> 9.01 us  [the longest x4 8.49 us: along(): return jnp.einsum(spec, a, b, preferred_element_type=full)]
    all_gather x0 -> x2, waiting for transfers between devices: none -> 268 us  [to_all(): full_rows = lax.all_gather(shard, ('dp', 'fsdp'), axis=0, tiled=True)]
    pallas_call x13 -> x33, Pallas kernels: 157 us -> 408 us  [call(): pl.pallas_call(body, grid_spec=pltpu.PrefetchScalarGridSpec(num_scalar_pr...]
    ppermute x115 -> x43, waiting for transfers between devices: 367 us -> 155 us  [swap(): lax.ppermute(values, axis_name, [(i, i ^ 1 << bit) for i in range(size)])]
    ppermute x115 -> x43, starting transfers between devices: 104 us -> 43.9 us  [swap(): lax.ppermute(values, axis_name, [(i, i ^ 1 << bit) for i in range(size)])]
    concatenate x34 -> x3, other arithmetic: 60.5 us -> 3.19 us  [the longest x1 2.03 us: local(): jnp.concatenate([normed_two, mapped, jnp.zeros((key_pad, width), low)], a...]
    reduce_sum x11 -> x7, other arithmetic: 52.4 us -> 7.17 us  [the longest x1 2.2 us: local(): jnp.sum(grad_proj.astype(full), axis=0)]
    select_n x3 -> x0, other arithmetic: 36.3 us -> none  [depthwise(): result = result + jnp.where(chosen[..., None], shifted, 0.0) * weight_row]
  transfers between devices with their start and end apart: 115 -> 45, of which waited for: 45 -> 14; matrix products, arithmetic and copies ran while one was open for 31% -> 6% of each run, Pallas kernels for 5% -> 23%
where the time goes in v2:
time: 989 us; the launch traced here: 979 us
  waiting for transfers between devices  423 us (43%)
  Pallas kernels  408 us (41%)
  local copies, waits for them, and re-layouts  55.3 us (6%)
  starting transfers between devices  44 us (4%)
  other arithmetic  24.4 us (2%)
  between operations  15.4 us (2%)
    pallas_call x33, Pallas kernels, call(): pl.pallas_call(body, grid_spec=pltpu.PrefetchScalarGridSpec(num_scalar_pr...  408 us
    all_gather x2, waiting for transfers between devices, to_all(): full_rows = lax.all_gather(shard, ('dp', 'fsdp'), axis=0, tiled=True)  268 us
    ppermute x43, waiting for transfers between devices, swap(): lax.ppermute(values, axis_name, [(i, i ^ 1 << bit) for i in range(size)])  155 us
    ppermute x43, starting transfers between devices, swap(): lax.ppermute(values, axis_name, [(i, i ^ 1 << bit) for i in range(size)])  43.9 us
    unnamed x128, local copies, waits for them, and re-layouts  23.3 us
  transfers between devices with their start and end apart: 45, of which 14 were waited for; matrix products, arithmetic and copies ran while one was open for 6% of the time, Pallas kernels for 23%

profile of v2, /device:TPU:0, one launch (start us, length us, event | category | flops | bytes accessed | tf_op | source)
XLA Modules:
  0.0 979.0 jit_solution(3824929892048620663)
XLA Ops:
  17.1 238.4 %all-gather.3.cloned.1.call-done = bf16[13824,1536]{1,0:T(8,128)(2,1)} async-done(((bf16[432,1536]{1,0:T(8,128)(2,1)}), bf16[13824,1536]{1,0:T(8,128)(2,1)}) %all-gather.3.cloned.1.call-update) | async-done | bytes 42467344 | tf_op jit(solution)/shard_map/all_gather | solution.py:1015
  255.5 2.6 shard_map.247
  268.8 4.3 slice.121
  279.2 11.2 %shard_map.248 = (bf16[576,1536]{1,0:T(8,128)(2,1)}, f32[576,1536]{1,0:T(8,128)}, f32[576,128]{1,0:T(8,128)}, f32[8,128]{1,0:T(8,128)}) custom-call(f32[576,1536]{1,0:T(8,128)} %bitcast.89, f32[16,1536]{1,0:T(8,128)} %pad.18.refs_1_.refs_5_, f32[576,16]{1,0:T(8,128)} %copy-done.1, f32[8,128]{1,0:T(8,128)} %get-tuple-element.154.refs_3_), custom_call_target="tpu_custom_call" | custom-call | tf_op jit(solution)/shard_map/pallas_call | solution.py:60
  290.4 25.0 %shard_map.249 = (f32[576,6144]{1,0:T(8,128)}, f32[576,6144]{1,0:T(8,128)}, f32[8,6144]{1,0:T(8,128)}, f32[8,128]{1,0:T(8,128)}) custom-call(bf16[576,1536]{1,0:T(8,128)(2,1)} %get-tuple-element.155.refs_0_.refs_2_, f32[8,6144]{1,0:T(8,128)} %pad.19.refs_1_.refs_2_.refs_3_, f32[36,8]{1,0:T(8,128)} %pad_convert_fusion.refs_2_.refs_3_.refs_5_.refs_6_, ...), custom_call_target="tpu_custom_call" | custom-call | tf_op jit(solution)/shard_map/pallas_call | solution.py:60
  319.0 29.3 %shard_map.250 = (bf16[576,6144]{1,0:T(8,128)(2,1)}, f32[576,1536]{1,0:T(8,128)}, f32[576,1536]{1,0:T(8,128)}, bf16[576,1536]{1,0:T(8,128)(2,1)}, f32[8,128]{1,0:T(8,128)}) custom-call(f32[576,6144]{1,0:T(8,128)} %get-tuple-element.157.refs_0_.refs_1_, f32[8,6144]{1,0:T(8,128)} %fusion.10.refs_1_.refs_4_, f32[8,6144]{1,0:T(8,128)} %pad.19.refs_1_.refs_2_.refs_3_, ...), custom_call_target="tpu_custom_call" | custom-call | tf_op jit(solution)/shard_map/pallas_call | solution.py:60
  351.9 30.0 %all-gather.5.cloned.1.call-done = bf16[6144,1536]{1,0:T(8,128)(2,1)} async-done(((bf16[192,1536]{1,0:T(8,128)(2,1)}), bf16[6144,1536]{1,0:T(8,128)(2,1)}) %all-gather.5.cloned.1.call-update) | async-done | bytes 18874384 | tf_op jit(solution)/shard_map/all_gather | solution.py:1015
  382.5 23.9 %shard_map.251 = (bf16[896,4608]{1,0:T(8,128)(2,1)}, bf16[576,1536]{1,0:T(8,128)(2,1)}, f32[8,128]{1,0:T(8,128)}) custom-call(bf16[896,1536]{1,0:T(8,128)(2,1)} %maximum_maximum_fusion.refs_0_.refs_5_, bf16[576,1536]{1,0:T(8,128)(2,1)} %get-tuple-element.366.refs_1_.refs_4_, f32[8,4608]{1,0:T(8,128)} %broadcast_in_dim.132.refs_2_, ...), custom_call_target="tpu_custom_call" | custom-call | tf_op jit(solution)/shard_map/pallas_call | solution.py:60
  406.5 65.1 %shard_map.252 = (bf16[576,1536]{1,0:T(8,128)(2,1)}, bf16[576,1536]{1,0:T(8,128)(2,1)}, bf16[896,1536]{1,0:T(8,128)(2,1)}, bf16[896,1536]{1,0:T(8,128)(2,1)}, f32[8,128]{1,0:T(8,128)}) custom-call(bf16[896,4608]{1,0:T(8,128)(2,1)} %get-tuple-element.163.refs_0_.refs_1_.refs_2_, bf16[896,4608]{1,0:T(8,128)(2,1)} %get-tuple-element.163.refs_0_.refs_1_.refs_2_, ...), custom_call_target="tpu_custom_call" | custom-call | tf_op jit(solution)/shard_map/pallas_call | solution.py:60
  471.6 14.7 %shard_map.253 = (bf16[3072,1536]{1,0:T(8,128)(2,1)}, f32[8,128]{1,0:T(8,128)}) custom-call(s32[1]{0:T(128)} %bitcast.20.refs_0_, bf16[576,1536]{1,0:T(8,128)(2,1)} %get-tuple-element.168.refs_1_.refs_0_, bf16[896,1536]{1,0:T(8,128)(2,1)} %get-tuple-element.169.refs_2_.refs_1_, bf16[896,1536]{1,0:T(8,128)(2,1)} %get-tuple-element.170.refs_3_.refs_2_, ...), custom_call_target="tpu_custom_call" | custom-call | tf_op jit(solution)/shard_map/pallas_call | solution.py:60
  486.9 19.5 %shard_map.254 = (f32[576,1536]{1,0:T(8,128)}, bf16[320,1536]{1,0:T(8,128)(2,1)}, f32[8,128]{1,0:T(8,128)}) custom-call(bf16[576,1536]{1,0:T(8,128)(2,1)} %get-tuple-element.168.refs_1_.refs_0_, bf16[896,1536]{1,0:T(8,128)(2,1)} %get-tuple-element.169.refs_2_.refs_1_, bf16[896,1536]{1,0:T(8,128)(2,1)} %get-tuple-element.170.refs_3_.refs_2_, ...), custom_call_target="tpu_custom_call" | custom-call | tf_op jit(solution)/shard_map/pallas_call | solution.py:60
  506.4 3.5 convolution_convert_fusion
  512.4 16.4 %shard_map.255 = (bf16[3072,1536]{1,0:T(8,128)(2,1)}, f32[8,128]{1,0:T(8,128)}) custom-call(s32[1]{0:T(128)} %bitcast.19.refs_0_, bf16[576,1536]{1,0:T(8,128)(2,1)} %get-tuple-element.168.refs_1_.refs_0_, bf16[896,1536]{1,0:T(8,128)(2,1)} %get-tuple-element.169.refs_2_.refs_1_, bf16[896,1536]{1,0:T(8,128)(2,1)} %get-tuple-element.170.refs_3_.refs_2_, ...), custom_call_target="tpu_custom_call" | custom-call | tf_op jit(solution)/shard_map/pallas_call | solution.py:60
  530.0 5.7 shard_map.256
  535.7 11.6 %shard_map.257 = (f32[576,1536]{1,0:T(8,128)}, bf16[576,1536]{1,0:T(8,128)(2,1)}, f32[8,3072]{1,0:T(8,128)}, f32[8,1536]{1,0:T(8,128)}, f32[8,128]{1,0:T(8,128)}) custom-call(f32[576,1536]{1,0:T(8,128)} %get-tuple-element.173.refs_0_, f32[576,1536]{1,0:T(8,128)} %get-tuple-element.167.refs_1_, f32[576,1536]{1,0:T(8,128)} %get-tuple-element.174.refs_2_, ...), custom_call_target="tpu_custom_call" | custom-call | tf_op jit(solution)/shard_map/pallas_call | solution.py:60
  547.3 11.6 %shard_map.258 = (bf16[3072,1536]{1,0:T(8,128)(2,1)}, f32[8,128]{1,0:T(8,128)}) custom-call(s32[1]{0:T(128)} %bitcast.20.refs_0_, bf16[576,6144]{1,0:T(8,128)(2,1)} %get-tuple-element.182.refs_1_, bf16[576,1536]{1,0:T(8,128)(2,1)} %get-tuple-element.181.refs_2_.refs_0_, f32[8,128]{1,0:T(8,128)} %get-tuple-element.183.refs_3_), custom_call_target="tpu_custom_call" | custom-call | tf_op jit(solution)/shard_map/pallas_call | solution.py:60
  562.9 22.0 %shard_map.259 = (f32[576,6144]{1,0:T(8,128)}, f32[8,6144]{1,0:T(8,128)}, f32[8,6144]{1,0:T(8,128)}, f32[8,128]{1,0:T(8,128)}) custom-call(bf16[576,1536]{1,0:T(8,128)(2,1)} %get-tuple-element.181.refs_2_.refs_0_, f32[576,6144]{1,0:T(8,128)} %get-tuple-element.157.refs_0_.refs_1_, f32[36,8]{1,0:T(8,128)} %pad_convert_fusion.refs_2_.refs_3_.refs_5_.refs_6_, ...), custom_call_target="tpu_custom_call" | custom-call | tf_op jit(solution)/shard_map/pallas_call | solution.py:60
  584.9 41.6 %collective-permute-done.6.refs_8_ = bf16[2,2,2,40,1536]{4,3,2,1,0:T(8,128)(2,1)S(1)} collective-permute-done((bf16[2,2,2,40,1536]{4,3,2,1,0:T(8,128)(2,1)}, bf16[2,2,2,40,1536]{4,3,2,1,0:T(8,128)(2,1)S(1)}, u32[]{:S(2)}, u32[]{:S(2)}) %collective-permute-start.6) | collective-permute-done | bytes 983072 | tf_op jit(solution)/shard_map/ppermute | solution.py:31
  628.8 6.9 shard_map.260
  639.8 13.0 %shard_map.261 = (bf16[3072,1536]{1,0:T(8,128)(2,1)}, f32[8,128]{1,0:T(8,128)}) custom-call(s32[1]{0:T(128)} %bitcast.19.refs_0_, bf16[576,6144]{1,0:T(8,128)(2,1)} %get-tuple-element.182.refs_1_, bf16[576,1536]{1,0:T(8,128)(2,1)} %get-tuple-element.181.refs_2_.refs_0_, bf16[3072,1536]{1,0:T(8,128)(2,1)} %collective-permute-done.2.refs_3_, ...), custom_call_target="tpu_custom_call" | custom-call | tf_op jit(solution)/shard_map/pallas_call | solution.py:60
  652.8 16.7 %collective-permute-done.10.refs_8_ = bf16[2,2,40,1536]{3,2,1,0:T(8,128)(2,1)S(1)} collective-permute-done((bf16[2,2,40,1536]{3,2,1,0:T(8,128)(2,1)}, bf16[2,2,40,1536]{3,2,1,0:T(8,128)(2,1)S(1)}, u32[]{:S(2)}, u32[]{:S(2)}) %collective-permute-start.10) | collective-permute-done | bytes 491552 | tf_op jit(solution)/shard_map/ppermute | solution.py:31
  671.0 4.0 shard_map.262
  678.7 4.5 collective-permute-done.13.refs_6_
  683.2 8.4 collective-permute-done.14.refs_8_
  692.6 3.1 shard_map.263
  695.8 4.1 shard_map.264
  707.8 28.2 %shard_map.265 = (bf16[576,6144]{1,0:T(8,128)(2,1)}, f32[8,6144]{1,0:T(8,128)}, f32[576,1536]{1,0:T(8,128)}, f32[8,128]{1,0:T(8,128)}) custom-call(f32[576,6144]{1,0:T(8,128)} %get-tuple-element.185.refs_0_, f32[576,6144]{1,0:T(8,128)} %get-tuple-element.157.refs_0_.refs_1_, f32[576,6144]{1,0:T(8,128)} %get-tuple-element.186.refs_2_, ...), custom_call_target="tpu_custom_call" | custom-call | tf_op jit(solution)/shard_map/pallas_call | solution.py:60
  736.8 3.0 shard_map.266
  742.9 5.7 shard_map.267
  748.6 11.7 %shard_map.268 = (bf16[3072,1536]{1,0:T(8,128)(2,1)}, f32[8,128]{1,0:T(8,128)}) custom-call(s32[1]{0:T(128)} %bitcast.20.refs_0_, bf16[576,6144]{1,0:T(8,128)(2,1)} %get-tuple-element.217.refs_1_, bf16[576,1536]{1,0:T(8,128)(2,1)} %get-tuple-element.155.refs_0_.refs_2_, f32[8,128]{1,0:T(8,128)} %get-tuple-element.227.refs_3_), custom_call_target="tpu_custom_call" | custom-call | tf_op jit(solution)/shard_map/pallas_call | solution.py:60
  773.0 19.9 %shard_map.269 = (f32[576,1536]{1,0:T(8,128)}, f32[16,1536]{1,0:T(8,128)}, f32[8,128]{1,0:T(8,128)}) custom-call(f32[576,1536]{1,0:T(8,128)} %get-tuple-element.235.refs_0_, f32[576,1536]{1,0:T(8,128)} %get-tuple-element.236.refs_1_, f32[576,128]{1,0:T(8,128)} %get-tuple-element.237.refs_2_, f32[576,1536]{1,0:T(8,128)} %bitcast.91, ...), custom_call_target="tpu_custom_call" | custom-call | tf_op jit(solution)/shard_map/pallas_call | solution.py:60
  796.8 3.5 shard_map.270
  802.9 13.0 %shard_map.271 = (bf16[3072,1536]{1,0:T(8,128)(2,1)}, f32[8,128]{1,0:T(8,128)}) custom-call(s32[1]{0:T(128)} %bitcast.19.refs_0_, bf16[576,6144]{1,0:T(8,128)(2,1)} %get-tuple-element.217.refs_1_, bf16[576,1536]{1,0:T(8,128)(2,1)} %get-tuple-element.155.refs_0_.refs_2_, bf16[3072,1536]{1,0:T(8,128)(2,1)} %collective-permute-done.20.refs_3_, ...), custom_call_target="tpu_custom_call" | custom-call | tf_op jit(solution)/shard_map/pallas_call | solution.py:60
  817.0 2.9 shard_map.272
  820.7 4.4 shard_map.273
  832.3 7.8 shard_map.274
  840.0 17.6 %collective-permute-done.32.refs_1_ = bf16[1,192,1536]{2,1,0:T(8,128)(2,1)S(1)} collective-permute-done((bf16[1,192,1536]{2,1,0:T(8,128)(2,1)}, bf16[1,192,1536]{2,1,0:T(8,128)(2,1)S(1)}, u32[]{:S(2)}, u32[]{:S(2)}) %collective-permute-start.32) | collective-permute-done | bytes 589856 | tf_op jit(solution)/shard_map/ppermute | solution.py:31
  860.8 15.8 %collective-permute-done.31.refs_8_ = f32[2,2,2,64,128]{4,3,2,1,0:T(8,128)} collective-permute-done((f32[2,2,2,64,128]{4,3,2,1,0:T(8,128)}, f32[2,2,2,64,128]{4,3,2,1,0:T(8,128)}, u32[]{:S(2)}, u32[]{:S(2)}) %collective-permute-start.31) | collective-permute-done | bytes 262176 | tf_op jit(solution)/shard_map/ppermute | solution.py:31
  878.1 6.0 shard_map.276
  888.1 21.5 %collective-permute-done.36.refs_8_ = f32[2,2,64,128]{3,2,1,0:T(8,128)S(1)} collective-permute-done((f32[2,2,64,128]{3,2,1,0:T(8,128)}, f32[2,2,64,128]{3,2,1,0:T(8,128)S(1)}, u32[]{:S(2)}, u32[]{:S(2)}) %collective-permute-start.36) | collective-permute-done | bytes 131104 | tf_op jit(solution)/shard_map/ppermute | solution.py:31
  911.0 3.9 shard_map.277
  920.0 8.2 collective-permute-done.40.refs_8_
  929.3 2.9 shard_map.278
  935.2 2.8 fusion.2
  941.8 5.1 collective-permute-done.42.refs_3_
  946.9 12.3 %collective-permute-done.41.refs_1_ = bf16[1,192,1536]{2,1,0:T(8,128)(2,1)} collective-permute-done((bf16[1,192,1536]{2,1,0:T(8,128)(2,1)}, bf16[1,192,1536]{2,1,0:T(8,128)(2,1)}, u32[]{:S(2)}, u32[]{:S(2)}) %collective-permute-start.41) | collective-permute-done | bytes 589856 | tf_op jit(solution)/shard_map/ppermute | solution.py:31
  959.2 2.9 shard_map.279
  969.1 2.9 copy.109
  (339 shorter events, 124.7 us)
Async XLA Ops:
  7.2 248.3 %all-gather.3.cloned.1.call-start = ((), (), s32[]{:S(2)}) async-start(), calls=%async_computation | async-start | bytes 43794432 | tf_op jit(solution)/shard_map/all_gather | solution.py:1015
  14.9 366.9 %all-gather.5.cloned.1.call-start = ((), (), s32[]{:S(2)}) async-start(), calls=%async_computation.1 | async-start | bytes 19464192 | tf_op jit(solution)/shard_map/all_gather | solution.py:1015
  263.1 53.4 %copy-start.52 = (bf16[4,64]{1,0:T(4,128)(2,1)}, bf16[4,64]{1,0:T(4,128)(2,1)S(1)}, u32[]{:S(2)}) copy-start(bf16[4,64]{1,0:T(4,128)(2,1)S(1)} %convert_bitcast_fusion.1) | copy-start | bytes 1540
  319.0 29.3 %copy-start.23 = (bf16[308,1280]{1,0:T(8,128)(2,1)S(1)}, bf16[308,1280]{1,0:T(8,128)(2,1)}, u32[]{:S(2)}) copy-start(bf16[308,1280]{1,0:T(8,128)(2,1)} %convert_element_type.158) | copy-start | bytes 2365444
  486.3 26.0 %collective-permute-start = (bf16[3072,1536]{1,0:T(8,128)(2,1)}, bf16[3072,1536]{1,0:T(8,128)(2,1)}, u32[]{:S(2)}, u32[]{:S(2)}) collective-permute-start(bf16[3072,1536]{1,0:T(8,128)(2,1)} %get-tuple-element.175), channel_id=1, source_target_pairs={{0,16},{16,0},{1,17},{17,1},{2,18},{18,2},{3,19},{19,3},{4,20},{20... | collective-permute-start | bytes 28311560 | tf_op jit(solution)/shard_map/ppermute | solution.py:31
  512.1 16.7 %collective-permute-start.1 = (bf16[16,40,1536]{2,1,0:T(8,128)(2,1)}, bf16[16,40,1536]{2,1,0:T(8,128)(2,1)S(1)}, u32[]{:S(2)}, u32[]{:S(2)}) collective-permute-start(bf16[16,40,1536]{2,1,0:T(8,128)(2,1)} %get-tuple-element.372), channel_id=1, source_target_pairs={{0,16},{16,0},{1,17},{17,1},{2,18},{18,2},{3,19},{19,3},{4,20},{20... | collective-permute-start | bytes 5898248 | tf_op jit(solution)/shard_map/ppermute | solution.py:31
  559.0 80.8 %collective-permute-start.2 = (bf16[3072,1536]{1,0:T(8,128)(2,1)}, bf16[3072,1536]{1,0:T(8,128)(2,1)}, u32[]{:S(2)}, u32[]{:S(2)}) collective-permute-start(bf16[3072,1536]{1,0:T(8,128)(2,1)} %get-tuple-element.188), channel_id=1, source_target_pairs={{0,16},{16,0},{1,17},{17,1},{2,18},{18,2},{3,19},{19,3},{4,20},{20... | collective-permute-start | bytes 28311560 | tf_op jit(solution)/shard_map/ppermute | solution.py:31
  559.3 67.2 %collective-permute-start.3 = (bf16[2,2,2,192,640]{4,3,2,1,0:T(8,128)(2,1)}, bf16[2,2,2,192,640]{4,3,2,1,0:T(8,128)(2,1)S(1)}, u32[]{:S(2)}, u32[]{:S(2)}) collective-permute-start(bf16[2,2,2,192,640]{4,3,2,1,0:T(8,128)(2,1)} %get-tuple-element.189), channel_id=1, source_target_pairs={{0,1},{1,0},{2,3},{3,2},{4,5},{5,4},{6,7},{7,6},{8,9},{9,8},{10,11... | collective-permute-start | bytes 5898248 | tf_op jit(solution)/shard_map/ppermute | solution.py:31
  560.7 65.7 %collective-permute-start.4 = (bf16[2,2,2,192,640]{4,3,2,1,0:T(8,128)(2,1)S(1)}, bf16[2,2,2,192,640]{4,3,2,1,0:T(8,128)(2,1)S(1)}, u32[]{:S(2)}, u32[]{:S(2)}) collective-permute-start(bf16[2,2,2,192,640]{4,3,2,1,0:T(8,128)(2,1)S(1)} %copy-done.58), channel_id=1, source_target_pairs={{0,2},{1,3},{2,0},{3,1},{4,6},{5,7},{6,4},{7,5},{8,10},{9,11},{10,... | collective-permute-start | bytes 5898248 | tf_op jit(solution)/shard_map/ppermute | solution.py:31
  561.3 65.1 %collective-permute-start.6 = (bf16[2,2,2,40,1536]{4,3,2,1,0:T(8,128)(2,1)}, bf16[2,2,2,40,1536]{4,3,2,1,0:T(8,128)(2,1)S(1)}, u32[]{:S(2)}, u32[]{:S(2)}) collective-permute-start(bf16[2,2,2,40,1536]{4,3,2,1,0:T(8,128)(2,1)} %get-tuple-element.193), channel_id=1, source_target_pairs={{0,2},{1,3},{2,0},{3,1},{4,6},{5,7},{6,4},{7,5},{8,10},{9,11},{10,... | collective-permute-start | bytes 2949128 | tf_op jit(solution)/shard_map/ppermute | solution.py:31
  562.8 22.1 %collective-permute-start.5 = (bf16[2,2,2,192,256]{4,3,2,1,0:T(8,128)(2,1)}, bf16[2,2,2,192,256]{4,3,2,1,0:T(8,128)(2,1)S(1)}, u32[]{:S(2)}, u32[]{:S(2)}) collective-permute-start(bf16[2,2,2,192,256]{4,3,2,1,0:T(8,128)(2,1)} %get-tuple-element.191), channel_id=1, source_target_pairs={{0,4},{1,5},{2,6},{3,7},{4,0},{5,1},{6,2},{7,3},{8,12},{9,13},{10,... | collective-permute-start | bytes 2359304 | tf_op jit(solution)/shard_map/ppermute | solution.py:31
  584.9 41.6 %copy-start.27 = (bf16[2,2,2,192,256]{4,3,2,1,0:T(8,128)(2,1)}, bf16[2,2,2,192,256]{4,3,2,1,0:T(8,128)(2,1)S(1)}, u32[]{:S(2)}) copy-start(bf16[2,2,2,192,256]{4,3,2,1,0:T(8,128)(2,1)S(1)} %collective-permute-done.5.refs_6_) | copy-start | bytes 2359300
  635.6 33.9 %collective-permute-start.7 = (bf16[2,2,192,640]{3,2,1,0:T(8,128)(2,1)}, bf16[2,2,192,640]{3,2,1,0:T(8,128)(2,1)S(1)}, u32[]{:S(2)}, u32[]{:S(2)}) collective-permute-start(bf16[2,2,192,640]{3,2,1,0:T(8,128)(2,1)} %get-tuple-element.198), channel_id=1, source_target_pairs={{0,2},{1,3},{2,0},{3,1},{4,6},{5,7},{6,4},{7,5},{8,10},{9,11},{10,... | collective-permute-start | bytes 2949128 | tf_op jit(solution)/shard_map/ppermute | solution.py:31
  636.3 33.2 %collective-permute-start.8 = (bf16[2,2,192,640]{3,2,1,0:T(8,128)(2,1)}, bf16[2,2,192,640]{3,2,1,0:T(8,128)(2,1)S(1)}, u32[]{:S(2)}, u32[]{:S(2)}) collective-permute-start(bf16[2,2,192,640]{3,2,1,0:T(8,128)(2,1)} %get-tuple-element.200), channel_id=1, source_target_pairs={{0,4},{1,5},{2,6},{3,7},{4,0},{5,1},{6,2},{7,3},{8,12},{9,13},{10,... | collective-permute-start | bytes 2949128 | tf_op jit(solution)/shard_map/ppermute | solution.py:31
  636.5 33.1 %collective-permute-start.10 = (bf16[2,2,40,1536]{3,2,1,0:T(8,128)(2,1)}, bf16[2,2,40,1536]{3,2,1,0:T(8,128)(2,1)S(1)}, u32[]{:S(2)}, u32[]{:S(2)}) collective-permute-start(bf16[2,2,40,1536]{3,2,1,0:T(8,128)(2,1)} %get-tuple-element.204), channel_id=1, source_target_pairs={{0,4},{1,5},{2,6},{3,7},{4,0},{5,1},{6,2},{7,3},{8,12},{9,13},{10,... | collective-permute-start | bytes 1474568 | tf_op jit(solution)/shard_map/ppermute | solution.py:31
  638.3 14.5 %collective-permute-start.9 = (bf16[2,2,192,256]{3,2,1,0:T(8,128)(2,1)}, bf16[2,2,192,256]{3,2,1,0:T(8,128)(2,1)S(1)}, u32[]{:S(2)}, u32[]{:S(2)}) collective-permute-start(bf16[2,2,192,256]{3,2,1,0:T(8,128)(2,1)} %get-tuple-element.202), channel_id=1, source_target_pairs={{0,1},{1,0},{2,3},{3,2},{4,5},{5,4},{6,7},{7,6},{8,9},{9,8},{10,11... | collective-permute-start | bytes 1179656 | tf_op jit(solution)/shard_map/ppermute | solution.py:31
  674.9 16.7 %collective-permute-start.11 = (bf16[2,192,640]{2,1,0:T(8,128)(2,1)}, bf16[2,192,640]{2,1,0:T(8,128)(2,1)S(1)}, u32[]{:S(2)}, u32[]{:S(2)}) collective-permute-start(bf16[2,192,640]{2,1,0:T(8,128)(2,1)} %get-tuple-element.207), channel_id=1, source_target_pairs={{0,4},{1,5},{2,6},{3,7},{4,0},{5,1},{6,2},{7,3},{8,12},{9,13},{10,... | collective-permute-start | bytes 1474568 | tf_op jit(solution)/shard_map/ppermute | solution.py:31
  675.3 16.3 %collective-permute-start.12 = (bf16[2,192,640]{2,1,0:T(8,128)(2,1)}, bf16[2,192,640]{2,1,0:T(8,128)(2,1)S(1)}, u32[]{:S(2)}, u32[]{:S(2)}) collective-permute-start(bf16[2,192,640]{2,1,0:T(8,128)(2,1)} %get-tuple-element.209), channel_id=1, source_target_pairs={{0,1},{1,0},{2,3},{3,2},{4,5},{5,4},{6,7},{7,6},{8,9},{9,8},{10,11... | collective-permute-start | bytes 1474568 | tf_op jit(solution)/shard_map/ppermute | solution.py:31
  676.7 14.9 %collective-permute-start.14 = (bf16[2,40,1536]{2,1,0:T(8,128)(2,1)}, bf16[2,40,1536]{2,1,0:T(8,128)(2,1)S(1)}, u32[]{:S(2)}, u32[]{:S(2)}) collective-permute-start(bf16[2,40,1536]{2,1,0:T(8,128)(2,1)} %get-tuple-element.213), channel_id=1, source_target_pairs={{0,1},{1,0},{2,3},{3,2},{4,5},{5,4},{6,7},{7,6},{8,9},{9,8},{10,11... | collective-permute-start | bytes 737288 | tf_op jit(solution)/shard_map/ppermute | solution.py:31
  677.3 5.9 collective-permute-start.13
  699.8 41.7 %collective-permute-start.15 = (bf16[2,2,2,192,640]{4,3,2,1,0:T(8,128)(2,1)}, bf16[2,2,2,192,640]{4,3,2,1,0:T(8,128)(2,1)S(1)}, u32[]{:S(2)}, u32[]{:S(2)}) collective-permute-start(bf16[2,2,2,192,640]{4,3,2,1,0:T(8,128)(2,1)} %get-tuple-element.218), channel_id=1, source_target_pairs={{0,1},{1,0},{2,3},{3,2},{4,5},{5,4},{6,7},{7,6},{8,9},{9,8},{10,11... | collective-permute-start | bytes 5898248 | tf_op jit(solution)/shard_map/ppermute | solution.py:31
  701.3 41.6 %collective-permute-start.16 = (bf16[2,2,2,192,640]{4,3,2,1,0:T(8,128)(2,1)}, bf16[2,2,2,192,640]{4,3,2,1,0:T(8,128)(2,1)}, u32[]{:S(2)}, u32[]{:S(2)}) collective-permute-start(bf16[2,2,2,192,640]{4,3,2,1,0:T(8,128)(2,1)} %get-tuple-element.219), channel_id=1, source_target_pairs={{0,2},{1,3},{2,0},{3,1},{4,6},{5,7},{6,4},{7,5},{8,10},{9,11},{10,... | collective-permute-start | bytes 5898248 | tf_op jit(solution)/shard_map/ppermute | solution.py:31
  702.4 33.6 %collective-permute-start.19 = (bf16[1,40,1536]{2,1,0:T(8,128)(2,1)S(1)}, bf16[1,40,1536]{2,1,0:T(8,128)(2,1)S(1)}, u32[]{:S(2)}, u32[]{:S(2)}) collective-permute-start(bf16[1,40,1536]{2,1,0:T(8,128)(2,1)S(1)} %copy-done.60), channel_id=1, source_target_pairs={{0,8},{1,9},{2,10},{3,11},{4,12},{5,13},{6,14},{7,15},{8,0},{9,1},... | collective-permute-start | bytes 368648 | tf_op jit(solution)/shard_map/ppermute | solution.py:31
  704.0 32.0 %collective-permute-start.18 = (bf16[1,192,1536]{2,1,0:T(8,128)(2,1)}, bf16[1,192,1536]{2,1,0:T(8,128)(2,1)S(1)}, u32[]{:S(2)}, u32[]{:S(2)}) collective-permute-start(bf16[1,192,1536]{2,1,0:T(8,128)(2,1)} %get-tuple-element.222), channel_id=1, source_target_pairs={{0,8},{1,9},{2,10},{3,11},{4,12},{5,13},{6,14},{7,15},{8,0},{9,1},... | collective-permute-start | bytes 1769480 | tf_op jit(solution)/shard_map/ppermute | solution.py:31
  705.3 34.5 %collective-permute-start.17 = (bf16[2,2,2,192,256]{4,3,2,1,0:T(8,128)(2,1)}, bf16[2,2,2,192,256]{4,3,2,1,0:T(8,128)(2,1)S(1)}, u32[]{:S(2)}, u32[]{:S(2)}) collective-permute-start(bf16[2,2,2,192,256]{4,3,2,1,0:T(8,128)(2,1)} %get-tuple-element.220), channel_id=1, source_target_pairs={{0,4},{1,5},{2,6},{3,7},{4,0},{5,1},{6,2},{7,3},{8,12},{9,13},{10,... | collective-permute-start | bytes 2359304 | tf_op jit(solution)/shard_map/ppermute | solution.py:31
  760.3 42.6 %collective-permute-start.20 = (bf16[3072,1536]{1,0:T(8,128)(2,1)}, bf16[3072,1536]{1,0:T(8,128)(2,1)}, u32[]{:S(2)}, u32[]{:S(2)}) collective-permute-start(bf16[3072,1536]{1,0:T(8,128)(2,1)} %get-tuple-element.228), channel_id=1, source_target_pairs={{0,16},{16,0},{1,17},{17,1},{2,18},{18,2},{3,19},{19,3},{4,20},{20... | collective-permute-start | bytes 28311560 | tf_op jit(solution)/shard_map/ppermute | solution.py:31
  762.9 33.1 %collective-permute-start.21 = (bf16[2,2,192,640]{3,2,1,0:T(8,128)(2,1)}, bf16[2,2,192,640]{3,2,1,0:T(8,128)(2,1)}, u32[]{:S(2)}, u32[]{:S(2)}) collective-permute-start(bf16[2,2,192,640]{3,2,1,0:T(8,128)(2,1)} %get-tuple-element.230), channel_id=1, source_target_pairs={{0,2},{1,3},{2,0},{3,1},{4,6},{5,7},{6,4},{7,5},{8,10},{9,11},{10,... | collective-permute-start | bytes 2949128 | tf_op jit(solution)/shard_map/ppermute | solution.py:31
  764.3 31.8 %collective-permute-start.22 = (bf16[2,2,192,640]{3,2,1,0:T(8,128)(2,1)}, bf16[2,2,192,640]{3,2,1,0:T(8,128)(2,1)}, u32[]{:S(2)}, u32[]{:S(2)}) collective-permute-start(bf16[2,2,192,640]{3,2,1,0:T(8,128)(2,1)} %get-tuple-element.232), channel_id=1, source_target_pairs={{0,4},{1,5},{2,6},{3,7},{4,0},{5,1},{6,2},{7,3},{8,12},{9,13},{10,... | collective-permute-start | bytes 2949128 | tf_op jit(solution)/shard_map/ppermute | solution.py:31
  771.0 25.0 %collective-permute-start.23 = (bf16[2,2,192,256]{3,2,1,0:T(8,128)(2,1)S(1)}, bf16[2,2,192,256]{3,2,1,0:T(8,128)(2,1)S(1)}, u32[]{:S(2)}, u32[]{:S(2)}) collective-permute-start(bf16[2,2,192,256]{3,2,1,0:T(8,128)(2,1)S(1)} %copy-done.59), channel_id=1, source_target_pairs={{0,1},{1,0},{2,3},{3,2},{4,5},{5,4},{6,7},{7,6},{8,9},{9,8},{10,11... | collective-permute-start | bytes 1179656 | tf_op jit(solution)/shard_map/ppermute | solution.py:31
  796.0 23.9 %collective-permute-start.24 = (f32[16,64,128]{2,1,0:T(8,128)S(1)}, f32[16,64,128]{2,1,0:T(8,128)S(1)}, u32[]{:S(2)}, u32[]{:S(2)}) collective-permute-start(f32[16,64,128]{2,1,0:T(8,128)S(1)} %get-tuple-element.374), channel_id=1, source_target_pairs={{0,16},{16,0},{1,17},{17,1},{2,18},{18,2},{3,19},{19,3},{4,20},{20... | collective-permute-start | bytes 1572872 | tf_op jit(solution)/shard_map/ppermute | solution.py:31
  800.3 15.7 %collective-permute-start.25 = (bf16[2,192,640]{2,1,0:T(8,128)(2,1)}, bf16[2,192,640]{2,1,0:T(8,128)(2,1)S(1)}, u32[]{:S(2)}, u32[]{:S(2)}) collective-permute-start(bf16[2,192,640]{2,1,0:T(8,128)(2,1)} %get-tuple-element.249), channel_id=1, source_target_pairs={{0,4},{1,5},{2,6},{3,7},{4,0},{5,1},{6,2},{7,3},{8,12},{9,13},{10,... | collective-permute-start | bytes 1474568 | tf_op jit(solution)/shard_map/ppermute | solution.py:31
  800.8 15.2 %collective-permute-start.26 = (bf16[2,192,640]{2,1,0:T(8,128)(2,1)}, bf16[2,192,640]{2,1,0:T(8,128)(2,1)S(1)}, u32[]{:S(2)}, u32[]{:S(2)}) collective-permute-start(bf16[2,192,640]{2,1,0:T(8,128)(2,1)} %get-tuple-element.251), channel_id=1, source_target_pairs={{0,1},{1,0},{2,3},{3,2},{4,5},{5,4},{6,7},{7,6},{8,9},{9,8},{10,11... | collective-permute-start | bytes 1474568 | tf_op jit(solution)/shard_map/ppermute | solution.py:31
  802.1 13.8 %collective-permute-start.27 = (bf16[2,192,256]{2,1,0:T(8,128)(2,1)}, bf16[2,192,256]{2,1,0:T(8,128)(2,1)S(1)}, u32[]{:S(2)}, u32[]{:S(2)}) collective-permute-start(bf16[2,192,256]{2,1,0:T(8,128)(2,1)} %get-tuple-element.253), channel_id=1, source_target_pairs={{0,2},{1,3},{2,0},{3,1},{4,6},{5,7},{6,4},{7,5},{8,10},{9,11},{10,... | collective-permute-start | bytes 589832 | tf_op jit(solution)/shard_map/ppermute | solution.py:31
  825.0 51.5 %collective-permute-start.28 = (bf16[2,2,2,192,640]{4,3,2,1,0:T(8,128)(2,1)}, bf16[2,2,2,192,640]{4,3,2,1,0:T(8,128)(2,1)S(1)}, u32[]{:S(2)}, u32[]{:S(2)}) collective-permute-start(bf16[2,2,2,192,640]{4,3,2,1,0:T(8,128)(2,1)} %get-tuple-element.259), channel_id=1, source_target_pairs={{0,1},{1,0},{2,3},{3,2},{4,5},{5,4},{6,7},{7,6},{8,9},{9,8},{10,11... | collective-permute-start | bytes 5898248 | tf_op jit(solution)/shard_map/ppermute | solution.py:31
  826.5 50.1 %collective-permute-start.29 = (bf16[2,2,2,192,640]{4,3,2,1,0:T(8,128)(2,1)}, bf16[2,2,2,192,640]{4,3,2,1,0:T(8,128)(2,1)}, u32[]{:S(2)}, u32[]{:S(2)}) collective-permute-start(bf16[2,2,2,192,640]{4,3,2,1,0:T(8,128)(2,1)} %get-tuple-element.260), channel_id=1, source_target_pairs={{0,2},{1,3},{2,0},{3,1},{4,6},{5,7},{6,4},{7,5},{8,10},{9,11},{10,... | collective-permute-start | bytes 5898248 | tf_op jit(solution)/shard_map/ppermute | solution.py:31
  827.0 49.5 %collective-permute-start.30 = (bf16[2,2,2,192,256]{4,3,2,1,0:T(8,128)(2,1)}, bf16[2,2,2,192,256]{4,3,2,1,0:T(8,128)(2,1)S(1)}, u32[]{:S(2)}, u32[]{:S(2)}) collective-permute-start(bf16[2,2,2,192,256]{4,3,2,1,0:T(8,128)(2,1)} %get-tuple-element.261), channel_id=1, source_target_pairs={{0,4},{1,5},{2,6},{3,7},{4,0},{5,1},{6,2},{7,3},{8,12},{9,13},{10,... | collective-permute-start | bytes 2359304 | tf_op jit(solution)/shard_map/ppermute | solution.py:31
  828.6 29.0 %collective-permute-start.32 = (bf16[1,192,1536]{2,1,0:T(8,128)(2,1)}, bf16[1,192,1536]{2,1,0:T(8,128)(2,1)S(1)}, u32[]{:S(2)}, u32[]{:S(2)}) collective-permute-start(bf16[1,192,1536]{2,1,0:T(8,128)(2,1)} %get-tuple-element.265), channel_id=1, source_target_pairs={{0,8},{1,9},{2,10},{3,11},{4,12},{5,13},{6,14},{7,15},{8,0},{9,1},... | collective-permute-start | bytes 1769480 | tf_op jit(solution)/shard_map/ppermute | solution.py:31
  830.1 46.5 %collective-permute-start.31 = (f32[2,2,2,64,128]{4,3,2,1,0:T(8,128)}, f32[2,2,2,64,128]{4,3,2,1,0:T(8,128)}, u32[]{:S(2)}, u32[]{:S(2)}) collective-permute-start(f32[2,2,2,64,128]{4,3,2,1,0:T(8,128)} %get-tuple-element.263), channel_id=1, source_target_pairs={{0,2},{1,3},{2,0},{3,1},{4,6},{5,7},{6,4},{7,5},{8,10},{9,11},{10,... | collective-permute-start | bytes 786440 | tf_op jit(solution)/shard_map/ppermute | solution.py:31
  884.1 25.5 %collective-permute-start.33 = (bf16[2,2,192,640]{3,2,1,0:T(8,128)(2,1)}, bf16[2,2,192,640]{3,2,1,0:T(8,128)(2,1)S(1)}, u32[]{:S(2)}, u32[]{:S(2)}) collective-permute-start(bf16[2,2,192,640]{3,2,1,0:T(8,128)(2,1)} %get-tuple-element.269), channel_id=1, source_target_pairs={{0,2},{1,3},{2,0},{3,1},{4,6},{5,7},{6,4},{7,5},{8,10},{9,11},{10,... | collective-permute-start | bytes 2949128 | tf_op jit(solution)/shard_map/ppermute | solution.py:31
  884.7 24.9 %collective-permute-start.34 = (bf16[2,2,192,640]{3,2,1,0:T(8,128)(2,1)}, bf16[2,2,192,640]{3,2,1,0:T(8,128)(2,1)S(1)}, u32[]{:S(2)}, u32[]{:S(2)}) collective-permute-start(bf16[2,2,192,640]{3,2,1,0:T(8,128)(2,1)} %get-tuple-element.271), channel_id=1, source_target_pairs={{0,4},{1,5},{2,6},{3,7},{4,0},{5,1},{6,2},{7,3},{8,12},{9,13},{10,... | collective-permute-start | bytes 2949128 | tf_op jit(solution)/shard_map/ppermute | solution.py:31
  886.2 23.3 %collective-permute-start.35 = (bf16[2,2,192,256]{3,2,1,0:T(8,128)(2,1)}, bf16[2,2,192,256]{3,2,1,0:T(8,128)(2,1)S(1)}, u32[]{:S(2)}, u32[]{:S(2)}) collective-permute-start(bf16[2,2,192,256]{3,2,1,0:T(8,128)(2,1)} %get-tuple-element.273), channel_id=1, source_target_pairs={{0,1},{1,0},{2,3},{3,2},{4,5},{5,4},{6,7},{7,6},{8,9},{9,8},{10,11... | collective-permute-start | bytes 1179656 | tf_op jit(solution)/shard_map/ppermute | solution.py:31
  887.8 21.8 %collective-permute-start.36 = (f32[2,2,64,128]{3,2,1,0:T(8,128)}, f32[2,2,64,128]{3,2,1,0:T(8,128)S(1)}, u32[]{:S(2)}, u32[]{:S(2)}) collective-permute-start(f32[2,2,64,128]{3,2,1,0:T(8,128)} %get-tuple-element.275), channel_id=1, source_target_pairs={{0,4},{1,5},{2,6},{3,7},{4,0},{5,1},{6,2},{7,3},{8,12},{9,13},{10,... | collective-permute-start | bytes 393224 | tf_op jit(solution)/shard_map/ppermute | solution.py:31
  914.9 13.3 %collective-permute-start.37 = (bf16[2,192,640]{2,1,0:T(8,128)(2,1)}, bf16[2,192,640]{2,1,0:T(8,128)(2,1)S(1)}, u32[]{:S(2)}, u32[]{:S(2)}) collective-permute-start(bf16[2,192,640]{2,1,0:T(8,128)(2,1)} %get-tuple-element.278), channel_id=1, source_target_pairs={{0,4},{1,5},{2,6},{3,7},{4,0},{5,1},{6,2},{7,3},{8,12},{9,13},{10,... | collective-permute-start | bytes 1474568 | tf_op jit(solution)/shard_map/ppermute | solution.py:31
  916.5 11.8 %collective-permute-start.38 = (bf16[2,192,640]{2,1,0:T(8,128)(2,1)}, bf16[2,192,640]{2,1,0:T(8,128)(2,1)S(1)}, u32[]{:S(2)}, u32[]{:S(2)}) collective-permute-start(bf16[2,192,640]{2,1,0:T(8,128)(2,1)} %get-tuple-element.280), channel_id=1, source_target_pairs={{0,1},{1,0},{2,3},{3,2},{4,5},{5,4},{6,7},{7,6},{8,9},{9,8},{10,11... | collective-permute-start | bytes 1474568 | tf_op jit(solution)/shard_map/ppermute | solution.py:31
  918.1 10.2 %collective-permute-start.39 = (bf16[2,192,256]{2,1,0:T(8,128)(2,1)}, bf16[2,192,256]{2,1,0:T(8,128)(2,1)S(1)}, u32[]{:S(2)}, u32[]{:S(2)}) collective-permute-start(bf16[2,192,256]{2,1,0:T(8,128)(2,1)} %get-tuple-element.282), channel_id=1, source_target_pairs={{0,2},{1,3},{2,0},{3,1},{4,6},{5,7},{6,4},{7,5},{8,10},{9,11},{10,... | collective-permute-start | bytes 589832 | tf_op jit(solution)/shard_map/ppermute | solution.py:31
  918.6 9.7 collective-permute-start.40
  932.2 14.7 %collective-permute-start.42 = (f32[1,64,128]{2,1,0:T(8,128)}, f32[1,64,128]{2,1,0:T(8,128)S(1)}, u32[]{:S(2)}, u32[]{:S(2)}) collective-permute-start(f32[1,64,128]{2,1,0:T(8,128)} %get-tuple-element.289), channel_id=1, source_target_pairs={{0,8},{1,9},{2,10},{3,11},{4,12},{5,13},{6,14},{7,15},{8,0},{9,1},... | collective-permute-start | bytes 98312 | tf_op jit(solution)/shard_map/ppermute | solution.py:31
  933.7 25.5 %collective-permute-start.41 = (bf16[1,192,1536]{2,1,0:T(8,128)(2,1)}, bf16[1,192,1536]{2,1,0:T(8,128)(2,1)}, u32[]{:S(2)}, u32[]{:S(2)}) collective-permute-start(bf16[1,192,1536]{2,1,0:T(8,128)(2,1)} %get-tuple-element.287), channel_id=1, source_target_pairs={{0,8},{1,9},{2,10},{3,11},{4,12},{5,13},{6,14},{7,15},{8,0},{9,1},... | collective-permute-start | bytes 1769480 | tf_op jit(solution)/shard_map/ppermute | solution.py:31
  (58 other events, 276.8 us)
Sparse Core Ops, SparseCore 0:
  15.0 240.4 all-gather.2
  259.0 122.8 all-gather.4

commit v3 on v2

--- a/solution.py
+++ b/solution.py
@@ -47,8 +47,8 @@
     def __init__(self):
         self.token = None
 
-    def call(self, kernel, grid, ins, outs, scratch, *operands, scalars=()):
-        earlier = () if self.token is None else (self.token,)
+    def call(self, kernel, grid, ins, outs, scratch, *operands, scalars=(), after=()):
+        earlier = (() if self.token is None else (self.token,)) + tuple(after)
         held, count = len(scalars), len(operands)
 
         def body(*refs):
@@ -79,7 +79,7 @@
 
 
 class Weight:
-    def __init__(self, gathered, place, rows, block=lambda step: step):
+    def __init__(self, gathered, place, rows, block=lambda step, *_: step):
         if rows % GROUP:
             some = gathered[:, place * rows : (place + 1) * rows]
             gathered, place, rows = some.reshape(-1, UNITS, some.shape[2]), 0, UNITS
@@ -92,7 +92,7 @@
 
     def spec(self):
         return pl.BlockSpec(
-            (UNITS // self.rows, self.rows, self.width), lambda i, *_: (self.block(i), self.place, 0)
+            (UNITS // self.rows, self.rows, self.width), lambda *at: (self.block(*at), self.place, 0)
         )
 
 
@@ -103,14 +103,13 @@
 class Piece:
     def __init__(self, base, order, bits, cut=0, width=None):
         self.base, self.order, self.bits, self.cut = base, list(order), list(bits), cut
-        self.free, self.fixed, self.come = list(bits), [], None
+        self.free, self.fixed, self.come, self.come_cut = list(bits), [], None, 0
         self.width = base.shape[-1] if width is None else width
 
 
-def fold(chain, pieces, inner, outer):
+def fold(chain, pieces, inner, outer, after=(), hold=False):
     if len(pieces[0].free) == 1:
-        return fold_last(chain, pieces, inner, outer)
-    low_bits = bit_count(outer)
+        return fold_last(chain, pieces, inner, outer, after)
     me = lax.axis_index("dp") * outer + lax.axis_index("fsdp")
     left = len(pieces[0].free) - 1
     inside = min(max(left - 1, 0), 2)
@@ -146,12 +145,12 @@
         ins.append(spec(piece.bits, piece.cut, piece.width, rows))
         operands.append(piece.base)
         if not lazy:
-            ins.append(spec(piece.free, 0, piece.width, rows))
+            ins.append(spec(piece.free, piece.come_cut, piece.width, rows))
             operands.append(piece.come)
         shape = (2,) * len(rest) + (rows, piece.width)
         outs += [(shape, piece.base.dtype, spec(rest, 0, piece.width, rows))] * (1 if lazy else 2)
         plans.append((lazy, bit, sum(1 for b in near if b > bit)))
-        piece.free = rest
+        piece.free, piece.come_cut = rest, 0
     done = list(
         chain.call(
             functools.partial(fold_kernel, plans),
@@ -161,6 +160,7 @@
             [],
             *operands,
             scalars=(me.astype(jnp.int32)[None],),
+            after=after,
         )
     )
     for piece, (lazy, bit, _) in zip(pieces, plans):
@@ -169,6 +169,16 @@
             piece.fixed.append(bit)
         else:
             piece.base, piece.cut, piece.fixed, piece.bits = done.pop(0), 0, [], list(piece.free)
+        piece.away = (away, bit)
+    if not hold:
+        send(chain, pieces, inner, outer, False)
+
+
+def send(chain, pieces, inner, outer, wait=True):
+    low_bits = bit_count(outer)
+    for piece in pieces:
+        away, bit = piece.away
+        away = late(chain, away) if wait else away
         if bit < low_bits:
             piece.come = swap(away, "fsdp", outer, bit)
         else:
@@ -189,14 +199,14 @@
             out[...] = (base[at].astype(jnp.float32) + come[at].astype(jnp.float32)).astype(out.dtype)
 
 
-def turn_kernel(values_ref, late_ref, out_ref):
-    out_ref[...] = values_ref[...].T.astype(jnp.bfloat16)
-
-
-def turn_late(chain, values, late):
-    shape = values.shape[::-1]
+def round_kernel(values_ref, late_ref, out_ref):
+    out_ref[...] = values_ref[...].astype(jnp.bfloat16)
+
+
+def round_late(chain, values, late):
+    shape = values.shape
     return chain.call(
-        turn_kernel,
+        round_kernel,
         (1,),
         [whole_array(values.shape), pl.BlockSpec(memory_space=pl.ANY)],
         [(shape, jnp.bfloat16, whole_array(shape))],
@@ -204,6 +214,30 @@
         values,
         late,
     )[0]
+
+
+def copy_kernel(values_ref, out_ref):
+    out_ref[...] = values_ref[...]
+
+
+def copy_late(chain, values):
+    spec = whole_array(values.shape)
+    return chain.call(copy_kernel, (1,), [spec], [(values.shape, values.dtype, spec)], [], values)[0]
+
+
+def keep_kernel(values_ref, token_ref, out_ref):
+    pass
+
+
+def late(chain, values):
+    some = pl.BlockSpec(memory_space=pl.ANY)
+    return pl.pallas_call(
+        keep_kernel,
+        out_shape=jax.ShapeDtypeStruct(values.shape, values.dtype),
+        in_specs=[some, some],
+        out_specs=some,
+        input_output_aliases={0: 0},
+    )(values, chain.token)
 
 
 def last_kernel(cuts, bit, me_ref, *refs):
@@ -216,7 +250,7 @@
         outs[2 * group + 1][:, :, cut] = jnp.where(own == 0, both[0:1], both[1:2])
 
 
-def fold_last(chain, pieces, inner, outer):
+def fold_last(chain, pieces, inner, outer, after):
     bit = pieces[0].order.pop(0)
     me = lax.axis_index("dp") * outer + lax.axis_index("fsdp")
     operands, cuts, shapes = [], [], []
@@ -237,25 +271,23 @@
         [],
         *operands,
         scalars=(me.astype(jnp.int32)[None],),
+        after=after,
     )
     pieces[:] = [Piece(kept, [], []) for kept in done[1::2]]
     for piece, away in zip(pieces, done[::2]):
         piece.come = swap(away, "fsdp", outer, bit)
 
 
-def total_kernel(turned, *refs):
-    for n, turn in enumerate(turned):
-        total = (refs[2 * n][...].astype(jnp.float32) + refs[2 * n + 1][...].astype(jnp.float32))[0]
-        refs[2 * len(turned) + n][...] = total.T if turn else total
-
-
-def totals_of(chain, pieces, turned):
-    shapes = [
-        piece.base.shape[:0:-1] if turn else piece.base.shape[1:] for piece, turn in zip(pieces, turned)
-    ]
+def total_kernel(count, *refs):
+    for n in range(count):
+        refs[2 * count + n][...] = (refs[2 * n][...].astype(jnp.float32) + refs[2 * n + 1][...].astype(jnp.float32))[0]
+
+
+def totals_of(chain, pieces):
     operands = [v for piece in pieces for v in (piece.base, piece.come)]
+    shapes = [piece.base.shape[1:] for piece in pieces]
     return chain.call(
-        functools.partial(total_kernel, turned),
+        functools.partial(total_kernel, len(pieces)),
         (1,),
         [whole_array(v.shape) for v in operands],
         [(shape, jnp.float32, whole_array(shape)) for shape in shapes],
@@ -547,48 +579,86 @@
     )
 
 
-def response_back_kernel(branch_ref, act_ref, member_ref, *refs):
-    weight_ref, grad_ref, sums_ref, shift_ref = refs
+def partner_first(half):
+    def block(step, mine_ref):
+        return jnp.where(step < half, 1 - mine_ref[0], mine_ref[0]) * half + step % half
+
+    return block
+
+
+def half_specs(units, width):
+    half = units // UNITS // 2
+    shape = (units // 2, width)
+    return [
+        (shape, jnp.bfloat16, pl.BlockSpec((UNITS, width), lambda i, _: (jnp.minimum(i, half - 1), 0))),
+        (shape, jnp.bfloat16, pl.BlockSpec((UNITS, width), lambda i, _: (jnp.maximum(i - half, 0), 0))),
+    ]
+
+
+def store_half(away_ref, kept_ref, left, right):
+    rows = product(left, right, 0, 0).astype(jnp.bfloat16)
+    half = pl.num_programs(0) // 2
+
+    @pl.when(pl.program_id(0) < half)
+    def _():
+        away_ref[...] = rows
+
+    @pl.when(pl.program_id(0) >= half)
+    def _():
+        kept_ref[...] = rows
+
+
+def response_back_kernel(mine_ref, branch_ref, act_ref, response_ref, member_ref, weight_ref, grad_ref, sums_ref, shift_ref, away_ref, kept_ref):
     grad = product(branch_ref[...], rows_of(weight_ref), 1, 1)
     grad_ref[...] = grad
     sums_ref[...] = gathered(grad * act_ref[...], member_ref[...])
     shift_ref[...] = jnp.broadcast_to(jnp.sum(grad, axis=0, keepdims=True), shift_ref.shape)
-
-
-def response_back(chain, branch, weight, act, member):
+    store_half(away_ref, kept_ref, response_ref[...], branch_ref[...])
+
+
+def response_back(chain, branch, weight, act, response, member, mine):
     slots, width = branch.shape
     units = weight.total
+    block = partner_first(units // UNITS // 2)
+
+    def columns(rows):
+        return pl.BlockSpec((rows, UNITS), lambda *at: (0, block(*at)))
+
     return chain.call(
         response_back_kernel,
         (units // UNITS,),
-        [whole_array(branch.shape), unit_columns(slots), whole_array(member.shape)] + [weight.spec()],
+        [whole_array(branch.shape), columns(slots), columns(slots), whole_array(member.shape)]
+        + [weight.by(block).spec()],
         [
-            ((slots, units), jnp.float32, unit_columns(slots)),
-            ((SEATS, units), jnp.float32, unit_columns(SEATS)),
-            ((SEATS, units), jnp.float32, unit_columns(SEATS)),
-        ],
+            ((slots, units), jnp.float32, columns(slots)),
+            ((SEATS, units), jnp.float32, columns(SEATS)),
+            ((SEATS, units), jnp.float32, columns(SEATS)),
+        ]
+        + half_specs(units, width),
         [],
         branch,
         act,
+        response,
         member,
         weight.gathered,
-    )
-
-
-def hidden_back_kernel(grad_ref, act_ref, slope_ref, vecs_ref, norms_ref, ratio_ref, member_ref, *refs):
-    weight_ref, low_ref, bias_ref, normed_grad_ref, total_ref = refs
+        scalars=(mine,),
+    )
+
+
+def hidden_back_kernel(added, side_ref, grad_ref, act_ref, slope_ref, vecs_ref, norms_ref, ratio_ref, member_ref, normed_ref, weight_ref, *refs):
+    bias_ref, normed_grad_ref, rows_ref, total_ref = refs[-4:]
     step = pl.program_id(0)
     member = member_ref[...]
     grad = by_group(grad_ref[...]) * (1.0 + vecs_ref[1:2, :][None] * spread(norms_ref[...], member))
     grad = grad + by_group(act_ref[...]) * spread(ratio_ref[...], member)
     low = (grad.reshape(act_ref.shape) * slope_ref[...]).astype(jnp.bfloat16)
-    low_ref[...] = low
     bias_ref[...] = jnp.broadcast_to(jnp.sum(low.astype(jnp.float32), axis=0, keepdims=True), bias_ref.shape)
+    rows_ref[...] = product(low, normed_ref[...], 0, 0).astype(jnp.bfloat16)
     part = product(low, rows_of(weight_ref), 1, 0)
 
     @pl.when(step == 0)
     def _():
-        total_ref[...] = part
+        total_ref[...] = part + refs[0][...] if added else part
 
     @pl.when(step > 0)
     def _():
@@ -599,20 +669,29 @@
         normed_grad_ref[...] = total_ref[...]
 
 
-def hidden_back(chain, grad, act, slope, vecs, norms, ratio, member, weight):
+def hidden_back(chain, grad, act, slope, vecs, norms, ratio, member, normed, weight, side, before=None):
     slots, units = act.shape
     width = weight.width
+    half = units // UNITS // 2
+
+    def block(step, side_ref):
+        return side_ref[0] * half + step
+
+    def columns(rows):
+        return pl.BlockSpec((rows, UNITS), lambda *at: (0, block(*at)))
+
+    before = () if before is None else (before,)
     return chain.call(
-        hidden_back_kernel,
-        (units // UNITS,),
-        [unit_columns(slots)] * 3
-        + [unit_columns(vecs.shape[0]), unit_columns(SEATS), unit_columns(SEATS)]
-        + [whole_array(member.shape)]
-        + [weight.spec()],
+        functools.partial(hidden_back_kernel, len(before) > 0),
+        (half,),
+        [columns(slots)] * 3
+        + [columns(vecs.shape[0]), columns(SEATS), columns(SEATS)]
+        + [whole_array(member.shape), whole_array(normed.shape), weight.by(block).spec()]
+        + [whole_array(v.shape) for v in before],
         [
-            ((slots, units), jnp.bfloat16, unit_columns(slots)),
-            ((SEATS, units), jnp.float32, unit_columns(SEATS)),
+            ((SEATS, units // 2), jnp.float32, unit_columns(SEATS)),
             ((slots, width), jnp.float32, whole_array((slots, width))),
+            ((units // 2, width), jnp.bfloat16, pl.BlockSpec((UNITS, width), lambda i, *_: (i, 0))),
         ],
         [pltpu.VMEM((slots, width), jnp.float32)],
         grad,
@@ -622,7 +701,10 @@
         norms,
         ratio,
         member,
+        normed,
         weight.gathered,
+        *before,
+        scalars=(side,),
     )
 
 
@@ -764,35 +846,6 @@
         live,
         bias,
         weight.gathered,
-    )[0]
-
-
-def half_kernel(added, half_ref, left_ref, right_ref, *refs):
-    total = product(left_ref[...], right_ref[...], 0, 0)
-    if added:
-        total = total + refs[0][...].astype(jnp.float32)
-    refs[-1][...] = total.astype(jnp.bfloat16)
-
-
-def half_rows(chain, left, right, half, come=None):
-    slots, units = left.shape
-    width = right.shape[1]
-    steps = units // 2 // UNITS
-    rows = pl.BlockSpec((UNITS, width), lambda i, *_: (i, 0))
-    return chain.call(
-        functools.partial(half_kernel, come is not None),
-        (steps,),
-        [
-            pl.BlockSpec((slots, UNITS), lambda i, half_ref: (0, half_ref[0] * steps + i)),
-            whole_array(right.shape),
-        ]
-        + ([] if come is None else [rows]),
-        [((units // 2, width), jnp.bfloat16, rows)],
-        [],
-        left,
-        right,
-        *(() if come is None else (come,)),
-        scalars=(half.astype(jnp.int32)[None],),
     )[0]
 
 
@@ -1018,7 +1071,7 @@
     rows, kv_rows = fc2_w.shape[0], kv_w.shape[0]
     small_rows = small_shard.size // width
     res_weights = to_all(fc1_w.T, fc2_w, kv_w, small_shard.reshape(-1, width))
-    attn_weights = to_all(turn_late(chain, attn_w, res_weights))
+    attn_weights = to_all(round_late(chain, attn_w.T, res_weights))
     fc1_t, fc2_full = Weight(res_weights, 0, rows), Weight(res_weights, 1, rows)
     attn_t = Weight(attn_weights, 0, rows)
     kv_full = res_weights[:, 2 * rows : 2 * rows + kv_rows].reshape(-1, width)
@@ -1066,12 +1119,14 @@
     free = list(reversed(range(outer_bits + inner_bits - 1)))
     early = [b for b in free if b >= outer_bits]
 
-    def pieces_of(both):
-        both = both.reshape((2,) * len(free) + (-1, width))
-        return [
-            Piece(both, early + order, free, start // size, size)
-            for order, (start, size) in zip(orders, column_pieces(width, len(orders)))
-        ]
+    def pieces_of(kept, come=None):
+        kept = kept.reshape((2,) * len(free) + (-1, width))
+        pieces = []
+        for order, (start, size) in zip(orders, column_pieces(width, len(orders))):
+            pieces.append(Piece(kept, early + order, free, start // size, size))
+            if come is not None:
+                pieces[-1].come, pieces[-1].come_cut = come.reshape(kept.shape), start // size
+        return pieces
 
     def to_partner(away):
         return swap(away, "dp", inner, inner_bits - 1)
@@ -1080,18 +1135,17 @@
         half = blocks // 2
         come = to_partner(lax.dynamic_slice_in_dim(terms, (1 - mine) * half, half, axis=0))
         kept = lax.dynamic_slice_in_dim(terms, mine * half, half, axis=0)
-        some = Piece(kept.reshape((2,) * len(free) + terms.shape[1:]), early + orders[1], free)
+        some = Piece(kept.reshape((2,) * len(free) + terms.shape[1:]), early + orders[2], free)
         some.come = come.reshape(some.base.shape)
         return some
 
-    def step(*groups):
-        for group in groups:
-            fold(chain, group, inner, outer)
-
-    def finished(group, *turned):
+    def step(group, hold=False):
+        fold(chain, group, inner, outer, (), hold)
+
+    def finished(group):
         while group[0].order:
             step(group)
-        return totals_of(chain, group, turned)
+        return totals_of(chain, group)
 
     parts = (grad_query, grad_key, grad_value, grad_proj, source, attended)
     come = to_partner(attn_half(chain, *parts, 1 - mine))
@@ -1100,7 +1154,7 @@
         grad_query,
         grad_key,
         grad_value,
-        attn_t.by(lambda i: jnp.where(i < 2 * each, i + each, i - 2 * each)),
+        attn_t.by(lambda i, *_: jnp.where(i < 2 * each, i + each, i - 2 * each)),
     )
     grad_mapped = grad_text[:text_total]
     kv_terms = along("tk,tc->kc", silu_low, grad_mapped).astype(low)
@@ -1112,31 +1166,48 @@
     grad_res, grad_branch, pair_grad, res_bias_grad = time_back(
         chain, grad_normed_two, after_time, after_res, cot, pair, member, live
     )
-    come = to_partner(half_rows(chain, response, grad_branch, 1 - mine))
-    grad_response, act_sums, shift_grad = response_back(chain, grad_branch, fc2_full, act, member)
+    mine_index = mine.astype(jnp.int32)[None]
+    grad_response, act_sums, shift_grad, fc2_away, fc2_kept = response_back(
+        chain, grad_branch, fc2_full, act, response, member, mine_index
+    )
     step(attn_sum)
-    fc2_sum = pieces_of(half_rows(chain, response, grad_branch, mine, come))
-    step(attn_sum)
-    for _ in early:
-        step(fc2_sum)
-    for _ in range(outer_bits - 3):
-        step(attn_sum)
-    step(fc2_sum)
+    fc2_come = to_partner(late(chain, fc2_away))
     gain_grad = jnp.sum(act_sums * norms, axis=0, keepdims=True)
     norms_grad = vecs[1:2] * act_sums
     norm_grad = norms_grad / norm_mean - jnp.sum(norms_grad * norm, axis=1, keepdims=True) / (
         units * norm_mean * norm_mean
     )
-    hidden_low, hidden_bias_grad, grad_normed = hidden_back(
-        chain, grad_response, act, slope, vecs, norms, norm_grad / norm, member, fc1_t
-    )
-    attn_grad, kv_grad = finished(attn_sum, True, False)
-    step(fc2_sum)
-    come = to_partner(half_rows(chain, hidden_low, normed_low, 1 - mine))
+    hidden_parts = (grad_response, act, slope, vecs, norms, norm_grad / norm, member, normed_low, fc1_t)
+    bias_away, grad_normed, fc1_away = hidden_back(chain, *hidden_parts, 1 - mine_index)
+    step(attn_sum)
+    fc2_sum = pieces_of(fc2_kept, fc2_come)
+    for _ in early:
+        step(fc2_sum)
+    step(fc2_sum, True)
+    for _ in range(outer_bits - 3):
+        step(attn_sum)
+    send(chain, fc2_sum, inner, outer)
+    bias_kept, grad_normed, fc1_kept = hidden_back(chain, *hidden_parts, mine_index, grad_normed)
+    hidden_bias_grad = jnp.where(
+        mine == 0,
+        jnp.concatenate([bias_kept[:1], bias_away[:1]], axis=1),
+        jnp.concatenate([bias_away[:1], bias_kept[:1]], axis=1),
+    )
     latents_grad, taps_grad = entry_back(
         chain, grad_normed, normed, entry_scale, x, grad_res, taps, geometry, res_bias_grad
     )
+    output = output_step(
+        chain,
+        attended,
+        after_time,
+        live,
+        jnp.broadcast_to(vecs_all[2], (SEATS, width)),
+        attn_t.by(lambda i, *_: 3 * each + i),
+    )
+    attn_grad, kv_grad = finished(attn_sum)
     step(fc2_sum)
+    taps_grad = copy_late(chain, taps_grad)
+    fc1_come = to_partner(late(chain, fc1_away))
     time_grad = jnp.einsum("lt,lc->tc", time_low.astype(full), pair_grad, precision=HIGHEST)
     small_terms = (
         taps_grad[: res_vecs.shape[0]],
@@ -1158,24 +1229,18 @@
         axis=1,
     ).reshape(blocks, -1, 128)
     small_piece = halved(small_blocks)
-    fc1_sum = pieces_of(half_rows(chain, hidden_low, normed_low, mine, come)) + [small_piece]
+    step(fc2_sum)
+    fc1_sum = pieces_of(fc1_kept, fc1_come) + [small_piece]
     for _ in early:
         step(fc1_sum)
+    step(fc1_sum, True)
     for _ in range(outer_bits - 3):
         step(fc2_sum)
-    step(fc1_sum)
-    output = output_step(
-        chain,
-        attended,
-        after_time,
-        live,
-        jnp.broadcast_to(vecs_all[2], (SEATS, width)),
-        attn_t.by(lambda i: 3 * each + i),
-    )
-    (fc2_grad,) = finished(fc2_sum, False)
+    send(chain, fc1_sum, inner, outer)
+    (fc2_grad,) = finished(fc2_sum)
     step(fc1_sum)
     step(fc1_sum)
-    fc1_grad, small_total = finished(fc1_sum, True, False)
+    fc1_grad, small_total = finished(fc1_sum)
     small_total = small_total.reshape(-1)
     text_grad = silu_back(along("tc,kc->tk", grad_mapped, kv_full))[0]
 
@@ -1189,13 +1254,13 @@
         latents_grad[None],
         text_grad.reshape(text_embed.shape),
         small_grads[0],
-        fc1_grad,
+        fc1_grad.T,
         small_grads[1],
         fc2_grad,
         small_grads[2],
         small_grads[3][0],
         kv_grad,
-        attn_grad,
+        attn_grad.T,
         small_grads[4],
     )
 

time: 989 us -> 918 us (0.928)
  waiting for transfers between devices: 423 us -> 360 us
    ppermute x43, waiting for transfers between devices: 155 us -> 88.4 us  [swap(): lax.ppermute(values, axis_name, [(i, i ^ 1 << bit) for i in range(size)])]
    unnamed x128 -> x127, local copies, waits for them, and re-layouts: 23.3 us -> 16.6 us
    pallas_call x33 -> x31, Pallas kernels: 408 us -> 407 us  [call(): pl.pallas_call(body, grid_spec=pltpu.PrefetchScalarGridSpec(num_scalar_pr...]
  transfers between devices with their start and end apart: 45 -> 45, of which waited for: 14 -> 17; matrix products, arithmetic and copies ran while one was open for 6% -> 6% of each run, Pallas kernels for 23% -> 29%
where the time goes in v3:
time: 918 us; the launch traced here: 907 us
  Pallas kernels  407 us (44%)
  waiting for transfers between devices  360 us (39%)
  local copies, waits for them, and re-layouts  48.5 us (5%)
  starting transfers between devices  43.5 us (5%)
  other arithmetic  24.5 us (3%)
  between operations  15.4 us (2%)
    pallas_call x31, Pallas kernels, call(): pl.pallas_call(body, grid_spec=pltpu.PrefetchScalarGridSpec(num_scalar_pr...  407 us
    all_gather x2, waiting for transfers between devices, to_all(): full_rows = lax.all_gather(shard, ('dp', 'fsdp'), axis=0, tiled=True)  271 us
    ppermute x43, waiting for transfers between devices, swap(): lax.ppermute(values, axis_name, [(i, i ^ 1 << bit) for i in range(size)])  88.4 us
    ppermute x43, starting transfers between devices, swap(): lax.ppermute(values, axis_name, [(i, i ^ 1 << bit) for i in range(size)])  43.4 us
  transfers between devices with their start and end apart: 45, of which 17 were waited for; matrix products, arithmetic and copies ran while one was open for 6% of the time, Pallas kernels for 29%

profile of v3, /device:TPU:0, one launch (start us, length us, event | category | flops | bytes accessed | tf_op | source)
XLA Modules:
  0.0 907.3 jit_solution(6204647897592859345)
XLA Ops:
  15.0 240.5 %all-gather.3.cloned.1.call-done = bf16[13824,1536]{1,0:T(8,128)(2,1)} async-done(((bf16[432,1536]{1,0:T(8,128)(2,1)}), bf16[13824,1536]{1,0:T(8,128)(2,1)}) %all-gather.3.cloned.1.call-update) | async-done | bytes 42467344 | tf_op jit(solution)/shard_map/all_gather | solution.py:1068
  255.5 2.2 shard_map.247
  265.1 2.2 convert_reduce_fusion.1
  268.4 4.2 slice.127
  278.7 11.1 %shard_map.248 = (bf16[576,1536]{1,0:T(8,128)(2,1)}, f32[576,1536]{1,0:T(8,128)}, f32[576,128]{1,0:T(8,128)}, f32[8,128]{1,0:T(8,128)}) custom-call(f32[576,1536]{1,0:T(8,128)} %bitcast.89, f32[16,1536]{1,0:T(8,128)} %pad.18.refs_1_.refs_5_, f32[576,16]{1,0:T(8,128)} %copy-done.1, f32[8,128]{1,0:T(8,128)} %get-tuple-element.160.refs_3_), custom_call_target="tpu_custom_call" | custom-call | tf_op jit(solution)/shard_map/pallas_call | solution.py:60
  289.8 25.0 %shard_map.249 = (f32[576,6144]{1,0:T(8,128)}, f32[576,6144]{1,0:T(8,128)}, f32[8,6144]{1,0:T(8,128)}, f32[8,128]{1,0:T(8,128)}) custom-call(bf16[576,1536]{1,0:T(8,128)(2,1)} %get-tuple-element.161.refs_0_.refs_8_, f32[8,6144]{1,0:T(8,128)} %pad.19.refs_1_.refs_2_.refs_4_, f32[36,8]{1,0:T(8,128)} %pad_convert_fusion.refs_2_.refs_3_.refs_5_.refs_4_.refs_7_, ...), custom_call_target="tpu_custom_call" | custom-call | tf_op jit(solution)/shard_map/pallas_call | solution.py:60
  318.4 29.2 %shard_map.250 = (bf16[576,6144]{1,0:T(8,128)(2,1)}, f32[576,1536]{1,0:T(8,128)}, f32[576,1536]{1,0:T(8,128)}, bf16[576,1536]{1,0:T(8,128)(2,1)}, f32[8,128]{1,0:T(8,128)}) custom-call(f32[576,6144]{1,0:T(8,128)} %get-tuple-element.163.refs_0_.refs_2_, f32[8,6144]{1,0:T(8,128)} %fusion.10.refs_1_.refs_5_, f32[8,6144]{1,0:T(8,128)} %pad.19.refs_1_.refs_2_.refs_4_, ...), custom_call_target="tpu_custom_call" | custom-call | tf_op jit(solution)/shard_map/pallas_call | solution.py:60
  349.2 2.1 maximum_maximum_fusion.refs_0_.refs_5_
  351.2 30.6 %all-gather.5.cloned.1.call-done = bf16[6144,1536]{1,0:T(8,128)(2,1)} async-done(((bf16[192,1536]{1,0:T(8,128)(2,1)}), bf16[6144,1536]{1,0:T(8,128)(2,1)}) %all-gather.5.cloned.1.call-update) | async-done | bytes 18874384 | tf_op jit(solution)/shard_map/all_gather | solution.py:1068
  382.5 23.9 %shard_map.251 = (bf16[896,4608]{1,0:T(8,128)(2,1)}, bf16[576,1536]{1,0:T(8,128)(2,1)}, f32[8,128]{1,0:T(8,128)}) custom-call(bf16[896,1536]{1,0:T(8,128)(2,1)} %maximum_maximum_fusion.refs_0_.refs_5_, bf16[576,1536]{1,0:T(8,128)(2,1)} %get-tuple-element.378.refs_1_.refs_4_, f32[8,4608]{1,0:T(8,128)} %broadcast_in_dim.129.refs_2_, ...), custom_call_target="tpu_custom_call" | custom-call | tf_op jit(solution)/shard_map/pallas_call | solution.py:60
  406.4 65.1 %shard_map.252 = (bf16[576,1536]{1,0:T(8,128)(2,1)}, bf16[576,1536]{1,0:T(8,128)(2,1)}, bf16[896,1536]{1,0:T(8,128)(2,1)}, bf16[896,1536]{1,0:T(8,128)(2,1)}, f32[8,128]{1,0:T(8,128)}) custom-call(bf16[896,4608]{1,0:T(8,128)(2,1)} %get-tuple-element.169.refs_0_.refs_1_.refs_2_, bf16[896,4608]{1,0:T(8,128)(2,1)} %get-tuple-element.169.refs_0_.refs_1_.refs_2_, ...), custom_call_target="tpu_custom_call" | custom-call | tf_op jit(solution)/shard_map/pallas_call | solution.py:60
  471.5 14.8 %shard_map.253 = (bf16[3072,1536]{1,0:T(8,128)(2,1)}, f32[8,128]{1,0:T(8,128)}) custom-call(s32[1]{0:T(128)} %bitcast.20.refs_0_, bf16[576,1536]{1,0:T(8,128)(2,1)} %get-tuple-element.174.refs_1_.refs_0_, bf16[896,1536]{1,0:T(8,128)(2,1)} %get-tuple-element.175.refs_2_.refs_1_, bf16[896,1536]{1,0:T(8,128)(2,1)} %get-tuple-element.176.refs_3_.refs_2_, ...), custom_call_target="tpu_custom_call" | custom-call | tf_op jit(solution)/shard_map/pallas_call | solution.py:60
  486.9 19.5 %shard_map.254 = (f32[576,1536]{1,0:T(8,128)}, bf16[320,1536]{1,0:T(8,128)(2,1)}, f32[8,128]{1,0:T(8,128)}) custom-call(bf16[576,1536]{1,0:T(8,128)(2,1)} %get-tuple-element.174.refs_1_.refs_0_, bf16[896,1536]{1,0:T(8,128)(2,1)} %get-tuple-element.175.refs_2_.refs_1_, bf16[896,1536]{1,0:T(8,128)(2,1)} %get-tuple-element.176.refs_3_.refs_2_, ...), custom_call_target="tpu_custom_call" | custom-call | tf_op jit(solution)/shard_map/pallas_call | solution.py:60
  506.4 3.5 convolution_convert_fusion
  509.9 2.2 constant_dynamic-slice_fusion
  512.3 16.4 %shard_map.255 = (bf16[3072,1536]{1,0:T(8,128)(2,1)}, f32[8,128]{1,0:T(8,128)}) custom-call(s32[1]{0:T(128)} %bitcast.19.refs_0_, bf16[576,1536]{1,0:T(8,128)(2,1)} %get-tuple-element.174.refs_1_.refs_0_, bf16[896,1536]{1,0:T(8,128)(2,1)} %get-tuple-element.175.refs_2_.refs_1_, bf16[896,1536]{1,0:T(8,128)(2,1)} %get-tuple-element.176.refs_3_.refs_2_, ...), custom_call_target="tpu_custom_call" | custom-call | tf_op jit(solution)/shard_map/pallas_call | solution.py:60
  530.0 5.7 shard_map.256
  539.7 11.6 %shard_map.257 = (f32[576,1536]{1,0:T(8,128)}, bf16[576,1536]{1,0:T(8,128)(2,1)}, f32[8,3072]{1,0:T(8,128)}, f32[8,1536]{1,0:T(8,128)}, f32[8,128]{1,0:T(8,128)}) custom-call(f32[576,1536]{1,0:T(8,128)} %get-tuple-element.179.refs_0_, f32[576,1536]{1,0:T(8,128)} %get-tuple-element.173.refs_1_, f32[576,1536]{1,0:T(8,128)} %get-tuple-element.180.refs_2_, ...), custom_call_target="tpu_custom_call" | custom-call | tf_op jit(solution)/shard_map/pallas_call | solution.py:60
  551.4 36.4 %shard_map.258 = (f32[576,6144]{1,0:T(8,128)}, f32[8,6144]{1,0:T(8,128)}, f32[8,6144]{1,0:T(8,128)}, bf16[3072,1536]{1,0:T(8,128)(2,1)}, bf16[3072,1536]{1,0:T(8,128)(2,1)}, /*index=5*/f32[8,128]{1,0:T(8,128)}) custom-call(s32[1]{0:T(128)} %bitcast.19.refs_0_, bf16[576,1536]{1,0:T(8,128)(2,1)} %get-tuple-element.187.refs_1_, ...), custom_call_target="tpu_custom_call" | custom-call | tf_op jit(solution)/shard_map/pallas_call | solution.py:60
  590.4 6.8 shard_map.259
  603.0 23.2 %shard_map.260 = (f32[8,3072]{1,0:T(8,128)}, f32[576,1536]{1,0:T(8,128)}, bf16[3072,1536]{1,0:T(8,128)(2,1)}, f32[8,128]{1,0:T(8,128)}) custom-call(s32[1]{0:T(128)S(6)} %sub.83.refs_0_, f32[576,6144]{1,0:T(8,128)} %get-tuple-element.190.refs_1_, f32[576,6144]{1,0:T(8,128)} %get-tuple-element.163.refs_0_.refs_2_, f32[576,6144]{1,0:T(8,128)} %get-tuple-element.191.refs_3_, ...), custom_call_target="tpu_custom_call" | custom-call | tf_op jit(solution)/shard_map/pallas_call | solution.py:60
  627.7 4.0 shard_map.261
  636.3 11.4 %shard_map.263 = (bf16[2,2,2,192,640]{4,3,2,1,0:T(8,128)(2,1)}, bf16[2,2,2,192,640]{4,3,2,1,0:T(8,128)(2,1)}, bf16[2,2,2,192,640]{4,3,2,1,0:T(8,128)(2,1)}, bf16...) custom-call(s32[1]{0:T(128)} %bitcast.21.refs_0_, ...), custom_call_target="tpu_custom_call" | custom-call | tf_op jit(solution)/shard_map/pallas_call | solution.py:60
  648.9 3.1 shard_map.264
  658.2 24.7 %shard_map.265 = (f32[8,3072]{1,0:T(8,128)}, f32[576,1536]{1,0:T(8,128)}, bf16[3072,1536]{1,0:T(8,128)(2,1)}, f32[8,128]{1,0:T(8,128)}) custom-call(s32[1]{0:T(128)} %bitcast.19.refs_0_, f32[576,6144]{1,0:T(8,128)} %get-tuple-element.190.refs_1_, f32[576,6144]{1,0:T(8,128)} %get-tuple-element.163.refs_0_.refs_2_, f32[576,6144]{1,0:T(8,128)} %get-tuple-element.191.refs_3_, ...), custom_call_target="tpu_custom_call" | custom-call | tf_op jit(solution)/shard_map/pallas_call | solution.py:60
  682.9 19.6 %shard_map.266 = (f32[576,1536]{1,0:T(8,128)}, f32[16,1536]{1,0:T(8,128)}, f32[8,128]{1,0:T(8,128)}) custom-call(f32[576,1536]{1,0:T(8,128)} %get-tuple-element.223.refs_0_, f32[576,1536]{1,0:T(8,128)} %get-tuple-element.224.refs_1_, f32[576,128]{1,0:T(8,128)} %get-tuple-element.225.refs_2_, f32[576,1536]{1,0:T(8,128)} %bitcast.91, ...), custom_call_target="tpu_custom_call" | custom-call | tf_op jit(solution)/shard_map/pallas_call | solution.py:60
  703.1 7.8 shard_map.267
  711.8 2.4 shard_map.271
  715.1 5.5 shard_map.272
  739.1 6.3 collective-permute-done.24.refs_6_
  745.4 5.6 collective-permute-done.22.refs_2_
  751.4 3.4 shard_map.275
  759.5 11.8 %shard_map.276 = (bf16[2,2,2,192,640]{4,3,2,1,0:T(8,128)(2,1)}, bf16[2,2,2,192,640]{4,3,2,1,0:T(8,128)(2,1)}, bf16[2,2,2,192,640]{4,3,2,1,0:T(8,128)(2,1)}, bf16...) custom-call(s32[1]{0:T(128)} %bitcast.21.refs_0_, ...), custom_call_target="tpu_custom_call" | custom-call | tf_op jit(solution)/shard_map/pallas_call | solution.py:60
  772.3 2.9 shard_map.277
  781.7 27.1 %collective-permute-done.32.refs_1_ = bf16[1,192,1536]{2,1,0:T(8,128)(2,1)S(1)} collective-permute-done((bf16[1,192,1536]{2,1,0:T(8,128)(2,1)}, bf16[1,192,1536]{2,1,0:T(8,128)(2,1)S(1)}, u32[]{:S(2)}, u32[]{:S(2)}) %collective-permute-start.32) | collective-permute-done | bytes 589856 | tf_op jit(solution)/shard_map/ppermute | solution.py:31
  809.6 2.4 shard_map.282
  813.6 4.5 collective-permute-done.29.refs_4_
  819.3 6.1 shard_map.283
  829.3 8.4 collective-permute-done.36.refs_8_
  837.8 8.4 collective-permute-done.33.refs_2_
  848.2 3.7 shard_map.284
  855.2 4.6 collective-permute-done.40.refs_8_
  862.5 3.0 shard_map.285
  868.4 2.8 fusion.2
  871.4 2.2 copy.116
  873.5 6.0 collective-permute-done.42.refs_3_
  879.5 11.4 %collective-permute-done.41.refs_1_ = bf16[1,192,1536]{2,1,0:T(8,128)(2,1)} collective-permute-done((bf16[1,192,1536]{2,1,0:T(8,128)(2,1)}, bf16[1,192,1536]{2,1,0:T(8,128)(2,1)}, u32[]{:S(2)}, u32[]{:S(2)}) %collective-permute-start.41) | collective-permute-done | bytes 589856 | tf_op jit(solution)/shard_map/ppermute | solution.py:31
  890.9 2.4 shard_map.286
  (348 shorter events, 114.3 us)
Async XLA Ops:
  7.2 248.3 %all-gather.3.cloned.1.call-start = ((), (), s32[]{:S(2)}) async-start(), calls=%async_computation | async-start | bytes 43794432 | tf_op jit(solution)/shard_map/all_gather | solution.py:1068
  14.9 366.9 %all-gather.5.cloned.1.call-start = ((), (), s32[]{:S(2)}) async-start(), calls=%async_computation.1 | async-start | bytes 19464192 | tf_op jit(solution)/shard_map/all_gather | solution.py:1068
  262.8 53.2 %copy-start.52 = (bf16[4,64]{1,0:T(4,128)(2,1)}, bf16[4,64]{1,0:T(4,128)(2,1)S(1)}, u32[]{:S(2)}) copy-start(bf16[4,64]{1,0:T(4,128)(2,1)S(1)} %convert_bitcast_fusion.1) | copy-start | bytes 1540
  318.4 29.2 %copy-start.3 = (bf16[32,40,1536]{2,1,0:T(8,128)(2,1)S(1)}, bf16[32,40,1536]{2,1,0:T(8,128)(2,1)}, u32[]{:S(2)}) copy-start(bf16[32,40,1536]{2,1,0:T(8,128)(2,1)} %slice.127) | copy-start | bytes 11796484
  318.4 29.2 %copy-start.21 = (bf16[308,1280]{1,0:T(8,128)(2,1)S(1)}, bf16[308,1280]{1,0:T(8,128)(2,1)}, u32[]{:S(2)}) copy-start(bf16[308,1280]{1,0:T(8,128)(2,1)} %convert_element_type.158) | copy-start | bytes 2365444
  486.3 26.0 %collective-permute-start = (bf16[3072,1536]{1,0:T(8,128)(2,1)}, bf16[3072,1536]{1,0:T(8,128)(2,1)}, u32[]{:S(2)}, u32[]{:S(2)}) collective-permute-start(bf16[3072,1536]{1,0:T(8,128)(2,1)} %get-tuple-element.181), channel_id=1, source_target_pairs={{0,16},{16,0},{1,17},{17,1},{2,18},{18,2},{3,19},{19,3},{4,20},{20... | collective-permute-start | bytes 28311560 | tf_op jit(solution)/shard_map/ppermute | solution.py:31
  512.1 16.7 %collective-permute-start.1 = (bf16[16,40,1536]{2,1,0:T(8,128)(2,1)}, bf16[16,40,1536]{2,1,0:T(8,128)(2,1)S(1)}, u32[]{:S(2)}, u32[]{:S(2)}) collective-permute-start(bf16[16,40,1536]{2,1,0:T(8,128)(2,1)} %get-tuple-element.384), channel_id=1, source_target_pairs={{0,16},{16,0},{1,17},{17,1},{2,18},{18,2},{3,19},{19,3},{4,20},{20... | collective-permute-start | bytes 5898248 | tf_op jit(solution)/shard_map/ppermute | solution.py:31
  535.7 52.2 %collective-permute-start.2 = (bf16[2,2,2,192,640]{4,3,2,1,0:T(8,128)(2,1)}, bf16[2,2,2,192,640]{4,3,2,1,0:T(8,128)(2,1)S(1)}, u32[]{:S(2)}, u32[]{:S(2)}) collective-permute-start(bf16[2,2,2,192,640]{4,3,2,1,0:T(8,128)(2,1)} %get-tuple-element.193), channel_id=1, source_target_pairs={{0,1},{1,0},{2,3},{3,2},{4,5},{5,4},{6,7},{7,6},{8,9},{9,8},{10,11... | collective-permute-start | bytes 5898248 | tf_op jit(solution)/shard_map/ppermute | solution.py:31
  537.1 50.8 %collective-permute-start.3 = (bf16[2,2,2,192,640]{4,3,2,1,0:T(8,128)(2,1)}, bf16[2,2,2,192,640]{4,3,2,1,0:T(8,128)(2,1)S(1)}, u32[]{:S(2)}, u32[]{:S(2)}) collective-permute-start(bf16[2,2,2,192,640]{4,3,2,1,0:T(8,128)(2,1)} %get-tuple-element.194), channel_id=1, source_target_pairs={{0,2},{1,3},{2,0},{3,1},{4,6},{5,7},{6,4},{7,5},{8,10},{9,11},{10,... | collective-permute-start | bytes 5898248 | tf_op jit(solution)/shard_map/ppermute | solution.py:31
  537.7 50.1 %collective-permute-start.5 = (bf16[2,2,2,40,1536]{4,3,2,1,0:T(8,128)(2,1)}, bf16[2,2,2,40,1536]{4,3,2,1,0:T(8,128)(2,1)S(1)}, u32[]{:S(2)}, u32[]{:S(2)}) collective-permute-start(bf16[2,2,2,40,1536]{4,3,2,1,0:T(8,128)(2,1)} %get-tuple-element.197), channel_id=1, source_target_pairs={{0,4},{1,5},{2,6},{3,7},{4,0},{5,1},{6,2},{7,3},{8,12},{9,13},{10,... | collective-permute-start | bytes 2949128 | tf_op jit(solution)/shard_map/ppermute | solution.py:31
  537.9 49.9 %collective-permute-start.4 = (bf16[2,2,2,192,256]{4,3,2,1,0:T(8,128)(2,1)}, bf16[2,2,2,192,256]{4,3,2,1,0:T(8,128)(2,1)S(1)}, u32[]{:S(2)}, u32[]{:S(2)}) collective-permute-start(bf16[2,2,2,192,256]{4,3,2,1,0:T(8,128)(2,1)} %get-tuple-element.195), channel_id=1, source_target_pairs={{0,4},{1,5},{2,6},{3,7},{4,0},{5,1},{6,2},{7,3},{8,12},{9,13},{10,... | collective-permute-start | bytes 2359304 | tf_op jit(solution)/shard_map/ppermute | solution.py:31
  597.2 39.1 %collective-permute-start.14 = (bf16[3072,1536]{1,0:T(8,128)(2,1)}, bf16[3072,1536]{1,0:T(8,128)(2,1)}, u32[]{:S(2)}, u32[]{:S(2)}) collective-permute-start(bf16[3072,1536]{1,0:T(8,128)(2,1)} %shard_map.262), channel_id=1, source_target_pairs={{0,16},{16,0},{1,17},{17,1},{2,18},{18,2},{3,19},{19,3},{4,20},{20... | collective-permute-start | bytes 28311560 | tf_op jit(solution)/shard_map/ppermute | solution.py:31
  598.5 27.7 %collective-permute-start.8 = (bf16[2,2,192,256]{3,2,1,0:T(8,128)(2,1)}, bf16[2,2,192,256]{3,2,1,0:T(8,128)(2,1)S(1)}, u32[]{:S(2)}, u32[]{:S(2)}) collective-permute-start(bf16[2,2,192,256]{3,2,1,0:T(8,128)(2,1)} %get-tuple-element.206), channel_id=1, source_target_pairs={{0,1},{1,0},{2,3},{3,2},{4,5},{5,4},{6,7},{7,6},{8,9},{9,8},{10,11... | collective-permute-start | bytes 1179656 | tf_op jit(solution)/shard_map/ppermute | solution.py:31
  600.1 26.1 %collective-permute-start.9 = (bf16[2,2,40,1536]{3,2,1,0:T(8,128)(2,1)S(1)}, bf16[2,2,40,1536]{3,2,1,0:T(8,128)(2,1)S(1)}, u32[]{:S(2)}, u32[]{:S(2)}) collective-permute-start(bf16[2,2,40,1536]{3,2,1,0:T(8,128)(2,1)S(1)} %copy-done.60), channel_id=1, source_target_pairs={{0,1},{1,0},{2,3},{3,2},{4,5},{5,4},{6,7},{7,6},{8,9},{9,8},{10,11... | collective-permute-start | bytes 1474568 | tf_op jit(solution)/shard_map/ppermute | solution.py:31
  600.6 25.6 %collective-permute-start.6 = (bf16[2,2,192,640]{3,2,1,0:T(8,128)(2,1)S(1)}, bf16[2,2,192,640]{3,2,1,0:T(8,128)(2,1)S(1)}, u32[]{:S(2)}, u32[]{:S(2)}) collective-permute-start(bf16[2,2,192,640]{3,2,1,0:T(8,128)(2,1)S(1)} %copy-done.59), channel_id=1, source_target_pairs={{0,2},{1,3},{2,0},{3,1},{4,6},{5,7},{6,4},{7,5},{8,10},{9,11},{10,... | collective-permute-start | bytes 2949128 | tf_op jit(solution)/shard_map/ppermute | solution.py:31
  602.1 24.2 %collective-permute-start.7 = (bf16[2,2,192,640]{3,2,1,0:T(8,128)(2,1)S(1)}, bf16[2,2,192,640]{3,2,1,0:T(8,128)(2,1)S(1)}, u32[]{:S(2)}, u32[]{:S(2)}) collective-permute-start(bf16[2,2,192,640]{3,2,1,0:T(8,128)(2,1)S(1)} %copy-done.58), channel_id=1, source_target_pairs={{0,4},{1,5},{2,6},{3,7},{4,0},{5,1},{6,2},{7,3},{8,12},{9,13},{10,... | collective-permute-start | bytes 2949128 | tf_op jit(solution)/shard_map/ppermute | solution.py:31
  631.8 16.0 %collective-permute-start.10 = (bf16[2,192,640]{2,1,0:T(8,128)(2,1)}, bf16[2,192,640]{2,1,0:T(8,128)(2,1)S(1)}, u32[]{:S(2)}, u32[]{:S(2)}) collective-permute-start(bf16[2,192,640]{2,1,0:T(8,128)(2,1)} %get-tuple-element.211), channel_id=1, source_target_pairs={{0,4},{1,5},{2,6},{3,7},{4,0},{5,1},{6,2},{7,3},{8,12},{9,13},{10,... | collective-permute-start | bytes 1474568 | tf_op jit(solution)/shard_map/ppermute | solution.py:31
  633.7 14.1 %collective-permute-start.11 = (bf16[2,192,640]{2,1,0:T(8,128)(2,1)}, bf16[2,192,640]{2,1,0:T(8,128)(2,1)S(1)}, u32[]{:S(2)}, u32[]{:S(2)}) collective-permute-start(bf16[2,192,640]{2,1,0:T(8,128)(2,1)} %get-tuple-element.213), channel_id=1, source_target_pairs={{0,1},{1,0},{2,3},{3,2},{4,5},{5,4},{6,7},{7,6},{8,9},{9,8},{10,11... | collective-permute-start | bytes 1474568 | tf_op jit(solution)/shard_map/ppermute | solution.py:31
  634.3 13.5 %collective-permute-start.13 = (bf16[2,40,1536]{2,1,0:T(8,128)(2,1)}, bf16[2,40,1536]{2,1,0:T(8,128)(2,1)S(1)}, u32[]{:S(2)}, u32[]{:S(2)}) collective-permute-start(bf16[2,40,1536]{2,1,0:T(8,128)(2,1)} %get-tuple-element.217), channel_id=1, source_target_pairs={{0,2},{1,3},{2,0},{3,1},{4,6},{5,7},{6,4},{7,5},{8,10},{9,11},{10,... | collective-permute-start | bytes 737288 | tf_op jit(solution)/shard_map/ppermute | solution.py:31
  635.8 12.0 %collective-permute-start.12 = (bf16[2,192,256]{2,1,0:T(8,128)(2,1)}, bf16[2,192,256]{2,1,0:T(8,128)(2,1)S(1)}, u32[]{:S(2)}, u32[]{:S(2)}) collective-permute-start(bf16[2,192,256]{2,1,0:T(8,128)(2,1)} %get-tuple-element.215), channel_id=1, source_target_pairs={{0,2},{1,3},{2,0},{3,1},{4,6},{5,7},{6,4},{7,5},{8,10},{9,11},{10,... | collective-permute-start | bytes 589832 | tf_op jit(solution)/shard_map/ppermute | solution.py:31
  652.0 62.2 %collective-permute-start.15 = (bf16[2,2,2,192,640]{4,3,2,1,0:T(8,128)(2,1)}, bf16[2,2,2,192,640]{4,3,2,1,0:T(8,128)(2,1)}, u32[]{:S(2)}, u32[]{:S(2)}) collective-permute-start(bf16[2,2,2,192,640]{4,3,2,1,0:T(8,128)(2,1)} %shard_map.268), channel_id=1, source_target_pairs={{0,1},{1,0},{2,3},{3,2},{4,5},{5,4},{6,7},{7,6},{8,9},{9,8},{10,11... | collective-permute-start | bytes 5898248 | tf_op jit(solution)/shard_map/ppermute | solution.py:31
  653.5 60.7 %collective-permute-start.16 = (bf16[2,2,2,192,640]{4,3,2,1,0:T(8,128)(2,1)S(1)}, bf16[2,2,2,192,640]{4,3,2,1,0:T(8,128)(2,1)}, u32[]{:S(2)}, u32[]{:S(2)}) collective-permute-start(bf16[2,2,2,192,640]{4,3,2,1,0:T(8,128)(2,1)S(1)} %copy-done.7), channel_id=1, source_target_pairs={{0,2},{1,3},{2,0},{3,1},{4,6},{5,7},{6,4},{7,5},{8,10},{9,11},{10,... | collective-permute-start | bytes 5898248 | tf_op jit(solution)/shard_map/ppermute | solution.py:31
  655.0 59.2 %collective-permute-start.17 = (bf16[2,2,2,192,256]{4,3,2,1,0:T(8,128)(2,1)}, bf16[2,2,2,192,256]{4,3,2,1,0:T(8,128)(2,1)S(1)}, u32[]{:S(2)}, u32[]{:S(2)}) collective-permute-start(bf16[2,2,2,192,256]{4,3,2,1,0:T(8,128)(2,1)} %shard_map.270), channel_id=1, source_target_pairs={{0,4},{1,5},{2,6},{3,7},{4,0},{5,1},{6,2},{7,3},{8,12},{9,13},{10,... | collective-permute-start | bytes 2359304 | tf_op jit(solution)/shard_map/ppermute | solution.py:31
  655.2 55.7 %collective-permute-start.18 = (bf16[1,192,1536]{2,1,0:T(8,128)(2,1)}, bf16[1,192,1536]{2,1,0:T(8,128)(2,1)S(1)}, u32[]{:S(2)}, u32[]{:S(2)}) collective-permute-start(bf16[1,192,1536]{2,1,0:T(8,128)(2,1)} %get-tuple-element.242), channel_id=1, source_target_pairs={{0,8},{1,9},{2,10},{3,11},{4,12},{5,13},{6,14},{7,15},{8,0},{9,1},... | collective-permute-start | bytes 1769480 | tf_op jit(solution)/shard_map/ppermute | solution.py:31
  657.0 53.9 %collective-permute-start.19 = (bf16[1,40,1536]{2,1,0:T(8,128)(2,1)}, bf16[1,40,1536]{2,1,0:T(8,128)(2,1)S(1)}, u32[]{:S(2)}, u32[]{:S(2)}) collective-permute-start(bf16[1,40,1536]{2,1,0:T(8,128)(2,1)} %get-tuple-element.244), channel_id=1, source_target_pairs={{0,8},{1,9},{2,10},{3,11},{4,12},{5,13},{6,14},{7,15},{8,0},{9,1},... | collective-permute-start | bytes 368648 | tf_op jit(solution)/shard_map/ppermute | solution.py:31
  722.2 36.5 %collective-permute-start.20 = (bf16[3072,1536]{1,0:T(8,128)(2,1)}, bf16[3072,1536]{1,0:T(8,128)(2,1)}, u32[]{:S(2)}, u32[]{:S(2)}) collective-permute-start(bf16[3072,1536]{1,0:T(8,128)(2,1)} %shard_map.274), channel_id=1, source_target_pairs={{0,16},{16,0},{1,17},{17,1},{2,18},{18,2},{3,19},{19,3},{4,20},{20... | collective-permute-start | bytes 28311560 | tf_op jit(solution)/shard_map/ppermute | solution.py:31
  727.2 23.8 %collective-permute-start.22 = (bf16[2,2,192,640]{3,2,1,0:T(8,128)(2,1)}, bf16[2,2,192,640]{3,2,1,0:T(8,128)(2,1)}, u32[]{:S(2)}, u32[]{:S(2)}) collective-permute-start(bf16[2,2,192,640]{3,2,1,0:T(8,128)(2,1)} %get-tuple-element.255), channel_id=1, source_target_pairs={{0,2},{1,3},{2,0},{3,1},{4,6},{5,7},{6,4},{7,5},{8,10},{9,11},{10,... | collective-permute-start | bytes 2949128 | tf_op jit(solution)/shard_map/ppermute | solution.py:31
  727.8 23.6 %collective-permute-start.23 = (bf16[2,2,192,640]{3,2,1,0:T(8,128)(2,1)}, bf16[2,2,192,640]{3,2,1,0:T(8,128)(2,1)}, u32[]{:S(2)}, u32[]{:S(2)}) collective-permute-start(bf16[2,2,192,640]{3,2,1,0:T(8,128)(2,1)} %get-tuple-element.257), channel_id=1, source_target_pairs={{0,4},{1,5},{2,6},{3,7},{4,0},{5,1},{6,2},{7,3},{8,12},{9,13},{10,... | collective-permute-start | bytes 2949128 | tf_op jit(solution)/shard_map/ppermute | solution.py:31
  735.1 10.3 %collective-permute-start.24 = (bf16[2,2,192,256]{3,2,1,0:T(8,128)(2,1)S(1)}, bf16[2,2,192,256]{3,2,1,0:T(8,128)(2,1)S(1)}, u32[]{:S(2)}, u32[]{:S(2)}) collective-permute-start(bf16[2,2,192,256]{3,2,1,0:T(8,128)(2,1)S(1)} %copy-done.61), channel_id=1, source_target_pairs={{0,1},{1,0},{2,3},{3,2},{4,5},{5,4},{6,7},{7,6},{8,9},{9,8},{10,11... | collective-permute-start | bytes 1179656 | tf_op jit(solution)/shard_map/ppermute | solution.py:31
  739.1 19.6 %collective-permute-start.21 = (f32[16,64,128]{2,1,0:T(8,128)S(1)}, f32[16,64,128]{2,1,0:T(8,128)S(1)}, u32[]{:S(2)}, u32[]{:S(2)}) collective-permute-start(f32[16,64,128]{2,1,0:T(8,128)S(1)} %get-tuple-element.386), channel_id=1, source_target_pairs={{0,16},{16,0},{1,17},{17,1},{2,18},{18,2},{3,19},{19,3},{4,20},{20... | collective-permute-start | bytes 1572872 | tf_op jit(solution)/shard_map/ppermute | solution.py:31
  754.8 16.5 %collective-permute-start.25 = (bf16[2,192,640]{2,1,0:T(8,128)(2,1)}, bf16[2,192,640]{2,1,0:T(8,128)(2,1)S(1)}, u32[]{:S(2)}, u32[]{:S(2)}) collective-permute-start(bf16[2,192,640]{2,1,0:T(8,128)(2,1)} %get-tuple-element.264), channel_id=1, source_target_pairs={{0,4},{1,5},{2,6},{3,7},{4,0},{5,1},{6,2},{7,3},{8,12},{9,13},{10,... | collective-permute-start | bytes 1474568 | tf_op jit(solution)/shard_map/ppermute | solution.py:31
  756.6 14.7 %collective-permute-start.26 = (bf16[2,192,640]{2,1,0:T(8,128)(2,1)}, bf16[2,192,640]{2,1,0:T(8,128)(2,1)S(1)}, u32[]{:S(2)}, u32[]{:S(2)}) collective-permute-start(bf16[2,192,640]{2,1,0:T(8,128)(2,1)} %get-tuple-element.266), channel_id=1, source_target_pairs={{0,1},{1,0},{2,3},{3,2},{4,5},{5,4},{6,7},{7,6},{8,9},{9,8},{10,11... | collective-permute-start | bytes 1474568 | tf_op jit(solution)/shard_map/ppermute | solution.py:31
  758.1 13.2 %collective-permute-start.27 = (bf16[2,192,256]{2,1,0:T(8,128)(2,1)}, bf16[2,192,256]{2,1,0:T(8,128)(2,1)S(1)}, u32[]{:S(2)}, u32[]{:S(2)}) collective-permute-start(bf16[2,192,256]{2,1,0:T(8,128)(2,1)} %get-tuple-element.268), channel_id=1, source_target_pairs={{0,2},{1,3},{2,0},{3,1},{4,6},{5,7},{6,4},{7,5},{8,10},{9,11},{10,... | collective-permute-start | bytes 589832 | tf_op jit(solution)/shard_map/ppermute | solution.py:31
  775.2 42.8 %collective-permute-start.29 = (bf16[2,2,2,192,640]{4,3,2,1,0:T(8,128)(2,1)}, bf16[2,2,2,192,640]{4,3,2,1,0:T(8,128)(2,1)}, u32[]{:S(2)}, u32[]{:S(2)}) collective-permute-start(bf16[2,2,2,192,640]{4,3,2,1,0:T(8,128)(2,1)} %shard_map.279), channel_id=1, source_target_pairs={{0,2},{1,3},{2,0},{3,1},{4,6},{5,7},{6,4},{7,5},{8,10},{9,11},{10,... | collective-permute-start | bytes 5898248 | tf_op jit(solution)/shard_map/ppermute | solution.py:31
  776.7 42.6 %collective-permute-start.28 = (bf16[2,2,2,192,640]{4,3,2,1,0:T(8,128)(2,1)S(1)}, bf16[2,2,2,192,640]{4,3,2,1,0:T(8,128)(2,1)}, u32[]{:S(2)}, u32[]{:S(2)}) collective-permute-start(bf16[2,2,2,192,640]{4,3,2,1,0:T(8,128)(2,1)S(1)} %copy-done.8), channel_id=1, source_target_pairs={{0,1},{1,0},{2,3},{3,2},{4,5},{5,4},{6,7},{7,6},{8,9},{9,8},{10,11... | collective-permute-start | bytes 5898248 | tf_op jit(solution)/shard_map/ppermute | solution.py:31
  778.2 35.4 %collective-permute-start.30 = (bf16[2,2,2,192,256]{4,3,2,1,0:T(8,128)(2,1)}, bf16[2,2,2,192,256]{4,3,2,1,0:T(8,128)(2,1)S(1)}, u32[]{:S(2)}, u32[]{:S(2)}) collective-permute-start(bf16[2,2,2,192,256]{4,3,2,1,0:T(8,128)(2,1)} %shard_map.280), channel_id=1, source_target_pairs={{0,4},{1,5},{2,6},{3,7},{4,0},{5,1},{6,2},{7,3},{8,12},{9,13},{10,... | collective-permute-start | bytes 2359304 | tf_op jit(solution)/shard_map/ppermute | solution.py:31
  778.5 30.3 %collective-permute-start.32 = (bf16[1,192,1536]{2,1,0:T(8,128)(2,1)}, bf16[1,192,1536]{2,1,0:T(8,128)(2,1)S(1)}, u32[]{:S(2)}, u32[]{:S(2)}) collective-permute-start(bf16[1,192,1536]{2,1,0:T(8,128)(2,1)} %get-tuple-element.278), channel_id=1, source_target_pairs={{0,8},{1,9},{2,10},{3,11},{4,12},{5,13},{6,14},{7,15},{8,0},{9,1},... | collective-permute-start | bytes 1769480 | tf_op jit(solution)/shard_map/ppermute | solution.py:31
  780.2 33.4 %collective-permute-start.31 = (f32[2,2,2,64,128]{4,3,2,1,0:T(8,128)}, f32[2,2,2,64,128]{4,3,2,1,0:T(8,128)S(1)}, u32[]{:S(2)}, u32[]{:S(2)}) collective-permute-start(f32[2,2,2,64,128]{4,3,2,1,0:T(8,128)} %shard_map.281), channel_id=1, source_target_pairs={{0,4},{1,5},{2,6},{3,7},{4,0},{5,1},{6,2},{7,3},{8,12},{9,13},{10,... | collective-permute-start | bytes 786440 | tf_op jit(solution)/shard_map/ppermute | solution.py:31
  825.4 20.7 %collective-permute-start.33 = (bf16[2,2,192,640]{3,2,1,0:T(8,128)(2,1)}, bf16[2,2,192,640]{3,2,1,0:T(8,128)(2,1)S(1)}, u32[]{:S(2)}, u32[]{:S(2)}) collective-permute-start(bf16[2,2,192,640]{3,2,1,0:T(8,128)(2,1)} %get-tuple-element.281), channel_id=1, source_target_pairs={{0,2},{1,3},{2,0},{3,1},{4,6},{5,7},{6,4},{7,5},{8,10},{9,11},{10,... | collective-permute-start | bytes 2949128 | tf_op jit(solution)/shard_map/ppermute | solution.py:31
  826.8 20.4 %collective-permute-start.34 = (bf16[2,2,192,640]{3,2,1,0:T(8,128)(2,1)}, bf16[2,2,192,640]{3,2,1,0:T(8,128)(2,1)S(1)}, u32[]{:S(2)}, u32[]{:S(2)}) collective-permute-start(bf16[2,2,192,640]{3,2,1,0:T(8,128)(2,1)} %get-tuple-element.283), channel_id=1, source_target_pairs={{0,4},{1,5},{2,6},{3,7},{4,0},{5,1},{6,2},{7,3},{8,12},{9,13},{10,... | collective-permute-start | bytes 2949128 | tf_op jit(solution)/shard_map/ppermute | solution.py:31
  827.3 10.5 %collective-permute-start.35 = (bf16[2,2,192,256]{3,2,1,0:T(8,128)(2,1)}, bf16[2,2,192,256]{3,2,1,0:T(8,128)(2,1)S(1)}, u32[]{:S(2)}, u32[]{:S(2)}) collective-permute-start(bf16[2,2,192,256]{3,2,1,0:T(8,128)(2,1)} %get-tuple-element.285), channel_id=1, source_target_pairs={{0,1},{1,0},{2,3},{3,2},{4,5},{5,4},{6,7},{7,6},{8,9},{9,8},{10,11... | collective-permute-start | bytes 1179656 | tf_op jit(solution)/shard_map/ppermute | solution.py:31
  827.9 9.9 %collective-permute-start.36 = (f32[2,2,64,128]{3,2,1,0:T(8,128)}, f32[2,2,64,128]{3,2,1,0:T(8,128)S(1)}, u32[]{:S(2)}, u32[]{:S(2)}) collective-permute-start(f32[2,2,64,128]{3,2,1,0:T(8,128)} %get-tuple-element.287), channel_id=1, source_target_pairs={{0,1},{1,0},{2,3},{3,2},{4,5},{5,4},{6,7},{7,6},{8,9},{9,8},{10,11... | collective-permute-start | bytes 393224 | tf_op jit(solution)/shard_map/ppermute | solution.py:31
  851.9 9.1 %collective-permute-start.37 = (bf16[2,192,640]{2,1,0:T(8,128)(2,1)}, bf16[2,192,640]{2,1,0:T(8,128)(2,1)S(1)}, u32[]{:S(2)}, u32[]{:S(2)}) collective-permute-start(bf16[2,192,640]{2,1,0:T(8,128)(2,1)} %get-tuple-element.290), channel_id=1, source_target_pairs={{0,4},{1,5},{2,6},{3,7},{4,0},{5,1},{6,2},{7,3},{8,12},{9,13},{10,... | collective-permute-start | bytes 1474568 | tf_op jit(solution)/shard_map/ppermute | solution.py:31
  852.6 9.0 collective-permute-start.38
  853.2 6.6 collective-permute-start.39
  854.6 5.2 collective-permute-start.40
  865.4 14.1 %collective-permute-start.42 = (f32[1,64,128]{2,1,0:T(8,128)}, f32[1,64,128]{2,1,0:T(8,128)S(1)}, u32[]{:S(2)}, u32[]{:S(2)}) collective-permute-start(f32[1,64,128]{2,1,0:T(8,128)} %get-tuple-element.301), channel_id=1, source_target_pairs={{0,8},{1,9},{2,10},{3,11},{4,12},{5,13},{6,14},{7,15},{8,0},{9,1},... | collective-permute-start | bytes 98312 | tf_op jit(solution)/shard_map/ppermute | solution.py:31
  866.8 24.1 %collective-permute-start.41 = (bf16[1,192,1536]{2,1,0:T(8,128)(2,1)}, bf16[1,192,1536]{2,1,0:T(8,128)(2,1)}, u32[]{:S(2)}, u32[]{:S(2)}) collective-permute-start(bf16[1,192,1536]{2,1,0:T(8,128)(2,1)} %get-tuple-element.299), channel_id=1, source_target_pairs={{0,8},{1,9},{2,10},{3,11},{4,12},{5,13},{6,14},{7,15},{8,0},{9,1},... | collective-permute-start | bytes 1769480 | tf_op jit(solution)/shard_map/ppermute | solution.py:31
  (59 other events, 203.5 us)
Sparse Core Ops, SparseCore 0:
  15.0 240.4 all-gather.2
  259.0 122.8 all-gather.4

commit v4 on v3

--- a/solution.py
+++ b/solution.py
@@ -76,6 +76,164 @@
 
 def whole_array(shape):
     return pl.BlockSpec(shape, lambda *_: (0,) * len(shape))
+
+
+class Gather:
+    def __init__(self, chain, shards, orders, inner, outer):
+        self.chain, self.inner, self.outer = chain, inner, outer
+        self.counts = [len(some) for some in orders]
+        self.orders = [order[::-1] for some in orders for order in some]
+        first = self.orders[0][0]
+        self.held, self.came = [], []
+        for shard, some in zip(shards, orders):
+            came = swap(shard[None], "fsdp", outer, first)
+            for start, size in column_pieces(shard.shape[1], len(some)):
+                self.held.append((shard[None], start // size, size))
+                self.came.append((came, start // size, size))
+        self.offsets = [[0] for _ in self.orders]
+        self.number = 0
+
+    def step(self):
+        held = join(self.chain, self.held, self.came)
+        self.advance()
+        self.held = [(v, 0, v.shape[2]) for v in held]
+        self.came = []
+        for v, order in zip(held, self.orders):
+            came = swap(v, "fsdp", self.outer, order[self.number])
+            self.came.append((came, 0, v.shape[2]))
+
+    def advance(self):
+        for index, order in enumerate(self.orders):
+            bit = 1 << order[self.number]
+            self.offsets[index] = self.offsets[index] + [o ^ bit for o in self.offsets[index]]
+        self.number += 1
+
+    def finish(self, after=()):
+        half = len(self.offsets[0])
+        self.advance()
+        places = [[offs[:half] for offs in self.offsets], [offs[half:] for offs in self.offsets]]
+        parts = [[v for v, _, _ in self.held], [v for v, _, _ in self.came]]
+        own = place_blocks(self.chain, parts, places, self.counts, self.outer, after)
+        whole = []
+        for v in own:
+            some = [v]
+            for bit in range(bit_count(self.inner)):
+                some = some + [swap(p, "dp", self.inner, bit) for p in some]
+            whole.append(some)
+        return whole
+
+
+def in_order(parts):
+    stacked = jnp.stack(parts)
+    inner = lax.axis_index("dp")
+    return jnp.concatenate(
+        [lax.dynamic_index_in_dim(stacked, inner ^ n, 0, keepdims=False) for n in range(len(parts))], axis=0
+    )
+
+
+def sides(parts):
+    if len(parts) == 2:
+        return parts
+    whole = in_order(parts)
+    half = whole.shape[0] // 2
+    mine = lax.axis_index("dp") // (len(parts) // 2)
+    return [lax.dynamic_slice_in_dim(whole, side * half, half, axis=0) for side in (mine, 1 - mine)]
+
+
+def join_kernel(count, half, *refs):
+    step = pl.program_id(0)
+    for index in range(count):
+
+        @pl.when(step < half)
+        def _(index=index):
+            refs[2 * count + index][...] = refs[index][...]
+
+        @pl.when(step >= half)
+        def _(index=index):
+            refs[2 * count + index][...] = refs[count + index][...]
+
+
+def join(chain, first, second):
+    number = first[0][0].shape[0]
+    each = max(number // 2, 1)
+    half = number // each
+
+    def blocks(rows, width, cut, where):
+        return pl.BlockSpec((each, rows, width), lambda j, *_: (where(j), 0, cut))
+
+    return chain.call(
+        functools.partial(join_kernel, len(first), half),
+        (2 * half,),
+        [blocks(v.shape[1], w, n, lambda j: jnp.minimum(j, half - 1)) for v, n, w in first]
+        + [blocks(v.shape[1], w, n, lambda j: jnp.maximum(j - half, 0)) for v, n, w in second],
+        [
+            ((2 * number, v.shape[1], w), v.dtype, blocks(v.shape[1], w, 0, lambda j: j))
+            for v, n, w in first
+        ],
+        [],
+        *[v for v, _, _ in first],
+        *[v for v, _, _ in second],
+    )
+
+
+def place_blocks(chain, parts, places, counts, blocks, after):
+    count, pieces = len(parts), len(parts[0])
+    where = {}
+    for number, place in enumerate(places):
+        for index, offs in enumerate(place):
+            for k, o in enumerate(offs):
+                where[(index, o)] = (number, k)
+    me = lax.axis_index("fsdp")
+    offsets = [o for place in places for o in place[0]]
+    part_of = [[where[(i, o)][0] for o in offsets] for i in range(pieces)]
+    slot_of = [[where[(i, o)][1] for o in offsets] for i in range(pieces)]
+    goal = jnp.asarray(offsets, jnp.int32) ^ me.astype(jnp.int32)
+    shown = []
+    for i in range(pieces):
+        for p in range(count):
+            now, row = 0, []
+            for step in range(blocks):
+                if part_of[i][step] == p:
+                    now = slot_of[i][step]
+                row.append(now)
+            shown.append(row)
+    operands = [parts[p][i] for i in range(pieces) for p in range(count)]
+    outs, goals, at = [], [], 0
+    for n, some in enumerate(counts):
+        rows = parts[0][at].shape[1]
+        width = sum(v.shape[2] for v in parts[0][at : at + some])
+        goals += [(n, start, size) for start, size in column_pieces(width, some)]
+        outs.append(
+            (
+                (blocks, rows, width),
+                parts[0][at].dtype,
+                pl.BlockSpec((1, rows, width), lambda b, goal, shown, part: (goal[b], 0, 0)),
+            )
+        )
+        at += some
+    return chain.call(
+        functools.partial(place_kernel, count, goals),
+        (blocks,),
+        [
+            pl.BlockSpec((1,) + v.shape[1:], lambda b, goal, shown, part, n=n: (shown[n, b], 0, 0))
+            for n, v in enumerate(operands)
+        ],
+        outs,
+        [],
+        *operands,
+        scalars=(goal, jnp.asarray(shown, jnp.int32), jnp.asarray(part_of, jnp.int32)),
+        after=after,
+    )
+
+
+def place_kernel(count, goals, goal_ref, shown_ref, part_ref, *refs):
+    step = pl.program_id(0)
+    for i, (out, start, width) in enumerate(goals):
+        for p in range(count):
+
+            @pl.when(part_ref[i, step] == p)
+            def _(i=i, out=out, start=start, width=width, source=refs[i * count + p]):
+                refs[len(goals) * count + out][:, :, start : start + width] = source[...]
 
 
 class Weight:
@@ -197,23 +355,6 @@
         for out, side in ((outs.pop(0), 1 - own), (outs.pop(0), own)):
             at = (slice(None),) * before + (side,)
             out[...] = (base[at].astype(jnp.float32) + come[at].astype(jnp.float32)).astype(out.dtype)
-
-
-def round_kernel(values_ref, late_ref, out_ref):
-    out_ref[...] = values_ref[...].astype(jnp.bfloat16)
-
-
-def round_late(chain, values, late):
-    shape = values.shape
-    return chain.call(
-        round_kernel,
-        (1,),
-        [whole_array(values.shape), pl.BlockSpec(memory_space=pl.ANY)],
-        [(shape, jnp.bfloat16, whole_array(shape))],
-        [],
-        values,
-        late,
-    )[0]
 
 
 def copy_kernel(values_ref, out_ref):
@@ -477,19 +618,32 @@
     return center * scale, scale
 
 
-def branch_kernel(act_ref, norms_ref, vecs_ref, member_ref, live_ref, x_ref, bias_ref, pair_ref, *refs):
-    weight_ref, response_ref, res_ref, time_ref, low_ref, total_ref = refs
+def branch_kernel(last, side_ref, act_ref, norms_ref, vecs_ref, member_ref, weight_ref, *refs):
     step = pl.program_id(0)
     member = member_ref[...]
     act = by_group(act_ref[...])
     response = act * (1.0 + vecs_ref[1:2, :][None] * spread(norms_ref[...], member)) + vecs_ref[2:3, :][None]
     response = response.reshape(act_ref.shape).astype(jnp.bfloat16)
+    part = product(response, rows_of(weight_ref), 1, 0)
+    if not last:
+        response_ref, total_ref = refs
+        response_ref[...] = response
+
+        @pl.when(step == 0)
+        def _():
+            total_ref[...] = part
+
+        @pl.when(step > 0)
+        def _():
+            total_ref[...] += part
+
+        return
+    before_ref, live_ref, x_ref, bias_ref, pair_ref, response_ref, res_ref, time_ref, low_ref, total_ref = refs
     response_ref[...] = response
-    part = product(response, rows_of(weight_ref), 1, 0)
 
     @pl.when(step == 0)
     def _():
-        total_ref[...] = part
+        total_ref[...] = before_ref[...] + part
 
     @pl.when(step > 0)
     def _():
@@ -507,39 +661,38 @@
         low_ref[...] = norm_rows(after_time)[0].astype(jnp.bfloat16)
 
 
-def branch_step(chain, act, norms, vecs, weight, member, live, x, bias, pair):
+def side_block(half):
+    return lambda step, side_ref: side_ref[0] * half + step
+
+
+def branch_step(chain, act, norms, vecs, weight, member, side, rest=()):
     slots, units = act.shape
-    width = x.shape[1]
+    width = weight.width
+    steps = units // UNITS
+    whole = ((slots, width), jnp.float32, whole_array((slots, width)))
+    outs = [((slots, units), jnp.bfloat16, unit_columns(slots)), whole]
+    if rest:
+        outs += [whole, ((slots, width), jnp.bfloat16, whole_array((slots, width)))]
     return chain.call(
-        branch_kernel,
-        (units // UNITS,),
+        functools.partial(branch_kernel, len(rest) > 0),
+        (steps,),
         [
             unit_columns(slots),
             unit_columns(SEATS),
             unit_columns(vecs.shape[0]),
             whole_array(member.shape),
-            whole_array(live.shape),
-            whole_array(x.shape),
-            whole_array(bias.shape),
-            whole_array(pair.shape),
+            weight.by(side_block(steps)).spec(),
         ]
-        + [weight.spec()],
-        [
-            ((slots, units), jnp.bfloat16, unit_columns(slots)),
-            ((slots, width), jnp.float32, whole_array((slots, width))),
-            ((slots, width), jnp.float32, whole_array((slots, width))),
-            ((slots, width), jnp.bfloat16, whole_array((slots, width))),
-        ],
-        [pltpu.VMEM((slots, width), jnp.float32)],
+        + [whole_array(v.shape) for v in rest],
+        outs,
+        [pltpu.VMEM((slots, width), jnp.float32)] if rest else [],
         act,
         norms,
         vecs,
         member,
-        live,
-        x,
-        bias,
-        pair,
         weight.gathered,
+        *rest,
+        scalars=(side,),
     )
 
 
@@ -579,73 +732,45 @@
     )
 
 
-def partner_first(half):
-    def block(step, mine_ref):
-        return jnp.where(step < half, 1 - mine_ref[0], mine_ref[0]) * half + step % half
-
-    return block
-
-
-def half_specs(units, width):
-    half = units // UNITS // 2
-    shape = (units // 2, width)
-    return [
-        (shape, jnp.bfloat16, pl.BlockSpec((UNITS, width), lambda i, _: (jnp.minimum(i, half - 1), 0))),
-        (shape, jnp.bfloat16, pl.BlockSpec((UNITS, width), lambda i, _: (jnp.maximum(i - half, 0), 0))),
-    ]
-
-
-def store_half(away_ref, kept_ref, left, right):
-    rows = product(left, right, 0, 0).astype(jnp.bfloat16)
-    half = pl.num_programs(0) // 2
-
-    @pl.when(pl.program_id(0) < half)
-    def _():
-        away_ref[...] = rows
-
-    @pl.when(pl.program_id(0) >= half)
-    def _():
-        kept_ref[...] = rows
-
-
-def response_back_kernel(mine_ref, branch_ref, act_ref, response_ref, member_ref, weight_ref, grad_ref, sums_ref, shift_ref, away_ref, kept_ref):
+def response_back_kernel(side_ref, branch_ref, act_ref, response_ref, member_ref, weight_ref, grad_ref, sums_ref, shift_ref, rows_ref):
     grad = product(branch_ref[...], rows_of(weight_ref), 1, 1)
     grad_ref[...] = grad
     sums_ref[...] = gathered(grad * act_ref[...], member_ref[...])
     shift_ref[...] = jnp.broadcast_to(jnp.sum(grad, axis=0, keepdims=True), shift_ref.shape)
-    store_half(away_ref, kept_ref, response_ref[...], branch_ref[...])
-
-
-def response_back(chain, branch, weight, act, response, member, mine):
+    rows_ref[...] = product(response_ref[...], branch_ref[...], 0, 0).astype(jnp.bfloat16)
+
+
+def response_back(chain, branch, weight, act, response, member, side):
     slots, width = branch.shape
-    units = weight.total
-    block = partner_first(units // UNITS // 2)
-
-    def columns(rows):
-        return pl.BlockSpec((rows, UNITS), lambda *at: (0, block(*at)))
-
+    units = act.shape[1]
+    steps = units // UNITS
     return chain.call(
         response_back_kernel,
-        (units // UNITS,),
-        [whole_array(branch.shape), columns(slots), columns(slots), whole_array(member.shape)]
-        + [weight.by(block).spec()],
+        (steps,),
         [
-            ((slots, units), jnp.float32, columns(slots)),
-            ((SEATS, units), jnp.float32, columns(SEATS)),
-            ((SEATS, units), jnp.float32, columns(SEATS)),
-        ]
-        + half_specs(units, width),
+            whole_array(branch.shape),
+            unit_columns(slots),
+            unit_columns(slots),
+            whole_array(member.shape),
+            weight.by(side_block(steps)).spec(),
+        ],
+        [
+            ((slots, units), jnp.float32, unit_columns(slots)),
+            ((SEATS, units), jnp.float32, unit_columns(SEATS)),
+            ((SEATS, units), jnp.float32, unit_columns(SEATS)),
+            ((units, width), jnp.bfloat16, pl.BlockSpec((UNITS, width), lambda i, *_: (i, 0))),
+        ],
         [],
         branch,
         act,
         response,
         member,
         weight.gathered,
-        scalars=(mine,),
-    )
-
-
-def hidden_back_kernel(added, side_ref, grad_ref, act_ref, slope_ref, vecs_ref, norms_ref, ratio_ref, member_ref, normed_ref, weight_ref, *refs):
+        scalars=(side,),
+    )
+
+
+def hidden_back_kernel(added, grad_ref, act_ref, slope_ref, vecs_ref, norms_ref, ratio_ref, member_ref, normed_ref, weight_ref, *refs):
     bias_ref, normed_grad_ref, rows_ref, total_ref = refs[-4:]
     step = pl.program_id(0)
     member = member_ref[...]
@@ -669,29 +794,21 @@
         normed_grad_ref[...] = total_ref[...]
 
 
-def hidden_back(chain, grad, act, slope, vecs, norms, ratio, member, normed, weight, side, before=None):
+def hidden_back(chain, grad, act, slope, vecs, norms, ratio, member, normed, weight, before=None):
     slots, units = act.shape
     width = weight.width
-    half = units // UNITS // 2
-
-    def block(step, side_ref):
-        return side_ref[0] * half + step
-
-    def columns(rows):
-        return pl.BlockSpec((rows, UNITS), lambda *at: (0, block(*at)))
-
     before = () if before is None else (before,)
     return chain.call(
         functools.partial(hidden_back_kernel, len(before) > 0),
-        (half,),
-        [columns(slots)] * 3
-        + [columns(vecs.shape[0]), columns(SEATS), columns(SEATS)]
-        + [whole_array(member.shape), whole_array(normed.shape), weight.by(block).spec()]
+        (units // UNITS,),
+        [unit_columns(slots)] * 3
+        + [unit_columns(vecs.shape[0]), unit_columns(SEATS), unit_columns(SEATS)]
+        + [whole_array(member.shape), whole_array(normed.shape), weight.spec()]
         + [whole_array(v.shape) for v in before],
         [
-            ((SEATS, units // 2), jnp.float32, unit_columns(SEATS)),
+            ((SEATS, units), jnp.float32, unit_columns(SEATS)),
             ((slots, width), jnp.float32, whole_array((slots, width))),
-            ((units // 2, width), jnp.bfloat16, pl.BlockSpec((UNITS, width), lambda i, *_: (i, 0))),
+            ((units, width), jnp.bfloat16, pl.BlockSpec((UNITS, width), lambda i, *_: (i, 0))),
         ],
         [pltpu.VMEM((slots, width), jnp.float32)],
         grad,
@@ -704,7 +821,6 @@
         normed,
         weight.gathered,
         *before,
-        scalars=(side,),
     )
 
 
@@ -907,40 +1023,33 @@
 
 
 def attention_kernel(q_ref, k_ref, v_ref, g_ref, bias_ref, att_ref, dq_ref, dk_ref, dv_ref):
-    width = q_ref.shape[1]
+    slots, width = q_ref.shape
     half = width // 2
     low = jnp.bfloat16
     lanes = lax.broadcasted_iota(jnp.int32, (1, width), 1)
-    sublanes = lax.broadcasted_iota(jnp.int32, (width, 1), 0)
+    first = lanes < half
     keys, values = k_ref[...], v_ref[...]
-    att_t = dq_t = d_key = d_value = None
-
-    for head in range(2):
-        own = (lanes >= head * half) & (lanes < (head + 1) * half)
-        query = jnp.where(own, q_ref[...], jnp.zeros((), low))
-        grad = jnp.where(own, g_ref[...], jnp.zeros((), low))
-        scores = product(keys, query, 1, 1) + bias_ref[...]
-        exponent = jnp.exp(scores - jnp.max(scores, axis=0, keepdims=True))
-        probs = exponent * (1.0 / jnp.sum(exponent, axis=0, keepdims=True))
-        probs_low = probs.astype(low)
-        att_head = product(values, probs_low, 0, 0)
-        grad_probs = product(values, grad, 1, 1)
-        inner_sum = jnp.sum(probs * grad_probs, axis=0, keepdims=True)
-        grad_scores = (probs * (grad_probs - inner_sum)).astype(low)
-        value_part = product(probs_low, grad, 1, 0)
-        key_part = product(grad_scores, query, 1, 0)
-        dq_head = product(keys, grad_scores, 0, 0)
-        if head == 0:
-            att_t, dq_t, d_key, d_value = att_head, dq_head, key_part, value_part
-        else:
-            upper = sublanes < half
-            att_t = jnp.where(upper, att_t, att_head)
-            dq_t = jnp.where(upper, dq_t, dq_head)
-            d_key, d_value = d_key + key_part, d_value + value_part
-    att_ref[...] = att_t.T.astype(low)
-    dq_ref[...] = (dq_t.T * ((width // 2) ** -0.5)).astype(low)
-    dk_ref[...] = d_key.astype(low)
-    dv_ref[...] = d_value.astype(low)
+
+    def both(ref):
+        rows, none = ref[...], jnp.zeros((), low)
+        return jnp.concatenate([jnp.where(first, rows, none), jnp.where(first, none, rows)], axis=0)
+
+    def beside(turned):
+        rows = turned.T
+        return jnp.where(first, rows[:slots], rows[slots:])
+
+    query, grad = both(q_ref), both(g_ref)
+    scores = product(keys, query, 1, 1) + bias_ref[...]
+    exponent = jnp.exp(scores - jnp.max(scores, axis=0, keepdims=True))
+    probs = exponent * (1.0 / jnp.sum(exponent, axis=0, keepdims=True))
+    probs_low = probs.astype(low)
+    att_ref[...] = beside(product(values, probs_low, 0, 0)).astype(low)
+    grad_probs = product(values, grad, 1, 1)
+    inner_sum = jnp.sum(probs * grad_probs, axis=0, keepdims=True)
+    grad_scores = (probs * (grad_probs - inner_sum)).astype(low)
+    dv_ref[...] = product(probs_low, grad, 1, 0).astype(low)
+    dk_ref[...] = product(grad_scores, query, 1, 0).astype(low)
+    dq_ref[...] = (beside(product(keys, grad_scores, 0, 0)) * HEAD_SCALE).astype(low)
 
 
 def attention(chain, mixed, grad, bias):
@@ -1057,25 +1166,27 @@
 
     small_owned = (res_vecs, ff_vecs, time_w, time_b[None], attn_vecs)
     small_sizes = [v.size for v in small_owned]
-    small_pad = -sum(small_sizes) % (8 * width)
+    small_pad = -sum(small_sizes) % (16 * 128)
     small_shard = jnp.concatenate(
         [v.astype(low).reshape(-1) for v in small_owned] + [jnp.zeros((small_pad,), low)]
     )
-
-    def to_all(*shards):
-        shard = jnp.concatenate([v.astype(low) for v in shards], axis=0)
+    rows, kv_rows = fc2_w.shape[0], kv_w.shape[0]
+    def to_all(shard):
         shard = jnp.pad(shard, ((0, -shard.shape[0] % 8), (0, 0)))
-        full_rows = lax.all_gather(shard, ("dp", "fsdp"), axis=0, tiled=True)
-        return full_rows.reshape(blocks, -1, width)
-
-    rows, kv_rows = fc2_w.shape[0], kv_w.shape[0]
-    small_rows = small_shard.size // width
-    res_weights = to_all(fc1_w.T, fc2_w, kv_w, small_shard.reshape(-1, width))
-    attn_weights = to_all(round_late(chain, attn_w.T, res_weights))
-    fc1_t, fc2_full = Weight(res_weights, 0, rows), Weight(res_weights, 1, rows)
-    attn_t = Weight(attn_weights, 0, rows)
-    kv_full = res_weights[:, 2 * rows : 2 * rows + kv_rows].reshape(-1, width)
-    small_all = res_weights[:, 2 * rows + kv_rows : 2 * rows + kv_rows + small_rows].reshape(blocks, -1)
+        return lax.all_gather(late(chain, shard), ("dp", "fsdp"), axis=0, tiled=True).reshape(blocks, -1, width)
+
+    first = Gather(
+        chain, [fc1_w.T.astype(low), small_shard.reshape(-1, 128)], [orders, orders[2:]], inner, outer
+    )
+    first.step()
+    first.step()
+    second_all = to_all(jnp.concatenate([fc2_w.astype(low), kv_w.astype(low)], axis=0))
+    for _ in range(outer_bits - 3):
+        first.step()
+    fc1_parts, small_all = first.finish()
+    attn_all = to_all(attn_w.T.astype(low))
+    fc1_t = [Weight(part, 0, rows) for part in sides(fc1_parts)]
+    small_all = in_order(small_all).reshape(blocks, -1)
     small_full = []
     taken = 0
     for owned, size in zip(small_owned, small_sizes):
@@ -1084,23 +1195,42 @@
         taken += size
     res_all, ff_all, time_w_all, time_b_all, vecs_all = small_full
     taps = jnp.pad(res_all[:10], ((0, 6), (0, 0)))
-    vecs = jnp.pad(ff_all, ((0, 5), (0, 0)))
+    mine_index = mine.astype(jnp.int32)[None]
+    side_index = [mine_index, 1 - mine_index]
+
+    def halves(values):
+        half = values.shape[1] // 2
+        return [lax.dynamic_slice_in_dim(values, side * half, half, axis=1) for side in (mine, 1 - mine)]
+
+    def ordered(own, other):
+        return jnp.where(
+            mine == 0, jnp.concatenate([own, other], axis=1), jnp.concatenate([other, own], axis=1)
+        )
+
+    vecs = halves(jnp.pad(ff_all, ((0, 5), (0, 0))))
 
     segment, member_slots, geometry = geometry_table(heights[0], widths[0])
     member = jnp.pad(member_slots[::GROUP].astype(full), ((0, 0), (0, SEATS - LAT_ROW)))
     bias = score_bias(segment, text_counts[0], key_pad)
+    bias = jnp.concatenate([bias, bias], axis=1)
     live = geometry
 
     normed_low, normed, entry_scale = entry(chain, x, taps, geometry)
-    act, slope, power = hidden_step(chain, normed_low, fc1_t, vecs, member)
-    units = act.shape[1]
-    norm = jnp.sqrt(power + NORM_EPS)
-    norm_mean = jnp.mean(norm, axis=1, keepdims=True) + NORM_EPS
-    norms = norm / norm_mean
+    hidden = [hidden_step(chain, normed_low, fc1_t[n], vecs[n], member) for n in range(2)]
+    act, slope, power = zip(*hidden)
+    second_all = late(chain, second_all)
+    fc2_full = Weight(second_all, 0, rows)
+    kv_full = second_all[:, rows : rows + kv_rows].reshape(-1, width)
+    norm = [jnp.sqrt(v + NORM_EPS) for v in power]
+    units = 2 * act[0].shape[1]
+    norm_mean = sum(jnp.sum(v, axis=1, keepdims=True) for v in norm) * (1.0 / units) + NORM_EPS
+    norms = [v / norm_mean for v in norm]
     time_low = jnp.pad(time_embed[0].astype(low), ((0, SEATS - LAT_ROW), (0, 0)))
     pair = along("lt,tc->lc", time_low, time_w_all.astype(low)) + time_b_all
-    response, after_res, after_time, normed_two = branch_step(
-        chain, act, norms, vecs, fc2_full, member, live, x, res_all[10:11], pair
+    response_own, branch_part = branch_step(chain, act[0], norms[0], vecs[0], fc2_full, member, side_index[0])
+    response_other, after_res, after_time, normed_two = branch_step(
+        chain, act[1], norms[1], vecs[1], fc2_full, member, side_index[1],
+        (branch_part, live, x, res_all[10:11], pair),
     )
 
     each = width // UNITS
@@ -1109,6 +1239,8 @@
     silu_low = silu_text.astype(low)
     mapped = (along("tk,kc->tc", silu_low, kv_full) + vecs_all[3]).astype(low)
     source = jnp.concatenate([normed_two, mapped, jnp.zeros((key_pad, width), low)], axis=0)
+    source = copy_late(chain, source)
+    attn_t = Weight(late(chain, attn_all), 0, rows)
     grad_proj = (live[:, 0:1] * cot).astype(low)
     mixed_bias = jnp.concatenate([vecs_all[0], jnp.zeros((width,), full), vecs_all[1]])
     mixed, grad_attended = project(
@@ -1166,19 +1298,29 @@
     grad_res, grad_branch, pair_grad, res_bias_grad = time_back(
         chain, grad_normed_two, after_time, after_res, cot, pair, member, live
     )
-    mine_index = mine.astype(jnp.int32)[None]
-    grad_response, act_sums, shift_grad, fc2_away, fc2_kept = response_back(
-        chain, grad_branch, fc2_full, act, response, member, mine_index
+    grad_other, sums_other, shift_other, fc2_away = response_back(
+        chain, grad_branch, fc2_full, act[1], response_other, member, side_index[1]
+    )
+    grad_own, sums_own, shift_own, fc2_kept = response_back(
+        chain, grad_branch, fc2_full, act[0], response_own, member, side_index[0]
     )
     step(attn_sum)
     fc2_come = to_partner(late(chain, fc2_away))
-    gain_grad = jnp.sum(act_sums * norms, axis=0, keepdims=True)
-    norms_grad = vecs[1:2] * act_sums
-    norm_grad = norms_grad / norm_mean - jnp.sum(norms_grad * norm, axis=1, keepdims=True) / (
+    sums = [sums_own, sums_other]
+    gain_grad = ordered(*[jnp.sum(v * n, axis=0, keepdims=True) for v, n in zip(sums, norms)])
+    shift_grad = ordered(shift_own[:1], shift_other[:1])
+    norms_grad = [g[1:2] * v for g, v in zip(vecs, sums)]
+    common = sum(jnp.sum(g * n, axis=1, keepdims=True) for g, n in zip(norms_grad, norm)) / (
         units * norm_mean * norm_mean
     )
-    hidden_parts = (grad_response, act, slope, vecs, norms, norm_grad / norm, member, normed_low, fc1_t)
-    bias_away, grad_normed, fc1_away = hidden_back(chain, *hidden_parts, 1 - mine_index)
+    ratio = [(g / norm_mean - common) / n for g, n in zip(norms_grad, norm)]
+
+    def hidden_grads(n, grad, before=None):
+        return hidden_back(
+            chain, grad, act[n], slope[n], vecs[n], norms[n], ratio[n], member, normed_low, fc1_t[n], before
+        )
+
+    bias_away, grad_normed, fc1_away = hidden_grads(1, grad_other)
     step(attn_sum)
     fc2_sum = pieces_of(fc2_kept, fc2_come)
     for _ in early:
@@ -1187,22 +1329,10 @@
     for _ in range(outer_bits - 3):
         step(attn_sum)
     send(chain, fc2_sum, inner, outer)
-    bias_kept, grad_normed, fc1_kept = hidden_back(chain, *hidden_parts, mine_index, grad_normed)
-    hidden_bias_grad = jnp.where(
-        mine == 0,
-        jnp.concatenate([bias_kept[:1], bias_away[:1]], axis=1),
-        jnp.concatenate([bias_away[:1], bias_kept[:1]], axis=1),
-    )
+    bias_kept, grad_normed, fc1_kept = hidden_grads(0, grad_own, grad_normed)
+    hidden_bias_grad = ordered(bias_kept[:1], bias_away[:1])
     latents_grad, taps_grad = entry_back(
         chain, grad_normed, normed, entry_scale, x, grad_res, taps, geometry, res_bias_grad
-    )
-    output = output_step(
-        chain,
-        attended,
-        after_time,
-        live,
-        jnp.broadcast_to(vecs_all[2], (SEATS, width)),
-        attn_t.by(lambda i, *_: 3 * each + i),
     )
     attn_grad, kv_grad = finished(attn_sum)
     step(fc2_sum)
@@ -1237,6 +1367,14 @@
     for _ in range(outer_bits - 3):
         step(fc2_sum)
     send(chain, fc1_sum, inner, outer)
+    output = output_step(
+        chain,
+        attended,
+        after_time,
+        live,
+        jnp.broadcast_to(vecs_all[2], (SEATS, width)),
+        attn_t.by(lambda i, *_: 3 * each + i),
+    )
     (fc2_grad,) = finished(fc2_sum)
     step(fc1_sum)
     step(fc1_sum)

time: 918 us -> 884 us (0.963)
  waiting for transfers between devices: 360 us -> 275 us
  Pallas kernels: 407 us -> 437 us
  starting transfers between devices: 43.5 us -> 61 us
    all_gather x2, waiting for transfers between devices: 271 us -> 67 us  [to_all(): lax.all_gather(late(chain, shard), ('dp', 'fsdp'), axis=0, tiled=True)]
    ppermute x43 -> x59, waiting for transfers between devices: 88.4 us -> 208 us  [swap(): lax.ppermute(values, axis_name, [(i, i ^ 1 << bit) for i in range(size)])]
    pallas_call x31 -> x38, Pallas kernels: 407 us -> 437 us  [call(): pl.pallas_call(body, grid_spec=pltpu.PrefetchScalarGridSpec(num_scalar_pr...]
    ppermute x43 -> x59, starting transfers between devices: 43.4 us -> 61 us  [swap(): lax.ppermute(values, axis_name, [(i, i ^ 1 << bit) for i in range(size)])]
    unnamed x127 -> x173, local copies, waits for them, and re-layouts: 16.6 us -> 23 us
  transfers between devices with their start and end apart: 45 -> 61, of which waited for: 17 -> 27; matrix products, arithmetic and copies ran while one was open for 6% -> 7% of each run, Pallas kernels for 29% -> 33%
where the time goes in v4:
time: 884 us; the launch traced here: 879 us
  Pallas kernels  437 us (49%)
  waiting for transfers between devices  275 us (31%)
  starting transfers between devices  61 us (7%)
  local copies, waits for them, and re-layouts  52.2 us (6%)
  other arithmetic  29 us (3%)
  between operations  15.6 us (2%)
  matrix products  9.01 us (1%)
    pallas_call x38, Pallas kernels, call(): pl.pallas_call(body, grid_spec=pltpu.PrefetchScalarGridSpec(num_scalar_pr...  437 us
    ppermute x59, waiting for transfers between devices, swap(): lax.ppermute(values, axis_name, [(i, i ^ 1 << bit) for i in range(size)])  208 us
    all_gather x2, waiting for transfers between devices, to_all(): lax.all_gather(late(chain, shard), ('dp', 'fsdp'), axis=0, tiled=True)  67 us
    ppermute x59, starting transfers between devices, swap(): lax.ppermute(values, axis_name, [(i, i ^ 1 << bit) for i in range(size)])  61 us
    unnamed x173, local copies, waits for them, and re-layouts  23 us
  transfers between devices with their start and end apart: 61, of which 27 were waited for; matrix products, arithmetic and copies ran while one was open for 7% of the time, Pallas kernels for 33%

profile of v4, /device:TPU:0, one launch (start us, length us, event | category | flops | bytes accessed | tf_op | source)
XLA Modules:
  0.0 878.8 jit_solution(14837171408358367444)
XLA Ops:
  8.6 4.1 collective-permute-start
  17.0 22.4 %collective-permute-done.1.refs_7_ = bf16[1,64,128]{2,1,0:T(8,128)(2,1)S(1)} collective-permute-done((bf16[1,64,128]{2,1,0:T(8,128)(2,1)S(1)}, bf16[1,64,128]{2,1,0:T(8,128)(2,1)S(1)}, u32[]{:S(2)}, u32[]{:S(2)}) %collective-permute-start.1) | collective-permute-done | bytes 16416 | tf_op jit(solution)/shard_map/ppermute | solution.py:31
  50.0 3.6 collective-permute-done.4.refs_6_
  57.9 4.5 shard_map.275
  67.6 13.3 %collective-permute-done.9.refs_7_ = bf16[4,64,128]{2,1,0:T(8,128)(2,1)S(1)} collective-permute-done((bf16[4,64,128]{2,1,0:T(8,128)(2,1)S(1)}, bf16[4,64,128]{2,1,0:T(8,128)(2,1)S(1)}, u32[]{:S(2)}, u32[]{:S(2)}) %collective-permute-start.9) | collective-permute-done | bytes 65568 | tf_op jit(solution)/shard_map/ppermute | solution.py:31
  81.0 10.3 %collective-permute-done.6.refs_4_ = bf16[4,192,640]{2,1,0:T(8,128)(2,1)S(1)} collective-permute-done((bf16[4,192,640]{2,1,0:T(8,128)(2,1)S(1)}, bf16[4,192,640]{2,1,0:T(8,128)(2,1)S(1)}, u32[]{:S(2)}, u32[]{:S(2)}) %collective-permute-start.6) | collective-permute-done | bytes 983072 | tf_op jit(solution)/shard_map/ppermute | solution.py:31
  91.2 11.4 %collective-permute-done.7.refs_5_ = bf16[4,192,640]{2,1,0:T(8,128)(2,1)S(1)} collective-permute-done((bf16[4,192,640]{2,1,0:T(8,128)(2,1)S(1)}, bf16[4,192,640]{2,1,0:T(8,128)(2,1)S(1)}, u32[]{:S(2)}, u32[]{:S(2)}) %collective-permute-start.7) | collective-permute-done | bytes 983072 | tf_op jit(solution)/shard_map/ppermute | solution.py:31
  103.6 5.5 shard_map.276
  114.7 35.4 %collective-permute-done.13.refs_10_ = bf16[8,64,128]{2,1,0:T(8,128)(2,1)S(1)} collective-permute-done((bf16[8,64,128]{2,1,0:T(8,128)(2,1)}, bf16[8,64,128]{2,1,0:T(8,128)(2,1)S(1)}, u32[]{:S(2)}, u32[]{:S(2)}) %collective-permute-start.13) | collective-permute-done | bytes 131104 | tf_op jit(solution)/shard_map/ppermute | solution.py:31
  150.1 22.5 %collective-permute-done.10.refs_4_ = bf16[8,192,640]{2,1,0:T(8,128)(2,1)S(1)} collective-permute-done((bf16[8,192,640]{2,1,0:T(8,128)(2,1)}, bf16[8,192,640]{2,1,0:T(8,128)(2,1)S(1)}, u32[]{:S(2)}, u32[]{:S(2)}) %collective-permute-start.10) | collective-permute-done | bytes 1966112 | tf_op jit(solution)/shard_map/ppermute | solution.py:31
  173.9 14.1 %shard_map.277 = (bf16[16,192,1536]{2,1,0:T(8,128)(2,1)}, bf16[16,64,128]{2,1,0:T(8,128)(2,1)}, f32[8,128]{1,0:T(8,128)}) custom-call(s32[16]{0:T(128)} %broadcast_xor_fusion.refs_0_, s32[8,16]{1,0:T(8,128)} %constant.104.clone.refs_1_, s32[4,16]{1,0:T(4,128)} %constant.105.clone.refs_2_, bf16[8,192,640]{2,1,0:T(8,128)(2,1)} %get-tuple-element.199.refs_3_, ...), custom_call_target="tpu_custom_call" | custom-call | tf_op jit(solution)/shard_map/pallas_call | solution.py:60
  199.6 5.8 collective-permute-done.14
  212.0 11.4 %shard_map.278 = (bf16[576,1536]{1,0:T(8,128)(2,1)}, f32[576,1536]{1,0:T(8,128)}, f32[576,128]{1,0:T(8,128)}, f32[8,128]{1,0:T(8,128)}) custom-call(f32[576,1536]{1,0:T(8,128)} %bitcast.94, f32[16,1536]{1,0:T(8,128)} %pad.21.refs_1_.refs_5_, f32[576,16]{1,0:T(8,128)} %copy-done.1, f32[8,128]{1,0:T(8,128)} %get-tuple-element.205.refs_3_.token_ref), custom_call_target="tpu_custom_call" | custom-call | tf_op jit(solution)/shard_map/pallas_call | solution.py:60
  224.1 14.4 %shard_map.279 = (f32[576,3072]{1,0:T(8,128)}, f32[576,3072]{1,0:T(8,128)}, f32[8,3072]{1,0:T(8,128)}, f32[8,128]{1,0:T(8,128)}) custom-call(bf16[576,1536]{1,0:T(8,128)(2,1)} %get-tuple-element.206.refs_0_.refs_7_, f32[8,3072]{1,0:T(8,128)} %get-tuple-element.452.refs_1_.refs_3_, f32[36,8]{1,0:T(8,128)} %pad_convert_fusion.1.refs_2_.refs_4_.refs_5_.refs_6_, ...), custom_call_target="tpu_custom_call" | custom-call | tf_op jit(solution)/shard_map/pallas_call | solution.py:60
  240.4 14.2 %shard_map.280 = (f32[576,3072]{1,0:T(8,128)}, f32[576,3072]{1,0:T(8,128)}, f32[8,3072]{1,0:T(8,128)}, f32[8,128]{1,0:T(8,128)}) custom-call(bf16[576,1536]{1,0:T(8,128)(2,1)} %get-tuple-element.206.refs_0_.refs_7_, f32[8,3072]{1,0:T(8,128)} %get-tuple-element.453.refs_1_.refs_3_, f32[36,8]{1,0:T(8,128)} %pad_convert_fusion.1.refs_2_.refs_4_.refs_5_.refs_6_, ...), custom_call_target="tpu_custom_call" | custom-call | tf_op jit(solution)/shard_map/pallas_call | solution.py:60
  259.7 14.3 %shard_map.283 = (bf16[576,3072]{1,0:T(8,128)(2,1)}, f32[576,1536]{1,0:T(8,128)}, f32[8,128]{1,0:T(8,128)}) custom-call(s32[1]{0:T(128)} %bitcast.refs_0_, f32[576,3072]{1,0:T(8,128)} %get-tuple-element.214.refs_1_.refs_2_, f32[8,3072]{1,0:T(8,128)} %get-tuple-element.467.refs_2_.refs_4_, f32[8,3072]{1,0:T(8,128)} %get-tuple-element.452.refs_1_.refs_3_, ...), custom_call_target="tpu_custom_call" | custom-call | tf_op jit(solution)/shard_map/pallas_call | solution.py:60
  274.0 19.3 %shard_map.284 = (bf16[576,3072]{1,0:T(8,128)(2,1)}, f32[576,1536]{1,0:T(8,128)}, f32[576,1536]{1,0:T(8,128)}, bf16[576,1536]{1,0:T(8,128)(2,1)}, f32[8,128]{1,0:T(8,128)}) custom-call(s32[1]{0:T(128)S(6)} %sub.83.refs_0_, f32[576,3072]{1,0:T(8,128)} %get-tuple-element.210.refs_1_.refs_2_, f32[8,3072]{1,0:T(8,128)} %get-tuple-element.468.refs_2_.refs_4_, ...), custom_call_target="tpu_custom_call" | custom-call | tf_op jit(solution)/shard_map/pallas_call | solution.py:60
  296.9 3.5 shard_map.285
  300.4 67.0 %all-gather.5.cloned.1.call-done = bf16[6144,1536]{1,0:T(8,128)(2,1)} async-done(((bf16[192,1536]{1,0:T(8,128)(2,1)}), bf16[6144,1536]{1,0:T(8,128)(2,1)}) %all-gather.5.cloned.1.call-update) | async-done | bytes 18874384 | tf_op jit(solution)/shard_map/all_gather | solution.py:1176
  368.0 23.9 %shard_map.288 = (bf16[896,4608]{1,0:T(8,128)(2,1)}, bf16[576,1536]{1,0:T(8,128)(2,1)}, f32[8,128]{1,0:T(8,128)}) custom-call(bf16[896,1536]{1,0:T(8,128)(2,1)} %get-tuple-element.219.refs_0_.refs_5_, bf16[576,1536]{1,0:T(8,128)(2,1)} %get-tuple-element.438.refs_1_.refs_4_, f32[8,4608]{1,0:T(8,128)} %broadcast_in_dim.140.refs_2_, ...), custom_call_target="tpu_custom_call" | custom-call | tf_op jit(solution)/shard_map/pallas_call | solution.py:60
  391.9 57.1 %shard_map.289 = (bf16[576,1536]{1,0:T(8,128)(2,1)}, bf16[576,1536]{1,0:T(8,128)(2,1)}, bf16[896,1536]{1,0:T(8,128)(2,1)}, bf16[896,1536]{1,0:T(8,128)(2,1)}, f32[8,128]{1,0:T(8,128)}) custom-call(bf16[896,4608]{1,0:T(8,128)(2,1)} %get-tuple-element.221.refs_0_.refs_1_.refs_2_, bf16[896,4608]{1,0:T(8,128)(2,1)} %get-tuple-element.221.refs_0_.refs_1_.refs_2_, ...), custom_call_target="tpu_custom_call" | custom-call | tf_op jit(solution)/shard_map/pallas_call | solution.py:60
  449.1 14.9 %shard_map.290 = (bf16[3072,1536]{1,0:T(8,128)(2,1)}, f32[8,128]{1,0:T(8,128)}) custom-call(s32[1]{0:T(128)} %bitcast.26.refs_0_, bf16[576,1536]{1,0:T(8,128)(2,1)} %get-tuple-element.226.refs_1_.refs_0_, bf16[896,1536]{1,0:T(8,128)(2,1)} %get-tuple-element.227.refs_2_.refs_1_, bf16[896,1536]{1,0:T(8,128)(2,1)} %get-tuple-element.228.refs_3_.refs_2_, ...), custom_call_target="tpu_custom_call" | custom-call | tf_op jit(solution)/shard_map/pallas_call | solution.py:60
  464.6 19.5 %shard_map.291 = (f32[576,1536]{1,0:T(8,128)}, bf16[320,1536]{1,0:T(8,128)(2,1)}, f32[8,128]{1,0:T(8,128)}) custom-call(bf16[576,1536]{1,0:T(8,128)(2,1)} %get-tuple-element.226.refs_1_.refs_0_, bf16[896,1536]{1,0:T(8,128)(2,1)} %get-tuple-element.227.refs_2_.refs_1_, bf16[896,1536]{1,0:T(8,128)(2,1)} %get-tuple-element.228.refs_3_.refs_2_, ...), custom_call_target="tpu_custom_call" | custom-call | tf_op jit(solution)/shard_map/pallas_call | solution.py:60
  489.9 16.6 %shard_map.292 = (bf16[3072,1536]{1,0:T(8,128)(2,1)}, f32[8,128]{1,0:T(8,128)}) custom-call(s32[1]{0:T(128)} %bitcast.refs_0_, bf16[576,1536]{1,0:T(8,128)(2,1)} %get-tuple-element.226.refs_1_.refs_0_, bf16[896,1536]{1,0:T(8,128)(2,1)} %get-tuple-element.227.refs_2_.refs_1_, bf16[896,1536]{1,0:T(8,128)(2,1)} %get-tuple-element.228.refs_3_.refs_2_, ...), custom_call_target="tpu_custom_call" | custom-call | tf_op jit(solution)/shard_map/pallas_call | solution.py:60
  507.9 5.7 shard_map.293
  517.6 11.8 %shard_map.294 = (f32[576,1536]{1,0:T(8,128)}, bf16[576,1536]{1,0:T(8,128)(2,1)}, f32[8,3072]{1,0:T(8,128)}, f32[8,1536]{1,0:T(8,128)}, f32[8,128]{1,0:T(8,128)}) custom-call(f32[576,1536]{1,0:T(8,128)} %get-tuple-element.231.refs_0_, f32[576,1536]{1,0:T(8,128)} %get-tuple-element.225.refs_1_, f32[576,1536]{1,0:T(8,128)} %get-tuple-element.232.refs_2_, ...), custom_call_target="tpu_custom_call" | custom-call | tf_op jit(solution)/shard_map/pallas_call | solution.py:60
  529.3 18.6 %shard_map.295 = (f32[576,3072]{1,0:T(8,128)}, f32[8,3072]{1,0:T(8,128)}, f32[8,3072]{1,0:T(8,128)}, bf16[3072,1536]{1,0:T(8,128)(2,1)}, f32[8,128]{1,0:T(8,128)}) custom-call(s32[1]{0:T(128)S(6)} %sub.83.refs_0_, bf16[576,1536]{1,0:T(8,128)(2,1)} %get-tuple-element.239.refs_1_, f32[576,3072]{1,0:T(8,128)} %get-tuple-element.210.refs_1_.refs_2_, ...), custom_call_target="tpu_custom_call" | custom-call | tf_op jit(solution)/shard_map/pallas_call | solution.py:60
  548.0 18.4 %shard_map.296 = (f32[576,3072]{1,0:T(8,128)}, f32[8,3072]{1,0:T(8,128)}, f32[8,3072]{1,0:T(8,128)}, bf16[3072,1536]{1,0:T(8,128)(2,1)}, f32[8,128]{1,0:T(8,128)}) custom-call(s32[1]{0:T(128)} %bitcast.refs_0_, bf16[576,1536]{1,0:T(8,128)(2,1)} %get-tuple-element.239.refs_1_, f32[576,3072]{1,0:T(8,128)} %get-tuple-element.214.refs_1_.refs_2_, ...), custom_call_target="tpu_custom_call" | custom-call | tf_op jit(solution)/shard_map/pallas_call | solution.py:60
  568.8 6.9 shard_map.297
  582.4 23.4 %shard_map.299 = (f32[8,3072]{1,0:T(8,128)}, f32[576,1536]{1,0:T(8,128)}, bf16[3072,1536]{1,0:T(8,128)(2,1)}, f32[8,128]{1,0:T(8,128)}) custom-call(f32[576,3072]{1,0:T(8,128)} %get-tuple-element.261.refs_0_, f32[576,3072]{1,0:T(8,128)} %get-tuple-element.210.refs_1_.refs_2_, f32[576,3072]{1,0:T(8,128)} %get-tuple-element.262.refs_2_, ...), custom_call_target="tpu_custom_call" | custom-call | tf_op jit(solution)/shard_map/pallas_call | solution.py:60
  607.4 4.0 shard_map.300
  615.9 11.4 %shard_map.301 = (bf16[2,2,2,192,640]{4,3,2,1,0:T(8,128)(2,1)}, bf16[2,2,2,192,640]{4,3,2,1,0:T(8,128)(2,1)}, bf16[2,2,2,192,640]{4,3,2,1,0:T(8,128)(2,1)}, bf16...) custom-call(s32[1]{0:T(128)} %bitcast.25.refs_0_, ...), custom_call_target="tpu_custom_call" | custom-call | tf_op jit(solution)/shard_map/pallas_call | solution.py:60
  637.6 24.9 %shard_map.306 = (f32[8,3072]{1,0:T(8,128)}, f32[576,1536]{1,0:T(8,128)}, bf16[3072,1536]{1,0:T(8,128)(2,1)}, f32[8,128]{1,0:T(8,128)}) custom-call(f32[576,3072]{1,0:T(8,128)} %get-tuple-element.287.refs_0_, f32[576,3072]{1,0:T(8,128)} %get-tuple-element.214.refs_1_.refs_2_, f32[576,3072]{1,0:T(8,128)} %get-tuple-element.288.refs_2_, ...), custom_call_target="tpu_custom_call" | custom-call | tf_op jit(solution)/shard_map/pallas_call | solution.py:60
  662.5 19.7 %shard_map.307 = (f32[576,1536]{1,0:T(8,128)}, f32[16,1536]{1,0:T(8,128)}, f32[8,128]{1,0:T(8,128)}) custom-call(f32[576,1536]{1,0:T(8,128)} %get-tuple-element.290.refs_0_, f32[576,1536]{1,0:T(8,128)} %get-tuple-element.291.refs_1_, f32[576,128]{1,0:T(8,128)} %get-tuple-element.292.refs_2_, f32[576,1536]{1,0:T(8,128)} %bitcast.96, ...), custom_call_target="tpu_custom_call" | custom-call | tf_op jit(solution)/shard_map/pallas_call | solution.py:60
  686.4 5.7 shard_map.309
  711.7 6.5 collective-permute-done.38.refs_6_
  718.2 4.1 collective-permute-done.36.refs_2_
  730.9 11.8 %shard_map.313 = (bf16[2,2,2,192,640]{4,3,2,1,0:T(8,128)(2,1)}, bf16[2,2,2,192,640]{4,3,2,1,0:T(8,128)(2,1)}, bf16[2,2,2,192,640]{4,3,2,1,0:T(8,128)(2,1)}, bf16...) custom-call(s32[1]{0:T(128)} %bitcast.25.refs_0_, ...), custom_call_target="tpu_custom_call" | custom-call | tf_op jit(solution)/shard_map/pallas_call | solution.py:60
  753.9 7.8 shard_map.315
  761.7 18.6 %collective-permute-done.48.refs_1_ = bf16[1,192,1536]{2,1,0:T(8,128)(2,1)S(1)} collective-permute-done((bf16[1,192,1536]{2,1,0:T(8,128)(2,1)}, bf16[1,192,1536]{2,1,0:T(8,128)(2,1)S(1)}, u32[]{:S(2)}, u32[]{:S(2)}) %collective-permute-start.48) | collective-permute-done | bytes 589856 | tf_op jit(solution)/shard_map/ppermute | solution.py:31
  785.2 4.4 collective-permute-done.44.refs_2_
  790.8 6.1 shard_map.321
  800.8 8.4 collective-permute-done.52.refs_8_
  809.3 8.4 collective-permute-done.49.refs_2_
  819.7 3.7 shard_map.322
  826.7 4.6 collective-permute-done.56.refs_8_
  845.0 6.0 collective-permute-done.58.refs_3_
  851.0 11.4 %collective-permute-done.57.refs_1_ = bf16[1,192,1536]{2,1,0:T(8,128)(2,1)} collective-permute-done((bf16[1,192,1536]{2,1,0:T(8,128)(2,1)}, bf16[1,192,1536]{2,1,0:T(8,128)(2,1)}, u32[]{:S(2)}, u32[]{:S(2)}) %collective-permute-start.57) | collective-permute-done | bytes 589856 | tf_op jit(solution)/shard_map/ppermute | solution.py:31
  (447 shorter events, 182.2 us)
Async XLA Ops:
  7.2 250.1 %all-gather.3.cloned.1.call-start = ((), (), s32[]{:S(2)}) async-start(), calls=%async_computation | async-start | bytes 23519232 | tf_op jit(solution)/shard_map/all_gather | solution.py:1176
  8.6 30.8 %collective-permute-start = (bf16[1,192,1536]{2,1,0:T(8,128)(2,1)S(1)}, bf16[1,192,1536]{2,1,0:T(8,128)(2,1)S(1)}, u32[]{:S(2)}, u32[]{:S(2)}) collective-permute-start(bf16[1,192,1536]{2,1,0:T(8,128)(2,1)S(1)} %convert_bitcast_fusion.1.refs_0_.refs_1_.refs_2_), channel_id=1, source_target_pairs={{0,8},{1,9},{2,10},{3,11},{4,12},{5,13},{6,14},{7,15},{8,0},{9,1},... | collective-permute-start | bytes 1769480 | tf_op jit(solution)/shard_map/ppermute | solution.py:31
  16.7 22.7 %collective-permute-start.1 = (bf16[1,64,128]{2,1,0:T(8,128)(2,1)S(1)}, bf16[1,64,128]{2,1,0:T(8,128)(2,1)S(1)}, u32[]{:S(2)}, u32[]{:S(2)}) collective-permute-start(bf16[1,64,128]{2,1,0:T(8,128)(2,1)S(1)} %bitcast.122), channel_id=1, source_target_pairs={{0,8},{1,9},{2,10},{3,11},{4,12},{5,13},{6,14},{7,15},{8,0},{9,1},... | collective-permute-start | bytes 49160 | tf_op jit(solution)/shard_map/ppermute | solution.py:31
  62.5 304.8 %all-gather.5.cloned.1.call-start = ((), (), s32[]{:S(2)}) async-start(), calls=%async_computation.1 | async-start | bytes 19464192 | tf_op jit(solution)/shard_map/all_gather | solution.py:1176
  63.6 27.6 %collective-permute-start.6 = (bf16[4,192,640]{2,1,0:T(8,128)(2,1)S(1)}, bf16[4,192,640]{2,1,0:T(8,128)(2,1)S(1)}, u32[]{:S(2)}, u32[]{:S(2)}) collective-permute-start(bf16[4,192,640]{2,1,0:T(8,128)(2,1)S(1)} %copy-done.26), channel_id=1, source_target_pairs={{0,2},{1,3},{2,0},{3,1},{4,6},{5,7},{6,4},{7,5},{8,10},{9,11},{10,... | collective-permute-start | bytes 2949128 | tf_op jit(solution)/shard_map/ppermute | solution.py:31
  65.2 37.5 %collective-permute-start.7 = (bf16[4,192,640]{2,1,0:T(8,128)(2,1)S(1)}, bf16[4,192,640]{2,1,0:T(8,128)(2,1)S(1)}, u32[]{:S(2)}, u32[]{:S(2)}) collective-permute-start(bf16[4,192,640]{2,1,0:T(8,128)(2,1)S(1)} %copy-done.27), channel_id=1, source_target_pairs={{0,4},{1,5},{2,6},{3,7},{4,0},{5,1},{6,2},{7,3},{8,12},{9,13},{10,... | collective-permute-start | bytes 2949128 | tf_op jit(solution)/shard_map/ppermute | solution.py:31
  65.6 15.4 %collective-permute-start.8 = (bf16[4,192,256]{2,1,0:T(8,128)(2,1)}, bf16[4,192,256]{2,1,0:T(8,128)(2,1)S(1)}, u32[]{:S(2)}, u32[]{:S(2)}) collective-permute-start(bf16[4,192,256]{2,1,0:T(8,128)(2,1)} %get-tuple-element.196.refs_2_), channel_id=1, source_target_pairs={{0,1},{1,0},{2,3},{3,2},{4,5},{5,4},{6,7},{7,6},{8,9},{9,8},{10,11... | collective-permute-start | bytes 1179656 | tf_op jit(solution)/shard_map/ppermute | solution.py:31
  67.1 13.8 %collective-permute-start.9 = (bf16[4,64,128]{2,1,0:T(8,128)(2,1)S(1)}, bf16[4,64,128]{2,1,0:T(8,128)(2,1)S(1)}, u32[]{:S(2)}, u32[]{:S(2)}) collective-permute-start(bf16[4,64,128]{2,1,0:T(8,128)(2,1)S(1)} %copy-done.66), channel_id=1, source_target_pairs={{0,1},{1,0},{2,3},{3,2},{4,5},{5,4},{6,7},{7,6},{8,9},{9,8},{10,11... | collective-permute-start | bytes 196616 | tf_op jit(solution)/shard_map/ppermute | solution.py:31
  109.1 63.4 %collective-permute-start.10 = (bf16[8,192,640]{2,1,0:T(8,128)(2,1)}, bf16[8,192,640]{2,1,0:T(8,128)(2,1)S(1)}, u32[]{:S(2)}, u32[]{:S(2)}) collective-permute-start(bf16[8,192,640]{2,1,0:T(8,128)(2,1)} %get-tuple-element.199.refs_3_), channel_id=1, source_target_pairs={{0,1},{1,0},{2,3},{3,2},{4,5},{5,4},{6,7},{7,6},{8,9},{9,8},{10,11... | collective-permute-start | bytes 5898248 | tf_op jit(solution)/shard_map/ppermute | solution.py:31
  110.7 61.9 %collective-permute-start.11 = (bf16[8,192,640]{2,1,0:T(8,128)(2,1)}, bf16[8,192,640]{2,1,0:T(8,128)(2,1)}, u32[]{:S(2)}, u32[]{:S(2)}) collective-permute-start(bf16[8,192,640]{2,1,0:T(8,128)(2,1)} %get-tuple-element.200.refs_5_), channel_id=1, source_target_pairs={{0,2},{1,3},{2,0},{3,1},{4,6},{5,7},{6,4},{7,5},{8,10},{9,11},{10,... | collective-permute-start | bytes 5898248 | tf_op jit(solution)/shard_map/ppermute | solution.py:31
  111.3 38.8 %collective-permute-start.12 = (bf16[8,192,256]{2,1,0:T(8,128)(2,1)}, bf16[8,192,256]{2,1,0:T(8,128)(2,1)}, u32[]{:S(2)}, u32[]{:S(2)}) collective-permute-start(bf16[8,192,256]{2,1,0:T(8,128)(2,1)} %get-tuple-element.201.refs_7_), channel_id=1, source_target_pairs={{0,4},{1,5},{2,6},{3,7},{4,0},{5,1},{6,2},{7,3},{8,12},{9,13},{10,... | collective-permute-start | bytes 2359304 | tf_op jit(solution)/shard_map/ppermute | solution.py:31
  112.2 37.9 %collective-permute-start.13 = (bf16[8,64,128]{2,1,0:T(8,128)(2,1)}, bf16[8,64,128]{2,1,0:T(8,128)(2,1)S(1)}, u32[]{:S(2)}, u32[]{:S(2)}) collective-permute-start(bf16[8,64,128]{2,1,0:T(8,128)(2,1)} %get-tuple-element.202.refs_9_), channel_id=1, source_target_pairs={{0,4},{1,5},{2,6},{3,7},{4,0},{5,1},{6,2},{7,3},{8,12},{9,13},{10,... | collective-permute-start | bytes 393224 | tf_op jit(solution)/shard_map/ppermute | solution.py:31
  189.8 50.6 %collective-permute-start.15 = (bf16[16,192,1536]{2,1,0:T(8,128)(2,1)}, bf16[16,192,1536]{2,1,0:T(8,128)(2,1)}, u32[]{:S(2)}, u32[]{:S(2)}) collective-permute-start(bf16[16,192,1536]{2,1,0:T(8,128)(2,1)} %get-tuple-element.207.refs_3_.refs_8_), channel_id=1, source_target_pairs={{0,16},{16,0},{1,17},{17,1},{2,18},{18,2},{3,19},{19,3},{4,20},{20... | collective-permute-start | bytes 28311560 | tf_op jit(solution)/shard_map/ppermute | solution.py:31
  463.9 26.0 %collective-permute-start.16 = (bf16[3072,1536]{1,0:T(8,128)(2,1)}, bf16[3072,1536]{1,0:T(8,128)(2,1)}, u32[]{:S(2)}, u32[]{:S(2)}) collective-permute-start(bf16[3072,1536]{1,0:T(8,128)(2,1)} %get-tuple-element.233), channel_id=1, source_target_pairs={{0,16},{16,0},{1,17},{17,1},{2,18},{18,2},{3,19},{19,3},{4,20},{20... | collective-permute-start | bytes 28311560 | tf_op jit(solution)/shard_map/ppermute | solution.py:31
  489.7 16.8 %collective-permute-start.17 = (bf16[16,40,1536]{2,1,0:T(8,128)(2,1)}, bf16[16,40,1536]{2,1,0:T(8,128)(2,1)S(1)}, u32[]{:S(2)}, u32[]{:S(2)}) collective-permute-start(bf16[16,40,1536]{2,1,0:T(8,128)(2,1)} %get-tuple-element.444), channel_id=1, source_target_pairs={{0,16},{16,0},{1,17},{17,1},{2,18},{18,2},{3,19},{19,3},{4,20},{20... | collective-permute-start | bytes 5898248 | tf_op jit(solution)/shard_map/ppermute | solution.py:31
  513.5 52.9 %collective-permute-start.18 = (bf16[2,2,2,192,640]{4,3,2,1,0:T(8,128)(2,1)}, bf16[2,2,2,192,640]{4,3,2,1,0:T(8,128)(2,1)S(1)}, u32[]{:S(2)}, u32[]{:S(2)}) collective-permute-start(bf16[2,2,2,192,640]{4,3,2,1,0:T(8,128)(2,1)} %get-tuple-element.246), channel_id=1, source_target_pairs={{0,1},{1,0},{2,3},{3,2},{4,5},{5,4},{6,7},{7,6},{8,9},{9,8},{10,11... | collective-permute-start | bytes 5898248 | tf_op jit(solution)/shard_map/ppermute | solution.py:31
  514.9 51.5 %collective-permute-start.19 = (bf16[2,2,2,192,640]{4,3,2,1,0:T(8,128)(2,1)}, bf16[2,2,2,192,640]{4,3,2,1,0:T(8,128)(2,1)S(1)}, u32[]{:S(2)}, u32[]{:S(2)}) collective-permute-start(bf16[2,2,2,192,640]{4,3,2,1,0:T(8,128)(2,1)} %get-tuple-element.247), channel_id=1, source_target_pairs={{0,2},{1,3},{2,0},{3,1},{4,6},{5,7},{6,4},{7,5},{8,10},{9,11},{10,... | collective-permute-start | bytes 5898248 | tf_op jit(solution)/shard_map/ppermute | solution.py:31
  515.6 50.8 %collective-permute-start.21 = (bf16[2,2,2,40,1536]{4,3,2,1,0:T(8,128)(2,1)}, bf16[2,2,2,40,1536]{4,3,2,1,0:T(8,128)(2,1)S(1)}, u32[]{:S(2)}, u32[]{:S(2)}) collective-permute-start(bf16[2,2,2,40,1536]{4,3,2,1,0:T(8,128)(2,1)} %get-tuple-element.250), channel_id=1, source_target_pairs={{0,4},{1,5},{2,6},{3,7},{4,0},{5,1},{6,2},{7,3},{8,12},{9,13},{10,... | collective-permute-start | bytes 2949128 | tf_op jit(solution)/shard_map/ppermute | solution.py:31
  515.7 50.6 %collective-permute-start.20 = (bf16[2,2,2,192,256]{4,3,2,1,0:T(8,128)(2,1)}, bf16[2,2,2,192,256]{4,3,2,1,0:T(8,128)(2,1)S(1)}, u32[]{:S(2)}, u32[]{:S(2)}) collective-permute-start(bf16[2,2,2,192,256]{4,3,2,1,0:T(8,128)(2,1)} %get-tuple-element.248), channel_id=1, source_target_pairs={{0,4},{1,5},{2,6},{3,7},{4,0},{5,1},{6,2},{7,3},{8,12},{9,13},{10,... | collective-permute-start | bytes 2359304 | tf_op jit(solution)/shard_map/ppermute | solution.py:31
  575.8 40.1 %collective-permute-start.22 = (bf16[3072,1536]{1,0:T(8,128)(2,1)}, bf16[3072,1536]{1,0:T(8,128)(2,1)}, u32[]{:S(2)}, u32[]{:S(2)}) collective-permute-start(bf16[3072,1536]{1,0:T(8,128)(2,1)} %shard_map.298), channel_id=1, source_target_pairs={{0,16},{16,0},{1,17},{17,1},{2,18},{18,2},{3,19},{19,3},{4,20},{20... | collective-permute-start | bytes 28311560 | tf_op jit(solution)/shard_map/ppermute | solution.py:31
  576.8 29.0 %collective-permute-start.23 = (bf16[2,2,192,640]{3,2,1,0:T(8,128)(2,1)}, bf16[2,2,192,640]{3,2,1,0:T(8,128)(2,1)S(1)}, u32[]{:S(2)}, u32[]{:S(2)}) collective-permute-start(bf16[2,2,192,640]{3,2,1,0:T(8,128)(2,1)} %get-tuple-element.254), channel_id=1, source_target_pairs={{0,2},{1,3},{2,0},{3,1},{4,6},{5,7},{6,4},{7,5},{8,10},{9,11},{10,... | collective-permute-start | bytes 2949128 | tf_op jit(solution)/shard_map/ppermute | solution.py:31
  578.3 27.6 %collective-permute-start.24 = (bf16[2,2,192,640]{3,2,1,0:T(8,128)(2,1)}, bf16[2,2,192,640]{3,2,1,0:T(8,128)(2,1)S(1)}, u32[]{:S(2)}, u32[]{:S(2)}) collective-permute-start(bf16[2,2,192,640]{3,2,1,0:T(8,128)(2,1)} %get-tuple-element.256), channel_id=1, source_target_pairs={{0,4},{1,5},{2,6},{3,7},{4,0},{5,1},{6,2},{7,3},{8,12},{9,13},{10,... | collective-permute-start | bytes 2949128 | tf_op jit(solution)/shard_map/ppermute | solution.py:31
  578.6 27.2 %collective-permute-start.25 = (bf16[2,2,192,256]{3,2,1,0:T(8,128)(2,1)}, bf16[2,2,192,256]{3,2,1,0:T(8,128)(2,1)S(1)}, u32[]{:S(2)}, u32[]{:S(2)}) collective-permute-start(bf16[2,2,192,256]{3,2,1,0:T(8,128)(2,1)} %get-tuple-element.258), channel_id=1, source_target_pairs={{0,1},{1,0},{2,3},{3,2},{4,5},{5,4},{6,7},{7,6},{8,9},{9,8},{10,11... | collective-permute-start | bytes 1179656 | tf_op jit(solution)/shard_map/ppermute | solution.py:31
  579.2 26.6 %collective-permute-start.26 = (bf16[2,2,40,1536]{3,2,1,0:T(8,128)(2,1)}, bf16[2,2,40,1536]{3,2,1,0:T(8,128)(2,1)S(1)}, u32[]{:S(2)}, u32[]{:S(2)}) collective-permute-start(bf16[2,2,40,1536]{3,2,1,0:T(8,128)(2,1)} %get-tuple-element.260), channel_id=1, source_target_pairs={{0,1},{1,0},{2,3},{3,2},{4,5},{5,4},{6,7},{7,6},{8,9},{9,8},{10,11... | collective-permute-start | bytes 1474568 | tf_op jit(solution)/shard_map/ppermute | solution.py:31
  611.3 16.0 %collective-permute-start.27 = (bf16[2,192,640]{2,1,0:T(8,128)(2,1)}, bf16[2,192,640]{2,1,0:T(8,128)(2,1)S(1)}, u32[]{:S(2)}, u32[]{:S(2)}) collective-permute-start(bf16[2,192,640]{2,1,0:T(8,128)(2,1)} %get-tuple-element.270), channel_id=1, source_target_pairs={{0,4},{1,5},{2,6},{3,7},{4,0},{5,1},{6,2},{7,3},{8,12},{9,13},{10,... | collective-permute-start | bytes 1474568 | tf_op jit(solution)/shard_map/ppermute | solution.py:31
  613.2 14.1 %collective-permute-start.28 = (bf16[2,192,640]{2,1,0:T(8,128)(2,1)}, bf16[2,192,640]{2,1,0:T(8,128)(2,1)S(1)}, u32[]{:S(2)}, u32[]{:S(2)}) collective-permute-start(bf16[2,192,640]{2,1,0:T(8,128)(2,1)} %get-tuple-element.272), channel_id=1, source_target_pairs={{0,1},{1,0},{2,3},{3,2},{4,5},{5,4},{6,7},{7,6},{8,9},{9,8},{10,11... | collective-permute-start | bytes 1474568 | tf_op jit(solution)/shard_map/ppermute | solution.py:31
  613.8 13.5 %collective-permute-start.30 = (bf16[2,40,1536]{2,1,0:T(8,128)(2,1)}, bf16[2,40,1536]{2,1,0:T(8,128)(2,1)S(1)}, u32[]{:S(2)}, u32[]{:S(2)}) collective-permute-start(bf16[2,40,1536]{2,1,0:T(8,128)(2,1)} %get-tuple-element.276), channel_id=1, source_target_pairs={{0,2},{1,3},{2,0},{3,1},{4,6},{5,7},{6,4},{7,5},{8,10},{9,11},{10,... | collective-permute-start | bytes 737288 | tf_op jit(solution)/shard_map/ppermute | solution.py:31
  631.5 54.0 %collective-permute-start.32 = (bf16[2,2,2,192,640]{4,3,2,1,0:T(8,128)(2,1)}, bf16[2,2,2,192,640]{4,3,2,1,0:T(8,128)(2,1)}, u32[]{:S(2)}, u32[]{:S(2)}) collective-permute-start(bf16[2,2,2,192,640]{4,3,2,1,0:T(8,128)(2,1)} %shard_map.304), channel_id=1, source_target_pairs={{0,2},{1,3},{2,0},{3,1},{4,6},{5,7},{6,4},{7,5},{8,10},{9,11},{10,... | collective-permute-start | bytes 5898248 | tf_op jit(solution)/shard_map/ppermute | solution.py:31
  633.1 52.4 %collective-permute-start.31 = (bf16[2,2,2,192,640]{4,3,2,1,0:T(8,128)(2,1)S(1)}, bf16[2,2,2,192,640]{4,3,2,1,0:T(8,128)(2,1)}, u32[]{:S(2)}, u32[]{:S(2)}) collective-permute-start(bf16[2,2,2,192,640]{4,3,2,1,0:T(8,128)(2,1)S(1)} %copy-done.9), channel_id=1, source_target_pairs={{0,1},{1,0},{2,3},{3,2},{4,5},{5,4},{6,7},{7,6},{8,9},{9,8},{10,11... | collective-permute-start | bytes 5898248 | tf_op jit(solution)/shard_map/ppermute | solution.py:31
  634.5 51.0 %collective-permute-start.33 = (bf16[2,2,2,192,256]{4,3,2,1,0:T(8,128)(2,1)}, bf16[2,2,2,192,256]{4,3,2,1,0:T(8,128)(2,1)S(1)}, u32[]{:S(2)}, u32[]{:S(2)}) collective-permute-start(bf16[2,2,2,192,256]{4,3,2,1,0:T(8,128)(2,1)} %shard_map.305), channel_id=1, source_target_pairs={{0,4},{1,5},{2,6},{3,7},{4,0},{5,1},{6,2},{7,3},{8,12},{9,13},{10,... | collective-permute-start | bytes 2359304 | tf_op jit(solution)/shard_map/ppermute | solution.py:31
  634.7 47.5 %collective-permute-start.34 = (bf16[1,192,1536]{2,1,0:T(8,128)(2,1)S(1)}, bf16[1,192,1536]{2,1,0:T(8,128)(2,1)S(1)}, u32[]{:S(2)}, u32[]{:S(2)}) collective-permute-start(bf16[1,192,1536]{2,1,0:T(8,128)(2,1)S(1)} %copy-done.82), channel_id=1, source_target_pairs={{0,8},{1,9},{2,10},{3,11},{4,12},{5,13},{6,14},{7,15},{8,0},{9,1},... | collective-permute-start | bytes 1769480 | tf_op jit(solution)/shard_map/ppermute | solution.py:31
  636.5 45.7 %collective-permute-start.35 = (bf16[1,40,1536]{2,1,0:T(8,128)(2,1)S(1)}, bf16[1,40,1536]{2,1,0:T(8,128)(2,1)S(1)}, u32[]{:S(2)}, u32[]{:S(2)}) collective-permute-start(bf16[1,40,1536]{2,1,0:T(8,128)(2,1)S(1)} %copy-done.83), channel_id=1, source_target_pairs={{0,8},{1,9},{2,10},{3,11},{4,12},{5,13},{6,14},{7,15},{8,0},{9,1},... | collective-permute-start | bytes 368648 | tf_op jit(solution)/shard_map/ppermute | solution.py:31
  693.6 36.5 %collective-permute-start.42 = (bf16[3072,1536]{1,0:T(8,128)(2,1)}, bf16[3072,1536]{1,0:T(8,128)(2,1)}, u32[]{:S(2)}, u32[]{:S(2)}) collective-permute-start(bf16[3072,1536]{1,0:T(8,128)(2,1)} %shard_map.312), channel_id=1, source_target_pairs={{0,16},{16,0},{1,17},{17,1},{2,18},{18,2},{3,19},{19,3},{4,20},{20... | collective-permute-start | bytes 28311560 | tf_op jit(solution)/shard_map/ppermute | solution.py:31
  698.5 23.8 %collective-permute-start.36 = (bf16[2,2,192,640]{3,2,1,0:T(8,128)(2,1)}, bf16[2,2,192,640]{3,2,1,0:T(8,128)(2,1)}, u32[]{:S(2)}, u32[]{:S(2)}) collective-permute-start(bf16[2,2,192,640]{3,2,1,0:T(8,128)(2,1)} %get-tuple-element.299), channel_id=1, source_target_pairs={{0,2},{1,3},{2,0},{3,1},{4,6},{5,7},{6,4},{7,5},{8,10},{9,11},{10,... | collective-permute-start | bytes 2949128 | tf_op jit(solution)/shard_map/ppermute | solution.py:31
  699.2 23.6 %collective-permute-start.37 = (bf16[2,2,192,640]{3,2,1,0:T(8,128)(2,1)}, bf16[2,2,192,640]{3,2,1,0:T(8,128)(2,1)}, u32[]{:S(2)}, u32[]{:S(2)}) collective-permute-start(bf16[2,2,192,640]{3,2,1,0:T(8,128)(2,1)} %get-tuple-element.301), channel_id=1, source_target_pairs={{0,4},{1,5},{2,6},{3,7},{4,0},{5,1},{6,2},{7,3},{8,12},{9,13},{10,... | collective-permute-start | bytes 2949128 | tf_op jit(solution)/shard_map/ppermute | solution.py:31
  711.7 18.4 %collective-permute-start.43 = (f32[16,64,128]{2,1,0:T(8,128)S(1)}, f32[16,64,128]{2,1,0:T(8,128)S(1)}, u32[]{:S(2)}, u32[]{:S(2)}) collective-permute-start(f32[16,64,128]{2,1,0:T(8,128)S(1)} %get-tuple-element.446), channel_id=1, source_target_pairs={{0,16},{16,0},{1,17},{17,1},{2,18},{18,2},{3,19},{19,3},{4,20},{20... | collective-permute-start | bytes 1572872 | tf_op jit(solution)/shard_map/ppermute | solution.py:31
  726.3 16.5 %collective-permute-start.39 = (bf16[2,192,640]{2,1,0:T(8,128)(2,1)}, bf16[2,192,640]{2,1,0:T(8,128)(2,1)S(1)}, u32[]{:S(2)}, u32[]{:S(2)}) collective-permute-start(bf16[2,192,640]{2,1,0:T(8,128)(2,1)} %get-tuple-element.308), channel_id=1, source_target_pairs={{0,4},{1,5},{2,6},{3,7},{4,0},{5,1},{6,2},{7,3},{8,12},{9,13},{10,... | collective-permute-start | bytes 1474568 | tf_op jit(solution)/shard_map/ppermute | solution.py:31
  728.1 14.7 %collective-permute-start.40 = (bf16[2,192,640]{2,1,0:T(8,128)(2,1)}, bf16[2,192,640]{2,1,0:T(8,128)(2,1)S(1)}, u32[]{:S(2)}, u32[]{:S(2)}) collective-permute-start(bf16[2,192,640]{2,1,0:T(8,128)(2,1)} %get-tuple-element.310), channel_id=1, source_target_pairs={{0,1},{1,0},{2,3},{3,2},{4,5},{5,4},{6,7},{7,6},{8,9},{9,8},{10,11... | collective-permute-start | bytes 1474568 | tf_op jit(solution)/shard_map/ppermute | solution.py:31
  729.5 13.2 %collective-permute-start.41 = (bf16[2,192,256]{2,1,0:T(8,128)(2,1)}, bf16[2,192,256]{2,1,0:T(8,128)(2,1)S(1)}, u32[]{:S(2)}, u32[]{:S(2)}) collective-permute-start(bf16[2,192,256]{2,1,0:T(8,128)(2,1)} %get-tuple-element.312), channel_id=1, source_target_pairs={{0,2},{1,3},{2,0},{3,1},{4,6},{5,7},{6,4},{7,5},{8,10},{9,11},{10,... | collective-permute-start | bytes 589832 | tf_op jit(solution)/shard_map/ppermute | solution.py:31
  746.7 42.9 %collective-permute-start.44 = (bf16[2,2,2,192,640]{4,3,2,1,0:T(8,128)(2,1)}, bf16[2,2,2,192,640]{4,3,2,1,0:T(8,128)(2,1)}, u32[]{:S(2)}, u32[]{:S(2)}) collective-permute-start(bf16[2,2,2,192,640]{4,3,2,1,0:T(8,128)(2,1)} %shard_map.316), channel_id=1, source_target_pairs={{0,1},{1,0},{2,3},{3,2},{4,5},{5,4},{6,7},{7,6},{8,9},{9,8},{10,11... | collective-permute-start | bytes 5898248 | tf_op jit(solution)/shard_map/ppermute | solution.py:31
  748.2 42.6 %collective-permute-start.45 = (bf16[2,2,2,192,640]{4,3,2,1,0:T(8,128)(2,1)S(1)}, bf16[2,2,2,192,640]{4,3,2,1,0:T(8,128)(2,1)}, u32[]{:S(2)}, u32[]{:S(2)}) collective-permute-start(bf16[2,2,2,192,640]{4,3,2,1,0:T(8,128)(2,1)S(1)} %copy-done.10), channel_id=1, source_target_pairs={{0,2},{1,3},{2,0},{3,1},{4,6},{5,7},{6,4},{7,5},{8,10},{9,11},{10,... | collective-permute-start | bytes 5898248 | tf_op jit(solution)/shard_map/ppermute | solution.py:31
  749.7 35.5 %collective-permute-start.46 = (bf16[2,2,2,192,256]{4,3,2,1,0:T(8,128)(2,1)}, bf16[2,2,2,192,256]{4,3,2,1,0:T(8,128)(2,1)S(1)}, u32[]{:S(2)}, u32[]{:S(2)}) collective-permute-start(bf16[2,2,2,192,256]{4,3,2,1,0:T(8,128)(2,1)} %shard_map.318), channel_id=1, source_target_pairs={{0,4},{1,5},{2,6},{3,7},{4,0},{5,1},{6,2},{7,3},{8,12},{9,13},{10,... | collective-permute-start | bytes 2359304 | tf_op jit(solution)/shard_map/ppermute | solution.py:31
  750.0 30.3 %collective-permute-start.48 = (bf16[1,192,1536]{2,1,0:T(8,128)(2,1)}, bf16[1,192,1536]{2,1,0:T(8,128)(2,1)S(1)}, u32[]{:S(2)}, u32[]{:S(2)}) collective-permute-start(bf16[1,192,1536]{2,1,0:T(8,128)(2,1)} %get-tuple-element.335), channel_id=1, source_target_pairs={{0,8},{1,9},{2,10},{3,11},{4,12},{5,13},{6,14},{7,15},{8,0},{9,1},... | collective-permute-start | bytes 1769480 | tf_op jit(solution)/shard_map/ppermute | solution.py:31
  751.7 33.5 %collective-permute-start.47 = (f32[2,2,2,64,128]{4,3,2,1,0:T(8,128)}, f32[2,2,2,64,128]{4,3,2,1,0:T(8,128)}, u32[]{:S(2)}, u32[]{:S(2)}) collective-permute-start(f32[2,2,2,64,128]{4,3,2,1,0:T(8,128)} %shard_map.319), channel_id=1, source_target_pairs={{0,4},{1,5},{2,6},{3,7},{4,0},{5,1},{6,2},{7,3},{8,12},{9,13},{10,... | collective-permute-start | bytes 786440 | tf_op jit(solution)/shard_map/ppermute | solution.py:31
  796.9 20.8 %collective-permute-start.49 = (bf16[2,2,192,640]{3,2,1,0:T(8,128)(2,1)}, bf16[2,2,192,640]{3,2,1,0:T(8,128)(2,1)S(1)}, u32[]{:S(2)}, u32[]{:S(2)}) collective-permute-start(bf16[2,2,192,640]{3,2,1,0:T(8,128)(2,1)} %get-tuple-element.339), channel_id=1, source_target_pairs={{0,2},{1,3},{2,0},{3,1},{4,6},{5,7},{6,4},{7,5},{8,10},{9,11},{10,... | collective-permute-start | bytes 2949128 | tf_op jit(solution)/shard_map/ppermute | solution.py:31
  798.4 20.4 %collective-permute-start.50 = (bf16[2,2,192,640]{3,2,1,0:T(8,128)(2,1)}, bf16[2,2,192,640]{3,2,1,0:T(8,128)(2,1)S(1)}, u32[]{:S(2)}, u32[]{:S(2)}) collective-permute-start(bf16[2,2,192,640]{3,2,1,0:T(8,128)(2,1)} %get-tuple-element.341), channel_id=1, source_target_pairs={{0,4},{1,5},{2,6},{3,7},{4,0},{5,1},{6,2},{7,3},{8,12},{9,13},{10,... | collective-permute-start | bytes 2949128 | tf_op jit(solution)/shard_map/ppermute | solution.py:31
  836.9 14.1 %collective-permute-start.58 = (f32[1,64,128]{2,1,0:T(8,128)}, f32[1,64,128]{2,1,0:T(8,128)S(1)}, u32[]{:S(2)}, u32[]{:S(2)}) collective-permute-start(f32[1,64,128]{2,1,0:T(8,128)} %get-tuple-element.359), channel_id=1, source_target_pairs={{0,8},{1,9},{2,10},{3,11},{4,12},{5,13},{6,14},{7,15},{8,0},{9,1},... | collective-permute-start | bytes 98312 | tf_op jit(solution)/shard_map/ppermute | solution.py:31
  838.3 24.1 %collective-permute-start.57 = (bf16[1,192,1536]{2,1,0:T(8,128)(2,1)}, bf16[1,192,1536]{2,1,0:T(8,128)(2,1)}, u32[]{:S(2)}, u32[]{:S(2)}) collective-permute-start(bf16[1,192,1536]{2,1,0:T(8,128)(2,1)} %get-tuple-element.357), channel_id=1, source_target_pairs={{0,8},{1,9},{2,10},{3,11},{4,12},{5,13},{6,14},{7,15},{8,0},{9,1},... | collective-permute-start | bytes 1769480 | tf_op jit(solution)/shard_map/ppermute | solution.py:31
  (98 other events, 745.2 us)
Sparse Core Ops, SparseCore 0:
  62.6 177.2 all-gather.2
  243.4 123.8 all-gather.4

commit v5 on v4

--- a/solution.py
+++ b/solution.py
@@ -424,7 +424,7 @@
         refs[2 * count + n][...] = (refs[2 * n][...].astype(jnp.float32) + refs[2 * n + 1][...].astype(jnp.float32))[0]
 
 
-def totals_of(chain, pieces):
+def totals_of(chain, pieces, after=()):
     operands = [v for piece in pieces for v in (piece.base, piece.come)]
     shapes = [piece.base.shape[1:] for piece in pieces]
     return chain.call(
@@ -434,6 +434,7 @@
         [(shape, jnp.float32, whole_array(shape)) for shape in shapes],
         [],
         *operands,
+        after=after,
     )
 
 
@@ -1179,12 +1180,11 @@
         chain, [fc1_w.T.astype(low), small_shard.reshape(-1, 128)], [orders, orders[2:]], inner, outer
     )
     first.step()
-    first.step()
     second_all = to_all(jnp.concatenate([fc2_w.astype(low), kv_w.astype(low)], axis=0))
-    for _ in range(outer_bits - 3):
+    for _ in range(outer_bits - 2):
         first.step()
+    attn_all = to_all(attn_w.T.astype(low))
     fc1_parts, small_all = first.finish()
-    attn_all = to_all(attn_w.T.astype(low))
     fc1_t = [Weight(part, 0, rows) for part in sides(fc1_parts)]
     small_all = in_order(small_all).reshape(blocks, -1)
     small_full = []
@@ -1331,13 +1331,22 @@
     send(chain, fc2_sum, inner, outer)
     bias_kept, grad_normed, fc1_kept = hidden_grads(0, grad_own, grad_normed)
     hidden_bias_grad = ordered(bias_kept[:1], bias_away[:1])
+    output = output_step(
+        chain,
+        attended,
+        after_time,
+        live,
+        jnp.broadcast_to(vecs_all[2], (SEATS, width)),
+        attn_t.by(lambda i, *_: 3 * each + i),
+    )
+    attn_grad, kv_grad = finished(attn_sum)
+    step(fc2_sum)
+    fc1_come = to_partner(late(chain, fc1_away))
     latents_grad, taps_grad = entry_back(
         chain, grad_normed, normed, entry_scale, x, grad_res, taps, geometry, res_bias_grad
     )
-    attn_grad, kv_grad = finished(attn_sum)
     step(fc2_sum)
     taps_grad = copy_late(chain, taps_grad)
-    fc1_come = to_partner(late(chain, fc1_away))
     time_grad = jnp.einsum("lt,lc->tc", time_low.astype(full), pair_grad, precision=HIGHEST)
     small_terms = (
         taps_grad[: res_vecs.shape[0]],
@@ -1359,7 +1368,6 @@
         axis=1,
     ).reshape(blocks, -1, 128)
     small_piece = halved(small_blocks)
-    step(fc2_sum)
     fc1_sum = pieces_of(fc1_kept, fc1_come) + [small_piece]
     for _ in early:
         step(fc1_sum)
@@ -1367,26 +1375,20 @@
     for _ in range(outer_bits - 3):
         step(fc2_sum)
     send(chain, fc1_sum, inner, outer)
-    output = output_step(
-        chain,
-        attended,
-        after_time,
-        live,
-        jnp.broadcast_to(vecs_all[2], (SEATS, width)),
-        attn_t.by(lambda i, *_: 3 * each + i),
-    )
     (fc2_grad,) = finished(fc2_sum)
     step(fc1_sum)
     step(fc1_sum)
-    fc1_grad, small_total = finished(fc1_sum)
+    while fc1_sum[0].order:
+        step(fc1_sum)
+    (small_total,) = totals_of(chain, fc1_sum[1:])
     small_total = small_total.reshape(-1)
-    text_grad = silu_back(along("tc,kc->tk", grad_mapped, kv_full))[0]
-
     small_grads = []
     taken = 0
     for owned, size in zip(small_owned, small_sizes):
         small_grads.append(small_total[taken : taken + size].reshape(owned.shape))
         taken += size
+    text_grad = silu_back(along("tc,kc->tk", grad_mapped, kv_full))[0]
+    (fc1_grad,) = totals_of(chain, fc1_sum[:1], small_grads)
     return (
         output[None],
         latents_grad[None],

time: 884 us -> 880 us (level)
    all_gather x2, waiting for transfers between devices: 67 us -> 38.5 us  [to_all(): lax.all_gather(late(chain, shard), ('dp', 'fsdp'), axis=0, tiled=True)]
    ppermute x59, waiting for transfers between devices: 208 us -> 228 us  [swap(): lax.ppermute(values, axis_name, [(i, i ^ 1 << bit) for i in range(size)])]
    pallas_call x38 -> x39, Pallas kernels: 437 us -> 439 us  [call(): pl.pallas_call(body, grid_spec=pltpu.PrefetchScalarGridSpec(num_scalar_pr...]
    unnamed x173 -> x179, local copies, waits for them, and re-layouts: 23 us -> 21.7 us
  transfers between devices with their start and end apart: 61 -> 61, of which waited for: 27 -> 27; matrix products, arithmetic and copies ran while one was open for 7% -> 8% of each run, Pallas kernels for 33% -> 34%
where the time goes in v5:
time: 880 us; the launch traced here: 874 us
  Pallas kernels  439 us (50%)
  waiting for transfers between devices  267 us (30%)
  starting transfers between devices  61.1 us (7%)
  local copies, waits for them, and re-layouts  53 us (6%)
  other arithmetic  29.1 us (3%)
  between operations  15.7 us (2%)
  matrix products  9.02 us (1%)
    pallas_call x39, Pallas kernels, call(): pl.pallas_call(body, grid_spec=pltpu.PrefetchScalarGridSpec(num_scalar_pr...  439 us
    ppermute x59, waiting for transfers between devices, swap(): lax.ppermute(values, axis_name, [(i, i ^ 1 << bit) for i in range(size)])  228 us
    ppermute x59, starting transfers between devices, swap(): lax.ppermute(values, axis_name, [(i, i ^ 1 << bit) for i in range(size)])  61 us
    all_gather x2, waiting for transfers between devices, to_all(): lax.all_gather(late(chain, shard), ('dp', 'fsdp'), axis=0, tiled=True)  38.5 us
    unnamed x179, local copies, waits for them, and re-layouts  21.7 us
  transfers between devices with their start and end apart: 61, of which 27 were waited for; matrix products, arithmetic and copies ran while one was open for 8% of the time, Pallas kernels for 34%

profile of v5, /device:TPU:0, one launch (start us, length us, event | category | flops | bytes accessed | tf_op | source)
XLA Modules:
  0.0 873.6 jit_solution(7811141853176762162)
XLA Ops:
  8.7 4.1 collective-permute-start
  17.9 21.5 %collective-permute-done.1.refs_7_ = bf16[1,64,128]{2,1,0:T(8,128)(2,1)S(1)} collective-permute-done((bf16[1,64,128]{2,1,0:T(8,128)(2,1)S(1)}, bf16[1,64,128]{2,1,0:T(8,128)(2,1)S(1)}, u32[]{:S(2)}, u32[]{:S(2)}) %collective-permute-start.1) | collective-permute-done | bytes 16416 | tf_op jit(solution)/shard_map/ppermute | solution.py:31
  48.7 4.9 collective-permute-done.5.refs_7_
  53.6 4.3 collective-permute-done.2.refs_4_
  61.9 4.5 shard_map.275
  73.5 4.8 collective-permute-done.8.refs_6_
  78.3 13.8 %collective-permute-done.6.refs_4_ = bf16[4,192,640]{2,1,0:T(8,128)(2,1)S(1)} collective-permute-done((bf16[4,192,640]{2,1,0:T(8,128)(2,1)}, bf16[4,192,640]{2,1,0:T(8,128)(2,1)S(1)}, u32[]{:S(2)}, u32[]{:S(2)}) %collective-permute-start.6) | collective-permute-done | bytes 983072 | tf_op jit(solution)/shard_map/ppermute | solution.py:31
  92.1 24.1 %collective-permute-done.7.refs_5_ = bf16[4,192,640]{2,1,0:T(8,128)(2,1)S(1)} collective-permute-done((bf16[4,192,640]{2,1,0:T(8,128)(2,1)}, bf16[4,192,640]{2,1,0:T(8,128)(2,1)S(1)}, u32[]{:S(2)}, u32[]{:S(2)}) %collective-permute-start.7) | collective-permute-done | bytes 983072 | tf_op jit(solution)/shard_map/ppermute | solution.py:31
  117.2 5.5 shard_map.276
  130.0 42.4 %collective-permute-done.13.refs_10_ = bf16[8,64,128]{2,1,0:T(8,128)(2,1)S(1)} collective-permute-done((bf16[8,64,128]{2,1,0:T(8,128)(2,1)S(1)}, bf16[8,64,128]{2,1,0:T(8,128)(2,1)S(1)}, u32[]{:S(2)}, u32[]{:S(2)}) %collective-permute-start.13) | collective-permute-done | bytes 131104 | tf_op jit(solution)/shard_map/ppermute | solution.py:31
  172.5 24.2 %collective-permute-done.10.refs_4_ = bf16[8,192,640]{2,1,0:T(8,128)(2,1)S(1)} collective-permute-done((bf16[8,192,640]{2,1,0:T(8,128)(2,1)}, bf16[8,192,640]{2,1,0:T(8,128)(2,1)S(1)}, u32[]{:S(2)}, u32[]{:S(2)}) %collective-permute-start.10) | collective-permute-done | bytes 1966112 | tf_op jit(solution)/shard_map/ppermute | solution.py:31
  199.1 14.1 %shard_map.277 = (bf16[16,192,1536]{2,1,0:T(8,128)(2,1)}, bf16[16,64,128]{2,1,0:T(8,128)(2,1)}, f32[8,128]{1,0:T(8,128)}) custom-call(s32[16]{0:T(128)} %broadcast_xor_fusion.refs_0_, s32[8,16]{1,0:T(8,128)} %constant.104.clone.refs_1_, s32[4,16]{1,0:T(4,128)} %constant.105.clone.refs_2_, bf16[8,192,640]{2,1,0:T(8,128)(2,1)} %get-tuple-element.200.refs_3_, ...), custom_call_target="tpu_custom_call" | custom-call | tf_op jit(solution)/shard_map/pallas_call | solution.py:60
  223.4 5.6 collective-permute-done.14
  235.6 11.0 %shard_map.278 = (bf16[576,1536]{1,0:T(8,128)(2,1)}, f32[576,1536]{1,0:T(8,128)}, f32[576,128]{1,0:T(8,128)}, f32[8,128]{1,0:T(8,128)}) custom-call(f32[576,1536]{1,0:T(8,128)} %bitcast.96, f32[16,1536]{1,0:T(8,128)} %pad.21.refs_1_.refs_5_, f32[576,16]{1,0:T(8,128)} %copy-done.1, f32[8,128]{1,0:T(8,128)} %get-tuple-element.206.refs_3_), custom_call_target="tpu_custom_call" | custom-call | tf_op jit(solution)/shard_map/pallas_call | solution.py:60
  247.3 14.4 %shard_map.279 = (f32[576,3072]{1,0:T(8,128)}, f32[576,3072]{1,0:T(8,128)}, f32[8,3072]{1,0:T(8,128)}, f32[8,128]{1,0:T(8,128)}) custom-call(bf16[576,1536]{1,0:T(8,128)(2,1)} %get-tuple-element.207.refs_0_.refs_7_, f32[8,3072]{1,0:T(8,128)} %get-tuple-element.454.refs_1_.refs_3_, f32[36,8]{1,0:T(8,128)} %pad_convert_fusion.1.refs_2_.refs_4_.refs_5_.refs_6_, ...), custom_call_target="tpu_custom_call" | custom-call | tf_op jit(solution)/shard_map/pallas_call | solution.py:60
  263.6 14.2 %shard_map.280 = (f32[576,3072]{1,0:T(8,128)}, f32[576,3072]{1,0:T(8,128)}, f32[8,3072]{1,0:T(8,128)}, f32[8,128]{1,0:T(8,128)}) custom-call(bf16[576,1536]{1,0:T(8,128)(2,1)} %get-tuple-element.207.refs_0_.refs_7_, f32[8,3072]{1,0:T(8,128)} %get-tuple-element.455.refs_1_.refs_3_, f32[36,8]{1,0:T(8,128)} %pad_convert_fusion.1.refs_2_.refs_4_.refs_5_.refs_6_, ...), custom_call_target="tpu_custom_call" | custom-call | tf_op jit(solution)/shard_map/pallas_call | solution.py:60
  283.0 14.4 %shard_map.283 = (bf16[576,3072]{1,0:T(8,128)(2,1)}, f32[576,1536]{1,0:T(8,128)}, f32[8,128]{1,0:T(8,128)}) custom-call(s32[1]{0:T(128)} %bitcast.refs_0_, f32[576,3072]{1,0:T(8,128)} %get-tuple-element.215.refs_1_.refs_2_, f32[8,3072]{1,0:T(8,128)} %get-tuple-element.469.refs_2_.refs_4_, f32[8,3072]{1,0:T(8,128)} %get-tuple-element.454.refs_1_.refs_3_, ...), custom_call_target="tpu_custom_call" | custom-call | tf_op jit(solution)/shard_map/pallas_call | solution.py:60
  297.4 20.8 %shard_map.284 = (bf16[576,3072]{1,0:T(8,128)(2,1)}, f32[576,1536]{1,0:T(8,128)}, f32[576,1536]{1,0:T(8,128)}, bf16[576,1536]{1,0:T(8,128)(2,1)}, f32[8,128]{1,0:T(8,128)}) custom-call(s32[1]{0:T(128)S(6)} %sub.83.refs_0_, f32[576,3072]{1,0:T(8,128)} %get-tuple-element.211.refs_1_.refs_2_, f32[8,3072]{1,0:T(8,128)} %get-tuple-element.470.refs_2_.refs_4_, ...), custom_call_target="tpu_custom_call" | custom-call | tf_op jit(solution)/shard_map/pallas_call | solution.py:60
  321.7 3.5 shard_map.285
  325.3 38.5 %all-gather.5.cloned.1.call-done = bf16[6144,1536]{1,0:T(8,128)(2,1)} async-done(((bf16[192,1536]{1,0:T(8,128)(2,1)}), bf16[6144,1536]{1,0:T(8,128)(2,1)}) %all-gather.5.cloned.1.call-update) | async-done | bytes 18874384 | tf_op jit(solution)/shard_map/all_gather | solution.py:1177
  364.4 23.9 %shard_map.288 = (bf16[896,4608]{1,0:T(8,128)(2,1)}, bf16[576,1536]{1,0:T(8,128)(2,1)}, f32[8,128]{1,0:T(8,128)}) custom-call(bf16[896,1536]{1,0:T(8,128)(2,1)} %get-tuple-element.220.refs_0_.refs_5_, bf16[576,1536]{1,0:T(8,128)(2,1)} %get-tuple-element.440.refs_1_.refs_4_, f32[8,4608]{1,0:T(8,128)} %broadcast_in_dim.140.refs_2_, ...), custom_call_target="tpu_custom_call" | custom-call | tf_op jit(solution)/shard_map/pallas_call | solution.py:60
  388.3 57.0 %shard_map.289 = (bf16[576,1536]{1,0:T(8,128)(2,1)}, bf16[576,1536]{1,0:T(8,128)(2,1)}, bf16[896,1536]{1,0:T(8,128)(2,1)}, bf16[896,1536]{1,0:T(8,128)(2,1)}, f32[8,128]{1,0:T(8,128)}) custom-call(bf16[896,4608]{1,0:T(8,128)(2,1)} %get-tuple-element.222.refs_0_.refs_1_.refs_2_, bf16[896,4608]{1,0:T(8,128)(2,1)} %get-tuple-element.222.refs_0_.refs_1_.refs_2_, ...), custom_call_target="tpu_custom_call" | custom-call | tf_op jit(solution)/shard_map/pallas_call | solution.py:60
  445.3 15.0 %shard_map.290 = (bf16[3072,1536]{1,0:T(8,128)(2,1)}, f32[8,128]{1,0:T(8,128)}) custom-call(s32[1]{0:T(128)} %bitcast.25.refs_0_, bf16[576,1536]{1,0:T(8,128)(2,1)} %get-tuple-element.227.refs_1_.refs_0_, bf16[896,1536]{1,0:T(8,128)(2,1)} %get-tuple-element.228.refs_2_.refs_1_, bf16[896,1536]{1,0:T(8,128)(2,1)} %get-tuple-element.229.refs_3_.refs_2_, ...), custom_call_target="tpu_custom_call" | custom-call | tf_op jit(solution)/shard_map/pallas_call | solution.py:60
  460.9 19.7 %shard_map.291 = (f32[576,1536]{1,0:T(8,128)}, bf16[320,1536]{1,0:T(8,128)(2,1)}, f32[8,128]{1,0:T(8,128)}) custom-call(bf16[576,1536]{1,0:T(8,128)(2,1)} %get-tuple-element.227.refs_1_.refs_0_, bf16[896,1536]{1,0:T(8,128)(2,1)} %get-tuple-element.228.refs_2_.refs_1_, bf16[896,1536]{1,0:T(8,128)(2,1)} %get-tuple-element.229.refs_3_.refs_2_, ...), custom_call_target="tpu_custom_call" | custom-call | tf_op jit(solution)/shard_map/pallas_call | solution.py:60
  480.6 3.5 convolution_convert_fusion
  486.5 16.1 %shard_map.292 = (bf16[3072,1536]{1,0:T(8,128)(2,1)}, f32[8,128]{1,0:T(8,128)}) custom-call(s32[1]{0:T(128)} %bitcast.refs_0_, bf16[576,1536]{1,0:T(8,128)(2,1)} %get-tuple-element.227.refs_1_.refs_0_, bf16[896,1536]{1,0:T(8,128)(2,1)} %get-tuple-element.228.refs_2_.refs_1_, bf16[896,1536]{1,0:T(8,128)(2,1)} %get-tuple-element.229.refs_3_.refs_2_, ...), custom_call_target="tpu_custom_call" | custom-call | tf_op jit(solution)/shard_map/pallas_call | solution.py:60
  503.9 6.0 shard_map.293
  514.1 11.7 %shard_map.294 = (f32[576,1536]{1,0:T(8,128)}, bf16[576,1536]{1,0:T(8,128)(2,1)}, f32[8,3072]{1,0:T(8,128)}, f32[8,1536]{1,0:T(8,128)}, f32[8,128]{1,0:T(8,128)}) custom-call(f32[576,1536]{1,0:T(8,128)} %get-tuple-element.232.refs_0_, f32[576,1536]{1,0:T(8,128)} %get-tuple-element.226.refs_1_, f32[576,1536]{1,0:T(8,128)} %get-tuple-element.233.refs_2_, ...), custom_call_target="tpu_custom_call" | custom-call | tf_op jit(solution)/shard_map/pallas_call | solution.py:60
  525.8 18.4 %shard_map.295 = (f32[576,3072]{1,0:T(8,128)}, f32[8,3072]{1,0:T(8,128)}, f32[8,3072]{1,0:T(8,128)}, bf16[3072,1536]{1,0:T(8,128)(2,1)}, f32[8,128]{1,0:T(8,128)}) custom-call(s32[1]{0:T(128)S(6)} %sub.83.refs_0_, bf16[576,1536]{1,0:T(8,128)(2,1)} %get-tuple-element.240.refs_1_, f32[576,3072]{1,0:T(8,128)} %get-tuple-element.211.refs_1_.refs_2_, ...), custom_call_target="tpu_custom_call" | custom-call | tf_op jit(solution)/shard_map/pallas_call | solution.py:60
  544.1 18.4 %shard_map.296 = (f32[576,3072]{1,0:T(8,128)}, f32[8,3072]{1,0:T(8,128)}, f32[8,3072]{1,0:T(8,128)}, bf16[3072,1536]{1,0:T(8,128)(2,1)}, f32[8,128]{1,0:T(8,128)}) custom-call(s32[1]{0:T(128)} %bitcast.refs_0_, bf16[576,1536]{1,0:T(8,128)(2,1)} %get-tuple-element.240.refs_1_, f32[576,3072]{1,0:T(8,128)} %get-tuple-element.215.refs_1_.refs_2_, ...), custom_call_target="tpu_custom_call" | custom-call | tf_op jit(solution)/shard_map/pallas_call | solution.py:60
  565.1 6.8 shard_map.297
  578.6 23.6 %shard_map.298 = (f32[8,3072]{1,0:T(8,128)}, f32[576,1536]{1,0:T(8,128)}, bf16[3072,1536]{1,0:T(8,128)(2,1)}, f32[8,128]{1,0:T(8,128)}) custom-call(f32[576,3072]{1,0:T(8,128)} %get-tuple-element.249.refs_0_, f32[576,3072]{1,0:T(8,128)} %get-tuple-element.211.refs_1_.refs_2_, f32[576,3072]{1,0:T(8,128)} %get-tuple-element.250.refs_2_, ...), custom_call_target="tpu_custom_call" | custom-call | tf_op jit(solution)/shard_map/pallas_call | solution.py:60
  603.8 4.0 shard_map.299
  612.2 11.4 %shard_map.301 = (bf16[2,2,2,192,640]{4,3,2,1,0:T(8,128)(2,1)}, bf16[2,2,2,192,640]{4,3,2,1,0:T(8,128)(2,1)}, bf16[2,2,2,192,640]{4,3,2,1,0:T(8,128)(2,1)}, bf16...) custom-call(s32[1]{0:T(128)} %bitcast.26.refs_0_, ...), custom_call_target="tpu_custom_call" | custom-call | tf_op jit(solution)/shard_map/pallas_call | solution.py:60
  634.1 24.6 %shard_map.303 = (f32[8,3072]{1,0:T(8,128)}, f32[576,1536]{1,0:T(8,128)}, bf16[3072,1536]{1,0:T(8,128)(2,1)}, f32[8,128]{1,0:T(8,128)}) custom-call(f32[576,3072]{1,0:T(8,128)} %get-tuple-element.245.refs_0_, f32[576,3072]{1,0:T(8,128)} %get-tuple-element.215.refs_1_.refs_2_, f32[576,3072]{1,0:T(8,128)} %get-tuple-element.246.refs_2_, ...), custom_call_target="tpu_custom_call" | custom-call | tf_op jit(solution)/shard_map/pallas_call | solution.py:60
  659.3 7.8 shard_map.304
  671.9 5.7 shard_map.309
  692.7 19.9 %shard_map.310 = (f32[576,1536]{1,0:T(8,128)}, f32[16,1536]{1,0:T(8,128)}, f32[8,128]{1,0:T(8,128)}) custom-call(f32[576,1536]{1,0:T(8,128)} %get-tuple-element.283.refs_0_, f32[576,1536]{1,0:T(8,128)} %get-tuple-element.284.refs_1_, f32[576,128]{1,0:T(8,128)} %get-tuple-element.285.refs_2_, f32[576,1536]{1,0:T(8,128)} %bitcast.98, ...), custom_call_target="tpu_custom_call" | custom-call | tf_op jit(solution)/shard_map/pallas_call | solution.py:60
  713.4 3.4 shard_map.312
  725.1 11.8 %shard_map.314 = (bf16[2,2,2,192,640]{4,3,2,1,0:T(8,128)(2,1)}, bf16[2,2,2,192,640]{4,3,2,1,0:T(8,128)(2,1)}, bf16[2,2,2,192,640]{4,3,2,1,0:T(8,128)(2,1)}, bf16...) custom-call(s32[1]{0:T(128)} %bitcast.26.refs_0_, ...), custom_call_target="tpu_custom_call" | custom-call | tf_op jit(solution)/shard_map/pallas_call | solution.py:60
  747.4 27.8 %collective-permute-done.48.refs_1_ = bf16[1,192,1536]{2,1,0:T(8,128)(2,1)S(1)} collective-permute-done((bf16[1,192,1536]{2,1,0:T(8,128)(2,1)}, bf16[1,192,1536]{2,1,0:T(8,128)(2,1)S(1)}, u32[]{:S(2)}, u32[]{:S(2)}) %collective-permute-start.48) | collective-permute-done | bytes 589856 | tf_op jit(solution)/shard_map/ppermute | solution.py:31
  781.2 4.4 collective-permute-done.45.refs_4_
  786.9 5.9 shard_map.321
  796.8 10.2 %collective-permute-done.52.refs_8_ = f32[2,2,64,128]{3,2,1,0:T(8,128)S(1)} collective-permute-done((f32[2,2,64,128]{3,2,1,0:T(8,128)}, f32[2,2,64,128]{3,2,1,0:T(8,128)S(1)}, u32[]{:S(2)}, u32[]{:S(2)}) %collective-permute-start.52) | collective-permute-done | bytes 131104 | tf_op jit(solution)/shard_map/ppermute | solution.py:31
  807.0 8.4 collective-permute-done.49.refs_2_
  817.7 3.9 shard_map.322
  825.4 4.6 collective-permute-done.56.refs_8_
  844.7 7.9 collective-permute-done.57.refs_1_
  (455 shorter events, 185.4 us)
Async XLA Ops:
  7.2 273.4 %all-gather.3.cloned.1.call-start = ((), (), s32[]{:S(2)}) async-start(), calls=%async_computation | async-start | bytes 23519232 | tf_op jit(solution)/shard_map/all_gather | solution.py:1177
  8.7 30.8 %collective-permute-start = (bf16[1,192,1536]{2,1,0:T(8,128)(2,1)S(1)}, bf16[1,192,1536]{2,1,0:T(8,128)(2,1)S(1)}, u32[]{:S(2)}, u32[]{:S(2)}) collective-permute-start(bf16[1,192,1536]{2,1,0:T(8,128)(2,1)S(1)} %convert_bitcast_fusion.1.refs_0_.refs_1_.refs_2_), channel_id=1, source_target_pairs={{0,8},{1,9},{2,10},{3,11},{4,12},{5,13},{6,14},{7,15},{8,0},{9,1},... | collective-permute-start | bytes 1769480 | tf_op jit(solution)/shard_map/ppermute | solution.py:31
  16.8 22.7 %collective-permute-start.1 = (bf16[1,64,128]{2,1,0:T(8,128)(2,1)S(1)}, bf16[1,64,128]{2,1,0:T(8,128)(2,1)S(1)}, u32[]{:S(2)}, u32[]{:S(2)}) collective-permute-start(bf16[1,64,128]{2,1,0:T(8,128)(2,1)S(1)} %bitcast.124), channel_id=1, source_target_pairs={{0,8},{1,9},{2,10},{3,11},{4,12},{5,13},{6,14},{7,15},{8,0},{9,1},... | collective-permute-start | bytes 49160 | tf_op jit(solution)/shard_map/ppermute | solution.py:31
  43.5 320.3 %all-gather.5.cloned.1.call-start = ((), (), s32[]{:S(2)}) async-start(), calls=%async_computation.1 | async-start | bytes 19464192 | tf_op jit(solution)/shard_map/all_gather | solution.py:1177
  44.4 13.5 %collective-permute-start.2 = (bf16[2,192,640]{2,1,0:T(8,128)(2,1)S(1)}, bf16[2,192,640]{2,1,0:T(8,128)(2,1)S(1)}, u32[]{:S(2)}, u32[]{:S(2)}) collective-permute-start(bf16[2,192,640]{2,1,0:T(8,128)(2,1)S(1)} %copy-done.37), channel_id=1, source_target_pairs={{0,4},{1,5},{2,6},{3,7},{4,0},{5,1},{6,2},{7,3},{8,12},{9,13},{10,... | collective-permute-start | bytes 1474568 | tf_op jit(solution)/shard_map/ppermute | solution.py:31
  45.1 16.0 %collective-permute-start.3 = (bf16[2,192,640]{2,1,0:T(8,128)(2,1)S(1)}, bf16[2,192,640]{2,1,0:T(8,128)(2,1)S(1)}, u32[]{:S(2)}, u32[]{:S(2)}) collective-permute-start(bf16[2,192,640]{2,1,0:T(8,128)(2,1)S(1)} %copy-done.38), channel_id=1, source_target_pairs={{0,1},{1,0},{2,3},{3,2},{4,5},{5,4},{6,7},{7,6},{8,9},{9,8},{10,11... | collective-permute-start | bytes 1474568 | tf_op jit(solution)/shard_map/ppermute | solution.py:31
  66.4 25.7 %collective-permute-start.6 = (bf16[4,192,640]{2,1,0:T(8,128)(2,1)}, bf16[4,192,640]{2,1,0:T(8,128)(2,1)S(1)}, u32[]{:S(2)}, u32[]{:S(2)}) collective-permute-start(bf16[4,192,640]{2,1,0:T(8,128)(2,1)} %get-tuple-element.195.refs_0_), channel_id=1, source_target_pairs={{0,2},{1,3},{2,0},{3,1},{4,6},{5,7},{6,4},{7,5},{8,10},{9,11},{10,... | collective-permute-start | bytes 2949128 | tf_op jit(solution)/shard_map/ppermute | solution.py:31
  67.9 48.4 %collective-permute-start.7 = (bf16[4,192,640]{2,1,0:T(8,128)(2,1)}, bf16[4,192,640]{2,1,0:T(8,128)(2,1)S(1)}, u32[]{:S(2)}, u32[]{:S(2)}) collective-permute-start(bf16[4,192,640]{2,1,0:T(8,128)(2,1)} %get-tuple-element.196.refs_1_), channel_id=1, source_target_pairs={{0,4},{1,5},{2,6},{3,7},{4,0},{5,1},{6,2},{7,3},{8,12},{9,13},{10,... | collective-permute-start | bytes 2949128 | tf_op jit(solution)/shard_map/ppermute | solution.py:31
  122.8 73.8 %collective-permute-start.10 = (bf16[8,192,640]{2,1,0:T(8,128)(2,1)}, bf16[8,192,640]{2,1,0:T(8,128)(2,1)S(1)}, u32[]{:S(2)}, u32[]{:S(2)}) collective-permute-start(bf16[8,192,640]{2,1,0:T(8,128)(2,1)} %get-tuple-element.200.refs_3_), channel_id=1, source_target_pairs={{0,1},{1,0},{2,3},{3,2},{4,5},{5,4},{6,7},{7,6},{8,9},{9,8},{10,11... | collective-permute-start | bytes 5898248 | tf_op jit(solution)/shard_map/ppermute | solution.py:31
  124.3 74.8 %collective-permute-start.11 = (bf16[8,192,640]{2,1,0:T(8,128)(2,1)}, bf16[8,192,640]{2,1,0:T(8,128)(2,1)}, u32[]{:S(2)}, u32[]{:S(2)}) collective-permute-start(bf16[8,192,640]{2,1,0:T(8,128)(2,1)} %get-tuple-element.201.refs_5_), channel_id=1, source_target_pairs={{0,2},{1,3},{2,0},{3,1},{4,6},{5,7},{6,4},{7,5},{8,10},{9,11},{10,... | collective-permute-start | bytes 5898248 | tf_op jit(solution)/shard_map/ppermute | solution.py:31
  126.0 46.5 %collective-permute-start.12 = (bf16[8,192,256]{2,1,0:T(8,128)(2,1)}, bf16[8,192,256]{2,1,0:T(8,128)(2,1)S(1)}, u32[]{:S(2)}, u32[]{:S(2)}) collective-permute-start(bf16[8,192,256]{2,1,0:T(8,128)(2,1)} %get-tuple-element.202.refs_7_), channel_id=1, source_target_pairs={{0,4},{1,5},{2,6},{3,7},{4,0},{5,1},{6,2},{7,3},{8,12},{9,13},{10,... | collective-permute-start | bytes 2359304 | tf_op jit(solution)/shard_map/ppermute | solution.py:31
  127.4 45.0 %collective-permute-start.13 = (bf16[8,64,128]{2,1,0:T(8,128)(2,1)S(1)}, bf16[8,64,128]{2,1,0:T(8,128)(2,1)S(1)}, u32[]{:S(2)}, u32[]{:S(2)}) collective-permute-start(bf16[8,64,128]{2,1,0:T(8,128)(2,1)S(1)} %copy-done.64), channel_id=1, source_target_pairs={{0,4},{1,5},{2,6},{3,7},{4,0},{5,1},{6,2},{7,3},{8,12},{9,13},{10,... | collective-permute-start | bytes 393224 | tf_op jit(solution)/shard_map/ppermute | solution.py:31
  213.2 50.4 %collective-permute-start.15 = (bf16[16,192,1536]{2,1,0:T(8,128)(2,1)}, bf16[16,192,1536]{2,1,0:T(8,128)(2,1)}, u32[]{:S(2)}, u32[]{:S(2)}) collective-permute-start(bf16[16,192,1536]{2,1,0:T(8,128)(2,1)} %get-tuple-element.208.refs_3_.refs_8_), channel_id=1, source_target_pairs={{0,16},{16,0},{1,17},{17,1},{2,18},{18,2},{3,19},{19,3},{4,20},{20... | collective-permute-start | bytes 28311560 | tf_op jit(solution)/shard_map/ppermute | solution.py:31
  460.3 26.2 %collective-permute-start.16 = (bf16[3072,1536]{1,0:T(8,128)(2,1)}, bf16[3072,1536]{1,0:T(8,128)(2,1)}, u32[]{:S(2)}, u32[]{:S(2)}) collective-permute-start(bf16[3072,1536]{1,0:T(8,128)(2,1)} %get-tuple-element.234), channel_id=1, source_target_pairs={{0,16},{16,0},{1,17},{17,1},{2,18},{18,2},{3,19},{19,3},{4,20},{20... | collective-permute-start | bytes 28311560 | tf_op jit(solution)/shard_map/ppermute | solution.py:31
  486.2 16.3 %collective-permute-start.17 = (bf16[16,40,1536]{2,1,0:T(8,128)(2,1)}, bf16[16,40,1536]{2,1,0:T(8,128)(2,1)S(1)}, u32[]{:S(2)}, u32[]{:S(2)}) collective-permute-start(bf16[16,40,1536]{2,1,0:T(8,128)(2,1)} %get-tuple-element.446), channel_id=1, source_target_pairs={{0,16},{16,0},{1,17},{17,1},{2,18},{18,2},{3,19},{19,3},{4,20},{20... | collective-permute-start | bytes 5898248 | tf_op jit(solution)/shard_map/ppermute | solution.py:31
  509.9 52.7 %collective-permute-start.18 = (bf16[2,2,2,192,640]{4,3,2,1,0:T(8,128)(2,1)}, bf16[2,2,2,192,640]{4,3,2,1,0:T(8,128)(2,1)S(1)}, u32[]{:S(2)}, u32[]{:S(2)}) collective-permute-start(bf16[2,2,2,192,640]{4,3,2,1,0:T(8,128)(2,1)} %get-tuple-element.251), channel_id=1, source_target_pairs={{0,1},{1,0},{2,3},{3,2},{4,5},{5,4},{6,7},{7,6},{8,9},{9,8},{10,11... | collective-permute-start | bytes 5898248 | tf_op jit(solution)/shard_map/ppermute | solution.py:31
  511.4 51.2 %collective-permute-start.19 = (bf16[2,2,2,192,640]{4,3,2,1,0:T(8,128)(2,1)}, bf16[2,2,2,192,640]{4,3,2,1,0:T(8,128)(2,1)S(1)}, u32[]{:S(2)}, u32[]{:S(2)}) collective-permute-start(bf16[2,2,2,192,640]{4,3,2,1,0:T(8,128)(2,1)} %get-tuple-element.252), channel_id=1, source_target_pairs={{0,2},{1,3},{2,0},{3,1},{4,6},{5,7},{6,4},{7,5},{8,10},{9,11},{10,... | collective-permute-start | bytes 5898248 | tf_op jit(solution)/shard_map/ppermute | solution.py:31
  512.0 50.5 %collective-permute-start.21 = (bf16[2,2,2,40,1536]{4,3,2,1,0:T(8,128)(2,1)}, bf16[2,2,2,40,1536]{4,3,2,1,0:T(8,128)(2,1)S(1)}, u32[]{:S(2)}, u32[]{:S(2)}) collective-permute-start(bf16[2,2,2,40,1536]{4,3,2,1,0:T(8,128)(2,1)} %get-tuple-element.255), channel_id=1, source_target_pairs={{0,4},{1,5},{2,6},{3,7},{4,0},{5,1},{6,2},{7,3},{8,12},{9,13},{10,... | collective-permute-start | bytes 2949128 | tf_op jit(solution)/shard_map/ppermute | solution.py:31
  512.2 50.4 %collective-permute-start.20 = (bf16[2,2,2,192,256]{4,3,2,1,0:T(8,128)(2,1)}, bf16[2,2,2,192,256]{4,3,2,1,0:T(8,128)(2,1)S(1)}, u32[]{:S(2)}, u32[]{:S(2)}) collective-permute-start(bf16[2,2,2,192,256]{4,3,2,1,0:T(8,128)(2,1)} %get-tuple-element.253), channel_id=1, source_target_pairs={{0,4},{1,5},{2,6},{3,7},{4,0},{5,1},{6,2},{7,3},{8,12},{9,13},{10,... | collective-permute-start | bytes 2359304 | tf_op jit(solution)/shard_map/ppermute | solution.py:31
  572.0 40.3 %collective-permute-start.30 = (bf16[3072,1536]{1,0:T(8,128)(2,1)}, bf16[3072,1536]{1,0:T(8,128)(2,1)}, u32[]{:S(2)}, u32[]{:S(2)}) collective-permute-start(bf16[3072,1536]{1,0:T(8,128)(2,1)} %shard_map.300), channel_id=1, source_target_pairs={{0,16},{16,0},{1,17},{17,1},{2,18},{18,2},{3,19},{19,3},{4,20},{20... | collective-permute-start | bytes 28311560 | tf_op jit(solution)/shard_map/ppermute | solution.py:31
  573.0 29.2 %collective-permute-start.22 = (bf16[2,2,192,640]{3,2,1,0:T(8,128)(2,1)}, bf16[2,2,192,640]{3,2,1,0:T(8,128)(2,1)S(1)}, u32[]{:S(2)}, u32[]{:S(2)}) collective-permute-start(bf16[2,2,192,640]{3,2,1,0:T(8,128)(2,1)} %get-tuple-element.260), channel_id=1, source_target_pairs={{0,2},{1,3},{2,0},{3,1},{4,6},{5,7},{6,4},{7,5},{8,10},{9,11},{10,... | collective-permute-start | bytes 2949128 | tf_op jit(solution)/shard_map/ppermute | solution.py:31
  574.5 27.8 %collective-permute-start.23 = (bf16[2,2,192,640]{3,2,1,0:T(8,128)(2,1)}, bf16[2,2,192,640]{3,2,1,0:T(8,128)(2,1)S(1)}, u32[]{:S(2)}, u32[]{:S(2)}) collective-permute-start(bf16[2,2,192,640]{3,2,1,0:T(8,128)(2,1)} %get-tuple-element.262), channel_id=1, source_target_pairs={{0,4},{1,5},{2,6},{3,7},{4,0},{5,1},{6,2},{7,3},{8,12},{9,13},{10,... | collective-permute-start | bytes 2949128 | tf_op jit(solution)/shard_map/ppermute | solution.py:31
  574.8 27.4 %collective-permute-start.24 = (bf16[2,2,192,256]{3,2,1,0:T(8,128)(2,1)}, bf16[2,2,192,256]{3,2,1,0:T(8,128)(2,1)S(1)}, u32[]{:S(2)}, u32[]{:S(2)}) collective-permute-start(bf16[2,2,192,256]{3,2,1,0:T(8,128)(2,1)} %get-tuple-element.264), channel_id=1, source_target_pairs={{0,1},{1,0},{2,3},{3,2},{4,5},{5,4},{6,7},{7,6},{8,9},{9,8},{10,11... | collective-permute-start | bytes 1179656 | tf_op jit(solution)/shard_map/ppermute | solution.py:31
  575.5 26.8 %collective-permute-start.25 = (bf16[2,2,40,1536]{3,2,1,0:T(8,128)(2,1)}, bf16[2,2,40,1536]{3,2,1,0:T(8,128)(2,1)S(1)}, u32[]{:S(2)}, u32[]{:S(2)}) collective-permute-start(bf16[2,2,40,1536]{3,2,1,0:T(8,128)(2,1)} %get-tuple-element.266), channel_id=1, source_target_pairs={{0,1},{1,0},{2,3},{3,2},{4,5},{5,4},{6,7},{7,6},{8,9},{9,8},{10,11... | collective-permute-start | bytes 1474568 | tf_op jit(solution)/shard_map/ppermute | solution.py:31
  607.7 16.0 %collective-permute-start.26 = (bf16[2,192,640]{2,1,0:T(8,128)(2,1)}, bf16[2,192,640]{2,1,0:T(8,128)(2,1)S(1)}, u32[]{:S(2)}, u32[]{:S(2)}) collective-permute-start(bf16[2,192,640]{2,1,0:T(8,128)(2,1)} %get-tuple-element.269), channel_id=1, source_target_pairs={{0,4},{1,5},{2,6},{3,7},{4,0},{5,1},{6,2},{7,3},{8,12},{9,13},{10,... | collective-permute-start | bytes 1474568 | tf_op jit(solution)/shard_map/ppermute | solution.py:31
  609.7 14.1 %collective-permute-start.27 = (bf16[2,192,640]{2,1,0:T(8,128)(2,1)}, bf16[2,192,640]{2,1,0:T(8,128)(2,1)S(1)}, u32[]{:S(2)}, u32[]{:S(2)}) collective-permute-start(bf16[2,192,640]{2,1,0:T(8,128)(2,1)} %get-tuple-element.271), channel_id=1, source_target_pairs={{0,1},{1,0},{2,3},{3,2},{4,5},{5,4},{6,7},{7,6},{8,9},{9,8},{10,11... | collective-permute-start | bytes 1474568 | tf_op jit(solution)/shard_map/ppermute | solution.py:31
  610.2 13.5 %collective-permute-start.29 = (bf16[2,40,1536]{2,1,0:T(8,128)(2,1)}, bf16[2,40,1536]{2,1,0:T(8,128)(2,1)S(1)}, u32[]{:S(2)}, u32[]{:S(2)}) collective-permute-start(bf16[2,40,1536]{2,1,0:T(8,128)(2,1)} %get-tuple-element.275), channel_id=1, source_target_pairs={{0,2},{1,3},{2,0},{3,1},{4,6},{5,7},{6,4},{7,5},{8,10},{9,11},{10,... | collective-permute-start | bytes 737288 | tf_op jit(solution)/shard_map/ppermute | solution.py:31
  627.9 42.7 %collective-permute-start.31 = (bf16[2,2,2,192,640]{4,3,2,1,0:T(8,128)(2,1)}, bf16[2,2,2,192,640]{4,3,2,1,0:T(8,128)(2,1)}, u32[]{:S(2)}, u32[]{:S(2)}) collective-permute-start(bf16[2,2,2,192,640]{4,3,2,1,0:T(8,128)(2,1)} %shard_map.305), channel_id=1, source_target_pairs={{0,1},{1,0},{2,3},{3,2},{4,5},{5,4},{6,7},{7,6},{8,9},{9,8},{10,11... | collective-permute-start | bytes 5898248 | tf_op jit(solution)/shard_map/ppermute | solution.py:31
  629.5 42.4 %collective-permute-start.32 = (bf16[2,2,2,192,640]{4,3,2,1,0:T(8,128)(2,1)S(1)}, bf16[2,2,2,192,640]{4,3,2,1,0:T(8,128)(2,1)}, u32[]{:S(2)}, u32[]{:S(2)}) collective-permute-start(bf16[2,2,2,192,640]{4,3,2,1,0:T(8,128)(2,1)S(1)} %copy-done.9), channel_id=1, source_target_pairs={{0,2},{1,3},{2,0},{3,1},{4,6},{5,7},{6,4},{7,5},{8,10},{9,11},{10,... | collective-permute-start | bytes 5898248 | tf_op jit(solution)/shard_map/ppermute | solution.py:31
  631.0 39.4 %collective-permute-start.33 = (bf16[2,2,2,192,256]{4,3,2,1,0:T(8,128)(2,1)}, bf16[2,2,2,192,256]{4,3,2,1,0:T(8,128)(2,1)S(1)}, u32[]{:S(2)}, u32[]{:S(2)}) collective-permute-start(bf16[2,2,2,192,256]{4,3,2,1,0:T(8,128)(2,1)} %shard_map.307), channel_id=1, source_target_pairs={{0,4},{1,5},{2,6},{3,7},{4,0},{5,1},{6,2},{7,3},{8,12},{9,13},{10,... | collective-permute-start | bytes 2359304 | tf_op jit(solution)/shard_map/ppermute | solution.py:31
  631.1 36.0 %collective-permute-start.34 = (bf16[1,192,1536]{2,1,0:T(8,128)(2,1)}, bf16[1,192,1536]{2,1,0:T(8,128)(2,1)S(1)}, u32[]{:S(2)}, u32[]{:S(2)}) collective-permute-start(bf16[1,192,1536]{2,1,0:T(8,128)(2,1)} %get-tuple-element.295), channel_id=1, source_target_pairs={{0,8},{1,9},{2,10},{3,11},{4,12},{5,13},{6,14},{7,15},{8,0},{9,1},... | collective-permute-start | bytes 1769480 | tf_op jit(solution)/shard_map/ppermute | solution.py:31
  633.0 34.1 %collective-permute-start.35 = (bf16[1,40,1536]{2,1,0:T(8,128)(2,1)}, bf16[1,40,1536]{2,1,0:T(8,128)(2,1)S(1)}, u32[]{:S(2)}, u32[]{:S(2)}) collective-permute-start(bf16[1,40,1536]{2,1,0:T(8,128)(2,1)} %get-tuple-element.297), channel_id=1, source_target_pairs={{0,8},{1,9},{2,10},{3,11},{4,12},{5,13},{6,14},{7,15},{8,0},{9,1},... | collective-permute-start | bytes 368648 | tf_op jit(solution)/shard_map/ppermute | solution.py:31
  677.6 46.7 %collective-permute-start.36 = (bf16[3072,1536]{1,0:T(8,128)(2,1)}, bf16[3072,1536]{1,0:T(8,128)(2,1)}, u32[]{:S(2)}, u32[]{:S(2)}) collective-permute-start(bf16[3072,1536]{1,0:T(8,128)(2,1)} %shard_map.311), channel_id=1, source_target_pairs={{0,16},{16,0},{1,17},{17,1},{2,18},{18,2},{3,19},{19,3},{4,20},{20... | collective-permute-start | bytes 28311560 | tf_op jit(solution)/shard_map/ppermute | solution.py:31
  682.6 30.0 %collective-permute-start.37 = (bf16[2,2,192,640]{3,2,1,0:T(8,128)(2,1)}, bf16[2,2,192,640]{3,2,1,0:T(8,128)(2,1)}, u32[]{:S(2)}, u32[]{:S(2)}) collective-permute-start(bf16[2,2,192,640]{3,2,1,0:T(8,128)(2,1)} %get-tuple-element.306), channel_id=1, source_target_pairs={{0,2},{1,3},{2,0},{3,1},{4,6},{5,7},{6,4},{7,5},{8,10},{9,11},{10,... | collective-permute-start | bytes 2949128 | tf_op jit(solution)/shard_map/ppermute | solution.py:31
  684.2 28.5 %collective-permute-start.38 = (bf16[2,2,192,640]{3,2,1,0:T(8,128)(2,1)}, bf16[2,2,192,640]{3,2,1,0:T(8,128)(2,1)}, u32[]{:S(2)}, u32[]{:S(2)}) collective-permute-start(bf16[2,2,192,640]{3,2,1,0:T(8,128)(2,1)} %get-tuple-element.308), channel_id=1, source_target_pairs={{0,4},{1,5},{2,6},{3,7},{4,0},{5,1},{6,2},{7,3},{8,12},{9,13},{10,... | collective-permute-start | bytes 2949128 | tf_op jit(solution)/shard_map/ppermute | solution.py:31
  689.0 23.6 %collective-permute-start.39 = (bf16[2,2,192,256]{3,2,1,0:T(8,128)(2,1)S(1)}, bf16[2,2,192,256]{3,2,1,0:T(8,128)(2,1)S(1)}, u32[]{:S(2)}, u32[]{:S(2)}) collective-permute-start(bf16[2,2,192,256]{3,2,1,0:T(8,128)(2,1)S(1)} %copy-done.85), channel_id=1, source_target_pairs={{0,1},{1,0},{2,3},{3,2},{4,5},{5,4},{6,7},{7,6},{8,9},{9,8},{10,11... | collective-permute-start | bytes 1179656 | tf_op jit(solution)/shard_map/ppermute | solution.py:31
  721.5 15.4 %collective-permute-start.41 = (bf16[2,192,640]{2,1,0:T(8,128)(2,1)S(1)}, bf16[2,192,640]{2,1,0:T(8,128)(2,1)S(1)}, u32[]{:S(2)}, u32[]{:S(2)}) collective-permute-start(bf16[2,192,640]{2,1,0:T(8,128)(2,1)S(1)} %copy-done.84), channel_id=1, source_target_pairs={{0,4},{1,5},{2,6},{3,7},{4,0},{5,1},{6,2},{7,3},{8,12},{9,13},{10,... | collective-permute-start | bytes 1474568 | tf_op jit(solution)/shard_map/ppermute | solution.py:31
  722.3 14.6 %collective-permute-start.42 = (bf16[2,192,640]{2,1,0:T(8,128)(2,1)S(1)}, bf16[2,192,640]{2,1,0:T(8,128)(2,1)S(1)}, u32[]{:S(2)}, u32[]{:S(2)}) collective-permute-start(bf16[2,192,640]{2,1,0:T(8,128)(2,1)S(1)} %copy-done.83), channel_id=1, source_target_pairs={{0,1},{1,0},{2,3},{3,2},{4,5},{5,4},{6,7},{7,6},{8,9},{9,8},{10,11... | collective-permute-start | bytes 1474568 | tf_op jit(solution)/shard_map/ppermute | solution.py:31
  723.8 13.1 %collective-permute-start.43 = (bf16[2,192,256]{2,1,0:T(8,128)(2,1)S(1)}, bf16[2,192,256]{2,1,0:T(8,128)(2,1)S(1)}, u32[]{:S(2)}, u32[]{:S(2)}) collective-permute-start(bf16[2,192,256]{2,1,0:T(8,128)(2,1)S(1)} %copy-done.86), channel_id=1, source_target_pairs={{0,2},{1,3},{2,0},{3,1},{4,6},{5,7},{6,4},{7,5},{8,10},{9,11},{10,... | collective-permute-start | bytes 589832 | tf_op jit(solution)/shard_map/ppermute | solution.py:31
  740.9 44.8 %collective-permute-start.45 = (bf16[2,2,2,192,640]{4,3,2,1,0:T(8,128)(2,1)}, bf16[2,2,2,192,640]{4,3,2,1,0:T(8,128)(2,1)}, u32[]{:S(2)}, u32[]{:S(2)}) collective-permute-start(bf16[2,2,2,192,640]{4,3,2,1,0:T(8,128)(2,1)} %shard_map.317), channel_id=1, source_target_pairs={{0,2},{1,3},{2,0},{3,1},{4,6},{5,7},{6,4},{7,5},{8,10},{9,11},{10,... | collective-permute-start | bytes 5898248 | tf_op jit(solution)/shard_map/ppermute | solution.py:31
  742.5 44.4 %collective-permute-start.44 = (bf16[2,2,2,192,640]{4,3,2,1,0:T(8,128)(2,1)S(1)}, bf16[2,2,2,192,640]{4,3,2,1,0:T(8,128)(2,1)}, u32[]{:S(2)}, u32[]{:S(2)}) collective-permute-start(bf16[2,2,2,192,640]{4,3,2,1,0:T(8,128)(2,1)S(1)} %copy-done.10), channel_id=1, source_target_pairs={{0,1},{1,0},{2,3},{3,2},{4,5},{5,4},{6,7},{7,6},{8,9},{9,8},{10,11... | collective-permute-start | bytes 5898248 | tf_op jit(solution)/shard_map/ppermute | solution.py:31
  743.9 37.3 %collective-permute-start.46 = (bf16[2,2,2,192,256]{4,3,2,1,0:T(8,128)(2,1)}, bf16[2,2,2,192,256]{4,3,2,1,0:T(8,128)(2,1)S(1)}, u32[]{:S(2)}, u32[]{:S(2)}) collective-permute-start(bf16[2,2,2,192,256]{4,3,2,1,0:T(8,128)(2,1)} %shard_map.318), channel_id=1, source_target_pairs={{0,4},{1,5},{2,6},{3,7},{4,0},{5,1},{6,2},{7,3},{8,12},{9,13},{10,... | collective-permute-start | bytes 2359304 | tf_op jit(solution)/shard_map/ppermute | solution.py:31
  744.3 31.0 %collective-permute-start.48 = (bf16[1,192,1536]{2,1,0:T(8,128)(2,1)}, bf16[1,192,1536]{2,1,0:T(8,128)(2,1)S(1)}, u32[]{:S(2)}, u32[]{:S(2)}) collective-permute-start(bf16[1,192,1536]{2,1,0:T(8,128)(2,1)} %get-tuple-element.337), channel_id=1, source_target_pairs={{0,8},{1,9},{2,10},{3,11},{4,12},{5,13},{6,14},{7,15},{8,0},{9,1},... | collective-permute-start | bytes 1769480 | tf_op jit(solution)/shard_map/ppermute | solution.py:31
  745.9 35.3 %collective-permute-start.47 = (f32[2,2,2,64,128]{4,3,2,1,0:T(8,128)}, f32[2,2,2,64,128]{4,3,2,1,0:T(8,128)S(1)}, u32[]{:S(2)}, u32[]{:S(2)}) collective-permute-start(f32[2,2,2,64,128]{4,3,2,1,0:T(8,128)} %shard_map.319), channel_id=1, source_target_pairs={{0,4},{1,5},{2,6},{3,7},{4,0},{5,1},{6,2},{7,3},{8,12},{9,13},{10,... | collective-permute-start | bytes 786440 | tf_op jit(solution)/shard_map/ppermute | solution.py:31
  792.8 22.6 %collective-permute-start.49 = (bf16[2,2,192,640]{3,2,1,0:T(8,128)(2,1)}, bf16[2,2,192,640]{3,2,1,0:T(8,128)(2,1)S(1)}, u32[]{:S(2)}, u32[]{:S(2)}) collective-permute-start(bf16[2,2,192,640]{3,2,1,0:T(8,128)(2,1)} %get-tuple-element.340), channel_id=1, source_target_pairs={{0,2},{1,3},{2,0},{3,1},{4,6},{5,7},{6,4},{7,5},{8,10},{9,11},{10,... | collective-permute-start | bytes 2949128 | tf_op jit(solution)/shard_map/ppermute | solution.py:31
  794.4 22.4 %collective-permute-start.50 = (bf16[2,2,192,640]{3,2,1,0:T(8,128)(2,1)}, bf16[2,2,192,640]{3,2,1,0:T(8,128)(2,1)S(1)}, u32[]{:S(2)}, u32[]{:S(2)}) collective-permute-start(bf16[2,2,192,640]{3,2,1,0:T(8,128)(2,1)} %get-tuple-element.342), channel_id=1, source_target_pairs={{0,4},{1,5},{2,6},{3,7},{4,0},{5,1},{6,2},{7,3},{8,12},{9,13},{10,... | collective-permute-start | bytes 2949128 | tf_op jit(solution)/shard_map/ppermute | solution.py:31
  836.6 16.0 %collective-permute-start.57 = (f32[1,64,128]{2,1,0:T(8,128)}, f32[1,64,128]{2,1,0:T(8,128)S(1)}, u32[]{:S(2)}, u32[]{:S(2)}) collective-permute-start(f32[1,64,128]{2,1,0:T(8,128)} %get-tuple-element.358), channel_id=1, source_target_pairs={{0,8},{1,9},{2,10},{3,11},{4,12},{5,13},{6,14},{7,15},{8,0},{9,1},... | collective-permute-start | bytes 98312 | tf_op jit(solution)/shard_map/ppermute | solution.py:31
  838.1 26.0 %collective-permute-start.58 = (bf16[1,192,1536]{2,1,0:T(8,128)(2,1)}, bf16[1,192,1536]{2,1,0:T(8,128)(2,1)}, u32[]{:S(2)}, u32[]{:S(2)}) collective-permute-start(bf16[1,192,1536]{2,1,0:T(8,128)(2,1)} %get-tuple-element.362), channel_id=1, source_target_pairs={{0,8},{1,9},{2,10},{3,11},{4,12},{5,13},{6,14},{7,15},{8,0},{9,1},... | collective-permute-start | bytes 1769480 | tf_op jit(solution)/shard_map/ppermute | solution.py:31
  (101 other events, 779.9 us)
Sparse Core Ops, SparseCore 0:
  43.6 190.2 all-gather.2
  236.8 126.9 all-gather.4
